TPU v7x, 32 devices: a whole 2x2x4 slice. The times are simulated.
32 devices in a mesh: sub: 8 (over y, x, core), grp: 4 (over z).
Axes of the slice: x: 2, y: 2, z: 4, core: 2. Of those that a mesh axis runs over, the one named last changes fastest.
Arguments:
- gap_data: float32 [96, 4, 1024], P(None, 'grp', 'sub'), may hold values from -6 to 6
- local_inverse: bfloat16 [96, 96, 4, 1024], P(None, None, 'grp', 'sub')
- stiffness: bfloat16 [2, 96, 96, 4, 1024], P(None, None, None, 'grp', 'sub')
- stiff_column: int32 [4, 1024], P('grp', 'sub'), may hold values from 0 to 1023, as said below
- neighbour: int32 [4, 1024], P('grp', 'sub'), may hold values from -1 to 1022, as said below
- corner_ops: bfloat16 [24, 96, 4, 1024], P(None, None, 'grp', 'sub'), may hold values from -0.625 to 0.625
- corner_index: int32 [4, 4, 1024], P(None, 'grp', 'sub'), may hold values from 0 to 1023
- coarse_inverse: bfloat16 [8, 768, 6144], P('grp', None, 'sub')
Outputs:
- multipliers: float32 [96, 4, 1024], P(None, 'grp', 'sub')
- residual: float32 [96, 4, 1024], P(None, 'grp', 'sub')
Inputs may be any that keep to these rules, and one draw needn't show every extreme that they name: neighbour[y, x] is -1 or lies in [x - 128, x - 1]; every aligned block of 128 subdomains past the first has one entry equal to x - 128. stiff_column[y, x] lies in the same aligned block of 128 subdomains as x, is never x, and stiff_column[y, stiff_column[y, x]] = x; stiffness[1, :, :, y, stiff_column[y, x]] is the transpose of stiffness[1, :, :, y, x].
All inputs are finite; a program needn't handle non-finite values.
Results may differ from a plain program's by a relative error of at most 0.0008.
Values may be sent and summed in bfloat16 or wider, within the bound.
No kernel may reach another device: no remote copies, remote signals or barrier semaphores. Data moves between devices by JAX's collectives and lax.ppermute only.
A program may use at most 128 MiB of HBM per device.

v0:
```python
import jax
import jax.numpy as jnp
from jax import lax
from jax.sharding import PartitionSpec as P

CORNER_DOF = 6
CORNERS_SUB = 4
ITERS = 5


precise = lax.Precision.HIGHEST


def from_behind(block, axis, distance):
    devices = range(lax.axis_size(axis))
    route = [(i - distance, i) for i in devices if i - distance in devices]
    return lax.ppermute(block, axis, route)


def on_device(
    gap_data,
    local_inverse,
    stiffness,
    stiff_column,
    neighbour,
    corner_ops,
    corner_index,
    coarse_inverse,
):
    cells = gap_data.shape[2]
    start = lax.axis_index("sub") * cells
    right_side = gap_data[:, 0, :]
    inverse = local_inverse[:, :, 0, :]
    main_block = stiffness[0, :, :, 0, :]
    coupled_block = stiffness[1, :, :, 0, :]
    column_local = stiff_column[0] - start
    slots = neighbour[0] - (start - cells)
    selector = (slots[None, :] == jnp.arange(2 * cells, dtype=jnp.int32)[:, None]).astype(
        jnp.float32
    )
    operators = corner_ops[:, :, 0, :]
    blocks_own = coarse_inverse.shape[0]
    order = coarse_inverse.shape[1]
    corner_block = order // CORNER_DOF
    owned_count = blocks_own * corner_block
    group_count = owned_count * lax.axis_size("grp")
    corner_table = (
        corner_index[:, 0, :, None] == jnp.arange(group_count, dtype=jnp.int32)[None, None, :]
    ).astype(jnp.float32)

    def jump_in(vector):
        previous = from_behind(vector, "sub", 1)
        joined = jnp.concatenate([previous, vector], axis=1)
        return vector - jnp.dot(
            joined, selector, precision=precise, preferred_element_type=jnp.float32
        )

    def jump_out(vector):
        spread = jnp.dot(vector, selector.T, precision=precise, preferred_element_type=jnp.float32)
        returned = from_behind(spread[:, :cells], "sub", -1)
        return vector - spread[:, cells:] - returned

    def precondition(vector):
        spread = jump_in(vector)
        taken = jnp.take(spread, column_local, axis=1)
        stiff = jnp.einsum(
            "ijx,jx->ix", main_block, spread, precision=precise, preferred_element_type=jnp.float32
        )
        stiff = stiff + jnp.einsum(
            "ijx,jx->ix",
            coupled_block,
            taken,
            precision=precise,
            preferred_element_type=jnp.float32,
        )
        return jump_out(stiff)

    def precond_dot(first, second):
        return lax.psum(jnp.sum(first * second), ("sub", "grp"))

    multipliers = jnp.zeros_like(right_side)
    residual = right_side
    direction = precondition(residual)
    norm_now = precond_dot(residual, direction)
    for iteration in range(ITERS):
        gap = jump_in(direction)
        local = jnp.einsum(
            "ijx,jx->ix", inverse, gap, precision=precise, preferred_element_type=jnp.float32
        )
        parts = jnp.einsum(
            "cix,ix->cx", operators, gap, precision=precise, preferred_element_type=jnp.float32
        )
        parts = parts.reshape(CORNERS_SUB, CORNER_DOF, cells)
        apply_sums = jnp.einsum(
            "kjx,kxm->jm",
            parts,
            corner_table,
            precision=precise,
            preferred_element_type=jnp.float32,
        )
        owned = lax.psum_scatter(apply_sums, "grp", scatter_dimension=1, tiled=True)
        arranged = (
            owned.reshape(CORNER_DOF, blocks_own, corner_block)
            .transpose(1, 0, 2)
            .reshape(blocks_own, order)
        )
        solved = jnp.einsum(
            "bpq,bq->bp",
            coarse_inverse,
            arranged,
            precision=precise,
            preferred_element_type=jnp.float32,
        )
        coarse_solved = (
            solved.reshape(blocks_own, CORNER_DOF, corner_block)
            .transpose(1, 0, 2)
            .reshape(CORNER_DOF, blocks_own * corner_block)
        )
        values = lax.all_gather(coarse_solved, "grp", axis=1, tiled=True)
        picked = jnp.einsum(
            "jm,kxm->kjx",
            values,
            corner_table,
            precision=precise,
            preferred_element_type=jnp.float32,
        )
        picked = picked.reshape(CORNERS_SUB * CORNER_DOF, cells)
        lifted = local + jnp.einsum(
            "cix,cx->ix", operators, picked, precision=precise, preferred_element_type=jnp.float32
        )
        image = jump_out(lifted)
        alpha = norm_now / lax.psum(jnp.sum(direction * image), ("sub", "grp"))
        multipliers = multipliers + alpha * direction
        residual = residual - alpha * image
        if iteration + 1 < ITERS:
            prepared = precondition(residual)
            norm_next = precond_dot(residual, prepared)
            direction = prepared + norm_next / norm_now * direction
            norm_now = norm_next
    return (multipliers[:, None, :], residual[:, None, :])


def solution(mesh):
    in_specs = (
        P(None, "grp", "sub"),
        P(None, None, "grp", "sub"),
        P(None, None, None, "grp", "sub"),
        P("grp", "sub"),
        P("grp", "sub"),
        P(None, None, "grp", "sub"),
        P(None, "grp", "sub"),
        P("grp", None, "sub"),
    )
    out_specs = (P(None, "grp", "sub"), P(None, "grp", "sub"))
    return jax.shard_map(
        on_device, mesh=mesh, in_specs=in_specs, out_specs=out_specs, check_vma=False
    )
```

profile of v0, /device:TPU:0, one launch (start us, length us, event | category | flops | bytes accessed | tf_op | source)
XLA Modules:
  0.0 712.7 jit_solution(5318268757197272331)
XLA Ops:
  22.9 5.2 collective-permute-start.2
  33.3 19.7 %reduce-scatter.6.cloned.1.call-done = f32[6,256]{1,0:T(8,128)} async-done(((f32[6,1024]{1,0:T(8,128)}), f32[6,256]{1,0:T(8,128)}) %reduce-scatter.6.cloned.1.call-update) | async-done | bytes 6160 | tf_op jit(solution)/shard_map/reduce_scatter | solution.py:101
  55.7 13.1 %all_gather.15 = f32[6,1024]{1,0:T(8,128)S(1)} all-gather(f32[6,256]{1,0:T(8,128)S(1)} %bitcast.312), channel_id=1, replica_groups=mesh['sub'=8,'grp'=4] {'grp'}, dimensions={1}, use_global_device_ids=true | all-gather | bytes 30720 | tf_op jit(solution)/shard_map/all_gather | solution.py:119
  74.0 39.3 %all-reduce = (f32[]{:T(128)}, f32[]{:T(128)}) all-reduce(f32[]{:T(128)} %get-tuple-element.18, f32[]{:T(128)} %get-tuple-element.17), channel_id=1, replica_groups=mesh['sub'=8,'grp'=4] {'sub','grp'}, use_global_device_ids=true, to_apply=%region_1.3 | all-reduce | flops 2 | bytes 16 | tf_op jit(solution)/shard_map/psum | solution.py:79
  123.7 4.6 collective-permute-done.5
  128.9 44.1 %psum.72 = f32[]{:T(128)} all-reduce(f32[]{:T(128)} %get-tuple-element.35), channel_id=1, replica_groups=mesh['sub'=8,'grp'=4] {'sub','grp'}, use_global_device_ids=true, to_apply=%region_6.8 | all-reduce | flops 1 | bytes 8 | tf_op jit(solution)/shard_map/psum | solution.py:79
  181.0 19.7 %reduce-scatter.8.cloned.1.call-done = f32[6,256]{1,0:T(8,128)} async-done(((f32[6,1024]{1,0:T(8,128)}), f32[6,256]{1,0:T(8,128)}) %reduce-scatter.8.cloned.1.call-update) | async-done | bytes 6160 | tf_op jit(solution)/shard_map/reduce_scatter | solution.py:101
  203.4 13.1 %all_gather.16 = f32[6,1024]{1,0:T(8,128)S(1)} all-gather(f32[6,256]{1,0:T(8,128)S(1)} %bitcast.313), channel_id=1, replica_groups=mesh['sub'=8,'grp'=4] {'grp'}, dimensions={1}, use_global_device_ids=true | all-gather | bytes 30720 | tf_op jit(solution)/shard_map/all_gather | solution.py:119
  221.7 39.3 %psum.73 = f32[]{:T(128)} all-reduce(f32[]{:T(128)} %get-tuple-element.33), channel_id=1, replica_groups=mesh['sub'=8,'grp'=4] {'sub','grp'}, use_global_device_ids=true, to_apply=%region_9.11 | all-reduce | flops 1 | bytes 8 | tf_op jit(solution)/shard_map/psum | solution.py:132
  271.3 4.6 collective-permute-done.9
  276.5 44.1 %psum.74 = f32[]{:T(128)} all-reduce(f32[]{:T(128)} %get-tuple-element.31), channel_id=1, replica_groups=mesh['sub'=8,'grp'=4] {'sub','grp'}, use_global_device_ids=true, to_apply=%region_11.13 | all-reduce | flops 1 | bytes 8 | tf_op jit(solution)/shard_map/psum | solution.py:79
  328.3 19.9 %reduce-scatter.10.cloned.1.call-done = f32[6,256]{1,0:T(8,128)} async-done(((f32[6,1024]{1,0:T(8,128)}), f32[6,256]{1,0:T(8,128)}) %reduce-scatter.10.cloned.1.call-update) | async-done | bytes 6160 | tf_op jit(solution)/shard_map/reduce_scatter | solution.py:101
  350.9 13.1 %all_gather.17 = f32[6,1024]{1,0:T(8,128)S(1)} all-gather(f32[6,256]{1,0:T(8,128)S(1)} %bitcast.314), channel_id=1, replica_groups=mesh['sub'=8,'grp'=4] {'grp'}, dimensions={1}, use_global_device_ids=true | all-gather | bytes 30720 | tf_op jit(solution)/shard_map/all_gather | solution.py:119
  369.3 39.3 %psum.75 = f32[]{:T(128)} all-reduce(f32[]{:T(128)} %get-tuple-element.29), channel_id=1, replica_groups=mesh['sub'=8,'grp'=4] {'sub','grp'}, use_global_device_ids=true, to_apply=%region_14.16 | all-reduce | flops 1 | bytes 8 | tf_op jit(solution)/shard_map/psum | solution.py:132
  418.9 4.6 collective-permute-done.13
  424.1 44.1 %psum.76 = f32[]{:T(128)} all-reduce(f32[]{:T(128)} %get-tuple-element.27), channel_id=1, replica_groups=mesh['sub'=8,'grp'=4] {'sub','grp'}, use_global_device_ids=true, to_apply=%region_16.18 | all-reduce | flops 1 | bytes 8 | tf_op jit(solution)/shard_map/psum | solution.py:79
  476.0 19.9 %reduce-scatter.12.cloned.1.call-done = f32[6,256]{1,0:T(8,128)} async-done(((f32[6,1024]{1,0:T(8,128)}), f32[6,256]{1,0:T(8,128)}) %reduce-scatter.12.cloned.1.call-update) | async-done | bytes 6160 | tf_op jit(solution)/shard_map/reduce_scatter | solution.py:101
  498.5 13.1 %all_gather.18 = f32[6,1024]{1,0:T(8,128)S(1)} all-gather(f32[6,256]{1,0:T(8,128)S(1)} %bitcast.315), channel_id=1, replica_groups=mesh['sub'=8,'grp'=4] {'grp'}, dimensions={1}, use_global_device_ids=true | all-gather | bytes 30720 | tf_op jit(solution)/shard_map/all_gather | solution.py:119
  516.9 39.3 %psum.77 = f32[]{:T(128)} all-reduce(f32[]{:T(128)} %get-tuple-element.25), channel_id=1, replica_groups=mesh['sub'=8,'grp'=4] {'sub','grp'}, use_global_device_ids=true, to_apply=%region_19.21 | all-reduce | flops 1 | bytes 8 | tf_op jit(solution)/shard_map/psum | solution.py:132
  566.5 4.6 collective-permute-done.17
  571.7 44.1 %psum.78 = f32[]{:T(128)} all-reduce(f32[]{:T(128)} %get-tuple-element.23), channel_id=1, replica_groups=mesh['sub'=8,'grp'=4] {'sub','grp'}, use_global_device_ids=true, to_apply=%region_21.23 | all-reduce | flops 1 | bytes 8 | tf_op jit(solution)/shard_map/psum | solution.py:79
  623.5 20.0 %reduce-scatter.14.cloned.1.call-done = f32[6,256]{1,0:T(8,128)} async-done(((f32[6,1024]{1,0:T(8,128)}), f32[6,256]{1,0:T(8,128)}) %reduce-scatter.14.cloned.1.call-update) | async-done | bytes 6160 | tf_op jit(solution)/shard_map/reduce_scatter | solution.py:101
  646.1 13.1 %all_gather.19 = f32[6,1024]{1,0:T(8,128)S(1)} all-gather(f32[6,256]{1,0:T(8,128)S(1)} %bitcast.316), channel_id=1, replica_groups=mesh['sub'=8,'grp'=4] {'grp'}, dimensions={1}, use_global_device_ids=true | all-gather | bytes 30720 | tf_op jit(solution)/shard_map/all_gather | solution.py:119
  664.5 39.3 %psum.79 = f32[]{:T(128)} all-reduce(f32[]{:T(128)} %get-tuple-element.21), channel_id=1, replica_groups=mesh['sub'=8,'grp'=4] {'sub','grp'}, use_global_device_ids=true, to_apply=%region_24.26 | all-reduce | flops 1 | bytes 8 | tf_op jit(solution)/shard_map/psum | solution.py:132
  (185 shorter events, 124.6 us)
Async XLA Ops:
  7.2 45.8 %reduce-scatter.6.cloned.1.call-start = ((), (), s32[]{:S(2)}) async-start(), calls=%async_computation.5 | async-start | bytes 40960 | tf_op jit(solution)/shard_map/reduce_scatter | solution.py:101
  7.2 3.8 collective-permute-start
  17.5 5.4 collective-permute-start.1
  22.9 6.1 collective-permute-start.2
  30.8 169.9 %reduce-scatter.8.cloned.1.call-start = ((), (), s32[]{:S(2)}) async-start(), calls=%async_computation.6 | async-start | bytes 40960 | tf_op jit(solution)/shard_map/reduce_scatter | solution.py:101
  70.3 3.1 collective-permute-start.3
  114.7 2.2 collective-permute-start.4
  122.4 5.9 collective-permute-start.5
  174.3 2.2 collective-permute-start.6
  178.3 170.0 %reduce-scatter.10.cloned.1.call-start = ((), (), s32[]{:S(2)}) async-start(), calls=%async_computation.7 | async-start | bytes 40960 | tf_op jit(solution)/shard_map/reduce_scatter | solution.py:101
  218.0 3.1 collective-permute-start.7
  262.3 2.2 collective-permute-start.8
  270.0 5.9 collective-permute-start.9
  321.9 2.2 collective-permute-start.10
  325.8 170.1 %reduce-scatter.12.cloned.1.call-start = ((), (), s32[]{:S(2)}) async-start(), calls=%async_computation.8 | async-start | bytes 40960 | tf_op jit(solution)/shard_map/reduce_scatter | solution.py:101
  365.5 3.1 collective-permute-start.11
  409.9 2.2 collective-permute-start.12
  417.6 5.9 collective-permute-start.13
  469.5 2.2 collective-permute-start.14
  473.5 170.0 %reduce-scatter.14.cloned.1.call-start = ((), (), s32[]{:S(2)}) async-start(), calls=%async_computation.9 | async-start | bytes 40960 | tf_op jit(solution)/shard_map/reduce_scatter | solution.py:101
  513.1 3.1 collective-permute-start.15
  557.5 2.2 collective-permute-start.16
  565.2 5.9 collective-permute-start.17
  660.7 3.1 collective-permute-start.19
  (5 other events, 121.2 us)
Sparse Core Ops, SparseCore 0:
  30.9 22.0 reduce-scatter.5
  178.4 22.2 reduce-scatter.7
  326.0 22.2 reduce-scatter.9
  473.6 22.2 reduce-scatter.11
  621.1 22.2 reduce-scatter.13
where the time goes:
time: 723 us; the launch traced here: 713 us
  blocking collectives  439 us (61%)
  waiting for transfers between devices  138 us (19%)
  other arithmetic  42.4 us (6%)
  starting transfers between devices  31.8 us (4%)
  matrix products  27.2 us (4%)
  between operations  26.5 us (4%)
  local copies, waits for them, and re-layouts  7.82 us (1%)
    psum x5, blocking collectives, precond_dot(): return lax.psum(jnp.sum(first * second), ('sub', 'grp'))  216 us
    psum x4, blocking collectives, on_device(): alpha = norm_now / lax.psum(jnp.sum(direction * image), ('sub', 'grp'))  157 us
    reduce_scatter x5, waiting for transfers between devices, on_device(): owned = lax.psum_scatter(apply_sums, 'grp', scatter_dimension=1, tiled=True)  99.3 us
    all_gather x5, blocking collectives, on_device(): values = lax.all_gather(coarse_solved, 'grp', axis=1, tiled=True)  65.6 us
    ppermute x20, waiting for transfers between devices, from_behind(): return lax.ppermute(block, axis, route)  39 us
    ppermute x20, starting transfers between devices, from_behind(): return lax.ppermute(block, axis, route)  31.4 us
    dot_general x5, other arithmetic, precondition(): jnp.einsum('ijx,jx->ix', coupled_block, taken, precision=precise, preferr...  20.7 us
  transfers between devices with their start and end apart: 25, of which 24 were waited for; matrix products, arithmetic and copies ran while one was open for 2% of the time, Pallas kernels for 0%

commit v1 on v0

v1 whole, which is shorter than its diff:
```python
import jax
import jax.numpy as jnp
from jax import lax
from jax.experimental import pallas as pl
from jax.experimental.pallas import tpu as pltpu
from jax.sharding import PartitionSpec as P

CORNER_DOF = 6
CORNERS_SUB = 4
ITERS = 5
ROWS = 8
NN = (((1,), (0,)), ((), ()))
NT = (((1,), (1,)), ((), ()))
F32 = jnp.float32
BF16 = jnp.bfloat16


def pieces_of(value):
    high = value.astype(BF16).astype(F32)
    rest = value - high
    middle = rest.astype(BF16).astype(F32)
    return [high, middle, rest - middle]


def exact_dot(value, table, dims):
    rows = value.shape[0]
    stacked = jnp.concatenate(pieces_of(value), axis=0).astype(BF16)
    product = lax.dot_general(stacked, table, dims, preferred_element_type=F32)
    return product[:rows] + product[rows : 2 * rows] + product[2 * rows :]


def lane_total(rows):
    return jnp.sum(rows, axis=1, keepdims=True)


def dot_rows(r, u, w, s=None, p=None):
    rows = [jnp.sum(r * u, axis=0, keepdims=True), jnp.sum(u * w, axis=0, keepdims=True)]
    if s is None:
        rows.append(jnp.zeros((ROWS - 2, r.shape[1]), F32))
    else:
        rows.append(jnp.sum(u * s, axis=0, keepdims=True))
        rows.append(jnp.sum(p * w, axis=0, keepdims=True))
        rows.append(jnp.zeros((ROWS - 4, r.shape[1]), F32))
    return jnp.concatenate(rows, axis=0)


def step_sizes(totals, before):
    sums = lane_total(totals)
    norm, curvature = sums[0:1], sums[1:2]
    if before is None:
        beta = None
    else:
        beta = norm / before[0:1, 0:1]
        curvature = curvature + beta * (sums[2:3] + sums[3:4]) + beta * beta * before[1:2, 0:1]
    return norm / curvature, beta, norm, curvature


def collect_to(vector, selector, low_ref, high_ref):
    iface, cells = vector.shape
    moved = exact_dot(vector, selector, NT)
    low_ref[:iface] = moved[:, :cells]
    high_ref[:iface] = vector - moved[:, cells:]


def spread_of(own, previous, selector):
    return own - exact_dot(jnp.concatenate([previous, own], axis=1), selector, NN)


def apply_blocks(blocks, vectors, out_ref):
    def step(index, carry):
        at = pl.ds(index * ROWS, ROWS)
        total = None
        for block, vector in zip(blocks, vectors):
            term = block[at].astype(F32) * vector[None]
            total = term if total is None else total + term
        out_ref[pl.ds(pl.multiple_of(index * ROWS, ROWS), ROWS)] = jnp.sum(total, axis=1)
        return carry

    lax.fori_loop(0, out_ref.shape[0] // ROWS, step, 0)


def table_kernel(slots_ref, column_ref, corner_ref, selector_ref, swap_ref, table_ref):
    def one_hot(row, count):
        places = lax.broadcasted_iota(jnp.int32, (count, row.shape[1]), 0)
        return jnp.where(places == row, 1.0, 0.0).astype(BF16)

    selector_ref[...] = one_hot(slots_ref[...], selector_ref.shape[0])
    swap_ref[...] = one_hot(column_ref[...], swap_ref.shape[0])
    chunk = 128

    def step(index, carry):
        row = corner_ref[...] - index * chunk
        table_ref[pl.ds(pl.multiple_of(index * chunk, chunk), chunk)] = one_hot(row, chunk)
        return carry

    lax.fori_loop(0, table_ref.shape[0] // chunk, step, 0)


def stiffen(own, previous, selector_ref, swap_ref, stiffness_ref, stiff_ref, low_ref, high_ref):
    gap = spread_of(own, previous, selector_ref[...])
    taken = exact_dot(gap, swap_ref[...], NN)
    apply_blocks([stiffness_ref.at[0], stiffness_ref.at[1]], [gap, taken], stiff_ref)
    collect_to(stiff_ref[...], selector_ref[...], low_ref, high_ref)


def first_kernel(own_ref, previous_ref, selector_ref, swap_ref, stiffness_ref, low_ref, high_ref, stiff_ref):
    iface, cells = own_ref.shape
    stiffen(
        own_ref[...], previous_ref[...], selector_ref, swap_ref, stiffness_ref, stiff_ref, low_ref, high_ref
    )
    low_ref[iface:] = jnp.zeros((ROWS, cells), F32)
    high_ref[iface:] = jnp.zeros((ROWS, cells), F32)


def arrived(low_ref, high_ref, from_right_ref, from_left_ref, iface):
    own = high_ref[:iface] - from_right_ref[:iface]
    previous = from_left_ref[:iface] - low_ref[:iface]
    return own, previous


def second_kernel(
    low_ref, high_ref, from_right_ref, from_left_ref, r_ref, u_ref, selector_ref, swap_ref, stiffness_ref,
    low_out, high_out, w_out, stiff_ref,
):
    iface = r_ref.shape[0]
    w, w_previous = arrived(low_ref, high_ref, from_right_ref, from_left_ref, iface)
    w_out[0] = w
    w_out[1] = w_previous
    dots = dot_rows(r_ref[...], u_ref[...], w)
    low_out[iface:] = dots
    high_out[iface:] = dots
    stiffen(w, w_previous, selector_ref, swap_ref, stiffness_ref, stiff_ref, low_out, high_out)


def update(first, last, refs, m, n, n_previous, totals):
    scalars_in, x_in, r_in, u_in, w_in, p_in, s_in, q_in, z_in = refs[:9]
    scalars_out, x_out, r_out, u_out, w_out, p_out, s_out, q_out, z_out = refs[9:]
    alpha, beta, norm, curvature = step_sizes(totals, None if first else scalars_in[...])
    cells = m.shape[1]
    scalars_out[...] = jnp.concatenate(
        [
            jnp.broadcast_to(norm, (1, cells)),
            jnp.broadcast_to(curvature, (1, cells)),
            jnp.zeros((ROWS - 2, cells), F32),
        ],
        axis=0,
    )

    def turned(fresh, kept):
        return fresh if first else fresh + beta * kept[...]

    u, w = u_in[...], w_in[0]
    p = turned(u, p_in)
    s = turned(w, s_in)
    q = turned(m, q_in)
    z = turned(n, None if first else z_in.at[0])
    p_out[...] = p
    s_out[...] = s
    x_out[...] = alpha * p if first else x_in[...] + alpha * p
    r = r_in[...] - alpha * s
    u = u - alpha * q
    w = w - alpha * z
    r_out[...] = r
    u_out[...] = u
    w_out[0] = w
    previous = None
    if not last:
        z_previous = turned(n_previous, None if first else z_in.at[1])
        previous = w_in[1] - alpha * z_previous
        q_out[...] = q
        z_out[0] = z
        z_out[1] = z_previous
        w_out[1] = previous
    return dot_rows(r, u, w, s, p), w, previous


def middle_kernel(first, last, *refs):
    (low_ref, high_ref, from_right_ref, from_left_ref, dots_ref, dots_other_ref, m_ref) = refs[:7]
    (selector_ref, swap_ref, stiffness_ref) = refs[7:10]
    ins = list(refs[10:19])
    outs = list(refs[19:28])
    m = m_ref[...]
    iface = m.shape[0]
    n, n_previous = arrived(low_ref, high_ref, from_right_ref, from_left_ref, iface)
    dots, w, previous = update(
        first, last, ins + outs, m, n, n_previous, dots_ref[...] + dots_other_ref[...]
    )
    if last:
        dots_out = refs[28]
        dots_out[...] = jnp.broadcast_to(dots[None], dots_out.shape)
    else:
        low_out, high_out, stiff_ref = refs[28:31]
        low_out[iface:] = dots
        high_out[iface:] = dots
        stiffen(w, previous, selector_ref, swap_ref, stiffness_ref, stiff_ref, low_out, high_out)


def corner_kernel(
    ranks, low_ref, high_ref, from_right_ref, from_left_ref, place_ref, selector_ref, operators_ref, table_ref,
    m_out, gap_out, *rest,
):
    outs, sums_ref = rest[:ranks], rest[ranks]
    iface, cells = m_out.shape
    own, previous = arrived(low_ref, high_ref, from_right_ref, from_left_ref, iface)
    m_out[...] = own
    odd = place_ref[0] % 2
    other = jnp.where(odd == 1, from_left_ref[iface:], from_right_ref[iface:])
    dots = high_ref[iface:] + other
    gap = spread_of(own, previous, selector_ref[...])
    gap_out[...] = gap
    parts = []
    for corner in range(CORNERS_SUB):
        at = slice(corner * CORNER_DOF, (corner + 1) * CORNER_DOF)
        part = jnp.sum(operators_ref[at].astype(F32) * gap[None], axis=1)
        parts.append(jnp.concatenate([part, jnp.zeros((ROWS - CORNER_DOF, cells), F32)], axis=0))
    sums_ref[...] = exact_dot(jnp.concatenate(parts, axis=1), table_ref[...], NT)
    owned = sums_ref.shape[1] // ranks
    pad = jnp.zeros((1, owned - 2 * cells), F32) if owned > 2 * cells else None
    tail = []
    for row in range(0, ROWS - CORNER_DOF):
        lanes = [dots[2 * row : 2 * row + 1], dots[2 * row + 1 : 2 * row + 2]]
        if pad is not None:
            lanes.append(pad)
        tail.append(jnp.concatenate(lanes, axis=1))
    tail = jnp.concatenate(tail, axis=0)
    for distance in range(ranks):
        rank = (place_ref[1] + distance) % ranks
        piece = sums_ref[:, pl.ds(pl.multiple_of(rank * owned, 128), owned)]
        outs[distance][...] = jnp.concatenate([piece[:CORNER_DOF], tail], axis=0)


def local_kernel(gap_ref, inverse_ref, local_ref):
    apply_blocks([inverse_ref], [gap_ref[...]], local_ref)


def coarse_kernel(ranks, place_ref, coarse_ref, *rest):
    pieces, (solved_ref, dots_ref, sums_ref) = rest[:ranks], rest[ranks:]
    cells = dots_ref.shape[1]
    for distance in range(ranks):
        rank = (place_ref[1] + ranks - distance) % ranks
        sums_ref[rank] = pieces[distance][...]
    total = sums_ref[0]
    for rank in range(1, ranks):
        total = total + sums_ref[rank]
    tail = total[CORNER_DOF:]
    dots_ref[...] = jnp.concatenate(
        [
            tail[0:1, :cells],
            tail[0:1, cells : 2 * cells],
            tail[1:2, :cells],
            tail[1:2, cells : 2 * cells],
            jnp.zeros((ROWS - 4, cells), F32),
        ],
        axis=0,
    )
    blocks, order = coarse_ref.shape[0], coarse_ref.shape[1]
    width = order // CORNER_DOF
    columns = []
    for block in range(blocks):
        lanes = slice(block * width, (block + 1) * width)
        row = jnp.concatenate([total[j : j + 1, lanes] for j in range(CORNER_DOF)], axis=1)
        parts = pieces_of(row) + [jnp.zeros((ROWS - 3, order), F32)]
        stacked = jnp.concatenate(parts, axis=0).astype(BF16)
        product = lax.dot_general(stacked, coarse_ref[block], NT, preferred_element_type=F32)
        result = product[0:1] + product[1:2] + product[2:3]
        rows = [result[:, j * width : (j + 1) * width] for j in range(CORNER_DOF)]
        columns.append(jnp.concatenate(rows, axis=0))
    solved = jnp.concatenate(columns, axis=1)
    solved_ref[...] = jnp.concatenate(
        [solved, jnp.zeros((ROWS - CORNER_DOF, solved.shape[1]), F32)], axis=0
    )


def lift_kernel(ranks, place_ref, local_ref, operators_ref, table_ref, selector_ref, dots_ref, other_ref, *rest):
    pieces, (low_ref, high_ref, dots_out, values_ref) = rest[:ranks], rest[ranks:]
    cells = local_ref.shape[1]
    owned = values_ref.shape[1] // ranks
    dots_out[...] = dots_ref[...] + other_ref[...]
    for distance in range(ranks):
        rank = (place_ref[1] + ranks - distance) % ranks
        values_ref[:, pl.ds(pl.multiple_of(rank * owned, 128), owned)] = pieces[distance][...]
    picked = exact_dot(values_ref[...], table_ref[...], NN)
    lifted = local_ref[...]
    for corner in range(CORNERS_SUB):
        lanes = slice(corner * cells, (corner + 1) * cells)
        for dof in range(CORNER_DOF):
            operator = operators_ref[corner * CORNER_DOF + dof].astype(F32)
            lifted = lifted + operator * picked[dof : dof + 1, lanes]
    collect_to(lifted, selector_ref[...], low_ref, high_ref)


def final_kernel(dots_ref, scalars_ref, x_ref, r_ref, u_ref, w_ref, p_ref, s_ref, x_out, r_out):
    totals = jnp.sum(dots_ref[...], axis=0)
    alpha, beta, _, _ = step_sizes(totals, scalars_ref[...])
    x_out[...] = x_ref[...] + alpha * (u_ref[...] + beta * p_ref[...])
    r_out[...] = r_ref[...] - alpha * (w_ref[0] + beta * s_ref[...])


def shifted(block, distance):
    count = lax.axis_size("sub")
    route = [(i, i + distance) for i in range(count) if 0 <= i + distance < count]
    return lax.ppermute(block, "sub", route)


def swapped(block, bit):
    return lax.ppermute(block, "sub", [(i, i ^ bit) for i in range(lax.axis_size("sub"))])


def rotated(block, distance):
    count = lax.axis_size("grp")
    return lax.ppermute(block, "grp", [(i, (i + distance) % count) for i in range(count)])


def shape(*dims, dtype=F32):
    return jax.ShapeDtypeStruct(dims, dtype)


def call(kernel, out_shape, in_smem=(), count=0, scratch=(), flops=0, moved=0, name=None):
    specs = [
        pl.BlockSpec(memory_space=pltpu.SMEM if i in in_smem else pltpu.VMEM) for i in range(count)
    ]
    out_specs = jax.tree.map(lambda _: pl.BlockSpec(memory_space=pltpu.VMEM), out_shape)
    return pl.pallas_call(
        kernel,
        out_shape=out_shape,
        in_specs=specs,
        out_specs=out_specs,
        scratch_shapes=list(scratch),
        compiler_params=pltpu.CompilerParams(vmem_limit_bytes=24 * 1024 * 1024),
        cost_estimate=pl.CostEstimate(flops=flops, bytes_accessed=moved, transcendentals=0),
        name=name,
    )


def on_device(
    gap_data,
    local_inverse,
    stiffness,
    stiff_column,
    neighbour,
    corner_ops,
    corner_index,
    coarse_inverse,
):
    iface, _, cells = gap_data.shape
    ranks = lax.axis_size("grp")
    sub_count = lax.axis_size("sub")
    start = lax.axis_index("sub") * cells
    place = jnp.stack([lax.axis_index("sub"), lax.axis_index("grp")]).astype(jnp.int32)
    right_side = gap_data[:, 0, :]
    inverse = local_inverse[:, :, 0, :]
    stiff = stiffness[:, :, :, 0, :]
    operators = corner_ops[:, :, 0, :]
    blocks_own, order = coarse_inverse.shape[:2]
    owned = blocks_own * (order // CORNER_DOF)
    group = owned * ranks
    slots = jnp.where(neighbour < 0, -1, neighbour - (start - cells))
    column = stiff_column - start
    corners = corner_index.reshape(1, CORNERS_SUB * cells)

    selector, swap, table = call(
        table_kernel,
        (
            shape(2 * cells, cells, dtype=BF16),
            shape(cells, cells, dtype=BF16),
            shape(group, CORNERS_SUB * cells, dtype=BF16),
        ),
        count=3,
        name="tables",
    )(slots, column, corners)

    field = shape(iface, cells)
    pair = shape(2, iface, cells)
    message = shape(iface + ROWS, cells)
    rows = shape(ROWS, cells)
    piece = shape(ROWS, owned)
    stiff_scratch = [pltpu.VMEM((iface, cells), F32)]
    stiff_cost = dict(flops=4 * iface * iface * cells, moved=4 * iface * iface * cells)

    def apply_operator(low, high):
        from_right = shifted(low, -1)
        from_left = shifted(high, 1)
        m, gap, *parts = call(
            lambda *refs: corner_kernel(ranks, *refs),
            (field, field) + (piece,) * ranks,
            in_smem=(4,),
            count=8,
            scratch=[pltpu.VMEM((ROWS, group), F32)],
            flops=2 * 24 * iface * cells,
            moved=2 * 24 * iface * cells + group * CORNERS_SUB * cells * 2,
            name="corners",
        )(low, high, from_right, from_left, place, selector, operators, table)
        arrivals = [parts[0]] + [rotated(parts[d], d) for d in range(1, ranks)]
        local = call(
            local_kernel,
            field,
            count=2,
            flops=2 * iface * iface * cells,
            moved=2 * iface * iface * cells,
            name="local",
        )(gap, inverse)
        solved, dots = call(
            lambda *refs: coarse_kernel(ranks, *refs),
            (piece, rows),
            in_smem=(0,),
            count=2 + ranks,
            scratch=[pltpu.VMEM((ranks, ROWS, owned), F32)],
            flops=2 * blocks_own * order * order,
            moved=2 * blocks_own * order * order,
            name="coarse",
        )(place, coarse_inverse, *arrivals)
        values = [solved] + [rotated(solved, d) for d in range(1, ranks)]
        other = swapped(dots, 2)
        low, high, dots = call(
            lambda *refs: lift_kernel(ranks, *refs),
            (field, field, rows),
            in_smem=(0,),
            count=7 + ranks,
            scratch=[pltpu.VMEM((ROWS, group), F32)],
            flops=2 * 24 * iface * cells,
            moved=2 * 24 * iface * cells + group * CORNERS_SUB * cells * 2,
            name="lift",
        )(place, local, operators, table, selector, dots, other, *values)
        return m, low, high, dots

    previous = shifted(right_side, 1)
    low, high = call(
        first_kernel, (message, message), count=5, scratch=stiff_scratch, name="first", **stiff_cost
    )(right_side, previous, selector, swap, stiff)
    u, low, high, dots = apply_operator(low, high)
    r = right_side
    from_right, from_left = shifted(low, -1), shifted(high, 1)
    low, high, w = call(
        second_kernel, (message, message, pair), count=9, scratch=stiff_scratch, name="second", **stiff_cost
    )(low, high, from_right, from_left, r, u, selector, swap, stiff)

    scalars, x, p, s, q, z = [jnp.zeros((ROWS, cells), F32)] + [r] * 4 + [w]
    for step in range(ITERS - 1):
        first, last = step == 0, step == ITERS - 2
        m, low, high, dots = apply_operator(low, high)
        from_right, from_left, other = shifted(low, -1), shifted(high, 1), swapped(dots, 4)
        bit = 8
        while bit < sub_count:
            dots = dots + other
            other = swapped(dots, bit)
            bit *= 2
        outs = (rows, field, field, field, pair, field, field, field, pair)
        if last:
            count = sub_count * ranks
            outs += (shape(count, ROWS, cells),)
        else:
            outs += (message, message)
        result = call(
            lambda *refs, first=first, last=last: middle_kernel(first, last, *refs),
            outs,
            count=19,
            scratch=() if last else stiff_scratch,
            name="last" if last else "middle",
            **({} if last else stiff_cost),
        )(
            low, high, from_right, from_left, dots, other, m, selector, swap, stiff,
            scalars, x, r, u, w, p, s, q, z,
        )
        scalars, x, r, u, w, p, s, q, z = result[:9]
        if not last:
            low, high = result[9:]
    everyone = lax.all_to_all(result[9], ("sub", "grp"), 0, 0, tiled=True)
    x, r = call(final_kernel, (field, field), count=8, name="final")(
        everyone, scalars, x, r, u, w, p, s
    )
    return (x[:, None, :], r[:, None, :])


def solution(mesh):
    in_specs = (
        P(None, "grp", "sub"),
        P(None, None, "grp", "sub"),
        P(None, None, None, "grp", "sub"),
        P("grp", "sub"),
        P("grp", "sub"),
        P(None, None, "grp", "sub"),
        P(None, "grp", "sub"),
        P("grp", None, "sub"),
    )
    out_specs = (P(None, "grp", "sub"), P(None, "grp", "sub"))
    return jax.shard_map(
        on_device, mesh=mesh, in_specs=in_specs, out_specs=out_specs, check_vma=False
    )
```

time: 723 us -> 217 us (0.30); the launches traced: 713 us -> 216 us
  blocking collectives: 439 us -> 12.3 us
  waiting for transfers between devices: 138 us -> 27.6 us
  starting transfers between devices: 31.8 us -> 136 us
  other arithmetic: 42.4 us -> 0.76 us
  Pallas kernels: 0 us -> 33.3 us
  matrix products: 27.2 us -> 0 us
  between operations: 26.5 us -> 1.07 us
    psum x9 -> x0, blocking collectives: 373 us -> none  [the longest x5 216 us: precond_dot(): return lax.psum(jnp.sum(first * second), ('sub', 'grp'))]
    ppermute x20 -> x60, starting transfers between devices: 31.4 us -> 136 us  [the longest x21 50.5 us: shifted(): return lax.ppermute(block, 'sub', route)]
    reduce_scatter x5 -> x0, waiting for transfers between devices: 99.3 us -> none  [on_device(): owned = lax.psum_scatter(apply_sums, 'grp', scatter_dimension=1, tiled=True)]
    all_gather x5 -> x0, blocking collectives: 65.6 us -> none  [on_device(): values = lax.all_gather(coarse_solved, 'grp', axis=1, tiled=True)]
    dot_general x20 -> x0, other arithmetic: 34.4 us -> none  [the longest x5 20.7 us: precondition(): jnp.einsum('ijx,jx->ix', coupled_block, taken, precision=precise, preferr...]
    pallas_call x0 -> x28, Pallas kernels: none -> 33.3 us  [the longest x4 6.84 us: on_device(): call(lambda *refs, first=first, last=last: middle_kernel(first, last, *re...]
    dot_general x35 -> x0, matrix products: 27.2 us -> none  [the longest x5 9.58 us: on_device(): jnp.einsum('bpq,bq->bp', coarse_inverse, arranged, precision=precise, pre...]
    all_to_all x0 -> x1, blocking collectives: none -> 12.3 us  [on_device(): everyone = lax.all_to_all(result[9], ('sub', 'grp'), 0, 0, tiled=True)]
  transfers between devices with their start and end apart: 25 -> 60, of which waited for: 24 -> 32; matrix products, arithmetic and copies ran while one was open for 2% -> 0% of each run, Pallas kernels for 0% -> 2%
where the time goes in v1:
time: 217 us; the launch traced here: 216 us
  starting transfers between devices  136 us (63%)
  Pallas kernels  33.3 us (15%)
  waiting for transfers between devices  27.6 us (13%)
  blocking collectives  12.3 us (6%)
  local copies, waits for them, and re-layouts  4.9 us (2%)
    ppermute x21, starting transfers between devices, shifted(): return lax.ppermute(block, 'sub', route)  50.5 us
    ppermute x9, starting transfers between devices, swapped(): lax.ppermute(block, 'sub', [(i, i ^ bit) for i in range(lax.axis_size('su...  43.7 us
    ppermute x30, starting transfers between devices, rotated(): lax.ppermute(block, 'grp', [(i, (i + distance) % count) for i in range(co...  41.9 us
    all_to_all x1, blocking collectives, on_device(): everyone = lax.all_to_all(result[9], ('sub', 'grp'), 0, 0, tiled=True)  12.3 us
    ppermute x30, waiting for transfers between devices, rotated(): lax.ppermute(block, 'grp', [(i, (i + distance) % count) for i in range(co...  11.6 us
    ppermute x9, waiting for transfers between devices, swapped(): lax.ppermute(block, 'sub', [(i, i ^ bit) for i in range(lax.axis_size('su...  10.8 us
    pallas_call x4, Pallas kernels, on_device(): call(lambda *refs, first=first, last=last: middle_kernel(first, last, *re...  6.84 us
    pallas_call x5, Pallas kernels, apply_operator(): call(lambda *refs: coarse_kernel(ranks, *refs), (piece, rows), in_smem=(0...  6.27 us
  transfers between devices with their start and end apart: 60, of which 32 were waited for; matrix products, arithmetic and copies ran while one was open for 0% of the time, Pallas kernels for 2%

profile of v1, /device:TPU:0, one launch (start us, length us, event | category | flops | bytes accessed | tf_op | source)
XLA Modules:
  0.0 216.0 jit_solution(6193305893336763427)
XLA Ops:
  11.1 5.1 %collective-permute-start.2 = (f32[104,128]{1,0:T(8,128)S(1)}, f32[104,128]{1,0:T(8,128)S(1)}, u32[]{:S(2)}, u32[]{:S(2)}) collective-permute-start(f32[104,128]{1,0:T(8,128)S(1)} %get-tuple-element.110.refs_1_), channel_id=1, source_target_pairs={{0,4},{4,8},{8,12},{12,16},{16,20},{20,24},{24,28},{1,5},{5,9},{9,... | collective-permute-start | bytes 159752 | tf_op jit(solution)/shard_map/ppermute | solution.py:302
  28.6 3.2 %collective-permute-start.9 = (f32[8,256]{1,0:T(8,128)S(1)}, f32[8,256]{1,0:T(8,128)S(1)}, u32[]{:S(2)}, u32[]{:S(2)}) collective-permute-start(f32[8,256]{1,0:T(8,128)S(1)} %get-tuple-element.118.refs_7_), channel_id=1, source_target_pairs={{0,3},{1,0},{2,1},{3,2},{4,7},{5,4},{6,5},{7,6},{8,11},{9,8},{10,9... | collective-permute-start | bytes 24584 | tf_op jit(solution)/shard_map/ppermute | solution.py:311
  32.4 4.6 %collective-permute-start.6 = (f32[8,128]{1,0:T(8,128)S(1)}, f32[8,128]{1,0:T(8,128)S(1)}, u32[]{:S(2)}, u32[]{:S(2)}) collective-permute-start(f32[8,128]{1,0:T(8,128)S(1)} %get-tuple-element.117.refs_5_), channel_id=1, source_target_pairs={{0,8},{4,12},{8,0},{12,4},{16,24},{20,28},{24,16},{28,20},{1,9},{5... | collective-permute-start | bytes 12296 | tf_op jit(solution)/shard_map/ppermute | solution.py:306
  41.5 3.0 %collective-permute-start.11 = (f32[96,128]{1,0:T(8,128)S(1)}, f32[96,128]{1,0:T(8,128)S(1)}, u32[]{:S(2)}, u32[]{:S(2)}) collective-permute-start(f32[96,128]{1,0:T(8,128)S(1)} %get-tuple-element.120.high_ref), channel_id=1, source_target_pairs={{0,4},{4,8},{8,12},{12,16},{16,20},{20,24},{24,28},{1,5},{5,9},{9,... | collective-permute-start | bytes 147464 | tf_op jit(solution)/shard_map/ppermute | solution.py:302
  48.6 5.7 %collective-permute-start.13 = (f32[104,128]{1,0:T(8,128)S(1)}, f32[104,128]{1,0:T(8,128)S(1)}, u32[]{:S(2)}, u32[]{:S(2)}) collective-permute-start(f32[104,128]{1,0:T(8,128)S(1)} %get-tuple-element.123.refs_1_), channel_id=1, source_target_pairs={{0,4},{4,8},{8,12},{12,16},{16,20},{20,24},{24,28},{1,5},{5,9},{9,... | collective-permute-start | bytes 159752 | tf_op jit(solution)/shard_map/ppermute | solution.py:302
  64.0 3.3 %collective-permute-start.20 = (f32[8,256]{1,0:T(8,128)S(1)}, f32[8,256]{1,0:T(8,128)S(1)}, u32[]{:S(2)}, u32[]{:S(2)}) collective-permute-start(f32[8,256]{1,0:T(8,128)S(1)} %get-tuple-element.130.refs_7_), channel_id=1, source_target_pairs={{0,3},{1,0},{2,1},{3,2},{4,7},{5,4},{6,5},{7,6},{8,11},{9,8},{10,9... | collective-permute-start | bytes 24584 | tf_op jit(solution)/shard_map/ppermute | solution.py:311
  67.9 4.9 %collective-permute-start.17 = (f32[8,128]{1,0:T(8,128)S(1)}, f32[8,128]{1,0:T(8,128)S(1)}, u32[]{:S(2)}, u32[]{:S(2)}) collective-permute-start(f32[8,128]{1,0:T(8,128)S(1)} %get-tuple-element.129.refs_5_), channel_id=1, source_target_pairs={{0,8},{4,12},{8,0},{12,4},{16,24},{20,28},{24,16},{28,20},{1,9},{5... | collective-permute-start | bytes 12296 | tf_op jit(solution)/shard_map/ppermute | solution.py:306
  76.8 3.0 %collective-permute-start.22 = (f32[96,128]{1,0:T(8,128)S(1)}, f32[96,128]{1,0:T(8,128)S(1)}, u32[]{:S(2)}, u32[]{:S(2)}) collective-permute-start(f32[96,128]{1,0:T(8,128)S(1)} %get-tuple-element.132.refs_1_), channel_id=1, source_target_pairs={{0,4},{4,8},{8,12},{12,16},{16,20},{20,24},{24,28},{1,5},{5,9},{9,... | collective-permute-start | bytes 147464 | tf_op jit(solution)/shard_map/ppermute | solution.py:302
  79.9 6.8 %collective-permute-start.23 = (f32[8,128]{1,0:T(8,128)S(1)}, f32[8,128]{1,0:T(8,128)S(1)}, u32[]{:S(2)}, u32[]{:S(2)}) collective-permute-start(f32[8,128]{1,0:T(8,128)S(1)} %get-tuple-element.133.refs_4_), channel_id=1, source_target_pairs={{0,16},{4,20},{8,24},{12,28},{16,0},{20,4},{24,8},{28,12},{1,17},{... | collective-permute-start | bytes 12296 | tf_op jit(solution)/shard_map/ppermute | solution.py:306
  91.7 3.0 %collective-permute-start.25 = (f32[104,128]{1,0:T(8,128)S(1)}, f32[104,128]{1,0:T(8,128)S(1)}, u32[]{:S(2)}, u32[]{:S(2)}) collective-permute-start(f32[104,128]{1,0:T(8,128)S(1)} %get-tuple-element.137.refs_1_), channel_id=1, source_target_pairs={{0,4},{4,8},{8,12},{12,16},{16,20},{20,24},{24,28},{1,5},{5,9},{9,... | collective-permute-start | bytes 159752 | tf_op jit(solution)/shard_map/ppermute | solution.py:302
  104.4 3.3 %collective-permute-start.32 = (f32[8,256]{1,0:T(8,128)S(1)}, f32[8,256]{1,0:T(8,128)S(1)}, u32[]{:S(2)}, u32[]{:S(2)}) collective-permute-start(f32[8,256]{1,0:T(8,128)S(1)} %get-tuple-element.144.refs_7_), channel_id=1, source_target_pairs={{0,3},{1,0},{2,1},{3,2},{4,7},{5,4},{6,5},{7,6},{8,11},{9,8},{10,9... | collective-permute-start | bytes 24584 | tf_op jit(solution)/shard_map/ppermute | solution.py:311
  108.4 3.0 %collective-permute-start.29 = (f32[8,128]{1,0:T(8,128)S(1)}, f32[8,128]{1,0:T(8,128)S(1)}, u32[]{:S(2)}, u32[]{:S(2)}) collective-permute-start(f32[8,128]{1,0:T(8,128)S(1)} %get-tuple-element.143.refs_5_), channel_id=1, source_target_pairs={{0,8},{4,12},{8,0},{12,4},{16,24},{20,28},{24,16},{28,20},{1,9},{5... | collective-permute-start | bytes 12296 | tf_op jit(solution)/shard_map/ppermute | solution.py:306
  115.5 3.0 %collective-permute-start.34 = (f32[96,128]{1,0:T(8,128)S(1)}, f32[96,128]{1,0:T(8,128)S(1)}, u32[]{:S(2)}, u32[]{:S(2)}) collective-permute-start(f32[96,128]{1,0:T(8,128)S(1)} %get-tuple-element.146.refs_1_), channel_id=1, source_target_pairs={{0,4},{4,8},{8,12},{12,16},{16,20},{20,24},{24,28},{1,5},{5,9},{9,... | collective-permute-start | bytes 147464 | tf_op jit(solution)/shard_map/ppermute | solution.py:302
  118.5 6.1 %collective-permute-start.35 = (f32[8,128]{1,0:T(8,128)S(1)}, f32[8,128]{1,0:T(8,128)S(1)}, u32[]{:S(2)}, u32[]{:S(2)}) collective-permute-start(f32[8,128]{1,0:T(8,128)S(1)} %get-tuple-element.147.refs_4_), channel_id=1, source_target_pairs={{0,16},{4,20},{8,24},{12,28},{16,0},{20,4},{24,8},{28,12},{1,17},{... | collective-permute-start | bytes 12296 | tf_op jit(solution)/shard_map/ppermute | solution.py:306
  129.7 3.0 %collective-permute-start.37 = (f32[104,128]{1,0:T(8,128)S(1)}, f32[104,128]{1,0:T(8,128)S(1)}, u32[]{:S(2)}, u32[]{:S(2)}) collective-permute-start(f32[104,128]{1,0:T(8,128)S(1)} %get-tuple-element.159.refs_1_), channel_id=1, source_target_pairs={{0,4},{4,8},{8,12},{12,16},{16,20},{20,24},{24,28},{1,5},{5,9},{9,... | collective-permute-start | bytes 159752 | tf_op jit(solution)/shard_map/ppermute | solution.py:302
  142.4 3.3 %collective-permute-start.44 = (f32[8,256]{1,0:T(8,128)S(1)}, f32[8,256]{1,0:T(8,128)S(1)}, u32[]{:S(2)}, u32[]{:S(2)}) collective-permute-start(f32[8,256]{1,0:T(8,128)S(1)} %get-tuple-element.166.refs_7_), channel_id=1, source_target_pairs={{0,3},{1,0},{2,1},{3,2},{4,7},{5,4},{6,5},{7,6},{8,11},{9,8},{10,9... | collective-permute-start | bytes 24584 | tf_op jit(solution)/shard_map/ppermute | solution.py:311
  146.3 3.0 %collective-permute-start.41 = (f32[8,128]{1,0:T(8,128)S(1)}, f32[8,128]{1,0:T(8,128)S(1)}, u32[]{:S(2)}, u32[]{:S(2)}) collective-permute-start(f32[8,128]{1,0:T(8,128)S(1)} %get-tuple-element.165.refs_5_), channel_id=1, source_target_pairs={{0,8},{4,12},{8,0},{12,4},{16,24},{20,28},{24,16},{28,20},{1,9},{5... | collective-permute-start | bytes 12296 | tf_op jit(solution)/shard_map/ppermute | solution.py:306
  153.5 3.0 %collective-permute-start.46 = (f32[96,128]{1,0:T(8,128)S(1)}, f32[96,128]{1,0:T(8,128)S(1)}, u32[]{:S(2)}, u32[]{:S(2)}) collective-permute-start(f32[96,128]{1,0:T(8,128)S(1)} %get-tuple-element.168.refs_1_), channel_id=1, source_target_pairs={{0,4},{4,8},{8,12},{12,16},{16,20},{20,24},{24,28},{1,5},{5,9},{9,... | collective-permute-start | bytes 147464 | tf_op jit(solution)/shard_map/ppermute | solution.py:302
  156.5 6.1 %collective-permute-start.47 = (f32[8,128]{1,0:T(8,128)S(1)}, f32[8,128]{1,0:T(8,128)S(1)}, u32[]{:S(2)}, u32[]{:S(2)}) collective-permute-start(f32[8,128]{1,0:T(8,128)S(1)} %get-tuple-element.169.refs_4_), channel_id=1, source_target_pairs={{0,16},{4,20},{8,24},{12,28},{16,0},{20,4},{24,8},{28,12},{1,17},{... | collective-permute-start | bytes 12296 | tf_op jit(solution)/shard_map/ppermute | solution.py:306
  167.6 3.0 %collective-permute-start.49 = (f32[104,128]{1,0:T(8,128)S(1)}, f32[104,128]{1,0:T(8,128)S(1)}, u32[]{:S(2)}, u32[]{:S(2)}) collective-permute-start(f32[104,128]{1,0:T(8,128)S(1)} %get-tuple-element.181.refs_1_), channel_id=1, source_target_pairs={{0,4},{4,8},{8,12},{12,16},{16,20},{20,24},{24,28},{1,5},{5,9},{9,... | collective-permute-start | bytes 159752 | tf_op jit(solution)/shard_map/ppermute | solution.py:302
  180.4 3.3 %collective-permute-start.56 = (f32[8,256]{1,0:T(8,128)S(1)}, f32[8,256]{1,0:T(8,128)S(1)}, u32[]{:S(2)}, u32[]{:S(2)}) collective-permute-start(f32[8,256]{1,0:T(8,128)S(1)} %get-tuple-element.188.refs_7_), channel_id=1, source_target_pairs={{0,3},{1,0},{2,1},{3,2},{4,7},{5,4},{6,5},{7,6},{8,11},{9,8},{10,9... | collective-permute-start | bytes 24584 | tf_op jit(solution)/shard_map/ppermute | solution.py:311
  191.5 3.0 %collective-permute-start.58 = (f32[96,128]{1,0:T(8,128)S(1)}, f32[96,128]{1,0:T(8,128)S(1)}, u32[]{:S(2)}, u32[]{:S(2)}) collective-permute-start(f32[96,128]{1,0:T(8,128)S(1)} %get-tuple-element.190.refs_1_), channel_id=1, source_target_pairs={{0,4},{4,8},{8,12},{12,16},{16,20},{20,24},{24,28},{1,5},{5,9},{9,... | collective-permute-start | bytes 147464 | tf_op jit(solution)/shard_map/ppermute | solution.py:302
  194.5 6.1 %collective-permute-start.59 = (f32[8,128]{1,0:T(8,128)S(1)}, f32[8,128]{1,0:T(8,128)S(1)}, u32[]{:S(2)}, u32[]{:S(2)}) collective-permute-start(f32[8,128]{1,0:T(8,128)S(1)} %get-tuple-element.191.refs_4_), channel_id=1, source_target_pairs={{0,16},{4,20},{8,24},{12,28},{16,0},{20,4},{24,8},{28,12},{1,17},{... | collective-permute-start | bytes 12296 | tf_op jit(solution)/shard_map/ppermute | solution.py:306
  202.9 12.3 %all_to_all.5.dots_ref = f32[32,8,128]{2,1,0:T(8,128)S(1)} all-to-all(f32[32,8,128]{2,1,0:T(8,128)S(1)} %get-tuple-element.202), channel_id=1, replica_groups=mesh['sub'=8,'grp'=4] {'sub','grp'}, dimensions={0} | all-to-all | bytes 262144 | tf_op jit(solution)/shard_map/all_to_all | solution.py:467
  (147 shorter events, 110.6 us)
Async XLA Ops:
  9.7 6.7 %collective-permute-start.1 = (f32[104,128]{1,0:T(8,128)S(1)}, f32[104,128]{1,0:T(8,128)S(1)}, u32[]{:S(2)}, u32[]{:S(2)}) collective-permute-start(f32[104,128]{1,0:T(8,128)S(1)} %get-tuple-element.109.refs_0_), channel_id=1, source_target_pairs={{4,0},{8,4},{12,8},{16,12},{20,16},{24,20},{28,24},{5,1},{9,5},{13... | collective-permute-start | bytes 159752 | tf_op jit(solution)/shard_map/ppermute | solution.py:302
  28.6 10.0 %collective-permute-start.9 = (f32[8,256]{1,0:T(8,128)S(1)}, f32[8,256]{1,0:T(8,128)S(1)}, u32[]{:S(2)}, u32[]{:S(2)}) collective-permute-start(f32[8,256]{1,0:T(8,128)S(1)} %get-tuple-element.118.refs_7_), channel_id=1, source_target_pairs={{0,3},{1,0},{2,1},{3,2},{4,7},{5,4},{6,5},{7,6},{8,11},{9,8},{10,9... | collective-permute-start | bytes 24584 | tf_op jit(solution)/shard_map/ppermute | solution.py:311
  31.7 6.9 %collective-permute-start.8 = (f32[8,256]{1,0:T(8,128)S(1)}, f32[8,256]{1,0:T(8,128)S(1)}, u32[]{:S(2)}, u32[]{:S(2)}) collective-permute-start(f32[8,256]{1,0:T(8,128)S(1)} %get-tuple-element.118.refs_7_), channel_id=1, source_target_pairs={{0,2},{1,3},{2,0},{3,1},{4,6},{5,7},{6,4},{7,5},{8,10},{9,11},{10,... | collective-permute-start | bytes 24584 | tf_op jit(solution)/shard_map/ppermute | solution.py:311
  31.7 6.9 %collective-permute-start.7 = (f32[8,256]{1,0:T(8,128)S(1)}, f32[8,256]{1,0:T(8,128)S(1)}, u32[]{:S(2)}, u32[]{:S(2)}) collective-permute-start(f32[8,256]{1,0:T(8,128)S(1)} %get-tuple-element.118.refs_7_), channel_id=1, source_target_pairs={{0,1},{1,2},{2,3},{3,0},{4,5},{5,6},{6,7},{7,4},{8,9},{9,10},{10,1... | collective-permute-start | bytes 24584 | tf_op jit(solution)/shard_map/ppermute | solution.py:311
  47.3 7.0 %collective-permute-start.12 = (f32[104,128]{1,0:T(8,128)S(1)}, f32[104,128]{1,0:T(8,128)S(1)}, u32[]{:S(2)}, u32[]{:S(2)}) collective-permute-start(f32[104,128]{1,0:T(8,128)S(1)} %get-tuple-element.122.refs_0_), channel_id=1, source_target_pairs={{4,0},{8,4},{12,8},{16,12},{20,16},{24,20},{28,24},{5,1},{9,5},{13... | collective-permute-start | bytes 159752 | tf_op jit(solution)/shard_map/ppermute | solution.py:302
  48.6 6.5 %collective-permute-start.13 = (f32[104,128]{1,0:T(8,128)S(1)}, f32[104,128]{1,0:T(8,128)S(1)}, u32[]{:S(2)}, u32[]{:S(2)}) collective-permute-start(f32[104,128]{1,0:T(8,128)S(1)} %get-tuple-element.123.refs_1_), channel_id=1, source_target_pairs={{0,4},{4,8},{8,12},{12,16},{16,20},{20,24},{24,28},{1,5},{5,9},{9,... | collective-permute-start | bytes 159752 | tf_op jit(solution)/shard_map/ppermute | solution.py:302
  64.0 10.5 %collective-permute-start.20 = (f32[8,256]{1,0:T(8,128)S(1)}, f32[8,256]{1,0:T(8,128)S(1)}, u32[]{:S(2)}, u32[]{:S(2)}) collective-permute-start(f32[8,256]{1,0:T(8,128)S(1)} %get-tuple-element.130.refs_7_), channel_id=1, source_target_pairs={{0,3},{1,0},{2,1},{3,2},{4,7},{5,4},{6,5},{7,6},{8,11},{9,8},{10,9... | collective-permute-start | bytes 24584 | tf_op jit(solution)/shard_map/ppermute | solution.py:311
  67.2 7.2 %collective-permute-start.19 = (f32[8,256]{1,0:T(8,128)S(1)}, f32[8,256]{1,0:T(8,128)S(1)}, u32[]{:S(2)}, u32[]{:S(2)}) collective-permute-start(f32[8,256]{1,0:T(8,128)S(1)} %get-tuple-element.130.refs_7_), channel_id=1, source_target_pairs={{0,2},{1,3},{2,0},{3,1},{4,6},{5,7},{6,4},{7,5},{8,10},{9,11},{10,... | collective-permute-start | bytes 24584 | tf_op jit(solution)/shard_map/ppermute | solution.py:311
  67.2 7.2 %collective-permute-start.18 = (f32[8,256]{1,0:T(8,128)S(1)}, f32[8,256]{1,0:T(8,128)S(1)}, u32[]{:S(2)}, u32[]{:S(2)}) collective-permute-start(f32[8,256]{1,0:T(8,128)S(1)} %get-tuple-element.130.refs_7_), channel_id=1, source_target_pairs={{0,1},{1,2},{2,3},{3,0},{4,5},{5,6},{6,7},{7,4},{8,9},{9,10},{10,1... | collective-permute-start | bytes 24584 | tf_op jit(solution)/shard_map/ppermute | solution.py:311
  75.5 12.8 %collective-permute-start.21 = (f32[96,128]{1,0:T(8,128)S(1)}, f32[96,128]{1,0:T(8,128)S(1)}, u32[]{:S(2)}, u32[]{:S(2)}) collective-permute-start(f32[96,128]{1,0:T(8,128)S(1)} %get-tuple-element.131.refs_0_), channel_id=1, source_target_pairs={{4,0},{8,4},{12,8},{16,12},{20,16},{24,20},{28,24},{5,1},{9,5},{13... | collective-permute-start | bytes 147464 | tf_op jit(solution)/shard_map/ppermute | solution.py:302
  76.8 11.5 %collective-permute-start.22 = (f32[96,128]{1,0:T(8,128)S(1)}, f32[96,128]{1,0:T(8,128)S(1)}, u32[]{:S(2)}, u32[]{:S(2)}) collective-permute-start(f32[96,128]{1,0:T(8,128)S(1)} %get-tuple-element.132.refs_1_), channel_id=1, source_target_pairs={{0,4},{4,8},{8,12},{12,16},{16,20},{20,24},{24,28},{1,5},{5,9},{9,... | collective-permute-start | bytes 147464 | tf_op jit(solution)/shard_map/ppermute | solution.py:302
  79.9 8.4 %collective-permute-start.23 = (f32[8,128]{1,0:T(8,128)S(1)}, f32[8,128]{1,0:T(8,128)S(1)}, u32[]{:S(2)}, u32[]{:S(2)}) collective-permute-start(f32[8,128]{1,0:T(8,128)S(1)} %get-tuple-element.133.refs_4_), channel_id=1, source_target_pairs={{0,16},{4,20},{8,24},{12,28},{16,0},{20,4},{24,8},{28,12},{1,17},{... | collective-permute-start | bytes 12296 | tf_op jit(solution)/shard_map/ppermute | solution.py:306
  104.4 8.5 %collective-permute-start.32 = (f32[8,256]{1,0:T(8,128)S(1)}, f32[8,256]{1,0:T(8,128)S(1)}, u32[]{:S(2)}, u32[]{:S(2)}) collective-permute-start(f32[8,256]{1,0:T(8,128)S(1)} %get-tuple-element.144.refs_7_), channel_id=1, source_target_pairs={{0,3},{1,0},{2,1},{3,2},{4,7},{5,4},{6,5},{7,6},{8,11},{9,8},{10,9... | collective-permute-start | bytes 24584 | tf_op jit(solution)/shard_map/ppermute | solution.py:311
  114.2 12.1 %collective-permute-start.33 = (f32[96,128]{1,0:T(8,128)S(1)}, f32[96,128]{1,0:T(8,128)S(1)}, u32[]{:S(2)}, u32[]{:S(2)}) collective-permute-start(f32[96,128]{1,0:T(8,128)S(1)} %get-tuple-element.145.refs_0_), channel_id=1, source_target_pairs={{4,0},{8,4},{12,8},{16,12},{20,16},{24,20},{28,24},{5,1},{9,5},{13... | collective-permute-start | bytes 147464 | tf_op jit(solution)/shard_map/ppermute | solution.py:302
  115.5 10.8 %collective-permute-start.34 = (f32[96,128]{1,0:T(8,128)S(1)}, f32[96,128]{1,0:T(8,128)S(1)}, u32[]{:S(2)}, u32[]{:S(2)}) collective-permute-start(f32[96,128]{1,0:T(8,128)S(1)} %get-tuple-element.146.refs_1_), channel_id=1, source_target_pairs={{0,4},{4,8},{8,12},{12,16},{16,20},{20,24},{24,28},{1,5},{5,9},{9,... | collective-permute-start | bytes 147464 | tf_op jit(solution)/shard_map/ppermute | solution.py:302
  118.5 7.7 %collective-permute-start.35 = (f32[8,128]{1,0:T(8,128)S(1)}, f32[8,128]{1,0:T(8,128)S(1)}, u32[]{:S(2)}, u32[]{:S(2)}) collective-permute-start(f32[8,128]{1,0:T(8,128)S(1)} %get-tuple-element.147.refs_4_), channel_id=1, source_target_pairs={{0,16},{4,20},{8,24},{12,28},{16,0},{20,4},{24,8},{28,12},{1,17},{... | collective-permute-start | bytes 12296 | tf_op jit(solution)/shard_map/ppermute | solution.py:306
  142.4 8.5 %collective-permute-start.44 = (f32[8,256]{1,0:T(8,128)S(1)}, f32[8,256]{1,0:T(8,128)S(1)}, u32[]{:S(2)}, u32[]{:S(2)}) collective-permute-start(f32[8,256]{1,0:T(8,128)S(1)} %get-tuple-element.166.refs_7_), channel_id=1, source_target_pairs={{0,3},{1,0},{2,1},{3,2},{4,7},{5,4},{6,5},{7,6},{8,11},{9,8},{10,9... | collective-permute-start | bytes 24584 | tf_op jit(solution)/shard_map/ppermute | solution.py:311
  152.2 12.1 %collective-permute-start.45 = (f32[96,128]{1,0:T(8,128)S(1)}, f32[96,128]{1,0:T(8,128)S(1)}, u32[]{:S(2)}, u32[]{:S(2)}) collective-permute-start(f32[96,128]{1,0:T(8,128)S(1)} %get-tuple-element.167.refs_0_), channel_id=1, source_target_pairs={{4,0},{8,4},{12,8},{16,12},{20,16},{24,20},{28,24},{5,1},{9,5},{13... | collective-permute-start | bytes 147464 | tf_op jit(solution)/shard_map/ppermute | solution.py:302
  153.5 10.8 %collective-permute-start.46 = (f32[96,128]{1,0:T(8,128)S(1)}, f32[96,128]{1,0:T(8,128)S(1)}, u32[]{:S(2)}, u32[]{:S(2)}) collective-permute-start(f32[96,128]{1,0:T(8,128)S(1)} %get-tuple-element.168.refs_1_), channel_id=1, source_target_pairs={{0,4},{4,8},{8,12},{12,16},{16,20},{20,24},{24,28},{1,5},{5,9},{9,... | collective-permute-start | bytes 147464 | tf_op jit(solution)/shard_map/ppermute | solution.py:302
  156.5 7.7 %collective-permute-start.47 = (f32[8,128]{1,0:T(8,128)S(1)}, f32[8,128]{1,0:T(8,128)S(1)}, u32[]{:S(2)}, u32[]{:S(2)}) collective-permute-start(f32[8,128]{1,0:T(8,128)S(1)} %get-tuple-element.169.refs_4_), channel_id=1, source_target_pairs={{0,16},{4,20},{8,24},{12,28},{16,0},{20,4},{24,8},{28,12},{1,17},{... | collective-permute-start | bytes 12296 | tf_op jit(solution)/shard_map/ppermute | solution.py:306
  180.4 8.5 %collective-permute-start.56 = (f32[8,256]{1,0:T(8,128)S(1)}, f32[8,256]{1,0:T(8,128)S(1)}, u32[]{:S(2)}, u32[]{:S(2)}) collective-permute-start(f32[8,256]{1,0:T(8,128)S(1)} %get-tuple-element.188.refs_7_), channel_id=1, source_target_pairs={{0,3},{1,0},{2,1},{3,2},{4,7},{5,4},{6,5},{7,6},{8,11},{9,8},{10,9... | collective-permute-start | bytes 24584 | tf_op jit(solution)/shard_map/ppermute | solution.py:311
  190.2 12.1 %collective-permute-start.57 = (f32[96,128]{1,0:T(8,128)S(1)}, f32[96,128]{1,0:T(8,128)S(1)}, u32[]{:S(2)}, u32[]{:S(2)}) collective-permute-start(f32[96,128]{1,0:T(8,128)S(1)} %get-tuple-element.189.refs_0_), channel_id=1, source_target_pairs={{4,0},{8,4},{12,8},{16,12},{20,16},{24,20},{28,24},{5,1},{9,5},{13... | collective-permute-start | bytes 147464 | tf_op jit(solution)/shard_map/ppermute | solution.py:302
  191.5 10.8 %collective-permute-start.58 = (f32[96,128]{1,0:T(8,128)S(1)}, f32[96,128]{1,0:T(8,128)S(1)}, u32[]{:S(2)}, u32[]{:S(2)}) collective-permute-start(f32[96,128]{1,0:T(8,128)S(1)} %get-tuple-element.190.refs_1_), channel_id=1, source_target_pairs={{0,4},{4,8},{8,12},{12,16},{16,20},{20,24},{24,28},{1,5},{5,9},{9,... | collective-permute-start | bytes 147464 | tf_op jit(solution)/shard_map/ppermute | solution.py:302
  194.5 7.7 %collective-permute-start.59 = (f32[8,128]{1,0:T(8,128)S(1)}, f32[8,128]{1,0:T(8,128)S(1)}, u32[]{:S(2)}, u32[]{:S(2)}) collective-permute-start(f32[8,128]{1,0:T(8,128)S(1)} %get-tuple-element.191.refs_4_), channel_id=1, source_target_pairs={{0,16},{4,20},{8,24},{12,28},{16,0},{20,4},{24,8},{28,12},{1,17},{... | collective-permute-start | bytes 12296 | tf_op jit(solution)/shard_map/ppermute | solution.py:306
  (45 other events, 298.5 us)

commit v2 on v1

--- a/solution.py
+++ b/solution.py
@@ -55,11 +55,13 @@
     return norm / curvature, beta, norm, curvature
 
 
-def collect_to(vector, selector, low_ref, high_ref):
+def collect_to(odd, vector, selector, near_ref, far_ref):
     iface, cells = vector.shape
     moved = exact_dot(vector, selector, NT)
-    low_ref[:iface] = moved[:, :cells]
-    high_ref[:iface] = vector - moved[:, cells:]
+    low = moved[:, :cells]
+    high = vector - moved[:, cells:]
+    near_ref[:iface] = jnp.where(odd, low, high)
+    far_ref[:iface] = jnp.where(odd, high, low)
 
 
 def spread_of(own, previous, selector):
@@ -96,40 +98,44 @@
     lax.fori_loop(0, table_ref.shape[0] // chunk, step, 0)
 
 
-def stiffen(own, previous, selector_ref, swap_ref, stiffness_ref, stiff_ref, low_ref, high_ref):
+def stiffen(odd, own, previous, selector_ref, swap_ref, stiffness_ref, stiff_ref, near_ref, far_ref):
     gap = spread_of(own, previous, selector_ref[...])
     taken = exact_dot(gap, swap_ref[...], NN)
     apply_blocks([stiffness_ref.at[0], stiffness_ref.at[1]], [gap, taken], stiff_ref)
-    collect_to(stiff_ref[...], selector_ref[...], low_ref, high_ref)
-
-
-def first_kernel(own_ref, previous_ref, selector_ref, swap_ref, stiffness_ref, low_ref, high_ref, stiff_ref):
+    collect_to(odd, stiff_ref[...], selector_ref[...], near_ref, far_ref)
+
+
+def first_kernel(
+    place_ref, own_ref, previous_ref, selector_ref, swap_ref, stiffness_ref, near_ref, far_ref, stiff_ref
+):
     iface, cells = own_ref.shape
+    odd = place_ref[0] % 2 == 1
     stiffen(
-        own_ref[...], previous_ref[...], selector_ref, swap_ref, stiffness_ref, stiff_ref, low_ref, high_ref
-    )
-    low_ref[iface:] = jnp.zeros((ROWS, cells), F32)
-    high_ref[iface:] = jnp.zeros((ROWS, cells), F32)
-
-
-def arrived(low_ref, high_ref, from_right_ref, from_left_ref, iface):
-    own = high_ref[:iface] - from_right_ref[:iface]
-    previous = from_left_ref[:iface] - low_ref[:iface]
+        odd, own_ref[...], previous_ref[...], selector_ref, swap_ref, stiffness_ref, stiff_ref, near_ref, far_ref
+    )
+    near_ref[iface:] = jnp.zeros((ROWS, cells), F32)
+
+
+def arrived(odd, near_ref, far_ref, from_near_ref, from_far_ref, iface):
+    near, far = near_ref[:iface], far_ref[...]
+    from_near, from_far = from_near_ref[:iface], from_far_ref[...]
+    own = jnp.where(odd, far - from_far, near - from_near)
+    previous = jnp.where(odd, from_near - near, from_far - far)
     return own, previous
 
 
 def second_kernel(
-    low_ref, high_ref, from_right_ref, from_left_ref, r_ref, u_ref, selector_ref, swap_ref, stiffness_ref,
-    low_out, high_out, w_out, stiff_ref,
+    place_ref, near_ref, far_ref, from_near_ref, from_far_ref, r_ref, u_ref, selector_ref, swap_ref, stiffness_ref,
+    near_out, far_out, w_out, stiff_ref,
 ):
     iface = r_ref.shape[0]
-    w, w_previous = arrived(low_ref, high_ref, from_right_ref, from_left_ref, iface)
+    odd = place_ref[0] % 2 == 1
+    w, w_previous = arrived(odd, near_ref, far_ref, from_near_ref, from_far_ref, iface)
     w_out[0] = w
     w_out[1] = w_previous
     dots = dot_rows(r_ref[...], u_ref[...], w)
-    low_out[iface:] = dots
-    high_out[iface:] = dots
-    stiffen(w, w_previous, selector_ref, swap_ref, stiffness_ref, stiff_ref, low_out, high_out)
+    near_out[iface:] = dots
+    stiffen(odd, w, w_previous, selector_ref, swap_ref, stiffness_ref, stiff_ref, near_out, far_out)
 
 
 def update(first, last, refs, m, n, n_previous, totals):
@@ -175,37 +181,36 @@
 
 
 def middle_kernel(first, last, *refs):
-    (low_ref, high_ref, from_right_ref, from_left_ref, dots_ref, dots_other_ref, m_ref) = refs[:7]
-    (selector_ref, swap_ref, stiffness_ref) = refs[7:10]
-    ins = list(refs[10:19])
-    outs = list(refs[19:28])
+    (place_ref, near_ref, far_ref, from_near_ref, from_far_ref, dots_ref, dots_other_ref, m_ref) = refs[:8]
+    (selector_ref, swap_ref, stiffness_ref) = refs[8:11]
+    ins = list(refs[11:20])
+    outs = list(refs[20:29])
     m = m_ref[...]
     iface = m.shape[0]
-    n, n_previous = arrived(low_ref, high_ref, from_right_ref, from_left_ref, iface)
+    odd = place_ref[0] % 2 == 1
+    n, n_previous = arrived(odd, near_ref, far_ref, from_near_ref, from_far_ref, iface)
     dots, w, previous = update(
         first, last, ins + outs, m, n, n_previous, dots_ref[...] + dots_other_ref[...]
     )
     if last:
-        dots_out = refs[28]
+        dots_out = refs[29]
         dots_out[...] = jnp.broadcast_to(dots[None], dots_out.shape)
     else:
-        low_out, high_out, stiff_ref = refs[28:31]
-        low_out[iface:] = dots
-        high_out[iface:] = dots
-        stiffen(w, previous, selector_ref, swap_ref, stiffness_ref, stiff_ref, low_out, high_out)
+        near_out, far_out, stiff_ref = refs[29:32]
+        near_out[iface:] = dots
+        stiffen(odd, w, previous, selector_ref, swap_ref, stiffness_ref, stiff_ref, near_out, far_out)
 
 
 def corner_kernel(
-    ranks, low_ref, high_ref, from_right_ref, from_left_ref, place_ref, selector_ref, operators_ref, table_ref,
+    ranks, place_ref, near_ref, far_ref, from_near_ref, from_far_ref, selector_ref, operators_ref, table_ref,
     m_out, gap_out, *rest,
 ):
     outs, sums_ref = rest[:ranks], rest[ranks]
     iface, cells = m_out.shape
-    own, previous = arrived(low_ref, high_ref, from_right_ref, from_left_ref, iface)
+    odd = place_ref[0] % 2 == 1
+    own, previous = arrived(odd, near_ref, far_ref, from_near_ref, from_far_ref, iface)
     m_out[...] = own
-    odd = place_ref[0] % 2
-    other = jnp.where(odd == 1, from_left_ref[iface:], from_right_ref[iface:])
-    dots = high_ref[iface:] + other
+    dots = near_ref[iface:] + from_near_ref[iface:]
     gap = spread_of(own, previous, selector_ref[...])
     gap_out[...] = gap
     parts = []
@@ -224,7 +229,7 @@
         tail.append(jnp.concatenate(lanes, axis=1))
     tail = jnp.concatenate(tail, axis=0)
     for distance in range(ranks):
-        rank = (place_ref[1] + distance) % ranks
+        rank = place_ref[1] ^ distance
         piece = sums_ref[:, pl.ds(pl.multiple_of(rank * owned, 128), owned)]
         outs[distance][...] = jnp.concatenate([piece[:CORNER_DOF], tail], axis=0)
 
@@ -237,7 +242,7 @@
     pieces, (solved_ref, dots_ref, sums_ref) = rest[:ranks], rest[ranks:]
     cells = dots_ref.shape[1]
     for distance in range(ranks):
-        rank = (place_ref[1] + ranks - distance) % ranks
+        rank = place_ref[1] ^ distance
         sums_ref[rank] = pieces[distance][...]
     total = sums_ref[0]
     for rank in range(1, ranks):
@@ -272,12 +277,12 @@
 
 
 def lift_kernel(ranks, place_ref, local_ref, operators_ref, table_ref, selector_ref, dots_ref, other_ref, *rest):
-    pieces, (low_ref, high_ref, dots_out, values_ref) = rest[:ranks], rest[ranks:]
+    pieces, (near_ref, far_ref, dots_out, values_ref) = rest[:ranks], rest[ranks:]
     cells = local_ref.shape[1]
     owned = values_ref.shape[1] // ranks
     dots_out[...] = dots_ref[...] + other_ref[...]
     for distance in range(ranks):
-        rank = (place_ref[1] + ranks - distance) % ranks
+        rank = place_ref[1] ^ distance
         values_ref[:, pl.ds(pl.multiple_of(rank * owned, 128), owned)] = pieces[distance][...]
     picked = exact_dot(values_ref[...], table_ref[...], NN)
     lifted = local_ref[...]
@@ -286,7 +291,7 @@
         for dof in range(CORNER_DOF):
             operator = operators_ref[corner * CORNER_DOF + dof].astype(F32)
             lifted = lifted + operator * picked[dof : dof + 1, lanes]
-    collect_to(lifted, selector_ref[...], low_ref, high_ref)
+    collect_to(place_ref[0] % 2 == 1, lifted, selector_ref[...], near_ref, far_ref)
 
 
 def final_kernel(dots_ref, scalars_ref, x_ref, r_ref, u_ref, w_ref, p_ref, s_ref, x_out, r_out):
@@ -306,9 +311,13 @@
     return lax.ppermute(block, "sub", [(i, i ^ bit) for i in range(lax.axis_size("sub"))])
 
 
-def rotated(block, distance):
-    count = lax.axis_size("grp")
-    return lax.ppermute(block, "grp", [(i, (i + distance) % count) for i in range(count)])
+def swapped_far(block):
+    inner = range(1, lax.axis_size("sub") - 1)
+    return lax.ppermute(block, "sub", [(i, i + 1 if i % 2 else i - 1) for i in inner])
+
+
+def exchanged(block, distance):
+    return lax.ppermute(block, "grp", [(i, i ^ distance) for i in range(lax.axis_size("grp"))])
 
 
 def shape(*dims, dtype=F32):
@@ -377,20 +386,19 @@
     stiff_scratch = [pltpu.VMEM((iface, cells), F32)]
     stiff_cost = dict(flops=4 * iface * iface * cells, moved=4 * iface * iface * cells)
 
-    def apply_operator(low, high):
-        from_right = shifted(low, -1)
-        from_left = shifted(high, 1)
+    def apply_operator(near, far):
+        from_far, from_near = swapped_far(far), swapped(near, 1)
         m, gap, *parts = call(
             lambda *refs: corner_kernel(ranks, *refs),
             (field, field) + (piece,) * ranks,
-            in_smem=(4,),
+            in_smem=(0,),
             count=8,
             scratch=[pltpu.VMEM((ROWS, group), F32)],
             flops=2 * 24 * iface * cells,
             moved=2 * 24 * iface * cells + group * CORNERS_SUB * cells * 2,
             name="corners",
-        )(low, high, from_right, from_left, place, selector, operators, table)
-        arrivals = [parts[0]] + [rotated(parts[d], d) for d in range(1, ranks)]
+        )(place, near, far, from_near, from_far, selector, operators, table)
+        arrivals = [parts[0]] + [exchanged(parts[d], d) for d in range(1, ranks)]
         local = call(
             local_kernel,
             field,
@@ -409,9 +417,9 @@
             moved=2 * blocks_own * order * order,
             name="coarse",
         )(place, coarse_inverse, *arrivals)
-        values = [solved] + [rotated(solved, d) for d in range(1, ranks)]
+        values = [solved] + [exchanged(solved, d) for d in range(1, ranks)]
         other = swapped(dots, 2)
-        low, high, dots = call(
+        near, far, dots = call(
             lambda *refs: lift_kernel(ranks, *refs),
             (field, field, rows),
             in_smem=(0,),
@@ -421,24 +429,30 @@
             moved=2 * 24 * iface * cells + group * CORNERS_SUB * cells * 2,
             name="lift",
         )(place, local, operators, table, selector, dots, other, *values)
-        return m, low, high, dots
+        return m, near, far, dots
 
     previous = shifted(right_side, 1)
-    low, high = call(
-        first_kernel, (message, message), count=5, scratch=stiff_scratch, name="first", **stiff_cost
-    )(right_side, previous, selector, swap, stiff)
-    u, low, high, dots = apply_operator(low, high)
+    near, far = call(
+        first_kernel, (message, field), in_smem=(0,), count=6, scratch=stiff_scratch, name="first", **stiff_cost
+    )(place, right_side, previous, selector, swap, stiff)
+    u, near, far, dots = apply_operator(near, far)
     r = right_side
-    from_right, from_left = shifted(low, -1), shifted(high, 1)
-    low, high, w = call(
-        second_kernel, (message, message, pair), count=9, scratch=stiff_scratch, name="second", **stiff_cost
-    )(low, high, from_right, from_left, r, u, selector, swap, stiff)
+    from_far, from_near = swapped_far(far), swapped(near, 1)
+    near, far, w = call(
+        second_kernel,
+        (message, field, pair),
+        in_smem=(0,),
+        count=10,
+        scratch=stiff_scratch,
+        name="second",
+        **stiff_cost,
+    )(place, near, far, from_near, from_far, r, u, selector, swap, stiff)
 
     scalars, x, p, s, q, z = [jnp.zeros((ROWS, cells), F32)] + [r] * 4 + [w]
     for step in range(ITERS - 1):
         first, last = step == 0, step == ITERS - 2
-        m, low, high, dots = apply_operator(low, high)
-        from_right, from_left, other = shifted(low, -1), shifted(high, 1), swapped(dots, 4)
+        m, near, far, dots = apply_operator(near, far)
+        from_far, from_near, other = swapped_far(far), swapped(near, 1), swapped(dots, 4)
         bit = 8
         while bit < sub_count:
             dots = dots + other
@@ -449,21 +463,22 @@
             count = sub_count * ranks
             outs += (shape(count, ROWS, cells),)
         else:
-            outs += (message, message)
+            outs += (message, field)
         result = call(
             lambda *refs, first=first, last=last: middle_kernel(first, last, *refs),
             outs,
-            count=19,
+            in_smem=(0,),
+            count=20,
             scratch=() if last else stiff_scratch,
             name="last" if last else "middle",
             **({} if last else stiff_cost),
         )(
-            low, high, from_right, from_left, dots, other, m, selector, swap, stiff,
+            place, near, far, from_near, from_far, dots, other, m, selector, swap, stiff,
             scalars, x, r, u, w, p, s, q, z,
         )
         scalars, x, r, u, w, p, s, q, z = result[:9]
         if not last:
-            low, high = result[9:]
+            near, far = result[9:]
     everyone = lax.all_to_all(result[9], ("sub", "grp"), 0, 0, tiled=True)
     x, r = call(final_kernel, (field, field), count=8, name="final")(
         everyone, scalars, x, r, u, w, p, s

time: 217 us -> 203 us (0.935)
  starting transfers between devices: 136 us -> 115 us
  waiting for transfers between devices: 27.6 us -> 32.9 us
  Pallas kernels: 33.3 us -> 36.7 us
    ppermute x21 -> x1, starting transfers between devices: 50.5 us -> 2.36 us  [shifted(): return lax.ppermute(block, 'sub', route)]
    ppermute x9 -> x19, starting transfers between devices: 43.7 us -> 61.4 us  [swapped(): lax.ppermute(block, 'sub', [(i, i ^ bit) for i in range(lax.axis_size('su...]
    ppermute x30 -> x40, starting transfers between devices: 41.9 us -> 50.9 us  [the longest x30 44.3 us: exchanged(): lax.ppermute(block, 'grp', [(i, i ^ distance) for i in range(lax.axis_siz...]
    ppermute x30 -> x40, waiting for transfers between devices: 11.6 us -> 19.5 us  [the longest x30 19.4 us: exchanged(): lax.ppermute(block, 'grp', [(i, i ^ distance) for i in range(lax.axis_siz...]
    ppermute x21 -> x1, waiting for transfers between devices: 5.09 us -> 0.01 us  [shifted(): return lax.ppermute(block, 'sub', route)]
    ppermute x9 -> x19, waiting for transfers between devices: 10.8 us -> 13.4 us  [swapped(): lax.ppermute(block, 'sub', [(i, i ^ bit) for i in range(lax.axis_size('su...]
    pallas_call x4, Pallas kernels: 6.84 us -> 9.05 us  [on_device(): call(lambda *refs, first=first, last=last: middle_kernel(first, last, *re...]
  transfers between devices with their start and end apart: 60 -> 60, of which waited for: 32 -> 25; matrix products, arithmetic and copies ran while one was open for 0% -> 0% of each run, Pallas kernels for 2% -> 2%
where the time goes in v2:
time: 203 us
  starting transfers between devices  115 us (57%)
  Pallas kernels  36.7 us (18%)
  waiting for transfers between devices  32.9 us (16%)
  blocking collectives  11.8 us (6%)
  local copies, waits for them, and re-layouts  4.9 us (2%)
    ppermute x19, starting transfers between devices, swapped(): lax.ppermute(block, 'sub', [(i, i ^ bit) for i in range(lax.axis_size('su...  61.4 us
    ppermute x30, starting transfers between devices, exchanged(): lax.ppermute(block, 'grp', [(i, i ^ distance) for i in range(lax.axis_siz...  44.3 us
    ppermute x30, waiting for transfers between devices, exchanged(): lax.ppermute(block, 'grp', [(i, i ^ distance) for i in range(lax.axis_siz...  19.4 us
    ppermute x19, waiting for transfers between devices, swapped(): lax.ppermute(block, 'sub', [(i, i ^ bit) for i in range(lax.axis_size('su...  13.4 us
    all_to_all x1, blocking collectives, on_device(): everyone = lax.all_to_all(result[9], ('sub', 'grp'), 0, 0, tiled=True)  11.8 us
    pallas_call x4, Pallas kernels, on_device(): call(lambda *refs, first=first, last=last: middle_kernel(first, last, *re...  9.05 us
    ppermute x10, starting transfers between devices, swapped_far(): lax.ppermute(block, 'sub', [(i, i + 1 if i % 2 else i - 1) for i in inner])  6.59 us
    pallas_call x5, Pallas kernels, apply_operator(): call(lambda *refs: coarse_kernel(ranks, *refs), (piece, rows), in_smem=(0...  6.26 us
  transfers between devices with their start and end apart: 60, of which 25 were waited for; matrix products, arithmetic and copies ran while one was open for 0% of the time, Pallas kernels for 2%

profile of v2, /device:TPU:0, one launch (start us, length us, event | category | flops | bytes accessed | tf_op | source)
XLA Modules:
  0.0 202.8 jit_solution(17412651427980631667)
XLA Ops:
  10.3 2.7 %collective-permute-start.1 = (f32[104,128]{1,0:T(8,128)S(1)}, f32[104,128]{1,0:T(8,128)S(1)}, u32[]{:S(2)}, u32[]{:S(2)}) collective-permute-start(f32[104,128]{1,0:T(8,128)S(1)} %get-tuple-element.109.refs_1_), channel_id=1, source_target_pairs={{0,4},{4,0},{8,12},{12,8},{16,20},{20,16},{24,28},{28,24},{1,5},{5... | collective-permute-start | bytes 159752 | tf_op jit(solution)/shard_map/ppermute | solution.py:311
  22.4 3.5 %collective-permute-done.5.refs_5_ = f32[8,256]{1,0:T(8,128)S(1)} collective-permute-done((f32[8,256]{1,0:T(8,128)S(1)}, f32[8,256]{1,0:T(8,128)S(1)}, u32[]{:S(2)}, u32[]{:S(2)}) %collective-permute-start.5) | collective-permute-done | bytes 8224 | tf_op jit(solution)/shard_map/ppermute | solution.py:320
  27.4 4.2 %collective-permute-start.7 = (f32[8,256]{1,0:T(8,128)S(1)}, f32[8,256]{1,0:T(8,128)S(1)}, u32[]{:S(2)}, u32[]{:S(2)}) collective-permute-start(f32[8,256]{1,0:T(8,128)S(1)} %get-tuple-element.118.refs_7_), channel_id=1, source_target_pairs={{0,1},{1,0},{2,3},{3,2},{4,5},{5,4},{6,7},{7,6},{8,9},{9,8},{10,11... | collective-permute-start | bytes 24584 | tf_op jit(solution)/shard_map/ppermute | solution.py:320
  31.6 6.5 %collective-permute-start.6 = (f32[8,128]{1,0:T(8,128)S(1)}, f32[8,128]{1,0:T(8,128)S(1)}, u32[]{:S(2)}, u32[]{:S(2)}) collective-permute-start(f32[8,128]{1,0:T(8,128)S(1)} %get-tuple-element.117.refs_5_), channel_id=1, source_target_pairs={{0,8},{4,12},{8,0},{12,4},{16,24},{20,28},{24,16},{28,20},{1,9},{5... | collective-permute-start | bytes 12296 | tf_op jit(solution)/shard_map/ppermute | solution.py:311
  45.0 4.7 %collective-permute-start.12 = (f32[104,128]{1,0:T(8,128)S(1)}, f32[104,128]{1,0:T(8,128)S(1)}, u32[]{:S(2)}, u32[]{:S(2)}) collective-permute-start(f32[104,128]{1,0:T(8,128)S(1)} %get-tuple-element.122.refs_1_), channel_id=1, source_target_pairs={{0,4},{4,0},{8,12},{12,8},{16,20},{20,16},{24,28},{28,24},{1,5},{5... | collective-permute-start | bytes 159752 | tf_op jit(solution)/shard_map/ppermute | solution.py:311
  52.7 3.6 %collective-permute-start.16 = (f32[8,256]{1,0:T(8,128)S(1)}, f32[8,256]{1,0:T(8,128)S(1)}, u32[]{:S(2)}, u32[]{:S(2)}) collective-permute-start(f32[8,256]{1,0:T(8,128)S(1)} %get-tuple-element.128), channel_id=1, source_target_pairs={{0,3},{1,2},{2,1},{3,0},{4,7},{5,6},{6,5},{7,4},{8,11},{9,10},{10,... | collective-permute-start | bytes 24584 | tf_op jit(solution)/shard_map/ppermute | solution.py:320
  59.4 3.6 %collective-permute-start.20 = (f32[8,256]{1,0:T(8,128)S(1)}, f32[8,256]{1,0:T(8,128)S(1)}, u32[]{:S(2)}, u32[]{:S(2)}) collective-permute-start(f32[8,256]{1,0:T(8,128)S(1)} %get-tuple-element.130.refs_7_), channel_id=1, source_target_pairs={{0,3},{1,2},{2,1},{3,0},{4,7},{5,6},{6,5},{7,4},{8,11},{9,10},{10,... | collective-permute-start | bytes 24584 | tf_op jit(solution)/shard_map/ppermute | solution.py:320
  63.8 8.2 %collective-permute-start.17 = (f32[8,128]{1,0:T(8,128)S(1)}, f32[8,128]{1,0:T(8,128)S(1)}, u32[]{:S(2)}, u32[]{:S(2)}) collective-permute-start(f32[8,128]{1,0:T(8,128)S(1)} %get-tuple-element.129.refs_5_), channel_id=1, source_target_pairs={{0,8},{4,12},{8,0},{12,4},{16,24},{20,28},{24,16},{28,20},{1,9},{5... | collective-permute-start | bytes 12296 | tf_op jit(solution)/shard_map/ppermute | solution.py:311
  75.5 5.0 %collective-permute-start.23 = (f32[8,128]{1,0:T(8,128)S(1)}, f32[8,128]{1,0:T(8,128)S(1)}, u32[]{:S(2)}, u32[]{:S(2)}) collective-permute-start(f32[8,128]{1,0:T(8,128)S(1)} %get-tuple-element.133.refs_5_), channel_id=1, source_target_pairs={{0,16},{4,20},{8,24},{12,28},{16,0},{20,4},{24,8},{28,12},{1,17},{... | collective-permute-start | bytes 12296 | tf_op jit(solution)/shard_map/ppermute | solution.py:311
  88.3 2.9 %collective-permute-start.27 = (f32[8,256]{1,0:T(8,128)S(1)}, f32[8,256]{1,0:T(8,128)S(1)}, u32[]{:S(2)}, u32[]{:S(2)}) collective-permute-start(f32[8,256]{1,0:T(8,128)S(1)} %get-tuple-element.141), channel_id=1, source_target_pairs={{0,2},{1,3},{2,0},{3,1},{4,6},{5,7},{6,4},{7,5},{8,10},{9,11},{10,... | collective-permute-start | bytes 24584 | tf_op jit(solution)/shard_map/ppermute | solution.py:320
  92.9 3.9 %collective-permute-done.28.refs_5_ = f32[8,256]{1,0:T(8,128)S(1)} collective-permute-done((f32[8,256]{1,0:T(8,128)S(1)}, f32[8,256]{1,0:T(8,128)S(1)}, u32[]{:S(2)}, u32[]{:S(2)}) %collective-permute-start.28) | collective-permute-done | bytes 8224 | tf_op jit(solution)/shard_map/ppermute | solution.py:320
  98.3 4.1 %collective-permute-start.30 = (f32[8,256]{1,0:T(8,128)S(1)}, f32[8,256]{1,0:T(8,128)S(1)}, u32[]{:S(2)}, u32[]{:S(2)}) collective-permute-start(f32[8,256]{1,0:T(8,128)S(1)} %get-tuple-element.144.refs_7_), channel_id=1, source_target_pairs={{0,1},{1,0},{2,3},{3,2},{4,5},{5,4},{6,7},{7,6},{8,9},{9,8},{10,11... | collective-permute-start | bytes 24584 | tf_op jit(solution)/shard_map/ppermute | solution.py:320
  102.4 6.6 %collective-permute-start.29 = (f32[8,128]{1,0:T(8,128)S(1)}, f32[8,128]{1,0:T(8,128)S(1)}, u32[]{:S(2)}, u32[]{:S(2)}) collective-permute-start(f32[8,128]{1,0:T(8,128)S(1)} %get-tuple-element.143.refs_5_), channel_id=1, source_target_pairs={{0,8},{4,12},{8,0},{12,4},{16,24},{20,28},{24,16},{28,20},{1,9},{5... | collective-permute-start | bytes 12296 | tf_op jit(solution)/shard_map/ppermute | solution.py:311
  112.5 4.9 %collective-permute-start.35 = (f32[8,128]{1,0:T(8,128)S(1)}, f32[8,128]{1,0:T(8,128)S(1)}, u32[]{:S(2)}, u32[]{:S(2)}) collective-permute-start(f32[8,128]{1,0:T(8,128)S(1)} %get-tuple-element.147.refs_5_), channel_id=1, source_target_pairs={{0,16},{4,20},{8,24},{12,28},{16,0},{20,4},{24,8},{28,12},{1,17},{... | collective-permute-start | bytes 12296 | tf_op jit(solution)/shard_map/ppermute | solution.py:311
  125.1 3.5 %collective-permute-start.40 = (f32[8,256]{1,0:T(8,128)S(1)}, f32[8,256]{1,0:T(8,128)S(1)}, u32[]{:S(2)}, u32[]{:S(2)}) collective-permute-start(f32[8,256]{1,0:T(8,128)S(1)} %get-tuple-element.164), channel_id=1, source_target_pairs={{0,3},{1,2},{2,1},{3,0},{4,7},{5,6},{6,5},{7,4},{8,11},{9,10},{10,... | collective-permute-start | bytes 24584 | tf_op jit(solution)/shard_map/ppermute | solution.py:320
  131.8 3.5 %collective-permute-start.44 = (f32[8,256]{1,0:T(8,128)S(1)}, f32[8,256]{1,0:T(8,128)S(1)}, u32[]{:S(2)}, u32[]{:S(2)}) collective-permute-start(f32[8,256]{1,0:T(8,128)S(1)} %get-tuple-element.166.refs_7_), channel_id=1, source_target_pairs={{0,3},{1,2},{2,1},{3,0},{4,7},{5,6},{6,5},{7,4},{8,11},{9,10},{10,... | collective-permute-start | bytes 24584 | tf_op jit(solution)/shard_map/ppermute | solution.py:320
  136.2 6.2 %collective-permute-start.41 = (f32[8,128]{1,0:T(8,128)S(1)}, f32[8,128]{1,0:T(8,128)S(1)}, u32[]{:S(2)}, u32[]{:S(2)}) collective-permute-start(f32[8,128]{1,0:T(8,128)S(1)} %get-tuple-element.165.refs_5_), channel_id=1, source_target_pairs={{0,8},{4,12},{8,0},{12,4},{16,24},{20,28},{24,16},{28,20},{1,9},{5... | collective-permute-start | bytes 12296 | tf_op jit(solution)/shard_map/ppermute | solution.py:311
  145.9 4.9 %collective-permute-start.47 = (f32[8,128]{1,0:T(8,128)S(1)}, f32[8,128]{1,0:T(8,128)S(1)}, u32[]{:S(2)}, u32[]{:S(2)}) collective-permute-start(f32[8,128]{1,0:T(8,128)S(1)} %get-tuple-element.169.refs_5_), channel_id=1, source_target_pairs={{0,16},{4,20},{8,24},{12,28},{16,0},{20,4},{24,8},{28,12},{1,17},{... | collective-permute-start | bytes 12296 | tf_op jit(solution)/shard_map/ppermute | solution.py:311
  158.7 2.9 %collective-permute-start.51 = (f32[8,256]{1,0:T(8,128)S(1)}, f32[8,256]{1,0:T(8,128)S(1)}, u32[]{:S(2)}, u32[]{:S(2)}) collective-permute-start(f32[8,256]{1,0:T(8,128)S(1)} %get-tuple-element.185), channel_id=1, source_target_pairs={{0,2},{1,3},{2,0},{3,1},{4,6},{5,7},{6,4},{7,5},{8,10},{9,11},{10,... | collective-permute-start | bytes 24584 | tf_op jit(solution)/shard_map/ppermute | solution.py:320
  163.3 3.8 %collective-permute-done.52.refs_5_ = f32[8,256]{1,0:T(8,128)S(1)} collective-permute-done((f32[8,256]{1,0:T(8,128)S(1)}, f32[8,256]{1,0:T(8,128)S(1)}, u32[]{:S(2)}, u32[]{:S(2)}) %collective-permute-start.52) | collective-permute-done | bytes 8224 | tf_op jit(solution)/shard_map/ppermute | solution.py:320
  168.7 4.0 %collective-permute-start.54 = (f32[8,256]{1,0:T(8,128)S(1)}, f32[8,256]{1,0:T(8,128)S(1)}, u32[]{:S(2)}, u32[]{:S(2)}) collective-permute-start(f32[8,256]{1,0:T(8,128)S(1)} %get-tuple-element.188.refs_7_), channel_id=1, source_target_pairs={{0,1},{1,0},{2,3},{3,2},{4,5},{5,4},{6,7},{7,6},{8,9},{9,8},{10,11... | collective-permute-start | bytes 24584 | tf_op jit(solution)/shard_map/ppermute | solution.py:320
  172.8 6.3 %collective-permute-start.53 = (f32[8,128]{1,0:T(8,128)S(1)}, f32[8,128]{1,0:T(8,128)S(1)}, u32[]{:S(2)}, u32[]{:S(2)}) collective-permute-start(f32[8,128]{1,0:T(8,128)S(1)} %get-tuple-element.187.refs_5_), channel_id=1, source_target_pairs={{0,8},{4,12},{8,0},{12,4},{16,24},{20,28},{24,16},{28,20},{1,9},{5... | collective-permute-start | bytes 12296 | tf_op jit(solution)/shard_map/ppermute | solution.py:311
  182.5 4.9 %collective-permute-start.59 = (f32[8,128]{1,0:T(8,128)S(1)}, f32[8,128]{1,0:T(8,128)S(1)}, u32[]{:S(2)}, u32[]{:S(2)}) collective-permute-start(f32[8,128]{1,0:T(8,128)S(1)} %get-tuple-element.191.refs_5_), channel_id=1, source_target_pairs={{0,16},{4,20},{8,24},{12,28},{16,0},{20,4},{24,8},{28,12},{1,17},{... | collective-permute-start | bytes 12296 | tf_op jit(solution)/shard_map/ppermute | solution.py:311
  190.2 11.8 %all_to_all.5.dots_ref = f32[32,8,128]{2,1,0:T(8,128)S(1)} all-to-all(f32[32,8,128]{2,1,0:T(8,128)S(1)} %get-tuple-element.202), channel_id=1, replica_groups=mesh['sub'=8,'grp'=4] {'sub','grp'}, dimensions={0} | all-to-all | bytes 262144 | tf_op jit(solution)/shard_map/all_to_all | solution.py:482
  (147 shorter events, 85.6 us)
Async XLA Ops:
  27.2 12.5 %collective-permute-start.9 = (f32[8,256]{1,0:T(8,128)S(1)}, f32[8,256]{1,0:T(8,128)S(1)}, u32[]{:S(2)}, u32[]{:S(2)}) collective-permute-start(f32[8,256]{1,0:T(8,128)S(1)} %get-tuple-element.118.refs_7_), channel_id=1, source_target_pairs={{0,3},{1,2},{2,1},{3,0},{4,7},{5,6},{6,5},{7,4},{8,11},{9,10},{10,... | collective-permute-start | bytes 24584 | tf_op jit(solution)/shard_map/ppermute | solution.py:320
  27.4 12.3 %collective-permute-start.8 = (f32[8,256]{1,0:T(8,128)S(1)}, f32[8,256]{1,0:T(8,128)S(1)}, u32[]{:S(2)}, u32[]{:S(2)}) collective-permute-start(f32[8,256]{1,0:T(8,128)S(1)} %get-tuple-element.118.refs_7_), channel_id=1, source_target_pairs={{0,2},{1,3},{2,0},{3,1},{4,6},{5,7},{6,4},{7,5},{8,10},{9,11},{10,... | collective-permute-start | bytes 24584 | tf_op jit(solution)/shard_map/ppermute | solution.py:320
  27.4 12.3 %collective-permute-start.7 = (f32[8,256]{1,0:T(8,128)S(1)}, f32[8,256]{1,0:T(8,128)S(1)}, u32[]{:S(2)}, u32[]{:S(2)}) collective-permute-start(f32[8,256]{1,0:T(8,128)S(1)} %get-tuple-element.118.refs_7_), channel_id=1, source_target_pairs={{0,1},{1,0},{2,3},{3,2},{4,5},{5,4},{6,7},{7,6},{8,9},{9,8},{10,11... | collective-permute-start | bytes 24584 | tf_op jit(solution)/shard_map/ppermute | solution.py:320
  31.6 8.1 %collective-permute-start.6 = (f32[8,128]{1,0:T(8,128)S(1)}, f32[8,128]{1,0:T(8,128)S(1)}, u32[]{:S(2)}, u32[]{:S(2)}) collective-permute-start(f32[8,128]{1,0:T(8,128)S(1)} %get-tuple-element.117.refs_5_), channel_id=1, source_target_pairs={{0,8},{4,12},{8,0},{12,4},{16,24},{20,28},{24,16},{28,20},{1,9},{5... | collective-permute-start | bytes 12296 | tf_op jit(solution)/shard_map/ppermute | solution.py:311
  59.4 14.2 %collective-permute-start.20 = (f32[8,256]{1,0:T(8,128)S(1)}, f32[8,256]{1,0:T(8,128)S(1)}, u32[]{:S(2)}, u32[]{:S(2)}) collective-permute-start(f32[8,256]{1,0:T(8,128)S(1)} %get-tuple-element.130.refs_7_), channel_id=1, source_target_pairs={{0,3},{1,2},{2,1},{3,0},{4,7},{5,6},{6,5},{7,4},{8,11},{9,10},{10,... | collective-permute-start | bytes 24584 | tf_op jit(solution)/shard_map/ppermute | solution.py:320
  63.0 10.6 %collective-permute-start.19 = (f32[8,256]{1,0:T(8,128)S(1)}, f32[8,256]{1,0:T(8,128)S(1)}, u32[]{:S(2)}, u32[]{:S(2)}) collective-permute-start(f32[8,256]{1,0:T(8,128)S(1)} %get-tuple-element.130.refs_7_), channel_id=1, source_target_pairs={{0,2},{1,3},{2,0},{3,1},{4,6},{5,7},{6,4},{7,5},{8,10},{9,11},{10,... | collective-permute-start | bytes 24584 | tf_op jit(solution)/shard_map/ppermute | solution.py:320
  63.0 10.6 %collective-permute-start.18 = (f32[8,256]{1,0:T(8,128)S(1)}, f32[8,256]{1,0:T(8,128)S(1)}, u32[]{:S(2)}, u32[]{:S(2)}) collective-permute-start(f32[8,256]{1,0:T(8,128)S(1)} %get-tuple-element.130.refs_7_), channel_id=1, source_target_pairs={{0,1},{1,0},{2,3},{3,2},{4,5},{5,4},{6,7},{7,6},{8,9},{9,8},{10,11... | collective-permute-start | bytes 24584 | tf_op jit(solution)/shard_map/ppermute | solution.py:320
  63.8 9.7 %collective-permute-start.17 = (f32[8,128]{1,0:T(8,128)S(1)}, f32[8,128]{1,0:T(8,128)S(1)}, u32[]{:S(2)}, u32[]{:S(2)}) collective-permute-start(f32[8,128]{1,0:T(8,128)S(1)} %get-tuple-element.129.refs_5_), channel_id=1, source_target_pairs={{0,8},{4,12},{8,0},{12,4},{16,24},{20,28},{24,16},{28,20},{1,9},{5... | collective-permute-start | bytes 12296 | tf_op jit(solution)/shard_map/ppermute | solution.py:311
  74.7 7.3 %collective-permute-start.21 = (f32[96,128]{1,0:T(8,128)S(1)}, f32[96,128]{1,0:T(8,128)S(1)}, u32[]{:S(2)}, u32[]{:S(2)}) collective-permute-start(f32[96,128]{1,0:T(8,128)S(1)} %get-tuple-element.131.refs_1_), channel_id=1, source_target_pairs={{0,4},{4,0},{8,12},{12,8},{16,20},{20,16},{24,28},{28,24},{1,5},{5... | collective-permute-start | bytes 147464 | tf_op jit(solution)/shard_map/ppermute | solution.py:311
  74.8 7.2 %collective-permute-start.22 = (f32[96,128]{1,0:T(8,128)S(1)}, f32[96,128]{1,0:T(8,128)S(1)}, u32[]{:S(2)}, u32[]{:S(2)}) collective-permute-start(f32[96,128]{1,0:T(8,128)S(1)} %get-tuple-element.132.refs_2_), channel_id=1, source_target_pairs={{4,8},{8,4},{12,16},{16,12},{20,24},{24,20},{5,9},{9,5},{13,17},{1... | collective-permute-start | bytes 147464 | tf_op jit(solution)/shard_map/ppermute | solution.py:316
  98.0 12.6 %collective-permute-start.32 = (f32[8,256]{1,0:T(8,128)S(1)}, f32[8,256]{1,0:T(8,128)S(1)}, u32[]{:S(2)}, u32[]{:S(2)}) collective-permute-start(f32[8,256]{1,0:T(8,128)S(1)} %get-tuple-element.144.refs_7_), channel_id=1, source_target_pairs={{0,3},{1,2},{2,1},{3,0},{4,7},{5,6},{6,5},{7,4},{8,11},{9,10},{10,... | collective-permute-start | bytes 24584 | tf_op jit(solution)/shard_map/ppermute | solution.py:320
  98.3 12.3 %collective-permute-start.31 = (f32[8,256]{1,0:T(8,128)S(1)}, f32[8,256]{1,0:T(8,128)S(1)}, u32[]{:S(2)}, u32[]{:S(2)}) collective-permute-start(f32[8,256]{1,0:T(8,128)S(1)} %get-tuple-element.144.refs_7_), channel_id=1, source_target_pairs={{0,2},{1,3},{2,0},{3,1},{4,6},{5,7},{6,4},{7,5},{8,10},{9,11},{10,... | collective-permute-start | bytes 24584 | tf_op jit(solution)/shard_map/ppermute | solution.py:320
  98.3 12.3 %collective-permute-start.30 = (f32[8,256]{1,0:T(8,128)S(1)}, f32[8,256]{1,0:T(8,128)S(1)}, u32[]{:S(2)}, u32[]{:S(2)}) collective-permute-start(f32[8,256]{1,0:T(8,128)S(1)} %get-tuple-element.144.refs_7_), channel_id=1, source_target_pairs={{0,1},{1,0},{2,3},{3,2},{4,5},{5,4},{6,7},{7,6},{8,9},{9,8},{10,11... | collective-permute-start | bytes 24584 | tf_op jit(solution)/shard_map/ppermute | solution.py:320
  102.4 8.2 %collective-permute-start.29 = (f32[8,128]{1,0:T(8,128)S(1)}, f32[8,128]{1,0:T(8,128)S(1)}, u32[]{:S(2)}, u32[]{:S(2)}) collective-permute-start(f32[8,128]{1,0:T(8,128)S(1)} %get-tuple-element.143.refs_5_), channel_id=1, source_target_pairs={{0,8},{4,12},{8,0},{12,4},{16,24},{20,28},{24,16},{28,20},{1,9},{5... | collective-permute-start | bytes 12296 | tf_op jit(solution)/shard_map/ppermute | solution.py:311
  131.8 12.2 %collective-permute-start.44 = (f32[8,256]{1,0:T(8,128)S(1)}, f32[8,256]{1,0:T(8,128)S(1)}, u32[]{:S(2)}, u32[]{:S(2)}) collective-permute-start(f32[8,256]{1,0:T(8,128)S(1)} %get-tuple-element.166.refs_7_), channel_id=1, source_target_pairs={{0,3},{1,2},{2,1},{3,0},{4,7},{5,6},{6,5},{7,4},{8,11},{9,10},{10,... | collective-permute-start | bytes 24584 | tf_op jit(solution)/shard_map/ppermute | solution.py:320
  135.3 8.8 %collective-permute-start.43 = (f32[8,256]{1,0:T(8,128)S(1)}, f32[8,256]{1,0:T(8,128)S(1)}, u32[]{:S(2)}, u32[]{:S(2)}) collective-permute-start(f32[8,256]{1,0:T(8,128)S(1)} %get-tuple-element.166.refs_7_), channel_id=1, source_target_pairs={{0,2},{1,3},{2,0},{3,1},{4,6},{5,7},{6,4},{7,5},{8,10},{9,11},{10,... | collective-permute-start | bytes 24584 | tf_op jit(solution)/shard_map/ppermute | solution.py:320
  135.3 8.8 %collective-permute-start.42 = (f32[8,256]{1,0:T(8,128)S(1)}, f32[8,256]{1,0:T(8,128)S(1)}, u32[]{:S(2)}, u32[]{:S(2)}) collective-permute-start(f32[8,256]{1,0:T(8,128)S(1)} %get-tuple-element.166.refs_7_), channel_id=1, source_target_pairs={{0,1},{1,0},{2,3},{3,2},{4,5},{5,4},{6,7},{7,6},{8,9},{9,8},{10,11... | collective-permute-start | bytes 24584 | tf_op jit(solution)/shard_map/ppermute | solution.py:320
  136.2 7.8 %collective-permute-start.41 = (f32[8,128]{1,0:T(8,128)S(1)}, f32[8,128]{1,0:T(8,128)S(1)}, u32[]{:S(2)}, u32[]{:S(2)}) collective-permute-start(f32[8,128]{1,0:T(8,128)S(1)} %get-tuple-element.165.refs_5_), channel_id=1, source_target_pairs={{0,8},{4,12},{8,0},{12,4},{16,24},{20,28},{24,16},{28,20},{1,9},{5... | collective-permute-start | bytes 12296 | tf_op jit(solution)/shard_map/ppermute | solution.py:311
  145.2 7.2 %collective-permute-start.45 = (f32[96,128]{1,0:T(8,128)S(1)}, f32[96,128]{1,0:T(8,128)S(1)}, u32[]{:S(2)}, u32[]{:S(2)}) collective-permute-start(f32[96,128]{1,0:T(8,128)S(1)} %get-tuple-element.167.refs_1_), channel_id=1, source_target_pairs={{0,4},{4,0},{8,12},{12,8},{16,20},{20,16},{24,28},{28,24},{1,5},{5... | collective-permute-start | bytes 147464 | tf_op jit(solution)/shard_map/ppermute | solution.py:311
  168.3 12.3 %collective-permute-start.56 = (f32[8,256]{1,0:T(8,128)S(1)}, f32[8,256]{1,0:T(8,128)S(1)}, u32[]{:S(2)}, u32[]{:S(2)}) collective-permute-start(f32[8,256]{1,0:T(8,128)S(1)} %get-tuple-element.188.refs_7_), channel_id=1, source_target_pairs={{0,3},{1,2},{2,1},{3,0},{4,7},{5,6},{6,5},{7,4},{8,11},{9,10},{10,... | collective-permute-start | bytes 24584 | tf_op jit(solution)/shard_map/ppermute | solution.py:320
  168.7 11.9 %collective-permute-start.55 = (f32[8,256]{1,0:T(8,128)S(1)}, f32[8,256]{1,0:T(8,128)S(1)}, u32[]{:S(2)}, u32[]{:S(2)}) collective-permute-start(f32[8,256]{1,0:T(8,128)S(1)} %get-tuple-element.188.refs_7_), channel_id=1, source_target_pairs={{0,2},{1,3},{2,0},{3,1},{4,6},{5,7},{6,4},{7,5},{8,10},{9,11},{10,... | collective-permute-start | bytes 24584 | tf_op jit(solution)/shard_map/ppermute | solution.py:320
  168.7 11.9 %collective-permute-start.54 = (f32[8,256]{1,0:T(8,128)S(1)}, f32[8,256]{1,0:T(8,128)S(1)}, u32[]{:S(2)}, u32[]{:S(2)}) collective-permute-start(f32[8,256]{1,0:T(8,128)S(1)} %get-tuple-element.188.refs_7_), channel_id=1, source_target_pairs={{0,1},{1,0},{2,3},{3,2},{4,5},{5,4},{6,7},{7,6},{8,9},{9,8},{10,11... | collective-permute-start | bytes 24584 | tf_op jit(solution)/shard_map/ppermute | solution.py:320
  172.8 7.9 %collective-permute-start.53 = (f32[8,128]{1,0:T(8,128)S(1)}, f32[8,128]{1,0:T(8,128)S(1)}, u32[]{:S(2)}, u32[]{:S(2)}) collective-permute-start(f32[8,128]{1,0:T(8,128)S(1)} %get-tuple-element.187.refs_5_), channel_id=1, source_target_pairs={{0,8},{4,12},{8,0},{12,4},{16,24},{20,28},{24,16},{28,20},{1,9},{5... | collective-permute-start | bytes 12296 | tf_op jit(solution)/shard_map/ppermute | solution.py:311
  181.8 7.2 %collective-permute-start.57 = (f32[96,128]{1,0:T(8,128)S(1)}, f32[96,128]{1,0:T(8,128)S(1)}, u32[]{:S(2)}, u32[]{:S(2)}) collective-permute-start(f32[96,128]{1,0:T(8,128)S(1)} %get-tuple-element.189.refs_1_), channel_id=1, source_target_pairs={{0,4},{4,0},{8,12},{12,8},{16,20},{20,16},{24,28},{28,24},{1,5},{5... | collective-permute-start | bytes 147464 | tf_op jit(solution)/shard_map/ppermute | solution.py:311
  (45 other events, 276.8 us)

commit v3 on v2

--- a/solution.py
+++ b/solution.py
@@ -9,6 +9,7 @@
 CORNERS_SUB = 4
 ITERS = 5
 ROWS = 8
+LANES = 128
 NN = (((1,), (0,)), ((), ()))
 NT = (((1,), (1,)), ((), ()))
 F32 = jnp.float32
@@ -29,29 +30,28 @@
     return product[:rows] + product[rows : 2 * rows] + product[2 * rows :]
 
 
-def lane_total(rows):
-    return jnp.sum(rows, axis=1, keepdims=True)
-
-
-def dot_rows(r, u, w, s=None, p=None):
-    rows = [jnp.sum(r * u, axis=0, keepdims=True), jnp.sum(u * w, axis=0, keepdims=True)]
-    if s is None:
-        rows.append(jnp.zeros((ROWS - 2, r.shape[1]), F32))
-    else:
-        rows.append(jnp.sum(u * s, axis=0, keepdims=True))
-        rows.append(jnp.sum(p * w, axis=0, keepdims=True))
-        rows.append(jnp.zeros((ROWS - 4, r.shape[1]), F32))
-    return jnp.concatenate(rows, axis=0)
-
-
-def step_sizes(totals, before):
-    sums = lane_total(totals)
-    norm, curvature = sums[0:1], sums[1:2]
+def dot_lanes(*pairs):
+    lane = lax.broadcasted_iota(jnp.int32, (1, LANES), 1)
+    row = jnp.zeros((1, LANES), F32)
+    for place, (first, second) in enumerate(pairs):
+        total = jnp.sum(jnp.sum(first * second, axis=0, keepdims=True), axis=1, keepdims=True)
+        row = jnp.where(lane == place, total, row)
+    return row
+
+
+def fill_lanes(out_ref, row):
+    block = jnp.broadcast_to(row, (ROWS, LANES))
+    for start in range(0, out_ref.shape[1], LANES):
+        out_ref[:, start : start + LANES] = block
+
+
+def step_sizes(sums, before):
+    norm, curvature = sums[:, 0:1], sums[:, 1:2]
     if before is None:
         beta = None
     else:
         beta = norm / before[0:1, 0:1]
-        curvature = curvature + beta * (sums[2:3] + sums[3:4]) + beta * beta * before[1:2, 0:1]
+        curvature = curvature + beta * (sums[:, 2:3] + sums[:, 3:4]) + beta * beta * before[1:2, 0:1]
     return norm / curvature, beta, norm, curvature
 
 
@@ -60,8 +60,8 @@
     moved = exact_dot(vector, selector, NT)
     low = moved[:, :cells]
     high = vector - moved[:, cells:]
-    near_ref[:iface] = jnp.where(odd, low, high)
-    far_ref[:iface] = jnp.where(odd, high, low)
+    near_ref[...] = jnp.where(odd, low, high)
+    far_ref[...] = jnp.where(odd, high, low)
 
 
 def spread_of(own, previous, selector):
@@ -106,35 +106,32 @@
 
 
 def first_kernel(
-    place_ref, own_ref, previous_ref, selector_ref, swap_ref, stiffness_ref, near_ref, far_ref, stiff_ref
+    own_ref, previous_ref, selector_ref, swap_ref, stiffness_ref, near_ref, far_ref, stiff_ref
 ):
-    iface, cells = own_ref.shape
-    odd = place_ref[0] % 2 == 1
+    odd = lax.axis_index("sub") % 2 == 1
     stiffen(
         odd, own_ref[...], previous_ref[...], selector_ref, swap_ref, stiffness_ref, stiff_ref, near_ref, far_ref
     )
-    near_ref[iface:] = jnp.zeros((ROWS, cells), F32)
-
-
-def arrived(odd, near_ref, far_ref, from_near_ref, from_far_ref, iface):
-    near, far = near_ref[:iface], far_ref[...]
-    from_near, from_far = from_near_ref[:iface], from_far_ref[...]
+
+
+def arrived(odd, near_ref, far_ref, from_near_ref, from_far_ref):
+    near, far = near_ref[...], far_ref[...]
+    from_near, from_far = from_near_ref[...], from_far_ref[...]
     own = jnp.where(odd, far - from_far, near - from_near)
     previous = jnp.where(odd, from_near - near, from_far - far)
     return own, previous
 
 
 def second_kernel(
-    place_ref, near_ref, far_ref, from_near_ref, from_far_ref, r_ref, u_ref, selector_ref, swap_ref, stiffness_ref,
-    near_out, far_out, w_out, stiff_ref,
+    near_ref, far_ref, from_near_ref, from_far_ref, r_ref, u_ref, selector_ref, swap_ref, stiffness_ref,
+    w_out, dots_out, near_out, far_out, stiff_ref,
 ):
-    iface = r_ref.shape[0]
-    odd = place_ref[0] % 2 == 1
-    w, w_previous = arrived(odd, near_ref, far_ref, from_near_ref, from_far_ref, iface)
+    odd = lax.axis_index("sub") % 2 == 1
+    w, w_previous = arrived(odd, near_ref, far_ref, from_near_ref, from_far_ref)
     w_out[0] = w
     w_out[1] = w_previous
-    dots = dot_rows(r_ref[...], u_ref[...], w)
-    near_out[iface:] = dots
+    r, u = r_ref[...], u_ref[...]
+    fill_lanes(dots_out, dot_lanes((r, u), (u, w)))
     stiffen(odd, w, w_previous, selector_ref, swap_ref, stiffness_ref, stiff_ref, near_out, far_out)
 
 
@@ -177,40 +174,39 @@
         z_out[0] = z
         z_out[1] = z_previous
         w_out[1] = previous
-    return dot_rows(r, u, w, s, p), w, previous
+    return dot_lanes((r, u), (u, w), (u, s), (p, w)), w, previous
 
 
 def middle_kernel(first, last, *refs):
-    (place_ref, near_ref, far_ref, from_near_ref, from_far_ref, dots_ref, dots_other_ref, m_ref) = refs[:8]
-    (selector_ref, swap_ref, stiffness_ref) = refs[8:11]
-    ins = list(refs[11:20])
-    outs = list(refs[20:29])
+    (near_ref, far_ref, from_near_ref, from_far_ref, dots_ref, m_ref) = refs[:6]
+    (selector_ref, swap_ref, stiffness_ref) = refs[6:9]
+    ins = list(refs[9:18])
+    outs = list(refs[18:27])
     m = m_ref[...]
-    iface = m.shape[0]
-    odd = place_ref[0] % 2 == 1
-    n, n_previous = arrived(odd, near_ref, far_ref, from_near_ref, from_far_ref, iface)
+    odd = lax.axis_index("sub") % 2 == 1
+    n, n_previous = arrived(odd, near_ref, far_ref, from_near_ref, from_far_ref)
     dots, w, previous = update(
-        first, last, ins + outs, m, n, n_previous, dots_ref[...] + dots_other_ref[...]
-    )
+        first, last, ins + outs, m, n, n_previous, dots_ref[0:1]
+    )
+    dots_out = refs[27]
     if last:
-        dots_out = refs[29]
-        dots_out[...] = jnp.broadcast_to(dots[None], dots_out.shape)
+        dots_out[...] = jnp.broadcast_to(dots, dots_out.shape)
     else:
-        near_out, far_out, stiff_ref = refs[29:32]
-        near_out[iface:] = dots
+        fill_lanes(dots_out, dots)
+    if not last:
+        near_out, far_out, stiff_ref = refs[28:31]
         stiffen(odd, w, previous, selector_ref, swap_ref, stiffness_ref, stiff_ref, near_out, far_out)
 
 
 def corner_kernel(
-    ranks, place_ref, near_ref, far_ref, from_near_ref, from_far_ref, selector_ref, operators_ref, table_ref,
+    ranks, near_ref, far_ref, from_near_ref, from_far_ref, selector_ref, operators_ref, table_ref,
     m_out, gap_out, *rest,
 ):
     outs, sums_ref = rest[:ranks], rest[ranks]
     iface, cells = m_out.shape
-    odd = place_ref[0] % 2 == 1
-    own, previous = arrived(odd, near_ref, far_ref, from_near_ref, from_far_ref, iface)
+    odd = lax.axis_index("sub") % 2 == 1
+    own, previous = arrived(odd, near_ref, far_ref, from_near_ref, from_far_ref)
     m_out[...] = own
-    dots = near_ref[iface:] + from_near_ref[iface:]
     gap = spread_of(own, previous, selector_ref[...])
     gap_out[...] = gap
     parts = []
@@ -220,44 +216,23 @@
         parts.append(jnp.concatenate([part, jnp.zeros((ROWS - CORNER_DOF, cells), F32)], axis=0))
     sums_ref[...] = exact_dot(jnp.concatenate(parts, axis=1), table_ref[...], NT)
     owned = sums_ref.shape[1] // ranks
-    pad = jnp.zeros((1, owned - 2 * cells), F32) if owned > 2 * cells else None
-    tail = []
-    for row in range(0, ROWS - CORNER_DOF):
-        lanes = [dots[2 * row : 2 * row + 1], dots[2 * row + 1 : 2 * row + 2]]
-        if pad is not None:
-            lanes.append(pad)
-        tail.append(jnp.concatenate(lanes, axis=1))
-    tail = jnp.concatenate(tail, axis=0)
     for distance in range(ranks):
-        rank = place_ref[1] ^ distance
-        piece = sums_ref[:, pl.ds(pl.multiple_of(rank * owned, 128), owned)]
-        outs[distance][...] = jnp.concatenate([piece[:CORNER_DOF], tail], axis=0)
+        rank = lax.axis_index("grp") ^ distance
+        outs[distance][...] = sums_ref[:, pl.ds(pl.multiple_of(rank * owned, LANES), owned)]
 
 
 def local_kernel(gap_ref, inverse_ref, local_ref):
     apply_blocks([inverse_ref], [gap_ref[...]], local_ref)
 
 
-def coarse_kernel(ranks, place_ref, coarse_ref, *rest):
-    pieces, (solved_ref, dots_ref, sums_ref) = rest[:ranks], rest[ranks:]
-    cells = dots_ref.shape[1]
+def coarse_kernel(ranks, coarse_ref, *rest):
+    pieces, (solved_ref, sums_ref) = rest[:ranks], rest[ranks:]
     for distance in range(ranks):
-        rank = place_ref[1] ^ distance
+        rank = lax.axis_index("grp") ^ distance
         sums_ref[rank] = pieces[distance][...]
     total = sums_ref[0]
     for rank in range(1, ranks):
         total = total + sums_ref[rank]
-    tail = total[CORNER_DOF:]
-    dots_ref[...] = jnp.concatenate(
-        [
-            tail[0:1, :cells],
-            tail[0:1, cells : 2 * cells],
-            tail[1:2, :cells],
-            tail[1:2, cells : 2 * cells],
-            jnp.zeros((ROWS - 4, cells), F32),
-        ],
-        axis=0,
-    )
     blocks, order = coarse_ref.shape[0], coarse_ref.shape[1]
     width = order // CORNER_DOF
     columns = []
@@ -276,14 +251,13 @@
     )
 
 
-def lift_kernel(ranks, place_ref, local_ref, operators_ref, table_ref, selector_ref, dots_ref, other_ref, *rest):
-    pieces, (near_ref, far_ref, dots_out, values_ref) = rest[:ranks], rest[ranks:]
+def lift_kernel(ranks, local_ref, operators_ref, table_ref, selector_ref, *rest):
+    pieces, (near_ref, far_ref, values_ref) = rest[:ranks], rest[ranks:]
     cells = local_ref.shape[1]
     owned = values_ref.shape[1] // ranks
-    dots_out[...] = dots_ref[...] + other_ref[...]
     for distance in range(ranks):
-        rank = place_ref[1] ^ distance
-        values_ref[:, pl.ds(pl.multiple_of(rank * owned, 128), owned)] = pieces[distance][...]
+        rank = lax.axis_index("grp") ^ distance
+        values_ref[:, pl.ds(pl.multiple_of(rank * owned, LANES), owned)] = pieces[distance][...]
     picked = exact_dot(values_ref[...], table_ref[...], NN)
     lifted = local_ref[...]
     for corner in range(CORNERS_SUB):
@@ -291,12 +265,11 @@
         for dof in range(CORNER_DOF):
             operator = operators_ref[corner * CORNER_DOF + dof].astype(F32)
             lifted = lifted + operator * picked[dof : dof + 1, lanes]
-    collect_to(place_ref[0] % 2 == 1, lifted, selector_ref[...], near_ref, far_ref)
+    collect_to(lax.axis_index("sub") % 2 == 1, lifted, selector_ref[...], near_ref, far_ref)
 
 
 def final_kernel(dots_ref, scalars_ref, x_ref, r_ref, u_ref, w_ref, p_ref, s_ref, x_out, r_out):
-    totals = jnp.sum(dots_ref[...], axis=0)
-    alpha, beta, _, _ = step_sizes(totals, scalars_ref[...])
+    alpha, beta, _, _ = step_sizes(jnp.sum(dots_ref[...], axis=0), scalars_ref[...])
     x_out[...] = x_ref[...] + alpha * (u_ref[...] + beta * p_ref[...])
     r_out[...] = r_ref[...] - alpha * (w_ref[0] + beta * s_ref[...])
 
@@ -355,7 +328,6 @@
     ranks = lax.axis_size("grp")
     sub_count = lax.axis_size("sub")
     start = lax.axis_index("sub") * cells
-    place = jnp.stack([lax.axis_index("sub"), lax.axis_index("grp")]).astype(jnp.int32)
     right_side = gap_data[:, 0, :]
     inverse = local_inverse[:, :, 0, :]
     stiff = stiffness[:, :, :, 0, :]
@@ -380,8 +352,9 @@
 
     field = shape(iface, cells)
     pair = shape(2, iface, cells)
-    message = shape(iface + ROWS, cells)
     rows = shape(ROWS, cells)
+    parts = shape(ROWS, sub_count * ranks * LANES)
+    last_parts = shape(sub_count * ranks, 1, LANES)
     piece = shape(ROWS, owned)
     stiff_scratch = [pltpu.VMEM((iface, cells), F32)]
     stiff_cost = dict(flops=4 * iface * iface * cells, moved=4 * iface * iface * cells)
@@ -391,13 +364,12 @@
         m, gap, *parts = call(
             lambda *refs: corner_kernel(ranks, *refs),
             (field, field) + (piece,) * ranks,
-            in_smem=(0,),
-            count=8,
+            count=7,
             scratch=[pltpu.VMEM((ROWS, group), F32)],
             flops=2 * 24 * iface * cells,
             moved=2 * 24 * iface * cells + group * CORNERS_SUB * cells * 2,
             name="corners",
-        )(place, near, far, from_near, from_far, selector, operators, table)
+        )(near, far, from_near, from_far, selector, operators, table)
         arrivals = [parts[0]] + [exchanged(parts[d], d) for d in range(1, ranks)]
         local = call(
             local_kernel,
@@ -407,79 +379,68 @@
             moved=2 * iface * iface * cells,
             name="local",
         )(gap, inverse)
-        solved, dots = call(
+        solved = call(
             lambda *refs: coarse_kernel(ranks, *refs),
-            (piece, rows),
-            in_smem=(0,),
-            count=2 + ranks,
+            piece,
+            count=1 + ranks,
             scratch=[pltpu.VMEM((ranks, ROWS, owned), F32)],
             flops=2 * blocks_own * order * order,
             moved=2 * blocks_own * order * order,
             name="coarse",
-        )(place, coarse_inverse, *arrivals)
+        )(coarse_inverse, *arrivals)
         values = [solved] + [exchanged(solved, d) for d in range(1, ranks)]
-        other = swapped(dots, 2)
-        near, far, dots = call(
+        near, far = call(
             lambda *refs: lift_kernel(ranks, *refs),
-            (field, field, rows),
-            in_smem=(0,),
-            count=7 + ranks,
+            (field, field),
+            count=4 + ranks,
             scratch=[pltpu.VMEM((ROWS, group), F32)],
             flops=2 * 24 * iface * cells,
             moved=2 * 24 * iface * cells + group * CORNERS_SUB * cells * 2,
             name="lift",
-        )(place, local, operators, table, selector, dots, other, *values)
-        return m, near, far, dots
+        )(local, operators, table, selector, *values)
+        return m, near, far
 
     previous = shifted(right_side, 1)
     near, far = call(
-        first_kernel, (message, field), in_smem=(0,), count=6, scratch=stiff_scratch, name="first", **stiff_cost
-    )(place, right_side, previous, selector, swap, stiff)
-    u, near, far, dots = apply_operator(near, far)
+        first_kernel, (field, field), count=5, scratch=stiff_scratch, name="first", **stiff_cost
+    )(right_side, previous, selector, swap, stiff)
+    u, near, far = apply_operator(near, far)
     r = right_side
     from_far, from_near = swapped_far(far), swapped(near, 1)
-    near, far, w = call(
+    w, dots, near, far = call(
         second_kernel,
-        (message, field, pair),
-        in_smem=(0,),
-        count=10,
+        (pair, parts, field, field),
+        count=9,
         scratch=stiff_scratch,
         name="second",
         **stiff_cost,
-    )(place, near, far, from_near, from_far, r, u, selector, swap, stiff)
+    )(near, far, from_near, from_far, r, u, selector, swap, stiff)
 
     scalars, x, p, s, q, z = [jnp.zeros((ROWS, cells), F32)] + [r] * 4 + [w]
     for step in range(ITERS - 1):
         first, last = step == 0, step == ITERS - 2
-        m, near, far, dots = apply_operator(near, far)
-        from_far, from_near, other = swapped_far(far), swapped(near, 1), swapped(dots, 4)
-        bit = 8
-        while bit < sub_count:
-            dots = dots + other
-            other = swapped(dots, bit)
-            bit *= 2
+        sums = lax.psum_scatter(dots, ("sub", "grp"), scatter_dimension=1, tiled=True)
+        m, near, far = apply_operator(near, far)
+        from_far, from_near = swapped_far(far), swapped(near, 1)
         outs = (rows, field, field, field, pair, field, field, field, pair)
-        if last:
-            count = sub_count * ranks
-            outs += (shape(count, ROWS, cells),)
-        else:
-            outs += (message, field)
+        outs += (last_parts if last else parts,)
+        if not last:
+            outs += (field, field)
         result = call(
             lambda *refs, first=first, last=last: middle_kernel(first, last, *refs),
             outs,
-            in_smem=(0,),
-            count=20,
+            count=18,
             scratch=() if last else stiff_scratch,
             name="last" if last else "middle",
             **({} if last else stiff_cost),
         )(
-            place, near, far, from_near, from_far, dots, other, m, selector, swap, stiff,
+            near, far, from_near, from_far, sums, m, selector, swap, stiff,
             scalars, x, r, u, w, p, s, q, z,
         )
-        scalars, x, r, u, w, p, s, q, z = result[:9]
+        scalars, x, r, u, w, p, s, q, z, dots = result[:10]
         if not last:
-            near, far = result[9:]
-    everyone = lax.all_to_all(result[9], ("sub", "grp"), 0, 0, tiled=True)
+            near, far = result[10:]
+    everyone = lax.all_to_all(dots, ("sub", "grp"), 0, 0, tiled=True)
     x, r = call(final_kernel, (field, field), count=8, name="final")(
         everyone, scalars, x, r, u, w, p, s
     )

time: 203 us -> 667 us (3.29)
  waiting for transfers between devices: 32.9 us -> 451 us
  local copies, waits for them, and re-layouts: 4.9 us -> 85.3 us
  starting transfers between devices: 115 us -> 78 us
  between operations: 1.08 us -> 14.5 us
  Pallas kernels: 36.7 us -> 25.5 us
    reduce_scatter x0 -> x4, waiting for transfers between devices: none -> 422 us  [on_device(): lax.psum_scatter(dots, ('sub', 'grp'), scatter_dimension=1, tiled=True)]
    unnamed x18 -> x260, local copies, waits for them, and re-layouts: 4.9 us -> 85.3 us
    ppermute x19 -> x10, starting transfers between devices: 61.4 us -> 24 us  [swapped(): lax.ppermute(block, 'sub', [(i, i ^ bit) for i in range(lax.axis_size('su...]
    ppermute x19 -> x10, waiting for transfers between devices: 13.4 us -> 2.77 us  [swapped(): lax.ppermute(block, 'sub', [(i, i ^ bit) for i in range(lax.axis_size('su...]
    pallas_call x12, Pallas kernels: 17.2 us -> 10.2 us  [the longest x5 3.57 us: apply_operator(): call(lambda *refs: coarse_kernel(ranks, *refs), piece, count=1 + ranks, s...]
  transfers between devices with their start and end apart: 60 -> 55, of which waited for: 25 -> 31; matrix products, arithmetic and copies ran while one was open for 0% -> 0% of each run, Pallas kernels for 2% -> 2%
where the time goes in v3:
time: 667 us; the launch traced here: 663 us
  waiting for transfers between devices  451 us (68%)
  local copies, waits for them, and re-layouts  85.3 us (13%)
  starting transfers between devices  78 us (12%)
  Pallas kernels  25.5 us (4%)
  between operations  14.5 us (2%)
  blocking collectives  8.85 us (1%)
    reduce_scatter x4, waiting for transfers between devices, on_device(): lax.psum_scatter(dots, ('sub', 'grp'), scatter_dimension=1, tiled=True)  422 us
    unnamed x260, local copies, waits for them, and re-layouts  85.3 us
    ppermute x30, starting transfers between devices, exchanged(): lax.ppermute(block, 'grp', [(i, i ^ distance) for i in range(lax.axis_siz...  44.5 us
    ppermute x30, waiting for transfers between devices, exchanged(): lax.ppermute(block, 'grp', [(i, i ^ distance) for i in range(lax.axis_siz...  26.1 us
    ppermute x10, starting transfers between devices, swapped(): lax.ppermute(block, 'sub', [(i, i ^ bit) for i in range(lax.axis_size('su...  24 us
  transfers between devices with their start and end apart: 55, of which 31 were waited for; matrix products, arithmetic and copies ran while one was open for 0% of the time, Pallas kernels for 2%

profile of v3, /device:TPU:0, one launch (start us, length us, event | category | flops | bytes accessed | tf_op | source)
XLA Modules:
  0.0 663.4 jit_solution(4083997341473519626)
XLA Ops:
  7.2 2.4 collective-permute-start
  16.3 2.7 collective-permute-start.1
  23.2 2.6 collective-permute-start.4
  27.8 3.5 collective-permute-done.5.refs_4_
  32.2 4.2 collective-permute-start.6
  45.4 7.7 %collective-permute-start.11 = (f32[96,128]{1,0:T(8,128)S(1)}, f32[96,128]{1,0:T(8,128)S(1)}, u32[]{:S(2)}, u32[]{:S(2)}) collective-permute-start(f32[96,128]{1,0:T(8,128)S(1)} %get-tuple-element.110.refs_0_), channel_id=1, source_target_pairs={{0,4},{4,0},{8,12},{12,8},{16,20},{20,16},{24,28},{28,24},{1,5},{5... | collective-permute-start | bytes 147464 | tf_op jit(solution)/shard_map/ppermute | solution.py:284
  67.3 2.8 collective-permute-start.16
  72.5 4.6 collective-permute-start.19
  80.2 108.3 %reduce-scatter.5.cloned.1.call-done.refs_4_ = f32[8,128]{1,0:T(8,128)} async-done(((f32[8,4096]{1,0:T(8,128)}), f32[8,128]{1,0:T(8,128)}) %reduce-scatter.5.cloned.1.call-update) | async-done | bytes 4112 | tf_op jit(solution)/shard_map/reduce_scatter | solution.py:422
  188.5 2.3 copy-done.1
  211.8 4.3 collective-permute-start.25
  218.5 3.8 collective-permute-start.28
  224.0 2.9 collective-permute-done.27.refs_6_
  232.9 103.7 %reduce-scatter.7.cloned.1.call-done.refs_4_ = f32[8,128]{1,0:T(8,128)} async-done(((f32[8,4096]{1,0:T(8,128)}), f32[8,128]{1,0:T(8,128)}) %reduce-scatter.7.cloned.1.call-update) | async-done | bytes 4112 | tf_op jit(solution)/shard_map/reduce_scatter | solution.py:422
  365.1 4.3 collective-permute-start.35
  371.8 3.8 collective-permute-start.38
  377.3 3.1 collective-permute-done.37.refs_6_
  386.1 103.7 %reduce-scatter.9.cloned.1.call-done.refs_4_ = f32[8,128]{1,0:T(8,128)} async-done(((f32[8,4096]{1,0:T(8,128)}), f32[8,128]{1,0:T(8,128)}) %reduce-scatter.9.cloned.1.call-update) | async-done | bytes 4112 | tf_op jit(solution)/shard_map/reduce_scatter | solution.py:422
  518.1 4.3 collective-permute-start.45
  524.9 3.8 collective-permute-start.48
  530.4 2.8 collective-permute-done.47.refs_6_
  533.8 2.5 collective-permute-start.49
  537.2 105.8 %reduce-scatter.11.cloned.1.call-done.refs_4_ = f32[8,128]{1,0:T(8,128)} async-done(((f32[8,4096]{1,0:T(8,128)}), f32[8,128]{1,0:T(8,128)}) %reduce-scatter.11.cloned.1.call-update) | async-done | bytes 4112 | tf_op jit(solution)/shard_map/reduce_scatter | solution.py:422
  647.1 8.8 %all_to_all.5.dots_ref = f32[32,1,128]{2,1,0:T(1,128)S(1)} all-to-all(f32[32,1,128]{2,1,0:T(1,128)S(1)} %get-tuple-element.182), channel_id=1, replica_groups=mesh['sub'=8,'grp'=4] {'sub','grp'}, dimensions={0} | all-to-all | bytes 32768 | tf_op jit(solution)/shard_map/all_to_all | solution.py:443
  (382 shorter events, 150.0 us)
Async XLA Ops:
  7.2 181.3 %reduce-scatter.5.cloned.1.call-start = ((), (), s32[]{:S(2)}) async-start(), calls=%async_computation.5 | async-start | bytes 135168 | tf_op jit(solution)/shard_map/reduce_scatter | solution.py:422
  25.8 5.4 collective-permute-start.5
  32.0 5.5 collective-permute-start.8
  32.2 5.2 collective-permute-start.7
  32.2 5.8 collective-permute-start.6
  45.3 291.3 %reduce-scatter.7.cloned.1.call-start = ((), (), s32[]{:S(2)}) async-start(), calls=%async_computation.6 | async-start | bytes 135168 | tf_op jit(solution)/shard_map/reduce_scatter | solution.py:422
  45.4 8.6 %collective-permute-start.11 = (f32[96,128]{1,0:T(8,128)S(1)}, f32[96,128]{1,0:T(8,128)S(1)}, u32[]{:S(2)}, u32[]{:S(2)}) collective-permute-start(f32[96,128]{1,0:T(8,128)S(1)} %get-tuple-element.110.refs_0_), channel_id=1, source_target_pairs={{0,4},{4,0},{8,12},{12,8},{16,20},{20,16},{24,28},{28,24},{1,5},{5... | collective-permute-start | bytes 147464 | tf_op jit(solution)/shard_map/ppermute | solution.py:284
  59.6 5.4 collective-permute-start.15
  65.7 5.5 collective-permute-start.18
  67.3 4.6 collective-permute-start.17
  72.5 6.5 collective-permute-start.19
  206.8 283.1 %reduce-scatter.9.cloned.1.call-start = ((), (), s32[]{:S(2)}) async-start(), calls=%async_computation.7 | async-start | bytes 135168 | tf_op jit(solution)/shard_map/reduce_scatter | solution.py:422
  211.7 4.6 collective-permute-start.24
  211.8 6.0 collective-permute-start.25
  218.5 5.5 collective-permute-start.28
  360.0 283.0 %reduce-scatter.11.cloned.1.call-start = ((), (), s32[]{:S(2)}) async-start(), calls=%async_computation.8 | async-start | bytes 135168 | tf_op jit(solution)/shard_map/reduce_scatter | solution.py:422
  365.0 4.6 collective-permute-start.34
  365.1 6.0 collective-permute-start.35
  371.8 5.5 collective-permute-start.38
  375.6 4.7 collective-permute-start.37
  375.6 4.7 collective-permute-start.36
  518.0 4.6 collective-permute-start.44
  518.1 6.0 collective-permute-start.45
  524.9 5.5 collective-permute-start.48
  (161 other events, 1589.5 us)
Sparse Core Ops, SparseCore 0:
  45.5 142.9 reduce-scatter.4
  206.9 129.7 reduce-scatter.6
  360.1 129.6 reduce-scatter.8
  513.2 129.8 reduce-scatter.10

commit v4 on v2

--- a/solution.py
+++ b/solution.py
@@ -44,14 +44,20 @@
     return jnp.concatenate(rows, axis=0)
 
 
-def step_sizes(totals, before):
-    sums = lane_total(totals)
-    norm, curvature = sums[0:1], sums[1:2]
+def packed(rows):
+    totals = jnp.broadcast_to(lane_total(rows), rows.shape)
+    row = lax.broadcasted_iota(jnp.int32, rows.shape, 0)
+    lane = lax.broadcasted_iota(jnp.int32, rows.shape, 1)
+    return jnp.sum(jnp.where(row == lane, totals, 0.0), axis=0, keepdims=True)
+
+
+def step_sizes(sums, before):
+    norm, curvature, crossed, other = sums
     if before is None:
         beta = None
     else:
         beta = norm / before[0:1, 0:1]
-        curvature = curvature + beta * (sums[2:3] + sums[3:4]) + beta * beta * before[1:2, 0:1]
+        curvature = curvature + beta * (crossed + other) + beta * beta * before[1:2, 0:1]
     return norm / curvature, beta, norm, curvature
 
 
@@ -106,17 +112,17 @@
 
 
 def first_kernel(
-    place_ref, own_ref, previous_ref, selector_ref, swap_ref, stiffness_ref, near_ref, far_ref, stiff_ref
+    own_ref, previous_ref, selector_ref, swap_ref, stiffness_ref, far_ref, near_ref, stiff_ref
 ):
     iface, cells = own_ref.shape
-    odd = place_ref[0] % 2 == 1
+    odd = lax.axis_index("sub") % 2 == 1
     stiffen(
         odd, own_ref[...], previous_ref[...], selector_ref, swap_ref, stiffness_ref, stiff_ref, near_ref, far_ref
     )
     near_ref[iface:] = jnp.zeros((ROWS, cells), F32)
 
 
-def arrived(odd, near_ref, far_ref, from_near_ref, from_far_ref, iface):
+def arrived(odd, near_ref, far_ref, from_far_ref, from_near_ref, iface):
     near, far = near_ref[:iface], far_ref[...]
     from_near, from_far = from_near_ref[:iface], from_far_ref[...]
     own = jnp.where(odd, far - from_far, near - from_near)
@@ -125,12 +131,12 @@
 
 
 def second_kernel(
-    place_ref, near_ref, far_ref, from_near_ref, from_far_ref, r_ref, u_ref, selector_ref, swap_ref, stiffness_ref,
-    near_out, far_out, w_out, stiff_ref,
+    near_ref, far_ref, from_far_ref, from_near_ref, r_ref, u_ref, selector_ref, swap_ref, stiffness_ref,
+    far_out, near_out, w_out, stiff_ref,
 ):
     iface = r_ref.shape[0]
-    odd = place_ref[0] % 2 == 1
-    w, w_previous = arrived(odd, near_ref, far_ref, from_near_ref, from_far_ref, iface)
+    odd = lax.axis_index("sub") % 2 == 1
+    w, w_previous = arrived(odd, near_ref, far_ref, from_far_ref, from_near_ref, iface)
     w_out[0] = w
     w_out[1] = w_previous
     dots = dot_rows(r_ref[...], u_ref[...], w)
@@ -141,7 +147,9 @@
 def update(first, last, refs, m, n, n_previous, totals):
     scalars_in, x_in, r_in, u_in, w_in, p_in, s_in, q_in, z_in = refs[:9]
     scalars_out, x_out, r_out, u_out, w_out, p_out, s_out, q_out, z_out = refs[9:]
-    alpha, beta, norm, curvature = step_sizes(totals, None if first else scalars_in[...])
+    sums = lane_total(totals)
+    sums = [sums[k : k + 1] for k in range(4)]
+    alpha, beta, norm, curvature = step_sizes(sums, None if first else scalars_in[...])
     cells = m.shape[1]
     scalars_out[...] = jnp.concatenate(
         [
@@ -181,34 +189,34 @@
 
 
 def middle_kernel(first, last, *refs):
-    (place_ref, near_ref, far_ref, from_near_ref, from_far_ref, dots_ref, dots_other_ref, m_ref) = refs[:8]
-    (selector_ref, swap_ref, stiffness_ref) = refs[8:11]
-    ins = list(refs[11:20])
-    outs = list(refs[20:29])
+    (near_ref, far_ref, from_far_ref, from_near_ref, dots_ref, dots_other_ref, m_ref) = refs[:7]
+    (selector_ref, swap_ref, stiffness_ref) = refs[7:10]
+    ins = list(refs[10:19])
+    outs = list(refs[19:28])
     m = m_ref[...]
     iface = m.shape[0]
-    odd = place_ref[0] % 2 == 1
-    n, n_previous = arrived(odd, near_ref, far_ref, from_near_ref, from_far_ref, iface)
+    odd = lax.axis_index("sub") % 2 == 1
+    n, n_previous = arrived(odd, near_ref, far_ref, from_far_ref, from_near_ref, iface)
     dots, w, previous = update(
         first, last, ins + outs, m, n, n_previous, dots_ref[...] + dots_other_ref[...]
     )
     if last:
-        dots_out = refs[29]
-        dots_out[...] = jnp.broadcast_to(dots[None], dots_out.shape)
+        dots_out = refs[28]
+        dots_out[...] = jnp.broadcast_to(packed(dots)[None], dots_out.shape)
     else:
-        near_out, far_out, stiff_ref = refs[29:32]
+        far_out, near_out, stiff_ref = refs[28:31]
         near_out[iface:] = dots
         stiffen(odd, w, previous, selector_ref, swap_ref, stiffness_ref, stiff_ref, near_out, far_out)
 
 
 def corner_kernel(
-    ranks, place_ref, near_ref, far_ref, from_near_ref, from_far_ref, selector_ref, operators_ref, table_ref,
+    ranks, near_ref, far_ref, from_far_ref, from_near_ref, selector_ref, operators_ref, table_ref,
     m_out, gap_out, *rest,
 ):
     outs, sums_ref = rest[:ranks], rest[ranks]
     iface, cells = m_out.shape
-    odd = place_ref[0] % 2 == 1
-    own, previous = arrived(odd, near_ref, far_ref, from_near_ref, from_far_ref, iface)
+    odd = lax.axis_index("sub") % 2 == 1
+    own, previous = arrived(odd, near_ref, far_ref, from_far_ref, from_near_ref, iface)
     m_out[...] = own
     dots = near_ref[iface:] + from_near_ref[iface:]
     gap = spread_of(own, previous, selector_ref[...])
@@ -229,7 +237,7 @@
         tail.append(jnp.concatenate(lanes, axis=1))
     tail = jnp.concatenate(tail, axis=0)
     for distance in range(ranks):
-        rank = place_ref[1] ^ distance
+        rank = lax.axis_index("grp") ^ distance
         piece = sums_ref[:, pl.ds(pl.multiple_of(rank * owned, 128), owned)]
         outs[distance][...] = jnp.concatenate([piece[:CORNER_DOF], tail], axis=0)
 
@@ -238,11 +246,11 @@
     apply_blocks([inverse_ref], [gap_ref[...]], local_ref)
 
 
-def coarse_kernel(ranks, place_ref, coarse_ref, *rest):
+def coarse_kernel(ranks, coarse_ref, *rest):
     pieces, (solved_ref, dots_ref, sums_ref) = rest[:ranks], rest[ranks:]
     cells = dots_ref.shape[1]
     for distance in range(ranks):
-        rank = place_ref[1] ^ distance
+        rank = lax.axis_index("grp") ^ distance
         sums_ref[rank] = pieces[distance][...]
     total = sums_ref[0]
     for rank in range(1, ranks):
@@ -276,13 +284,13 @@
     )
 
 
-def lift_kernel(ranks, place_ref, local_ref, operators_ref, table_ref, selector_ref, dots_ref, other_ref, *rest):
-    pieces, (near_ref, far_ref, dots_out, values_ref) = rest[:ranks], rest[ranks:]
+def lift_kernel(ranks, local_ref, operators_ref, table_ref, selector_ref, dots_ref, other_ref, *rest):
+    pieces, (far_ref, near_ref, dots_out, values_ref) = rest[:ranks], rest[ranks:]
     cells = local_ref.shape[1]
     owned = values_ref.shape[1] // ranks
     dots_out[...] = dots_ref[...] + other_ref[...]
     for distance in range(ranks):
-        rank = place_ref[1] ^ distance
+        rank = lax.axis_index("grp") ^ distance
         values_ref[:, pl.ds(pl.multiple_of(rank * owned, 128), owned)] = pieces[distance][...]
     picked = exact_dot(values_ref[...], table_ref[...], NN)
     lifted = local_ref[...]
@@ -291,12 +299,13 @@
         for dof in range(CORNER_DOF):
             operator = operators_ref[corner * CORNER_DOF + dof].astype(F32)
             lifted = lifted + operator * picked[dof : dof + 1, lanes]
-    collect_to(place_ref[0] % 2 == 1, lifted, selector_ref[...], near_ref, far_ref)
+    collect_to(lax.axis_index("sub") % 2 == 1, lifted, selector_ref[...], near_ref, far_ref)
 
 
 def final_kernel(dots_ref, scalars_ref, x_ref, r_ref, u_ref, w_ref, p_ref, s_ref, x_out, r_out):
     totals = jnp.sum(dots_ref[...], axis=0)
-    alpha, beta, _, _ = step_sizes(totals, scalars_ref[...])
+    sums = [totals[:, k : k + 1] for k in range(4)]
+    alpha, beta, _, _ = step_sizes(sums, scalars_ref[...])
     x_out[...] = x_ref[...] + alpha * (u_ref[...] + beta * p_ref[...])
     r_out[...] = r_ref[...] - alpha * (w_ref[0] + beta * s_ref[...])
 
@@ -324,10 +333,8 @@
     return jax.ShapeDtypeStruct(dims, dtype)
 
 
-def call(kernel, out_shape, in_smem=(), count=0, scratch=(), flops=0, moved=0, name=None):
-    specs = [
-        pl.BlockSpec(memory_space=pltpu.SMEM if i in in_smem else pltpu.VMEM) for i in range(count)
-    ]
+def call(kernel, out_shape, count=0, scratch=(), flops=0, moved=0, name=None):
+    specs = [pl.BlockSpec(memory_space=pltpu.VMEM)] * count
     out_specs = jax.tree.map(lambda _: pl.BlockSpec(memory_space=pltpu.VMEM), out_shape)
     return pl.pallas_call(
         kernel,
@@ -355,7 +362,6 @@
     ranks = lax.axis_size("grp")
     sub_count = lax.axis_size("sub")
     start = lax.axis_index("sub") * cells
-    place = jnp.stack([lax.axis_index("sub"), lax.axis_index("grp")]).astype(jnp.int32)
     right_side = gap_data[:, 0, :]
     inverse = local_inverse[:, :, 0, :]
     stiff = stiffness[:, :, :, 0, :]
@@ -391,13 +397,12 @@
         m, gap, *parts = call(
             lambda *refs: corner_kernel(ranks, *refs),
             (field, field) + (piece,) * ranks,
-            in_smem=(0,),
-            count=8,
+            count=7,
             scratch=[pltpu.VMEM((ROWS, group), F32)],
             flops=2 * 24 * iface * cells,
             moved=2 * 24 * iface * cells + group * CORNERS_SUB * cells * 2,
             name="corners",
-        )(place, near, far, from_near, from_far, selector, operators, table)
+        )(near, far, from_far, from_near, selector, operators, table)
         arrivals = [parts[0]] + [exchanged(parts[d], d) for d in range(1, ranks)]
         local = call(
             local_kernel,
@@ -410,43 +415,40 @@
         solved, dots = call(
             lambda *refs: coarse_kernel(ranks, *refs),
             (piece, rows),
-            in_smem=(0,),
-            count=2 + ranks,
+            count=1 + ranks,
             scratch=[pltpu.VMEM((ranks, ROWS, owned), F32)],
             flops=2 * blocks_own * order * order,
             moved=2 * blocks_own * order * order,
             name="coarse",
-        )(place, coarse_inverse, *arrivals)
+        )(coarse_inverse, *arrivals)
         values = [solved] + [exchanged(solved, d) for d in range(1, ranks)]
         other = swapped(dots, 2)
-        near, far, dots = call(
+        far, near, dots = call(
             lambda *refs: lift_kernel(ranks, *refs),
             (field, field, rows),
-            in_smem=(0,),
-            count=7 + ranks,
+            count=6 + ranks,
             scratch=[pltpu.VMEM((ROWS, group), F32)],
             flops=2 * 24 * iface * cells,
             moved=2 * 24 * iface * cells + group * CORNERS_SUB * cells * 2,
             name="lift",
-        )(place, local, operators, table, selector, dots, other, *values)
+        )(local, operators, table, selector, dots, other, *values)
         return m, near, far, dots
 
     previous = shifted(right_side, 1)
-    near, far = call(
-        first_kernel, (message, field), in_smem=(0,), count=6, scratch=stiff_scratch, name="first", **stiff_cost
-    )(place, right_side, previous, selector, swap, stiff)
+    far, near = call(
+        first_kernel, (field, message), count=5, scratch=stiff_scratch, name="first", **stiff_cost
+    )(right_side, previous, selector, swap, stiff)
     u, near, far, dots = apply_operator(near, far)
     r = right_side
     from_far, from_near = swapped_far(far), swapped(near, 1)
-    near, far, w = call(
+    far, near, w = call(
         second_kernel,
-        (message, field, pair),
-        in_smem=(0,),
-        count=10,
+        (field, message, pair),
+        count=9,
         scratch=stiff_scratch,
         name="second",
         **stiff_cost,
-    )(place, near, far, from_near, from_far, r, u, selector, swap, stiff)
+    )(near, far, from_far, from_near, r, u, selector, swap, stiff)
 
     scalars, x, p, s, q, z = [jnp.zeros((ROWS, cells), F32)] + [r] * 4 + [w]
     for step in range(ITERS - 1):
@@ -461,24 +463,23 @@
         outs = (rows, field, field, field, pair, field, field, field, pair)
         if last:
             count = sub_count * ranks
-            outs += (shape(count, ROWS, cells),)
+            outs += (shape(count, 1, cells),)
         else:
-            outs += (message, field)
+            outs += (field, message)
         result = call(
             lambda *refs, first=first, last=last: middle_kernel(first, last, *refs),
             outs,
-            in_smem=(0,),
-            count=20,
+            count=19,
             scratch=() if last else stiff_scratch,
             name="last" if last else "middle",
             **({} if last else stiff_cost),
         )(
-            place, near, far, from_near, from_far, dots, other, m, selector, swap, stiff,
+            near, far, from_far, from_near, dots, other, m, selector, swap, stiff,
             scalars, x, r, u, w, p, s, q, z,
         )
         scalars, x, r, u, w, p, s, q, z = result[:9]
         if not last:
-            near, far = result[9:]
+            far, near = result[9:]
     everyone = lax.all_to_all(result[9], ("sub", "grp"), 0, 0, tiled=True)
     x, r = call(final_kernel, (field, field), count=8, name="final")(
         everyone, scalars, x, r, u, w, p, s

time: 203 us -> 191 us (0.941)
  Pallas kernels: 36.7 us -> 25.7 us
    pallas_call x12, Pallas kernels: 17.2 us -> 10.7 us  [the longest x5 3.57 us: apply_operator(): call(lambda *refs: coarse_kernel(ranks, *refs), (piece, rows), count=1 +...]
    pallas_call x5, Pallas kernels: 5.99 us -> 3.31 us  [apply_operator(): call(lambda *refs: corner_kernel(ranks, *refs), (field, field) + (piece,)...]
where the time goes in v4:
time: 191 us
  starting transfers between devices  115 us (60%)
  waiting for transfers between devices  32.9 us (17%)
  Pallas kernels  25.7 us (13%)
  blocking collectives  10.6 us (6%)
  local copies, waits for them, and re-layouts  4.9 us (3%)
    ppermute x19, starting transfers between devices, swapped(): lax.ppermute(block, 'sub', [(i, i ^ bit) for i in range(lax.axis_size('su...  61.5 us
    ppermute x30, starting transfers between devices, exchanged(): lax.ppermute(block, 'grp', [(i, i ^ distance) for i in range(lax.axis_siz...  44.3 us
    ppermute x30, waiting for transfers between devices, exchanged(): lax.ppermute(block, 'grp', [(i, i ^ distance) for i in range(lax.axis_siz...  19.4 us
    ppermute x19, waiting for transfers between devices, swapped(): lax.ppermute(block, 'sub', [(i, i ^ bit) for i in range(lax.axis_size('su...  13.5 us
    all_to_all x1, blocking collectives, on_device(): everyone = lax.all_to_all(result[9], ('sub', 'grp'), 0, 0, tiled=True)  10.6 us
    pallas_call x4, Pallas kernels, on_device(): call(lambda *refs, first=first, last=last: middle_kernel(first, last, *re...  7.04 us
    ppermute x10, starting transfers between devices, swapped_far(): lax.ppermute(block, 'sub', [(i, i + 1 if i % 2 else i - 1) for i in inner])  6.6 us
    unnamed x18, local copies, waits for them, and re-layouts  4.9 us
  transfers between devices with their start and end apart: 60, of which 25 were waited for; matrix products, arithmetic and copies ran while one was open for 0% of the time, Pallas kernels for 2%

profile of v4, /device:TPU:0, one launch (start us, length us, event | category | flops | bytes accessed | tf_op | source)
XLA Modules:
  0.0 190.5 jit_solution(1715158049577049994)
XLA Ops:
  9.7 2.7 %collective-permute-start.2 = (f32[104,128]{1,0:T(8,128)S(1)}, f32[104,128]{1,0:T(8,128)S(1)}, u32[]{:S(2)}, u32[]{:S(2)}) collective-permute-start(f32[104,128]{1,0:T(8,128)S(1)} %get-tuple-element.109.refs_0_), channel_id=1, source_target_pairs={{0,4},{4,0},{8,12},{12,8},{16,20},{20,16},{24,28},{28,24},{1,5},{5... | collective-permute-start | bytes 159752 | tf_op jit(solution)/shard_map/ppermute | solution.py:320
  21.2 3.5 %collective-permute-done.5.refs_4_ = f32[8,256]{1,0:T(8,128)S(1)} collective-permute-done((f32[8,256]{1,0:T(8,128)S(1)}, f32[8,256]{1,0:T(8,128)S(1)}, u32[]{:S(2)}, u32[]{:S(2)}) %collective-permute-start.5) | collective-permute-done | bytes 8224 | tf_op jit(solution)/shard_map/ppermute | solution.py:329
  25.7 4.2 %collective-permute-start.7 = (f32[8,256]{1,0:T(8,128)S(1)}, f32[8,256]{1,0:T(8,128)S(1)}, u32[]{:S(2)}, u32[]{:S(2)}) collective-permute-start(f32[8,256]{1,0:T(8,128)S(1)} %get-tuple-element.118.refs_6_), channel_id=1, source_target_pairs={{0,1},{1,0},{2,3},{3,2},{4,5},{5,4},{6,7},{7,6},{8,9},{9,8},{10,11... | collective-permute-start | bytes 24584 | tf_op jit(solution)/shard_map/ppermute | solution.py:329
  29.8 6.6 %collective-permute-start.6 = (f32[8,128]{1,0:T(8,128)S(1)}, f32[8,128]{1,0:T(8,128)S(1)}, u32[]{:S(2)}, u32[]{:S(2)}) collective-permute-start(f32[8,128]{1,0:T(8,128)S(1)} %get-tuple-element.117.refs_4_), channel_id=1, source_target_pairs={{0,8},{4,12},{8,0},{12,4},{16,24},{20,28},{24,16},{28,20},{1,9},{5... | collective-permute-start | bytes 12296 | tf_op jit(solution)/shard_map/ppermute | solution.py:320
  42.3 4.7 %collective-permute-start.13 = (f32[104,128]{1,0:T(8,128)S(1)}, f32[104,128]{1,0:T(8,128)S(1)}, u32[]{:S(2)}, u32[]{:S(2)}) collective-permute-start(f32[104,128]{1,0:T(8,128)S(1)} %get-tuple-element.122.refs_0_), channel_id=1, source_target_pairs={{0,4},{4,0},{8,12},{12,8},{16,20},{20,16},{24,28},{28,24},{1,5},{5... | collective-permute-start | bytes 159752 | tf_op jit(solution)/shard_map/ppermute | solution.py:320
  49.5 3.6 %collective-permute-start.16 = (f32[8,256]{1,0:T(8,128)S(1)}, f32[8,256]{1,0:T(8,128)S(1)}, u32[]{:S(2)}, u32[]{:S(2)}) collective-permute-start(f32[8,256]{1,0:T(8,128)S(1)} %get-tuple-element.128), channel_id=1, source_target_pairs={{0,3},{1,2},{2,1},{3,0},{4,7},{5,6},{6,5},{7,4},{8,11},{9,10},{10,... | collective-permute-start | bytes 24584 | tf_op jit(solution)/shard_map/ppermute | solution.py:329
  55.6 3.6 %collective-permute-start.20 = (f32[8,256]{1,0:T(8,128)S(1)}, f32[8,256]{1,0:T(8,128)S(1)}, u32[]{:S(2)}, u32[]{:S(2)}) collective-permute-start(f32[8,256]{1,0:T(8,128)S(1)} %get-tuple-element.130.refs_6_), channel_id=1, source_target_pairs={{0,3},{1,2},{2,1},{3,0},{4,7},{5,6},{6,5},{7,4},{8,11},{9,10},{10,... | collective-permute-start | bytes 24584 | tf_op jit(solution)/shard_map/ppermute | solution.py:329
  60.1 8.2 %collective-permute-start.17 = (f32[8,128]{1,0:T(8,128)S(1)}, f32[8,128]{1,0:T(8,128)S(1)}, u32[]{:S(2)}, u32[]{:S(2)}) collective-permute-start(f32[8,128]{1,0:T(8,128)S(1)} %get-tuple-element.129.refs_4_), channel_id=1, source_target_pairs={{0,8},{4,12},{8,0},{12,4},{16,24},{20,28},{24,16},{28,20},{1,9},{5... | collective-permute-start | bytes 12296 | tf_op jit(solution)/shard_map/ppermute | solution.py:320
  71.1 5.0 %collective-permute-start.23 = (f32[8,128]{1,0:T(8,128)S(1)}, f32[8,128]{1,0:T(8,128)S(1)}, u32[]{:S(2)}, u32[]{:S(2)}) collective-permute-start(f32[8,128]{1,0:T(8,128)S(1)} %get-tuple-element.133.refs_4_), channel_id=1, source_target_pairs={{0,16},{4,20},{8,24},{12,28},{16,0},{20,4},{24,8},{28,12},{1,17},{... | collective-permute-start | bytes 12296 | tf_op jit(solution)/shard_map/ppermute | solution.py:320
  82.9 2.9 %collective-permute-start.27 = (f32[8,256]{1,0:T(8,128)S(1)}, f32[8,256]{1,0:T(8,128)S(1)}, u32[]{:S(2)}, u32[]{:S(2)}) collective-permute-start(f32[8,256]{1,0:T(8,128)S(1)} %get-tuple-element.141), channel_id=1, source_target_pairs={{0,2},{1,3},{2,0},{3,1},{4,6},{5,7},{6,4},{7,5},{8,10},{9,11},{10,... | collective-permute-start | bytes 24584 | tf_op jit(solution)/shard_map/ppermute | solution.py:329
  87.5 3.8 %collective-permute-done.28.refs_4_ = f32[8,256]{1,0:T(8,128)S(1)} collective-permute-done((f32[8,256]{1,0:T(8,128)S(1)}, f32[8,256]{1,0:T(8,128)S(1)}, u32[]{:S(2)}, u32[]{:S(2)}) %collective-permute-start.28) | collective-permute-done | bytes 8224 | tf_op jit(solution)/shard_map/ppermute | solution.py:329
  92.4 4.0 %collective-permute-start.30 = (f32[8,256]{1,0:T(8,128)S(1)}, f32[8,256]{1,0:T(8,128)S(1)}, u32[]{:S(2)}, u32[]{:S(2)}) collective-permute-start(f32[8,256]{1,0:T(8,128)S(1)} %get-tuple-element.144.refs_6_), channel_id=1, source_target_pairs={{0,1},{1,0},{2,3},{3,2},{4,5},{5,4},{6,7},{7,6},{8,9},{9,8},{10,11... | collective-permute-start | bytes 24584 | tf_op jit(solution)/shard_map/ppermute | solution.py:329
  96.4 6.7 %collective-permute-start.29 = (f32[8,128]{1,0:T(8,128)S(1)}, f32[8,128]{1,0:T(8,128)S(1)}, u32[]{:S(2)}, u32[]{:S(2)}) collective-permute-start(f32[8,128]{1,0:T(8,128)S(1)} %get-tuple-element.143.refs_4_), channel_id=1, source_target_pairs={{0,8},{4,12},{8,0},{12,4},{16,24},{20,28},{24,16},{28,20},{1,9},{5... | collective-permute-start | bytes 12296 | tf_op jit(solution)/shard_map/ppermute | solution.py:320
  106.0 4.9 %collective-permute-start.35 = (f32[8,128]{1,0:T(8,128)S(1)}, f32[8,128]{1,0:T(8,128)S(1)}, u32[]{:S(2)}, u32[]{:S(2)}) collective-permute-start(f32[8,128]{1,0:T(8,128)S(1)} %get-tuple-element.147.refs_4_), channel_id=1, source_target_pairs={{0,16},{4,20},{8,24},{12,28},{16,0},{20,4},{24,8},{28,12},{1,17},{... | collective-permute-start | bytes 12296 | tf_op jit(solution)/shard_map/ppermute | solution.py:320
  117.5 3.5 %collective-permute-start.40 = (f32[8,256]{1,0:T(8,128)S(1)}, f32[8,256]{1,0:T(8,128)S(1)}, u32[]{:S(2)}, u32[]{:S(2)}) collective-permute-start(f32[8,256]{1,0:T(8,128)S(1)} %get-tuple-element.164), channel_id=1, source_target_pairs={{0,3},{1,2},{2,1},{3,0},{4,7},{5,6},{6,5},{7,4},{8,11},{9,10},{10,... | collective-permute-start | bytes 24584 | tf_op jit(solution)/shard_map/ppermute | solution.py:329
  123.7 3.5 %collective-permute-start.44 = (f32[8,256]{1,0:T(8,128)S(1)}, f32[8,256]{1,0:T(8,128)S(1)}, u32[]{:S(2)}, u32[]{:S(2)}) collective-permute-start(f32[8,256]{1,0:T(8,128)S(1)} %get-tuple-element.166.refs_6_), channel_id=1, source_target_pairs={{0,3},{1,2},{2,1},{3,0},{4,7},{5,6},{6,5},{7,4},{8,11},{9,10},{10,... | collective-permute-start | bytes 24584 | tf_op jit(solution)/shard_map/ppermute | solution.py:329
  128.1 6.2 %collective-permute-start.41 = (f32[8,128]{1,0:T(8,128)S(1)}, f32[8,128]{1,0:T(8,128)S(1)}, u32[]{:S(2)}, u32[]{:S(2)}) collective-permute-start(f32[8,128]{1,0:T(8,128)S(1)} %get-tuple-element.165.refs_4_), channel_id=1, source_target_pairs={{0,8},{4,12},{8,0},{12,4},{16,24},{20,28},{24,16},{28,20},{1,9},{5... | collective-permute-start | bytes 12296 | tf_op jit(solution)/shard_map/ppermute | solution.py:320
  137.3 4.9 %collective-permute-start.47 = (f32[8,128]{1,0:T(8,128)S(1)}, f32[8,128]{1,0:T(8,128)S(1)}, u32[]{:S(2)}, u32[]{:S(2)}) collective-permute-start(f32[8,128]{1,0:T(8,128)S(1)} %get-tuple-element.169.refs_4_), channel_id=1, source_target_pairs={{0,16},{4,20},{8,24},{12,28},{16,0},{20,4},{24,8},{28,12},{1,17},{... | collective-permute-start | bytes 12296 | tf_op jit(solution)/shard_map/ppermute | solution.py:320
  149.0 2.9 %collective-permute-start.51 = (f32[8,256]{1,0:T(8,128)S(1)}, f32[8,256]{1,0:T(8,128)S(1)}, u32[]{:S(2)}, u32[]{:S(2)}) collective-permute-start(f32[8,256]{1,0:T(8,128)S(1)} %get-tuple-element.185), channel_id=1, source_target_pairs={{0,2},{1,3},{2,0},{3,1},{4,6},{5,7},{6,4},{7,5},{8,10},{9,11},{10,... | collective-permute-start | bytes 24584 | tf_op jit(solution)/shard_map/ppermute | solution.py:329
  153.5 3.9 %collective-permute-done.52.refs_4_ = f32[8,256]{1,0:T(8,128)S(1)} collective-permute-done((f32[8,256]{1,0:T(8,128)S(1)}, f32[8,256]{1,0:T(8,128)S(1)}, u32[]{:S(2)}, u32[]{:S(2)}) %collective-permute-start.52) | collective-permute-done | bytes 8224 | tf_op jit(solution)/shard_map/ppermute | solution.py:329
  158.4 4.1 %collective-permute-start.54 = (f32[8,256]{1,0:T(8,128)S(1)}, f32[8,256]{1,0:T(8,128)S(1)}, u32[]{:S(2)}, u32[]{:S(2)}) collective-permute-start(f32[8,256]{1,0:T(8,128)S(1)} %get-tuple-element.188.refs_6_), channel_id=1, source_target_pairs={{0,1},{1,0},{2,3},{3,2},{4,5},{5,4},{6,7},{7,6},{8,9},{9,8},{10,11... | collective-permute-start | bytes 24584 | tf_op jit(solution)/shard_map/ppermute | solution.py:329
  162.5 6.2 %collective-permute-start.53 = (f32[8,128]{1,0:T(8,128)S(1)}, f32[8,128]{1,0:T(8,128)S(1)}, u32[]{:S(2)}, u32[]{:S(2)}) collective-permute-start(f32[8,128]{1,0:T(8,128)S(1)} %get-tuple-element.187.refs_4_), channel_id=1, source_target_pairs={{0,8},{4,12},{8,0},{12,4},{16,24},{20,28},{24,16},{28,20},{1,9},{5... | collective-permute-start | bytes 12296 | tf_op jit(solution)/shard_map/ppermute | solution.py:320
  171.7 4.9 %collective-permute-start.59 = (f32[8,128]{1,0:T(8,128)S(1)}, f32[8,128]{1,0:T(8,128)S(1)}, u32[]{:S(2)}, u32[]{:S(2)}) collective-permute-start(f32[8,128]{1,0:T(8,128)S(1)} %get-tuple-element.191.refs_4_), channel_id=1, source_target_pairs={{0,16},{4,20},{8,24},{12,28},{16,0},{20,4},{24,8},{28,12},{1,17},{... | collective-permute-start | bytes 12296 | tf_op jit(solution)/shard_map/ppermute | solution.py:320
  179.0 10.6 %all_to_all.5.dots_ref = f32[32,1,128]{2,1,0:T(1,128)S(1)} all-to-all(f32[32,1,128]{2,1,0:T(1,128)S(1)} %get-tuple-element.202), channel_id=1, replica_groups=mesh['sub'=8,'grp'=4] {'sub','grp'}, dimensions={0} | all-to-all | bytes 32768 | tf_op jit(solution)/shard_map/all_to_all | solution.py:483
  (146 shorter events, 74.5 us)
Async XLA Ops:
  25.4 12.6 %collective-permute-start.9 = (f32[8,256]{1,0:T(8,128)S(1)}, f32[8,256]{1,0:T(8,128)S(1)}, u32[]{:S(2)}, u32[]{:S(2)}) collective-permute-start(f32[8,256]{1,0:T(8,128)S(1)} %get-tuple-element.118.refs_6_), channel_id=1, source_target_pairs={{0,3},{1,2},{2,1},{3,0},{4,7},{5,6},{6,5},{7,4},{8,11},{9,10},{10,... | collective-permute-start | bytes 24584 | tf_op jit(solution)/shard_map/ppermute | solution.py:329
  25.6 12.4 %collective-permute-start.8 = (f32[8,256]{1,0:T(8,128)S(1)}, f32[8,256]{1,0:T(8,128)S(1)}, u32[]{:S(2)}, u32[]{:S(2)}) collective-permute-start(f32[8,256]{1,0:T(8,128)S(1)} %get-tuple-element.118.refs_6_), channel_id=1, source_target_pairs={{0,2},{1,3},{2,0},{3,1},{4,6},{5,7},{6,4},{7,5},{8,10},{9,11},{10,... | collective-permute-start | bytes 24584 | tf_op jit(solution)/shard_map/ppermute | solution.py:329
  25.7 12.4 %collective-permute-start.7 = (f32[8,256]{1,0:T(8,128)S(1)}, f32[8,256]{1,0:T(8,128)S(1)}, u32[]{:S(2)}, u32[]{:S(2)}) collective-permute-start(f32[8,256]{1,0:T(8,128)S(1)} %get-tuple-element.118.refs_6_), channel_id=1, source_target_pairs={{0,1},{1,0},{2,3},{3,2},{4,5},{5,4},{6,7},{7,6},{8,9},{9,8},{10,11... | collective-permute-start | bytes 24584 | tf_op jit(solution)/shard_map/ppermute | solution.py:329
  29.8 8.2 %collective-permute-start.6 = (f32[8,128]{1,0:T(8,128)S(1)}, f32[8,128]{1,0:T(8,128)S(1)}, u32[]{:S(2)}, u32[]{:S(2)}) collective-permute-start(f32[8,128]{1,0:T(8,128)S(1)} %get-tuple-element.117.refs_4_), channel_id=1, source_target_pairs={{0,8},{4,12},{8,0},{12,4},{16,24},{20,28},{24,16},{28,20},{1,9},{5... | collective-permute-start | bytes 12296 | tf_op jit(solution)/shard_map/ppermute | solution.py:320
  55.6 14.2 %collective-permute-start.20 = (f32[8,256]{1,0:T(8,128)S(1)}, f32[8,256]{1,0:T(8,128)S(1)}, u32[]{:S(2)}, u32[]{:S(2)}) collective-permute-start(f32[8,256]{1,0:T(8,128)S(1)} %get-tuple-element.130.refs_6_), channel_id=1, source_target_pairs={{0,3},{1,2},{2,1},{3,0},{4,7},{5,6},{6,5},{7,4},{8,11},{9,10},{10,... | collective-permute-start | bytes 24584 | tf_op jit(solution)/shard_map/ppermute | solution.py:329
  59.2 10.6 %collective-permute-start.19 = (f32[8,256]{1,0:T(8,128)S(1)}, f32[8,256]{1,0:T(8,128)S(1)}, u32[]{:S(2)}, u32[]{:S(2)}) collective-permute-start(f32[8,256]{1,0:T(8,128)S(1)} %get-tuple-element.130.refs_6_), channel_id=1, source_target_pairs={{0,2},{1,3},{2,0},{3,1},{4,6},{5,7},{6,4},{7,5},{8,10},{9,11},{10,... | collective-permute-start | bytes 24584 | tf_op jit(solution)/shard_map/ppermute | solution.py:329
  59.2 10.6 %collective-permute-start.18 = (f32[8,256]{1,0:T(8,128)S(1)}, f32[8,256]{1,0:T(8,128)S(1)}, u32[]{:S(2)}, u32[]{:S(2)}) collective-permute-start(f32[8,256]{1,0:T(8,128)S(1)} %get-tuple-element.130.refs_6_), channel_id=1, source_target_pairs={{0,1},{1,0},{2,3},{3,2},{4,5},{5,4},{6,7},{7,6},{8,9},{9,8},{10,11... | collective-permute-start | bytes 24584 | tf_op jit(solution)/shard_map/ppermute | solution.py:329
  60.1 9.7 %collective-permute-start.17 = (f32[8,128]{1,0:T(8,128)S(1)}, f32[8,128]{1,0:T(8,128)S(1)}, u32[]{:S(2)}, u32[]{:S(2)}) collective-permute-start(f32[8,128]{1,0:T(8,128)S(1)} %get-tuple-element.129.refs_4_), channel_id=1, source_target_pairs={{0,8},{4,12},{8,0},{12,4},{16,24},{20,28},{24,16},{28,20},{1,9},{5... | collective-permute-start | bytes 12296 | tf_op jit(solution)/shard_map/ppermute | solution.py:320
  70.4 7.3 %collective-permute-start.22 = (f32[96,128]{1,0:T(8,128)S(1)}, f32[96,128]{1,0:T(8,128)S(1)}, u32[]{:S(2)}, u32[]{:S(2)}) collective-permute-start(f32[96,128]{1,0:T(8,128)S(1)} %get-tuple-element.131.refs_0_), channel_id=1, source_target_pairs={{0,4},{4,0},{8,12},{12,8},{16,20},{20,16},{24,28},{28,24},{1,5},{5... | collective-permute-start | bytes 147464 | tf_op jit(solution)/shard_map/ppermute | solution.py:320
  70.5 7.2 %collective-permute-start.21 = (f32[96,128]{1,0:T(8,128)S(1)}, f32[96,128]{1,0:T(8,128)S(1)}, u32[]{:S(2)}, u32[]{:S(2)}) collective-permute-start(f32[96,128]{1,0:T(8,128)S(1)} %get-tuple-element.132.refs_1_), channel_id=1, source_target_pairs={{4,8},{8,4},{12,16},{16,12},{20,24},{24,20},{5,9},{9,5},{13,17},{1... | collective-permute-start | bytes 147464 | tf_op jit(solution)/shard_map/ppermute | solution.py:325
  92.0 12.7 %collective-permute-start.32 = (f32[8,256]{1,0:T(8,128)S(1)}, f32[8,256]{1,0:T(8,128)S(1)}, u32[]{:S(2)}, u32[]{:S(2)}) collective-permute-start(f32[8,256]{1,0:T(8,128)S(1)} %get-tuple-element.144.refs_6_), channel_id=1, source_target_pairs={{0,3},{1,2},{2,1},{3,0},{4,7},{5,6},{6,5},{7,4},{8,11},{9,10},{10,... | collective-permute-start | bytes 24584 | tf_op jit(solution)/shard_map/ppermute | solution.py:329
  92.4 12.3 %collective-permute-start.31 = (f32[8,256]{1,0:T(8,128)S(1)}, f32[8,256]{1,0:T(8,128)S(1)}, u32[]{:S(2)}, u32[]{:S(2)}) collective-permute-start(f32[8,256]{1,0:T(8,128)S(1)} %get-tuple-element.144.refs_6_), channel_id=1, source_target_pairs={{0,2},{1,3},{2,0},{3,1},{4,6},{5,7},{6,4},{7,5},{8,10},{9,11},{10,... | collective-permute-start | bytes 24584 | tf_op jit(solution)/shard_map/ppermute | solution.py:329
  92.4 12.3 %collective-permute-start.30 = (f32[8,256]{1,0:T(8,128)S(1)}, f32[8,256]{1,0:T(8,128)S(1)}, u32[]{:S(2)}, u32[]{:S(2)}) collective-permute-start(f32[8,256]{1,0:T(8,128)S(1)} %get-tuple-element.144.refs_6_), channel_id=1, source_target_pairs={{0,1},{1,0},{2,3},{3,2},{4,5},{5,4},{6,7},{7,6},{8,9},{9,8},{10,11... | collective-permute-start | bytes 24584 | tf_op jit(solution)/shard_map/ppermute | solution.py:329
  96.4 8.2 %collective-permute-start.29 = (f32[8,128]{1,0:T(8,128)S(1)}, f32[8,128]{1,0:T(8,128)S(1)}, u32[]{:S(2)}, u32[]{:S(2)}) collective-permute-start(f32[8,128]{1,0:T(8,128)S(1)} %get-tuple-element.143.refs_4_), channel_id=1, source_target_pairs={{0,8},{4,12},{8,0},{12,4},{16,24},{20,28},{24,16},{28,20},{1,9},{5... | collective-permute-start | bytes 12296 | tf_op jit(solution)/shard_map/ppermute | solution.py:320
  123.7 12.2 %collective-permute-start.44 = (f32[8,256]{1,0:T(8,128)S(1)}, f32[8,256]{1,0:T(8,128)S(1)}, u32[]{:S(2)}, u32[]{:S(2)}) collective-permute-start(f32[8,256]{1,0:T(8,128)S(1)} %get-tuple-element.166.refs_6_), channel_id=1, source_target_pairs={{0,3},{1,2},{2,1},{3,0},{4,7},{5,6},{6,5},{7,4},{8,11},{9,10},{10,... | collective-permute-start | bytes 24584 | tf_op jit(solution)/shard_map/ppermute | solution.py:329
  127.2 8.7 %collective-permute-start.43 = (f32[8,256]{1,0:T(8,128)S(1)}, f32[8,256]{1,0:T(8,128)S(1)}, u32[]{:S(2)}, u32[]{:S(2)}) collective-permute-start(f32[8,256]{1,0:T(8,128)S(1)} %get-tuple-element.166.refs_6_), channel_id=1, source_target_pairs={{0,2},{1,3},{2,0},{3,1},{4,6},{5,7},{6,4},{7,5},{8,10},{9,11},{10,... | collective-permute-start | bytes 24584 | tf_op jit(solution)/shard_map/ppermute | solution.py:329
  127.2 8.7 %collective-permute-start.42 = (f32[8,256]{1,0:T(8,128)S(1)}, f32[8,256]{1,0:T(8,128)S(1)}, u32[]{:S(2)}, u32[]{:S(2)}) collective-permute-start(f32[8,256]{1,0:T(8,128)S(1)} %get-tuple-element.166.refs_6_), channel_id=1, source_target_pairs={{0,1},{1,0},{2,3},{3,2},{4,5},{5,4},{6,7},{7,6},{8,9},{9,8},{10,11... | collective-permute-start | bytes 24584 | tf_op jit(solution)/shard_map/ppermute | solution.py:329
  128.1 7.8 %collective-permute-start.41 = (f32[8,128]{1,0:T(8,128)S(1)}, f32[8,128]{1,0:T(8,128)S(1)}, u32[]{:S(2)}, u32[]{:S(2)}) collective-permute-start(f32[8,128]{1,0:T(8,128)S(1)} %get-tuple-element.165.refs_4_), channel_id=1, source_target_pairs={{0,8},{4,12},{8,0},{12,4},{16,24},{20,28},{24,16},{28,20},{1,9},{5... | collective-permute-start | bytes 12296 | tf_op jit(solution)/shard_map/ppermute | solution.py:320
  136.5 7.2 %collective-permute-start.46 = (f32[96,128]{1,0:T(8,128)S(1)}, f32[96,128]{1,0:T(8,128)S(1)}, u32[]{:S(2)}, u32[]{:S(2)}) collective-permute-start(f32[96,128]{1,0:T(8,128)S(1)} %get-tuple-element.167.refs_0_), channel_id=1, source_target_pairs={{0,4},{4,0},{8,12},{12,8},{16,20},{20,16},{24,28},{28,24},{1,5},{5... | collective-permute-start | bytes 147464 | tf_op jit(solution)/shard_map/ppermute | solution.py:320
  158.1 12.2 %collective-permute-start.56 = (f32[8,256]{1,0:T(8,128)S(1)}, f32[8,256]{1,0:T(8,128)S(1)}, u32[]{:S(2)}, u32[]{:S(2)}) collective-permute-start(f32[8,256]{1,0:T(8,128)S(1)} %get-tuple-element.188.refs_6_), channel_id=1, source_target_pairs={{0,3},{1,2},{2,1},{3,0},{4,7},{5,6},{6,5},{7,4},{8,11},{9,10},{10,... | collective-permute-start | bytes 24584 | tf_op jit(solution)/shard_map/ppermute | solution.py:329
  158.4 11.9 %collective-permute-start.55 = (f32[8,256]{1,0:T(8,128)S(1)}, f32[8,256]{1,0:T(8,128)S(1)}, u32[]{:S(2)}, u32[]{:S(2)}) collective-permute-start(f32[8,256]{1,0:T(8,128)S(1)} %get-tuple-element.188.refs_6_), channel_id=1, source_target_pairs={{0,2},{1,3},{2,0},{3,1},{4,6},{5,7},{6,4},{7,5},{8,10},{9,11},{10,... | collective-permute-start | bytes 24584 | tf_op jit(solution)/shard_map/ppermute | solution.py:329
  158.4 11.9 %collective-permute-start.54 = (f32[8,256]{1,0:T(8,128)S(1)}, f32[8,256]{1,0:T(8,128)S(1)}, u32[]{:S(2)}, u32[]{:S(2)}) collective-permute-start(f32[8,256]{1,0:T(8,128)S(1)} %get-tuple-element.188.refs_6_), channel_id=1, source_target_pairs={{0,1},{1,0},{2,3},{3,2},{4,5},{5,4},{6,7},{7,6},{8,9},{9,8},{10,11... | collective-permute-start | bytes 24584 | tf_op jit(solution)/shard_map/ppermute | solution.py:329
  162.5 7.8 %collective-permute-start.53 = (f32[8,128]{1,0:T(8,128)S(1)}, f32[8,128]{1,0:T(8,128)S(1)}, u32[]{:S(2)}, u32[]{:S(2)}) collective-permute-start(f32[8,128]{1,0:T(8,128)S(1)} %get-tuple-element.187.refs_4_), channel_id=1, source_target_pairs={{0,8},{4,12},{8,0},{12,4},{16,24},{20,28},{24,16},{28,20},{1,9},{5... | collective-permute-start | bytes 12296 | tf_op jit(solution)/shard_map/ppermute | solution.py:320
  170.9 7.2 %collective-permute-start.58 = (f32[96,128]{1,0:T(8,128)S(1)}, f32[96,128]{1,0:T(8,128)S(1)}, u32[]{:S(2)}, u32[]{:S(2)}) collective-permute-start(f32[96,128]{1,0:T(8,128)S(1)} %get-tuple-element.189.refs_0_), channel_id=1, source_target_pairs={{0,4},{4,0},{8,12},{12,8},{16,20},{20,16},{24,28},{28,24},{1,5},{5... | collective-permute-start | bytes 147464 | tf_op jit(solution)/shard_map/ppermute | solution.py:320
  (45 other events, 270.5 us)

commit v5 on v4

--- a/solution.py
+++ b/solution.py
@@ -84,16 +84,20 @@
         out_ref[pl.ds(pl.multiple_of(index * ROWS, ROWS), ROWS)] = jnp.sum(total, axis=1)
         return carry
 
-    lax.fori_loop(0, out_ref.shape[0] // ROWS, step, 0)
-
-
-def table_kernel(slots_ref, column_ref, corner_ref, selector_ref, swap_ref, table_ref):
+    lax.fori_loop(0, out_ref.shape[0] // ROWS, step, 0, unroll=True)
+
+
+def table_kernel(neighbour_ref, column_ref, corner_ref, selector_ref, swap_ref, table_ref):
+    cells = swap_ref.shape[0]
+    start = lax.axis_index("sub") * cells
     def one_hot(row, count):
         places = lax.broadcasted_iota(jnp.int32, (count, row.shape[1]), 0)
         return jnp.where(places == row, 1.0, 0.0).astype(BF16)
 
-    selector_ref[...] = one_hot(slots_ref[...], selector_ref.shape[0])
-    swap_ref[...] = one_hot(column_ref[...], swap_ref.shape[0])
+    neighbour = neighbour_ref[...]
+    slots = jnp.where(neighbour < 0, -1, neighbour - (start - cells))
+    selector_ref[...] = one_hot(slots, selector_ref.shape[0])
+    swap_ref[...] = one_hot(column_ref[...] - start, swap_ref.shape[0])
     chunk = 128
 
     def step(index, carry):
@@ -120,27 +124,29 @@
         odd, own_ref[...], previous_ref[...], selector_ref, swap_ref, stiffness_ref, stiff_ref, near_ref, far_ref
     )
     near_ref[iface:] = jnp.zeros((ROWS, cells), F32)
-
-
-def arrived(odd, near_ref, far_ref, from_far_ref, from_near_ref, iface):
-    near, far = near_ref[:iface], far_ref[...]
-    from_near, from_far = from_near_ref[:iface], from_far_ref[...]
+    far_ref[iface:] = jnp.zeros((ROWS, cells), F32)
+
+
+def arrived(odd, far_ref, near_ref, from_far_ref, from_near_ref, iface):
+    near, far = near_ref[:iface], far_ref[:iface]
+    from_near, from_far = from_near_ref[:iface], from_far_ref[:iface]
     own = jnp.where(odd, far - from_far, near - from_near)
     previous = jnp.where(odd, from_near - near, from_far - far)
     return own, previous
 
 
 def second_kernel(
-    near_ref, far_ref, from_far_ref, from_near_ref, r_ref, u_ref, selector_ref, swap_ref, stiffness_ref,
+    far_ref, near_ref, from_far_ref, from_near_ref, r_ref, u_ref, selector_ref, swap_ref, stiffness_ref,
     far_out, near_out, w_out, stiff_ref,
 ):
     iface = r_ref.shape[0]
     odd = lax.axis_index("sub") % 2 == 1
-    w, w_previous = arrived(odd, near_ref, far_ref, from_far_ref, from_near_ref, iface)
+    w, w_previous = arrived(odd, far_ref, near_ref, from_far_ref, from_near_ref, iface)
     w_out[0] = w
     w_out[1] = w_previous
     dots = dot_rows(r_ref[...], u_ref[...], w)
     near_out[iface:] = dots
+    far_out[iface:] = dots
     stiffen(odd, w, w_previous, selector_ref, swap_ref, stiffness_ref, stiff_ref, near_out, far_out)
 
 
@@ -189,14 +195,14 @@
 
 
 def middle_kernel(first, last, *refs):
-    (near_ref, far_ref, from_far_ref, from_near_ref, dots_ref, dots_other_ref, m_ref) = refs[:7]
+    (far_ref, near_ref, from_far_ref, from_near_ref, dots_ref, dots_other_ref, m_ref) = refs[:7]
     (selector_ref, swap_ref, stiffness_ref) = refs[7:10]
     ins = list(refs[10:19])
     outs = list(refs[19:28])
     m = m_ref[...]
     iface = m.shape[0]
     odd = lax.axis_index("sub") % 2 == 1
-    n, n_previous = arrived(odd, near_ref, far_ref, from_far_ref, from_near_ref, iface)
+    n, n_previous = arrived(odd, far_ref, near_ref, from_far_ref, from_near_ref, iface)
     dots, w, previous = update(
         first, last, ins + outs, m, n, n_previous, dots_ref[...] + dots_other_ref[...]
     )
@@ -206,19 +212,20 @@
     else:
         far_out, near_out, stiff_ref = refs[28:31]
         near_out[iface:] = dots
+        far_out[iface:] = dots
         stiffen(odd, w, previous, selector_ref, swap_ref, stiffness_ref, stiff_ref, near_out, far_out)
 
 
 def corner_kernel(
-    ranks, near_ref, far_ref, from_far_ref, from_near_ref, selector_ref, operators_ref, table_ref,
+    ranks, far_ref, near_ref, from_far_ref, from_near_ref, selector_ref, operators_ref, table_ref,
     m_out, gap_out, *rest,
 ):
-    outs, sums_ref = rest[:ranks], rest[ranks]
+    outs, (dots_out, sums_ref) = rest[:ranks], rest[ranks:]
     iface, cells = m_out.shape
     odd = lax.axis_index("sub") % 2 == 1
-    own, previous = arrived(odd, near_ref, far_ref, from_far_ref, from_near_ref, iface)
+    own, previous = arrived(odd, far_ref, near_ref, from_far_ref, from_near_ref, iface)
     m_out[...] = own
-    dots = near_ref[iface:] + from_near_ref[iface:]
+    dots_out[...] = near_ref[iface:] + from_near_ref[iface:]
     gap = spread_of(own, previous, selector_ref[...])
     gap_out[...] = gap
     parts = []
@@ -228,44 +235,24 @@
         parts.append(jnp.concatenate([part, jnp.zeros((ROWS - CORNER_DOF, cells), F32)], axis=0))
     sums_ref[...] = exact_dot(jnp.concatenate(parts, axis=1), table_ref[...], NT)
     owned = sums_ref.shape[1] // ranks
-    pad = jnp.zeros((1, owned - 2 * cells), F32) if owned > 2 * cells else None
-    tail = []
-    for row in range(0, ROWS - CORNER_DOF):
-        lanes = [dots[2 * row : 2 * row + 1], dots[2 * row + 1 : 2 * row + 2]]
-        if pad is not None:
-            lanes.append(pad)
-        tail.append(jnp.concatenate(lanes, axis=1))
-    tail = jnp.concatenate(tail, axis=0)
     for distance in range(ranks):
-        rank = lax.axis_index("grp") ^ distance
-        piece = sums_ref[:, pl.ds(pl.multiple_of(rank * owned, 128), owned)]
-        outs[distance][...] = jnp.concatenate([piece[:CORNER_DOF], tail], axis=0)
+        rank = lax.axis_index("grp") ^ (ranks - 1 - distance)
+        outs[distance][...] = sums_ref[:, pl.ds(pl.multiple_of(rank * owned, 128), owned)]
 
 
 def local_kernel(gap_ref, inverse_ref, local_ref):
     apply_blocks([inverse_ref], [gap_ref[...]], local_ref)
 
 
-def coarse_kernel(ranks, coarse_ref, *rest):
-    pieces, (solved_ref, dots_ref, sums_ref) = rest[:ranks], rest[ranks:]
+def coarse_kernel(ranks, coarse_ref, dots_ref, other_ref, *rest):
+    pieces, (solved_ref, sums_ref) = rest[:ranks], rest[ranks:]
     cells = dots_ref.shape[1]
     for distance in range(ranks):
         rank = lax.axis_index("grp") ^ distance
-        sums_ref[rank] = pieces[distance][...]
+        sums_ref[rank] = pieces[ranks - 1 - distance][...]
     total = sums_ref[0]
     for rank in range(1, ranks):
         total = total + sums_ref[rank]
-    tail = total[CORNER_DOF:]
-    dots_ref[...] = jnp.concatenate(
-        [
-            tail[0:1, :cells],
-            tail[0:1, cells : 2 * cells],
-            tail[1:2, :cells],
-            tail[1:2, cells : 2 * cells],
-            jnp.zeros((ROWS - 4, cells), F32),
-        ],
-        axis=0,
-    )
     blocks, order = coarse_ref.shape[0], coarse_ref.shape[1]
     width = order // CORNER_DOF
     columns = []
@@ -279,20 +266,38 @@
         rows = [result[:, j * width : (j + 1) * width] for j in range(CORNER_DOF)]
         columns.append(jnp.concatenate(rows, axis=0))
     solved = jnp.concatenate(columns, axis=1)
-    solved_ref[...] = jnp.concatenate(
-        [solved, jnp.zeros((ROWS - CORNER_DOF, solved.shape[1]), F32)], axis=0
-    )
-
-
-def lift_kernel(ranks, local_ref, operators_ref, table_ref, selector_ref, dots_ref, other_ref, *rest):
+    dots = dots_ref[...] + other_ref[...]
+    rows = [solved]
+    for first in (0, 2):
+        lanes = [dots[first : first + 1], dots[first + 1 : first + 2]]
+        if solved.shape[1] > 2 * cells:
+            lanes.append(jnp.zeros((1, solved.shape[1] - 2 * cells), F32))
+        rows.append(jnp.concatenate(lanes, axis=1))
+    solved_ref[...] = jnp.concatenate(rows, axis=0)
+
+
+def lift_kernel(ranks, local_ref, operators_ref, table_ref, selector_ref, *rest):
     pieces, (far_ref, near_ref, dots_out, values_ref) = rest[:ranks], rest[ranks:]
     cells = local_ref.shape[1]
     owned = values_ref.shape[1] // ranks
-    dots_out[...] = dots_ref[...] + other_ref[...]
     for distance in range(ranks):
         rank = lax.axis_index("grp") ^ distance
         values_ref[:, pl.ds(pl.multiple_of(rank * owned, 128), owned)] = pieces[distance][...]
-    picked = exact_dot(values_ref[...], table_ref[...], NN)
+    values = values_ref[...]
+    tail = values[CORNER_DOF:, :owned]
+    for rank in range(1, ranks):
+        tail = tail + values[CORNER_DOF:, rank * owned : (rank + 1) * owned]
+    dots_out[...] = jnp.concatenate(
+        [
+            tail[0:1, :cells],
+            tail[0:1, cells : 2 * cells],
+            tail[1:2, :cells],
+            tail[1:2, cells : 2 * cells],
+            jnp.zeros((ROWS - 4, cells), F32),
+        ],
+        axis=0,
+    )
+    picked = exact_dot(values, table_ref[...], NN)
     lifted = local_ref[...]
     for corner in range(CORNERS_SUB):
         lanes = slice(corner * cells, (corner + 1) * cells)
@@ -361,7 +366,6 @@
     iface, _, cells = gap_data.shape
     ranks = lax.axis_size("grp")
     sub_count = lax.axis_size("sub")
-    start = lax.axis_index("sub") * cells
     right_side = gap_data[:, 0, :]
     inverse = local_inverse[:, :, 0, :]
     stiff = stiffness[:, :, :, 0, :]
@@ -369,8 +373,6 @@
     blocks_own, order = coarse_inverse.shape[:2]
     owned = blocks_own * (order // CORNER_DOF)
     group = owned * ranks
-    slots = jnp.where(neighbour < 0, -1, neighbour - (start - cells))
-    column = stiff_column - start
     corners = corner_index.reshape(1, CORNERS_SUB * cells)
 
     selector, swap, table = call(
@@ -382,7 +384,7 @@
         ),
         count=3,
         name="tables",
-    )(slots, column, corners)
+    )(neighbour, stiff_column, corners)
 
     field = shape(iface, cells)
     pair = shape(2, iface, cells)
@@ -394,16 +396,16 @@
 
     def apply_operator(near, far):
         from_far, from_near = swapped_far(far), swapped(near, 1)
-        m, gap, *parts = call(
+        m, gap, *parts, dots = call(
             lambda *refs: corner_kernel(ranks, *refs),
-            (field, field) + (piece,) * ranks,
+            (field, field) + (piece,) * ranks + (rows,),
             count=7,
             scratch=[pltpu.VMEM((ROWS, group), F32)],
             flops=2 * 24 * iface * cells,
             moved=2 * 24 * iface * cells + group * CORNERS_SUB * cells * 2,
             name="corners",
-        )(near, far, from_far, from_near, selector, operators, table)
-        arrivals = [parts[0]] + [exchanged(parts[d], d) for d in range(1, ranks)]
+        )(far, near, from_far, from_near, selector, operators, table)
+        arrivals = [exchanged(parts[ranks - 1 - d], d) for d in range(ranks - 1, 0, -1)] + [parts[ranks - 1]]
         local = call(
             local_kernel,
             field,
@@ -412,43 +414,43 @@
             moved=2 * iface * iface * cells,
             name="local",
         )(gap, inverse)
-        solved, dots = call(
+        other = swapped(dots, 2)
+        solved = call(
             lambda *refs: coarse_kernel(ranks, *refs),
-            (piece, rows),
-            count=1 + ranks,
+            piece,
+            count=3 + ranks,
             scratch=[pltpu.VMEM((ranks, ROWS, owned), F32)],
             flops=2 * blocks_own * order * order,
             moved=2 * blocks_own * order * order,
             name="coarse",
-        )(coarse_inverse, *arrivals)
+        )(coarse_inverse, dots, other, *arrivals)
         values = [solved] + [exchanged(solved, d) for d in range(1, ranks)]
-        other = swapped(dots, 2)
         far, near, dots = call(
             lambda *refs: lift_kernel(ranks, *refs),
             (field, field, rows),
-            count=6 + ranks,
+            count=4 + ranks,
             scratch=[pltpu.VMEM((ROWS, group), F32)],
             flops=2 * 24 * iface * cells,
             moved=2 * 24 * iface * cells + group * CORNERS_SUB * cells * 2,
             name="lift",
-        )(local, operators, table, selector, dots, other, *values)
+        )(local, operators, table, selector, *values)
         return m, near, far, dots
 
     previous = shifted(right_side, 1)
     far, near = call(
-        first_kernel, (field, message), count=5, scratch=stiff_scratch, name="first", **stiff_cost
+        first_kernel, (message, message), count=5, scratch=stiff_scratch, name="first", **stiff_cost
     )(right_side, previous, selector, swap, stiff)
     u, near, far, dots = apply_operator(near, far)
     r = right_side
     from_far, from_near = swapped_far(far), swapped(near, 1)
     far, near, w = call(
         second_kernel,
-        (field, message, pair),
+        (message, message, pair),
         count=9,
         scratch=stiff_scratch,
         name="second",
         **stiff_cost,
-    )(near, far, from_far, from_near, r, u, selector, swap, stiff)
+    )(far, near, from_far, from_near, r, u, selector, swap, stiff)
 
     scalars, x, p, s, q, z = [jnp.zeros((ROWS, cells), F32)] + [r] * 4 + [w]
     for step in range(ITERS - 1):
@@ -465,7 +467,7 @@
             count = sub_count * ranks
             outs += (shape(count, 1, cells),)
         else:
-            outs += (field, message)
+            outs += (message, message)
         result = call(
             lambda *refs, first=first, last=last: middle_kernel(first, last, *refs),
             outs,
@@ -474,7 +476,7 @@
             name="last" if last else "middle",
             **({} if last else stiff_cost),
         )(
-            near, far, from_far, from_near, dots, other, m, selector, swap, stiff,
+            far, near, from_far, from_near, dots, other, m, selector, swap, stiff,
             scalars, x, r, u, w, p, s, q, z,
         )
         scalars, x, r, u, w, p, s, q, z = result[:9]

time: 191 us -> 185 us (0.969)
  starting transfers between devices: 115 us -> 110 us
    ppermute x19, waiting for transfers between devices: 13.5 us -> 24 us  [swapped(): lax.ppermute(block, 'sub', [(i, i ^ bit) for i in range(lax.axis_size('su...]
    ppermute x30, waiting for transfers between devices: 19.4 us -> 9.19 us  [exchanged(): lax.ppermute(block, 'grp', [(i, i ^ distance) for i in range(lax.axis_siz...]
    ppermute x19, starting transfers between devices: 61.5 us -> 56 us  [swapped(): lax.ppermute(block, 'sub', [(i, i ^ bit) for i in range(lax.axis_size('su...]
    unnamed x18 -> x22, local copies, waits for them, and re-layouts: 4.9 us -> 6.2 us
  transfers between devices with their start and end apart: 60 -> 60, of which waited for: 25 -> 26; matrix products, arithmetic and copies ran while one was open for 0% -> 0% of each run, Pallas kernels for 2% -> 2%
where the time goes in v5:
time: 185 us
  starting transfers between devices  110 us (59%)
  waiting for transfers between devices  33.2 us (18%)
  Pallas kernels  23.8 us (13%)
  blocking collectives  10.8 us (6%)
  local copies, waits for them, and re-layouts  6.2 us (3%)
    ppermute x19, starting transfers between devices, swapped(): lax.ppermute(block, 'sub', [(i, i ^ bit) for i in range(lax.axis_size('su...  56 us
    ppermute x30, starting transfers between devices, exchanged(): lax.ppermute(block, 'grp', [(i, i ^ distance) for i in range(lax.axis_siz...  44.3 us
    ppermute x19, waiting for transfers between devices, swapped(): lax.ppermute(block, 'sub', [(i, i ^ bit) for i in range(lax.axis_size('su...  24 us
    all_to_all x1, blocking collectives, on_device(): everyone = lax.all_to_all(result[9], ('sub', 'grp'), 0, 0, tiled=True)  10.8 us
    ppermute x30, waiting for transfers between devices, exchanged(): lax.ppermute(block, 'grp', [(i, i ^ distance) for i in range(lax.axis_siz...  9.19 us
    ppermute x10, starting transfers between devices, swapped_far(): lax.ppermute(block, 'sub', [(i, i + 1 if i % 2 else i - 1) for i in inner])  6.94 us
    pallas_call x4, Pallas kernels, on_device(): call(lambda *refs, first=first, last=last: middle_kernel(first, last, *re...  6.22 us
    unnamed x22, local copies, waits for them, and re-layouts  6.2 us
  transfers between devices with their start and end apart: 60, of which 26 were waited for; matrix products, arithmetic and copies ran while one was open for 0% of the time, Pallas kernels for 2%

profile of v5, /device:TPU:0, one launch (start us, length us, event | category | flops | bytes accessed | tf_op | source)
XLA Modules:
  0.0 184.6 jit_solution(147634129610147957)
XLA Ops:
  0.6 2.4 %collective-permute-start = (f32[96,128]{1,0:T(8,128)}, f32[96,128]{1,0:T(8,128)S(1)}, u32[]{:S(2)}, u32[]{:S(2)}) collective-permute-start(f32[96,128]{1,0:T(8,128)} %bitcast.34), channel_id=1, source_target_pairs={{0,4},{4,8},{8,12},{12,16},{16,20},{20,24},{24,28},{1,5},{5,9},{9,... | collective-permute-start | bytes 147464 | tf_op jit(solution)/shard_map/ppermute | solution.py:321
  10.9 5.5 %collective-permute-start.2 = (f32[104,128]{1,0:T(8,128)S(1)}, f32[104,128]{1,0:T(8,128)S(1)}, u32[]{:S(2)}, u32[]{:S(2)}) collective-permute-start(f32[104,128]{1,0:T(8,128)S(1)} %get-tuple-element.105.refs_1_), channel_id=1, source_target_pairs={{0,4},{4,0},{8,12},{12,8},{16,20},{20,16},{24,28},{28,24},{1,5},{5... | collective-permute-start | bytes 159752 | tf_op jit(solution)/shard_map/ppermute | solution.py:325
  19.0 3.7 %collective-permute-start.4 = (f32[8,256]{1,0:T(8,128)S(1)}, f32[8,256]{1,0:T(8,128)S(1)}, u32[]{:S(2)}, u32[]{:S(2)}) collective-permute-start(f32[8,256]{1,0:T(8,128)S(1)} %get-tuple-element.109), channel_id=1, source_target_pairs={{0,3},{1,2},{2,1},{3,0},{4,7},{5,6},{6,5},{7,4},{8,11},{9,10},{10,... | collective-permute-start | bytes 24584 | tf_op jit(solution)/shard_map/ppermute | solution.py:334
  23.4 2.5 %collective-permute-start.3 = (f32[8,128]{1,0:T(8,128)S(1)}, f32[8,128]{1,0:T(8,128)S(1)}, u32[]{:S(2)}, u32[]{:S(2)}) collective-permute-start(f32[8,128]{1,0:T(8,128)S(1)} %get-tuple-element.108.refs_1_), channel_id=1, source_target_pairs={{0,8},{4,12},{8,0},{12,4},{16,24},{20,28},{24,16},{28,20},{1,9},{5... | collective-permute-start | bytes 12296 | tf_op jit(solution)/shard_map/ppermute | solution.py:325
  28.3 3.6 %collective-permute-start.9 = (f32[8,256]{1,0:T(8,128)S(1)}, f32[8,256]{1,0:T(8,128)S(1)}, u32[]{:S(2)}, u32[]{:S(2)}) collective-permute-start(f32[8,256]{1,0:T(8,128)S(1)} %coarse.5.refs_4_), channel_id=1, source_target_pairs={{0,3},{1,2},{2,1},{3,0},{4,7},{5,6},{6,5},{7,4},{8,11},{9,10},{10,... | collective-permute-start | bytes 24584 | tf_op jit(solution)/shard_map/ppermute | solution.py:334
  33.7 2.7 %collective-permute-done.8.refs_6_ = f32[8,256]{1,0:T(8,128)S(1)} collective-permute-done((f32[8,256]{1,0:T(8,128)S(1)}, f32[8,256]{1,0:T(8,128)S(1)}, u32[]{:S(2)}, u32[]{:S(2)}) %collective-permute-start.8) | collective-permute-done | bytes 8224 | tf_op jit(solution)/shard_map/ppermute | solution.py:334
  38.1 3.4 %collective-permute-start.11 = (f32[96,128]{1,0:T(8,128)S(1)}, f32[96,128]{1,0:T(8,128)S(1)}, u32[]{:S(2)}, u32[]{:S(2)}) collective-permute-start(f32[96,128]{1,0:T(8,128)S(1)} %get-tuple-element.114.near_ref), channel_id=1, source_target_pairs={{0,4},{4,0},{8,12},{12,8},{16,20},{20,16},{24,28},{28,24},{1,5},{5... | collective-permute-start | bytes 147464 | tf_op jit(solution)/shard_map/ppermute | solution.py:325
  44.8 4.7 %collective-permute-start.13 = (f32[104,128]{1,0:T(8,128)S(1)}, f32[104,128]{1,0:T(8,128)S(1)}, u32[]{:S(2)}, u32[]{:S(2)}) collective-permute-start(f32[104,128]{1,0:T(8,128)S(1)} %get-tuple-element.117.refs_1_), channel_id=1, source_target_pairs={{0,4},{4,0},{8,12},{12,8},{16,20},{20,16},{24,28},{28,24},{1,5},{5... | collective-permute-start | bytes 159752 | tf_op jit(solution)/shard_map/ppermute | solution.py:325
  55.5 3.3 %collective-permute-start.14 = (f32[8,128]{1,0:T(8,128)S(1)}, f32[8,128]{1,0:T(8,128)S(1)}, u32[]{:S(2)}, u32[]{:S(2)}) collective-permute-start(f32[8,128]{1,0:T(8,128)S(1)} %get-tuple-element.119.refs_1_), channel_id=1, source_target_pairs={{0,8},{4,12},{8,0},{12,4},{16,24},{20,28},{24,16},{28,20},{1,9},{5... | collective-permute-start | bytes 12296 | tf_op jit(solution)/shard_map/ppermute | solution.py:325
  62.7 2.9 %collective-permute-start.18 = (f32[8,256]{1,0:T(8,128)S(1)}, f32[8,256]{1,0:T(8,128)S(1)}, u32[]{:S(2)}, u32[]{:S(2)}) collective-permute-start(f32[8,256]{1,0:T(8,128)S(1)} %coarse.6.refs_4_), channel_id=1, source_target_pairs={{0,1},{1,0},{2,3},{3,2},{4,5},{5,4},{6,7},{7,6},{8,9},{9,8},{10,11... | collective-permute-start | bytes 24584 | tf_op jit(solution)/shard_map/ppermute | solution.py:334
  68.6 3.4 %collective-permute-start.22 = (f32[96,128]{1,0:T(8,128)S(1)}, f32[96,128]{1,0:T(8,128)S(1)}, u32[]{:S(2)}, u32[]{:S(2)}) collective-permute-start(f32[96,128]{1,0:T(8,128)S(1)} %get-tuple-element.125.refs_1_), channel_id=1, source_target_pairs={{0,4},{4,0},{8,12},{12,8},{16,20},{20,16},{24,28},{28,24},{1,5},{5... | collective-permute-start | bytes 147464 | tf_op jit(solution)/shard_map/ppermute | solution.py:325
  78.3 4.8 %collective-permute-start.25 = (f32[104,128]{1,0:T(8,128)S(1)}, f32[104,128]{1,0:T(8,128)S(1)}, u32[]{:S(2)}, u32[]{:S(2)}) collective-permute-start(f32[104,128]{1,0:T(8,128)S(1)} %get-tuple-element.130.refs_1_), channel_id=1, source_target_pairs={{0,4},{4,0},{8,12},{12,8},{16,20},{20,16},{24,28},{28,24},{1,5},{5... | collective-permute-start | bytes 159752 | tf_op jit(solution)/shard_map/ppermute | solution.py:325
  101.8 3.4 %collective-permute-start.34 = (f32[96,128]{1,0:T(8,128)S(1)}, f32[96,128]{1,0:T(8,128)S(1)}, u32[]{:S(2)}, u32[]{:S(2)}) collective-permute-start(f32[96,128]{1,0:T(8,128)S(1)} %get-tuple-element.138.refs_1_), channel_id=1, source_target_pairs={{0,4},{4,0},{8,12},{12,8},{16,20},{20,16},{24,28},{28,24},{1,5},{5... | collective-permute-start | bytes 147464 | tf_op jit(solution)/shard_map/ppermute | solution.py:325
  105.8 3.0 %collective-permute-done.35.refs_5_ = f32[8,128]{1,0:T(8,128)S(1)} collective-permute-done((f32[8,128]{1,0:T(8,128)S(1)}, f32[8,128]{1,0:T(8,128)S(1)}, u32[]{:S(2)}, u32[]{:S(2)}) %collective-permute-start.35) | collective-permute-done | bytes 4128 | tf_op jit(solution)/shard_map/ppermute | solution.py:325
  111.3 3.5 %collective-permute-start.37 = (f32[104,128]{1,0:T(8,128)S(1)}, f32[104,128]{1,0:T(8,128)S(1)}, u32[]{:S(2)}, u32[]{:S(2)}) collective-permute-start(f32[104,128]{1,0:T(8,128)S(1)} %get-tuple-element.151.refs_1_), channel_id=1, source_target_pairs={{0,4},{4,0},{8,12},{12,8},{16,20},{20,16},{24,28},{28,24},{1,5},{5... | collective-permute-start | bytes 159752 | tf_op jit(solution)/shard_map/ppermute | solution.py:325
  120.8 2.5 %collective-permute-start.38 = (f32[8,128]{1,0:T(8,128)S(1)}, f32[8,128]{1,0:T(8,128)S(1)}, u32[]{:S(2)}, u32[]{:S(2)}) collective-permute-start(f32[8,128]{1,0:T(8,128)S(1)} %get-tuple-element.153.refs_1_), channel_id=1, source_target_pairs={{0,8},{4,12},{8,0},{12,4},{16,24},{20,28},{24,16},{28,20},{1,9},{5... | collective-permute-start | bytes 12296 | tf_op jit(solution)/shard_map/ppermute | solution.py:325
  127.4 2.6 %collective-permute-start.42 = (f32[8,256]{1,0:T(8,128)S(1)}, f32[8,256]{1,0:T(8,128)S(1)}, u32[]{:S(2)}, u32[]{:S(2)}) collective-permute-start(f32[8,256]{1,0:T(8,128)S(1)} %coarse.8.refs_4_), channel_id=1, source_target_pairs={{0,1},{1,0},{2,3},{3,2},{4,5},{5,4},{6,7},{7,6},{8,9},{9,8},{10,11... | collective-permute-start | bytes 24584 | tf_op jit(solution)/shard_map/ppermute | solution.py:334
  133.0 3.4 %collective-permute-start.46 = (f32[96,128]{1,0:T(8,128)S(1)}, f32[96,128]{1,0:T(8,128)S(1)}, u32[]{:S(2)}, u32[]{:S(2)}) collective-permute-start(f32[96,128]{1,0:T(8,128)S(1)} %get-tuple-element.159.refs_1_), channel_id=1, source_target_pairs={{0,4},{4,0},{8,12},{12,8},{16,20},{20,16},{24,28},{28,24},{1,5},{5... | collective-permute-start | bytes 147464 | tf_op jit(solution)/shard_map/ppermute | solution.py:325
  137.0 3.0 %collective-permute-done.47.refs_5_ = f32[8,128]{1,0:T(8,128)S(1)} collective-permute-done((f32[8,128]{1,0:T(8,128)S(1)}, f32[8,128]{1,0:T(8,128)S(1)}, u32[]{:S(2)}, u32[]{:S(2)}) %collective-permute-start.47) | collective-permute-done | bytes 4128 | tf_op jit(solution)/shard_map/ppermute | solution.py:325
  142.5 3.5 %collective-permute-start.49 = (f32[104,128]{1,0:T(8,128)S(1)}, f32[104,128]{1,0:T(8,128)S(1)}, u32[]{:S(2)}, u32[]{:S(2)}) collective-permute-start(f32[104,128]{1,0:T(8,128)S(1)} %get-tuple-element.172.refs_1_), channel_id=1, source_target_pairs={{0,4},{4,0},{8,12},{12,8},{16,20},{20,16},{24,28},{28,24},{1,5},{5... | collective-permute-start | bytes 159752 | tf_op jit(solution)/shard_map/ppermute | solution.py:325
  152.0 2.5 %collective-permute-start.50 = (f32[8,128]{1,0:T(8,128)S(1)}, f32[8,128]{1,0:T(8,128)S(1)}, u32[]{:S(2)}, u32[]{:S(2)}) collective-permute-start(f32[8,128]{1,0:T(8,128)S(1)} %get-tuple-element.174.refs_1_), channel_id=1, source_target_pairs={{0,8},{4,12},{8,0},{12,4},{16,24},{20,28},{24,16},{28,20},{1,9},{5... | collective-permute-start | bytes 12296 | tf_op jit(solution)/shard_map/ppermute | solution.py:325
  164.9 3.4 %collective-permute-start.58 = (f32[96,128]{1,0:T(8,128)S(1)}, f32[96,128]{1,0:T(8,128)S(1)}, u32[]{:S(2)}, u32[]{:S(2)}) collective-permute-start(f32[96,128]{1,0:T(8,128)S(1)} %get-tuple-element.180.refs_1_), channel_id=1, source_target_pairs={{0,4},{4,0},{8,12},{12,8},{16,20},{20,16},{24,28},{28,24},{1,5},{5... | collective-permute-start | bytes 147464 | tf_op jit(solution)/shard_map/ppermute | solution.py:325
  168.9 3.0 %collective-permute-done.59.refs_5_ = f32[8,128]{1,0:T(8,128)S(1)} collective-permute-done((f32[8,128]{1,0:T(8,128)S(1)}, f32[8,128]{1,0:T(8,128)S(1)}, u32[]{:S(2)}, u32[]{:S(2)}) %collective-permute-start.59) | collective-permute-done | bytes 4128 | tf_op jit(solution)/shard_map/ppermute | solution.py:325
  172.8 10.8 %all_to_all.5.dots_ref = f32[32,1,128]{2,1,0:T(1,128)S(1)} all-to-all(f32[32,1,128]{2,1,0:T(1,128)S(1)} %get-tuple-element.192), channel_id=1, replica_groups=mesh['sub'=8,'grp'=4] {'sub','grp'}, dimensions={0} | all-to-all | bytes 32768 | tf_op jit(solution)/shard_map/all_to_all | solution.py:485
  (149 shorter events, 95.9 us)
Async XLA Ops:
  10.1 6.3 %collective-permute-start.1 = (f32[104,128]{1,0:T(8,128)S(1)}, f32[104,128]{1,0:T(8,128)S(1)}, u32[]{:S(2)}, u32[]{:S(2)}) collective-permute-start(f32[104,128]{1,0:T(8,128)S(1)} %get-tuple-element.104.refs_0_), channel_id=1, source_target_pairs={{4,8},{8,4},{12,16},{16,12},{20,24},{24,20},{5,9},{9,5},{13,17},{1... | collective-permute-start | bytes 159752 | tf_op jit(solution)/shard_map/ppermute | solution.py:330
  10.9 6.4 %collective-permute-start.2 = (f32[104,128]{1,0:T(8,128)S(1)}, f32[104,128]{1,0:T(8,128)S(1)}, u32[]{:S(2)}, u32[]{:S(2)}) collective-permute-start(f32[104,128]{1,0:T(8,128)S(1)} %get-tuple-element.105.refs_1_), channel_id=1, source_target_pairs={{0,4},{4,0},{8,12},{12,8},{16,20},{20,16},{24,28},{28,24},{1,5},{5... | collective-permute-start | bytes 159752 | tf_op jit(solution)/shard_map/ppermute | solution.py:325
  19.0 8.5 %collective-permute-start.4 = (f32[8,256]{1,0:T(8,128)S(1)}, f32[8,256]{1,0:T(8,128)S(1)}, u32[]{:S(2)}, u32[]{:S(2)}) collective-permute-start(f32[8,256]{1,0:T(8,128)S(1)} %get-tuple-element.109), channel_id=1, source_target_pairs={{0,3},{1,2},{2,1},{3,0},{4,7},{5,6},{6,5},{7,4},{8,11},{9,10},{10,... | collective-permute-start | bytes 24584 | tf_op jit(solution)/shard_map/ppermute | solution.py:334
  44.8 5.6 %collective-permute-start.13 = (f32[104,128]{1,0:T(8,128)S(1)}, f32[104,128]{1,0:T(8,128)S(1)}, u32[]{:S(2)}, u32[]{:S(2)}) collective-permute-start(f32[104,128]{1,0:T(8,128)S(1)} %get-tuple-element.117.refs_1_), channel_id=1, source_target_pairs={{0,4},{4,0},{8,12},{12,8},{16,20},{20,16},{24,28},{28,24},{1,5},{5... | collective-permute-start | bytes 159752 | tf_op jit(solution)/shard_map/ppermute | solution.py:325
  51.1 9.4 %collective-permute-start.15 = (f32[8,256]{1,0:T(8,128)S(1)}, f32[8,256]{1,0:T(8,128)S(1)}, u32[]{:S(2)}, u32[]{:S(2)}) collective-permute-start(f32[8,256]{1,0:T(8,128)S(1)} %get-tuple-element.120), channel_id=1, source_target_pairs={{0,3},{1,2},{2,1},{3,0},{4,7},{5,6},{6,5},{7,4},{8,11},{9,10},{10,... | collective-permute-start | bytes 24584 | tf_op jit(solution)/shard_map/ppermute | solution.py:334
  52.6 7.9 %collective-permute-start.16 = (f32[8,256]{1,0:T(8,128)S(1)}, f32[8,256]{1,0:T(8,128)S(1)}, u32[]{:S(2)}, u32[]{:S(2)}) collective-permute-start(f32[8,256]{1,0:T(8,128)S(1)} %get-tuple-element.121), channel_id=1, source_target_pairs={{0,2},{1,3},{2,0},{3,1},{4,6},{5,7},{6,4},{7,5},{8,10},{9,11},{10,... | collective-permute-start | bytes 24584 | tf_op jit(solution)/shard_map/ppermute | solution.py:334
  53.3 7.2 %collective-permute-start.17 = (f32[8,256]{1,0:T(8,128)S(1)}, f32[8,256]{1,0:T(8,128)S(1)}, u32[]{:S(2)}, u32[]{:S(2)}) collective-permute-start(f32[8,256]{1,0:T(8,128)S(1)} %get-tuple-element.122), channel_id=1, source_target_pairs={{0,1},{1,0},{2,3},{3,2},{4,5},{5,4},{6,7},{7,6},{8,9},{9,8},{10,11... | collective-permute-start | bytes 24584 | tf_op jit(solution)/shard_map/ppermute | solution.py:334
  67.9 7.7 %collective-permute-start.21 = (f32[96,128]{1,0:T(8,128)S(1)}, f32[96,128]{1,0:T(8,128)S(1)}, u32[]{:S(2)}, u32[]{:S(2)}) collective-permute-start(f32[96,128]{1,0:T(8,128)S(1)} %get-tuple-element.124.refs_0_), channel_id=1, source_target_pairs={{4,8},{8,4},{12,16},{16,12},{20,24},{24,20},{5,9},{9,5},{13,17},{1... | collective-permute-start | bytes 147464 | tf_op jit(solution)/shard_map/ppermute | solution.py:330
  68.6 7.1 %collective-permute-start.22 = (f32[96,128]{1,0:T(8,128)S(1)}, f32[96,128]{1,0:T(8,128)S(1)}, u32[]{:S(2)}, u32[]{:S(2)}) collective-permute-start(f32[96,128]{1,0:T(8,128)S(1)} %get-tuple-element.125.refs_1_), channel_id=1, source_target_pairs={{0,4},{4,0},{8,12},{12,8},{16,20},{20,16},{24,28},{28,24},{1,5},{5... | collective-permute-start | bytes 147464 | tf_op jit(solution)/shard_map/ppermute | solution.py:325
  77.4 5.7 %collective-permute-start.24 = (f32[104,128]{1,0:T(8,128)S(1)}, f32[104,128]{1,0:T(8,128)S(1)}, u32[]{:S(2)}, u32[]{:S(2)}) collective-permute-start(f32[104,128]{1,0:T(8,128)S(1)} %get-tuple-element.129.refs_0_), channel_id=1, source_target_pairs={{4,8},{8,4},{12,16},{16,12},{20,24},{24,20},{5,9},{9,5},{13,17},{1... | collective-permute-start | bytes 159752 | tf_op jit(solution)/shard_map/ppermute | solution.py:330
  78.3 5.7 %collective-permute-start.25 = (f32[104,128]{1,0:T(8,128)S(1)}, f32[104,128]{1,0:T(8,128)S(1)}, u32[]{:S(2)}, u32[]{:S(2)}) collective-permute-start(f32[104,128]{1,0:T(8,128)S(1)} %get-tuple-element.130.refs_1_), channel_id=1, source_target_pairs={{0,4},{4,0},{8,12},{12,8},{16,20},{20,16},{24,28},{28,24},{1,5},{5... | collective-permute-start | bytes 159752 | tf_op jit(solution)/shard_map/ppermute | solution.py:325
  84.6 8.3 %collective-permute-start.27 = (f32[8,256]{1,0:T(8,128)S(1)}, f32[8,256]{1,0:T(8,128)S(1)}, u32[]{:S(2)}, u32[]{:S(2)}) collective-permute-start(f32[8,256]{1,0:T(8,128)S(1)} %get-tuple-element.133), channel_id=1, source_target_pairs={{0,3},{1,2},{2,1},{3,0},{4,7},{5,6},{6,5},{7,4},{8,11},{9,10},{10,... | collective-permute-start | bytes 24584 | tf_op jit(solution)/shard_map/ppermute | solution.py:334
  87.0 6.0 %collective-permute-start.28 = (f32[8,256]{1,0:T(8,128)S(1)}, f32[8,256]{1,0:T(8,128)S(1)}, u32[]{:S(2)}, u32[]{:S(2)}) collective-permute-start(f32[8,256]{1,0:T(8,128)S(1)} %get-tuple-element.134), channel_id=1, source_target_pairs={{0,2},{1,3},{2,0},{3,1},{4,6},{5,7},{6,4},{7,5},{8,10},{9,11},{10,... | collective-permute-start | bytes 24584 | tf_op jit(solution)/shard_map/ppermute | solution.py:334
  101.1 7.7 %collective-permute-start.33 = (f32[96,128]{1,0:T(8,128)S(1)}, f32[96,128]{1,0:T(8,128)S(1)}, u32[]{:S(2)}, u32[]{:S(2)}) collective-permute-start(f32[96,128]{1,0:T(8,128)S(1)} %get-tuple-element.137.refs_0_), channel_id=1, source_target_pairs={{4,8},{8,4},{12,16},{16,12},{20,24},{24,20},{5,9},{9,5},{13,17},{1... | collective-permute-start | bytes 147464 | tf_op jit(solution)/shard_map/ppermute | solution.py:330
  101.8 7.1 %collective-permute-start.34 = (f32[96,128]{1,0:T(8,128)S(1)}, f32[96,128]{1,0:T(8,128)S(1)}, u32[]{:S(2)}, u32[]{:S(2)}) collective-permute-start(f32[96,128]{1,0:T(8,128)S(1)} %get-tuple-element.138.refs_1_), channel_id=1, source_target_pairs={{0,4},{4,0},{8,12},{12,8},{16,20},{20,16},{24,28},{28,24},{1,5},{5... | collective-permute-start | bytes 147464 | tf_op jit(solution)/shard_map/ppermute | solution.py:325
  116.3 8.5 %collective-permute-start.39 = (f32[8,256]{1,0:T(8,128)S(1)}, f32[8,256]{1,0:T(8,128)S(1)}, u32[]{:S(2)}, u32[]{:S(2)}) collective-permute-start(f32[8,256]{1,0:T(8,128)S(1)} %get-tuple-element.154), channel_id=1, source_target_pairs={{0,3},{1,2},{2,1},{3,0},{4,7},{5,6},{6,5},{7,4},{8,11},{9,10},{10,... | collective-permute-start | bytes 24584 | tf_op jit(solution)/shard_map/ppermute | solution.py:334
  118.0 6.9 %collective-permute-start.40 = (f32[8,256]{1,0:T(8,128)S(1)}, f32[8,256]{1,0:T(8,128)S(1)}, u32[]{:S(2)}, u32[]{:S(2)}) collective-permute-start(f32[8,256]{1,0:T(8,128)S(1)} %get-tuple-element.155), channel_id=1, source_target_pairs={{0,2},{1,3},{2,0},{3,1},{4,6},{5,7},{6,4},{7,5},{8,10},{9,11},{10,... | collective-permute-start | bytes 24584 | tf_op jit(solution)/shard_map/ppermute | solution.py:334
  119.1 5.8 %collective-permute-start.41 = (f32[8,256]{1,0:T(8,128)S(1)}, f32[8,256]{1,0:T(8,128)S(1)}, u32[]{:S(2)}, u32[]{:S(2)}) collective-permute-start(f32[8,256]{1,0:T(8,128)S(1)} %get-tuple-element.156), channel_id=1, source_target_pairs={{0,1},{1,0},{2,3},{3,2},{4,5},{5,4},{6,7},{7,6},{8,9},{9,8},{10,11... | collective-permute-start | bytes 24584 | tf_op jit(solution)/shard_map/ppermute | solution.py:334
  132.3 7.7 %collective-permute-start.45 = (f32[96,128]{1,0:T(8,128)S(1)}, f32[96,128]{1,0:T(8,128)S(1)}, u32[]{:S(2)}, u32[]{:S(2)}) collective-permute-start(f32[96,128]{1,0:T(8,128)S(1)} %get-tuple-element.158.refs_0_), channel_id=1, source_target_pairs={{4,8},{8,4},{12,16},{16,12},{20,24},{24,20},{5,9},{9,5},{13,17},{1... | collective-permute-start | bytes 147464 | tf_op jit(solution)/shard_map/ppermute | solution.py:330
  133.0 7.1 %collective-permute-start.46 = (f32[96,128]{1,0:T(8,128)S(1)}, f32[96,128]{1,0:T(8,128)S(1)}, u32[]{:S(2)}, u32[]{:S(2)}) collective-permute-start(f32[96,128]{1,0:T(8,128)S(1)} %get-tuple-element.159.refs_1_), channel_id=1, source_target_pairs={{0,4},{4,0},{8,12},{12,8},{16,20},{20,16},{24,28},{28,24},{1,5},{5... | collective-permute-start | bytes 147464 | tf_op jit(solution)/shard_map/ppermute | solution.py:325
  147.5 8.5 %collective-permute-start.51 = (f32[8,256]{1,0:T(8,128)S(1)}, f32[8,256]{1,0:T(8,128)S(1)}, u32[]{:S(2)}, u32[]{:S(2)}) collective-permute-start(f32[8,256]{1,0:T(8,128)S(1)} %get-tuple-element.175), channel_id=1, source_target_pairs={{0,3},{1,2},{2,1},{3,0},{4,7},{5,6},{6,5},{7,4},{8,11},{9,10},{10,... | collective-permute-start | bytes 24584 | tf_op jit(solution)/shard_map/ppermute | solution.py:334
  149.9 6.2 %collective-permute-start.52 = (f32[8,256]{1,0:T(8,128)S(1)}, f32[8,256]{1,0:T(8,128)S(1)}, u32[]{:S(2)}, u32[]{:S(2)}) collective-permute-start(f32[8,256]{1,0:T(8,128)S(1)} %get-tuple-element.176), channel_id=1, source_target_pairs={{0,2},{1,3},{2,0},{3,1},{4,6},{5,7},{6,4},{7,5},{8,10},{9,11},{10,... | collective-permute-start | bytes 24584 | tf_op jit(solution)/shard_map/ppermute | solution.py:334
  164.2 7.7 %collective-permute-start.57 = (f32[96,128]{1,0:T(8,128)S(1)}, f32[96,128]{1,0:T(8,128)S(1)}, u32[]{:S(2)}, u32[]{:S(2)}) collective-permute-start(f32[96,128]{1,0:T(8,128)S(1)} %get-tuple-element.179.refs_0_), channel_id=1, source_target_pairs={{4,8},{8,4},{12,16},{16,12},{20,24},{24,20},{5,9},{9,5},{13,17},{1... | collective-permute-start | bytes 147464 | tf_op jit(solution)/shard_map/ppermute | solution.py:330
  164.9 7.1 %collective-permute-start.58 = (f32[96,128]{1,0:T(8,128)S(1)}, f32[96,128]{1,0:T(8,128)S(1)}, u32[]{:S(2)}, u32[]{:S(2)}) collective-permute-start(f32[96,128]{1,0:T(8,128)S(1)} %get-tuple-element.180.refs_1_), channel_id=1, source_target_pairs={{0,4},{4,0},{8,12},{12,8},{16,20},{20,16},{24,28},{28,24},{1,5},{5... | collective-permute-start | bytes 147464 | tf_op jit(solution)/shard_map/ppermute | solution.py:325
  (47 other events, 277.9 us)

commit v6 on v5

--- a/solution.py
+++ b/solution.py
@@ -87,7 +87,8 @@
     lax.fori_loop(0, out_ref.shape[0] // ROWS, step, 0, unroll=True)
 
 
-def table_kernel(neighbour_ref, column_ref, corner_ref, selector_ref, swap_ref, table_ref):
+def table_kernel(neighbour_ref, column_ref, corner_ref, *refs):
+    selector_ref, swap_ref, table_ref = refs[-3:]
     cells = swap_ref.shape[0]
     start = lax.axis_index("sub") * cells
     def one_hot(row, count):
@@ -220,12 +221,15 @@
     ranks, far_ref, near_ref, from_far_ref, from_near_ref, selector_ref, operators_ref, table_ref,
     m_out, gap_out, *rest,
 ):
-    outs, (dots_out, sums_ref) = rest[:ranks], rest[ranks:]
+    dots_sent, outs, (dots_out, sums_ref) = rest[0], rest[1 : ranks + 1], rest[ranks + 1 :]
     iface, cells = m_out.shape
     odd = lax.axis_index("sub") % 2 == 1
     own, previous = arrived(odd, far_ref, near_ref, from_far_ref, from_near_ref, iface)
     m_out[...] = own
-    dots_out[...] = near_ref[iface:] + from_near_ref[iface:]
+    dots_sent[...] = jnp.zeros_like(dots_sent)
+    dots = near_ref[iface:] + from_near_ref[iface:]
+    dots_out[...] = dots
+    dots_sent[:, :cells] = dots
     gap = spread_of(own, previous, selector_ref[...])
     gap_out[...] = gap
     parts = []
@@ -266,7 +270,7 @@
         rows = [result[:, j * width : (j + 1) * width] for j in range(CORNER_DOF)]
         columns.append(jnp.concatenate(rows, axis=0))
     solved = jnp.concatenate(columns, axis=1)
-    dots = dots_ref[...] + other_ref[...]
+    dots = dots_ref[...] + other_ref[:, :cells]
     rows = [solved]
     for first in (0, 2):
         lanes = [dots[first : first + 1], dots[first + 1 : first + 2]]
@@ -382,9 +386,9 @@
             shape(cells, cells, dtype=BF16),
             shape(group, CORNERS_SUB * cells, dtype=BF16),
         ),
-        count=3,
+        count=6,
         name="tables",
-    )(neighbour, stiff_column, corners)
+    )(neighbour, stiff_column, corners, stiff, operators, right_side)
 
     field = shape(iface, cells)
     pair = shape(2, iface, cells)
@@ -396,9 +400,9 @@
 
     def apply_operator(near, far):
         from_far, from_near = swapped_far(far), swapped(near, 1)
-        m, gap, *parts, dots = call(
+        m, gap, sent, *parts, dots = call(
             lambda *refs: corner_kernel(ranks, *refs),
-            (field, field) + (piece,) * ranks + (rows,),
+            (field, field) + (piece,) * (ranks + 1) + (rows,),
             count=7,
             scratch=[pltpu.VMEM((ROWS, group), F32)],
             flops=2 * 24 * iface * cells,
@@ -414,7 +418,7 @@
             moved=2 * iface * iface * cells,
             name="local",
         )(gap, inverse)
-        other = swapped(dots, 2)
+        other = swapped(sent, 2)
         solved = call(
             lambda *refs: coarse_kernel(ranks, *refs),
             piece,

time: 185 us -> 182 us (0.984)
  starting transfers between devices: 110 us -> 105 us
  local copies, waits for them, and re-layouts: 6.2 us -> 8.3 us
    ppermute x19, waiting for transfers between devices: 24 us -> 11.7 us  [swapped(): lax.ppermute(block, 'sub', [(i, i ^ bit) for i in range(lax.axis_size('su...]
    ppermute x30, waiting for transfers between devices: 9.19 us -> 20 us  [exchanged(): lax.ppermute(block, 'grp', [(i, i ^ distance) for i in range(lax.axis_siz...]
    ppermute x19, starting transfers between devices: 56 us -> 51.9 us  [swapped(): lax.ppermute(block, 'sub', [(i, i ^ bit) for i in range(lax.axis_size('su...]
    unnamed x22, local copies, waits for them, and re-layouts: 6.2 us -> 8.3 us
  transfers between devices with their start and end apart: 60 -> 60, of which waited for: 26 -> 39; matrix products, arithmetic and copies ran while one was open for 0% -> 0% of each run, Pallas kernels for 2% -> 2%
where the time goes in v6:
time: 182 us; the launch traced here: 181 us
  starting transfers between devices  105 us (58%)
  waiting for transfers between devices  31.7 us (17%)
  Pallas kernels  24 us (13%)
  blocking collectives  11.3 us (6%)
  local copies, waits for them, and re-layouts  8.3 us (5%)
    ppermute x19, starting transfers between devices, swapped(): lax.ppermute(block, 'sub', [(i, i ^ bit) for i in range(lax.axis_size('su...  51.9 us
    ppermute x30, starting transfers between devices, exchanged(): lax.ppermute(block, 'grp', [(i, i ^ distance) for i in range(lax.axis_siz...  44 us
    ppermute x30, waiting for transfers between devices, exchanged(): lax.ppermute(block, 'grp', [(i, i ^ distance) for i in range(lax.axis_siz...  20 us
    ppermute x19, waiting for transfers between devices, swapped(): lax.ppermute(block, 'sub', [(i, i ^ bit) for i in range(lax.axis_size('su...  11.7 us
    all_to_all x1, blocking collectives, on_device(): everyone = lax.all_to_all(result[9], ('sub', 'grp'), 0, 0, tiled=True)  11.3 us
    unnamed x22, local copies, waits for them, and re-layouts  8.3 us
    ppermute x10, starting transfers between devices, swapped_far(): lax.ppermute(block, 'sub', [(i, i + 1 if i % 2 else i - 1) for i in inner])  6.94 us
    pallas_call x4, Pallas kernels, on_device(): call(lambda *refs, first=first, last=last: middle_kernel(first, last, *re...  6.29 us
  transfers between devices with their start and end apart: 60, of which 39 were waited for; matrix products, arithmetic and copies ran while one was open for 0% of the time, Pallas kernels for 2%

profile of v6, /device:TPU:0, one launch (start us, length us, event | category | flops | bytes accessed | tf_op | source)
XLA Modules:
  0.0 181.5 jit_solution(5616818246857330300)
XLA Ops:
  0.6 2.4 %collective-permute-start = (f32[96,128]{1,0:T(8,128)}, f32[96,128]{1,0:T(8,128)S(1)}, u32[]{:S(2)}, u32[]{:S(2)}) collective-permute-start(f32[96,128]{1,0:T(8,128)} %bitcast.34), channel_id=1, source_target_pairs={{0,4},{4,8},{8,12},{12,16},{16,20},{20,24},{24,28},{1,5},{5,9},{9,... | collective-permute-start | bytes 147464 | tf_op jit(solution)/shard_map/ppermute | solution.py:325
  3.0 2.3 %copy-done = bf16[2,96,96,1,128]{4,2,3,1,0:T(8,128)(2,1)S(1)} copy-done((bf16[2,96,96,1,128]{4,2,3,1,0:T(8,128)(2,1)S(1)}, bf16[2,96,96,1,128]{4,2,3,1,0:T(8,128)(2,1)}, u32[]{:S(2)}) %copy-start) | copy-done | bytes 4718616
  14.1 3.9 %collective-permute-start.2 = (f32[104,128]{1,0:T(8,128)S(1)}, f32[104,128]{1,0:T(8,128)S(1)}, u32[]{:S(2)}, u32[]{:S(2)}) collective-permute-start(f32[104,128]{1,0:T(8,128)S(1)} %get-tuple-element.110.refs_1_), channel_id=1, source_target_pairs={{0,4},{4,0},{8,12},{12,8},{16,20},{20,16},{24,28},{28,24},{1,5},{5... | collective-permute-start | bytes 159752 | tf_op jit(solution)/shard_map/ppermute | solution.py:329
  19.5 2.5 %collective-permute-start.3 = (f32[8,256]{1,0:T(8,128)S(1)}, f32[8,256]{1,0:T(8,128)S(1)}, u32[]{:S(2)}, u32[]{:S(2)}) collective-permute-start(f32[8,256]{1,0:T(8,128)S(1)} %get-tuple-element.114), channel_id=1, source_target_pairs={{0,8},{4,12},{8,0},{12,4},{16,24},{20,28},{24,16},{28,20},{1,9},{5... | collective-permute-start | bytes 24584 | tf_op jit(solution)/shard_map/ppermute | solution.py:329
  22.1 3.6 %collective-permute-start.4 = (f32[8,256]{1,0:T(8,128)S(1)}, f32[8,256]{1,0:T(8,128)S(1)}, u32[]{:S(2)}, u32[]{:S(2)}) collective-permute-start(f32[8,256]{1,0:T(8,128)S(1)} %get-tuple-element.115), channel_id=1, source_target_pairs={{0,3},{1,2},{2,1},{3,0},{4,7},{5,6},{6,5},{7,4},{8,11},{9,10},{10,... | collective-permute-start | bytes 24584 | tf_op jit(solution)/shard_map/ppermute | solution.py:338
  27.5 2.7 %collective-permute-done.5.refs_4_ = f32[8,256]{1,0:T(8,128)S(1)} collective-permute-done((f32[8,256]{1,0:T(8,128)S(1)}, f32[8,256]{1,0:T(8,128)S(1)}, u32[]{:S(2)}, u32[]{:S(2)}) %collective-permute-start.5) | collective-permute-done | bytes 8224 | tf_op jit(solution)/shard_map/ppermute | solution.py:338
  33.1 2.3 %collective-permute-start.7 = (f32[8,256]{1,0:T(8,128)S(1)}, f32[8,256]{1,0:T(8,128)S(1)}, u32[]{:S(2)}, u32[]{:S(2)}) collective-permute-start(f32[8,256]{1,0:T(8,128)S(1)} %coarse.5.refs_4_), channel_id=1, source_target_pairs={{0,1},{1,0},{2,3},{3,2},{4,5},{5,4},{6,7},{7,6},{8,9},{9,8},{10,11... | collective-permute-start | bytes 24584 | tf_op jit(solution)/shard_map/ppermute | solution.py:338
  43.5 4.3 %collective-permute-start.13 = (f32[104,128]{1,0:T(8,128)S(1)}, f32[104,128]{1,0:T(8,128)S(1)}, u32[]{:S(2)}, u32[]{:S(2)}) collective-permute-start(f32[104,128]{1,0:T(8,128)S(1)} %get-tuple-element.123.refs_1_), channel_id=1, source_target_pairs={{0,4},{4,0},{8,12},{12,8},{16,20},{20,16},{24,28},{28,24},{1,5},{5... | collective-permute-start | bytes 159752 | tf_op jit(solution)/shard_map/ppermute | solution.py:329
  49.4 3.4 %collective-permute-start.14 = (f32[8,256]{1,0:T(8,128)S(1)}, f32[8,256]{1,0:T(8,128)S(1)}, u32[]{:S(2)}, u32[]{:S(2)}) collective-permute-start(f32[8,256]{1,0:T(8,128)S(1)} %get-tuple-element.126), channel_id=1, source_target_pairs={{0,8},{4,12},{8,0},{12,4},{16,24},{20,28},{24,16},{28,20},{1,9},{5... | collective-permute-start | bytes 24584 | tf_op jit(solution)/shard_map/ppermute | solution.py:329
  52.8 2.5 %collective-permute-start.15 = (f32[8,256]{1,0:T(8,128)S(1)}, f32[8,256]{1,0:T(8,128)S(1)}, u32[]{:S(2)}, u32[]{:S(2)}) collective-permute-start(f32[8,256]{1,0:T(8,128)S(1)} %get-tuple-element.127), channel_id=1, source_target_pairs={{0,3},{1,2},{2,1},{3,0},{4,7},{5,6},{6,5},{7,4},{8,11},{9,10},{10,... | collective-permute-start | bytes 24584 | tf_op jit(solution)/shard_map/ppermute | solution.py:338
  69.7 3.7 %collective-permute-start.23 = (f32[8,128]{1,0:T(8,128)S(1)}, f32[8,128]{1,0:T(8,128)S(1)}, u32[]{:S(2)}, u32[]{:S(2)}) collective-permute-start(f32[8,128]{1,0:T(8,128)S(1)} %get-tuple-element.133.refs_4_), channel_id=1, source_target_pairs={{0,16},{4,20},{8,24},{12,28},{16,0},{20,4},{24,8},{28,12},{1,17},{... | collective-permute-start | bytes 12296 | tf_op jit(solution)/shard_map/ppermute | solution.py:329
  77.7 3.0 %collective-permute-start.25 = (f32[104,128]{1,0:T(8,128)S(1)}, f32[104,128]{1,0:T(8,128)S(1)}, u32[]{:S(2)}, u32[]{:S(2)}) collective-permute-start(f32[104,128]{1,0:T(8,128)S(1)} %get-tuple-element.137.refs_1_), channel_id=1, source_target_pairs={{0,4},{4,0},{8,12},{12,8},{16,20},{20,16},{24,28},{28,24},{1,5},{5... | collective-permute-start | bytes 159752 | tf_op jit(solution)/shard_map/ppermute | solution.py:329
  82.2 2.4 %collective-permute-start.26 = (f32[8,256]{1,0:T(8,128)S(1)}, f32[8,256]{1,0:T(8,128)S(1)}, u32[]{:S(2)}, u32[]{:S(2)}) collective-permute-start(f32[8,256]{1,0:T(8,128)S(1)} %get-tuple-element.140), channel_id=1, source_target_pairs={{0,8},{4,12},{8,0},{12,4},{16,24},{20,28},{24,16},{28,20},{1,9},{5... | collective-permute-start | bytes 24584 | tf_op jit(solution)/shard_map/ppermute | solution.py:329
  84.6 2.5 %collective-permute-start.27 = (f32[8,256]{1,0:T(8,128)S(1)}, f32[8,256]{1,0:T(8,128)S(1)}, u32[]{:S(2)}, u32[]{:S(2)}) collective-permute-start(f32[8,256]{1,0:T(8,128)S(1)} %get-tuple-element.141), channel_id=1, source_target_pairs={{0,3},{1,2},{2,1},{3,0},{4,7},{5,6},{6,5},{7,4},{8,11},{9,10},{10,... | collective-permute-start | bytes 24584 | tf_op jit(solution)/shard_map/ppermute | solution.py:338
  101.2 3.3 %collective-permute-start.35 = (f32[8,128]{1,0:T(8,128)S(1)}, f32[8,128]{1,0:T(8,128)S(1)}, u32[]{:S(2)}, u32[]{:S(2)}) collective-permute-start(f32[8,128]{1,0:T(8,128)S(1)} %get-tuple-element.147.refs_4_), channel_id=1, source_target_pairs={{0,16},{4,20},{8,24},{12,28},{16,0},{20,4},{24,8},{28,12},{1,17},{... | collective-permute-start | bytes 12296 | tf_op jit(solution)/shard_map/ppermute | solution.py:329
  108.6 3.0 %collective-permute-start.37 = (f32[104,128]{1,0:T(8,128)S(1)}, f32[104,128]{1,0:T(8,128)S(1)}, u32[]{:S(2)}, u32[]{:S(2)}) collective-permute-start(f32[104,128]{1,0:T(8,128)S(1)} %get-tuple-element.159.refs_1_), channel_id=1, source_target_pairs={{0,4},{4,0},{8,12},{12,8},{16,20},{20,16},{24,28},{28,24},{1,5},{5... | collective-permute-start | bytes 159752 | tf_op jit(solution)/shard_map/ppermute | solution.py:329
  113.1 2.5 %collective-permute-start.38 = (f32[8,256]{1,0:T(8,128)S(1)}, f32[8,256]{1,0:T(8,128)S(1)}, u32[]{:S(2)}, u32[]{:S(2)}) collective-permute-start(f32[8,256]{1,0:T(8,128)S(1)} %get-tuple-element.162), channel_id=1, source_target_pairs={{0,8},{4,12},{8,0},{12,4},{16,24},{20,28},{24,16},{28,20},{1,9},{5... | collective-permute-start | bytes 24584 | tf_op jit(solution)/shard_map/ppermute | solution.py:329
  115.7 2.5 %collective-permute-start.39 = (f32[8,256]{1,0:T(8,128)S(1)}, f32[8,256]{1,0:T(8,128)S(1)}, u32[]{:S(2)}, u32[]{:S(2)}) collective-permute-start(f32[8,256]{1,0:T(8,128)S(1)} %get-tuple-element.163), channel_id=1, source_target_pairs={{0,3},{1,2},{2,1},{3,0},{4,7},{5,6},{6,5},{7,4},{8,11},{9,10},{10,... | collective-permute-start | bytes 24584 | tf_op jit(solution)/shard_map/ppermute | solution.py:338
  132.3 3.3 %collective-permute-start.47 = (f32[8,128]{1,0:T(8,128)S(1)}, f32[8,128]{1,0:T(8,128)S(1)}, u32[]{:S(2)}, u32[]{:S(2)}) collective-permute-start(f32[8,128]{1,0:T(8,128)S(1)} %get-tuple-element.169.refs_4_), channel_id=1, source_target_pairs={{0,16},{4,20},{8,24},{12,28},{16,0},{20,4},{24,8},{28,12},{1,17},{... | collective-permute-start | bytes 12296 | tf_op jit(solution)/shard_map/ppermute | solution.py:329
  139.7 3.0 %collective-permute-start.49 = (f32[104,128]{1,0:T(8,128)S(1)}, f32[104,128]{1,0:T(8,128)S(1)}, u32[]{:S(2)}, u32[]{:S(2)}) collective-permute-start(f32[104,128]{1,0:T(8,128)S(1)} %get-tuple-element.181.refs_1_), channel_id=1, source_target_pairs={{0,4},{4,0},{8,12},{12,8},{16,20},{20,16},{24,28},{28,24},{1,5},{5... | collective-permute-start | bytes 159752 | tf_op jit(solution)/shard_map/ppermute | solution.py:329
  144.2 2.5 %collective-permute-start.50 = (f32[8,256]{1,0:T(8,128)S(1)}, f32[8,256]{1,0:T(8,128)S(1)}, u32[]{:S(2)}, u32[]{:S(2)}) collective-permute-start(f32[8,256]{1,0:T(8,128)S(1)} %get-tuple-element.184), channel_id=1, source_target_pairs={{0,8},{4,12},{8,0},{12,4},{16,24},{20,28},{24,16},{28,20},{1,9},{5... | collective-permute-start | bytes 24584 | tf_op jit(solution)/shard_map/ppermute | solution.py:329
  146.8 2.5 %collective-permute-start.51 = (f32[8,256]{1,0:T(8,128)S(1)}, f32[8,256]{1,0:T(8,128)S(1)}, u32[]{:S(2)}, u32[]{:S(2)}) collective-permute-start(f32[8,256]{1,0:T(8,128)S(1)} %get-tuple-element.185), channel_id=1, source_target_pairs={{0,3},{1,2},{2,1},{3,0},{4,7},{5,6},{6,5},{7,4},{8,11},{9,10},{10,... | collective-permute-start | bytes 24584 | tf_op jit(solution)/shard_map/ppermute | solution.py:338
  163.4 3.3 %collective-permute-start.59 = (f32[8,128]{1,0:T(8,128)S(1)}, f32[8,128]{1,0:T(8,128)S(1)}, u32[]{:S(2)}, u32[]{:S(2)}) collective-permute-start(f32[8,128]{1,0:T(8,128)S(1)} %get-tuple-element.191.refs_4_), channel_id=1, source_target_pairs={{0,16},{4,20},{8,24},{12,28},{16,0},{20,4},{24,8},{28,12},{1,17},{... | collective-permute-start | bytes 12296 | tf_op jit(solution)/shard_map/ppermute | solution.py:329
  169.2 11.3 %all_to_all.5.dots_ref = f32[32,1,128]{2,1,0:T(1,128)S(1)} all-to-all(f32[32,1,128]{2,1,0:T(1,128)S(1)} %get-tuple-element.202), channel_id=1, replica_groups=mesh['sub'=8,'grp'=4] {'sub','grp'}, dimensions={0} | all-to-all | bytes 32768 | tf_op jit(solution)/shard_map/all_to_all | solution.py:489
  (148 shorter events, 101.7 us)
Async XLA Ops:
  0.6 8.8 %collective-permute-start = (f32[96,128]{1,0:T(8,128)}, f32[96,128]{1,0:T(8,128)S(1)}, u32[]{:S(2)}, u32[]{:S(2)}) collective-permute-start(f32[96,128]{1,0:T(8,128)} %bitcast.34), channel_id=1, source_target_pairs={{0,4},{4,8},{8,12},{12,16},{16,20},{20,24},{24,28},{1,5},{5,9},{9,... | collective-permute-start | bytes 147464 | tf_op jit(solution)/shard_map/ppermute | solution.py:325
  19.5 6.9 %collective-permute-start.3 = (f32[8,256]{1,0:T(8,128)S(1)}, f32[8,256]{1,0:T(8,128)S(1)}, u32[]{:S(2)}, u32[]{:S(2)}) collective-permute-start(f32[8,256]{1,0:T(8,128)S(1)} %get-tuple-element.114), channel_id=1, source_target_pairs={{0,8},{4,12},{8,0},{12,4},{16,24},{20,28},{24,16},{28,20},{1,9},{5... | collective-permute-start | bytes 24584 | tf_op jit(solution)/shard_map/ppermute | solution.py:329
  22.1 5.4 %collective-permute-start.4 = (f32[8,256]{1,0:T(8,128)S(1)}, f32[8,256]{1,0:T(8,128)S(1)}, u32[]{:S(2)}, u32[]{:S(2)}) collective-permute-start(f32[8,256]{1,0:T(8,128)S(1)} %get-tuple-element.115), channel_id=1, source_target_pairs={{0,3},{1,2},{2,1},{3,0},{4,7},{5,6},{6,5},{7,4},{8,11},{9,10},{10,... | collective-permute-start | bytes 24584 | tf_op jit(solution)/shard_map/ppermute | solution.py:338
  31.0 5.5 %collective-permute-start.9 = (f32[8,256]{1,0:T(8,128)S(1)}, f32[8,256]{1,0:T(8,128)S(1)}, u32[]{:S(2)}, u32[]{:S(2)}) collective-permute-start(f32[8,256]{1,0:T(8,128)S(1)} %coarse.5.refs_4_), channel_id=1, source_target_pairs={{0,3},{1,2},{2,1},{3,0},{4,7},{5,6},{6,5},{7,4},{8,11},{9,10},{10,... | collective-permute-start | bytes 24584 | tf_op jit(solution)/shard_map/ppermute | solution.py:338
  49.4 7.8 %collective-permute-start.14 = (f32[8,256]{1,0:T(8,128)S(1)}, f32[8,256]{1,0:T(8,128)S(1)}, u32[]{:S(2)}, u32[]{:S(2)}) collective-permute-start(f32[8,256]{1,0:T(8,128)S(1)} %get-tuple-element.126), channel_id=1, source_target_pairs={{0,8},{4,12},{8,0},{12,4},{16,24},{20,28},{24,16},{28,20},{1,9},{5... | collective-permute-start | bytes 24584 | tf_op jit(solution)/shard_map/ppermute | solution.py:329
  52.8 5.4 %collective-permute-start.15 = (f32[8,256]{1,0:T(8,128)S(1)}, f32[8,256]{1,0:T(8,128)S(1)}, u32[]{:S(2)}, u32[]{:S(2)}) collective-permute-start(f32[8,256]{1,0:T(8,128)S(1)} %get-tuple-element.127), channel_id=1, source_target_pairs={{0,3},{1,2},{2,1},{3,0},{4,7},{5,6},{6,5},{7,4},{8,11},{9,10},{10,... | collective-permute-start | bytes 24584 | tf_op jit(solution)/shard_map/ppermute | solution.py:338
  60.7 5.5 %collective-permute-start.20 = (f32[8,256]{1,0:T(8,128)S(1)}, f32[8,256]{1,0:T(8,128)S(1)}, u32[]{:S(2)}, u32[]{:S(2)}) collective-permute-start(f32[8,256]{1,0:T(8,128)S(1)} %coarse.6.refs_4_), channel_id=1, source_target_pairs={{0,3},{1,2},{2,1},{3,0},{4,7},{5,6},{6,5},{7,4},{8,11},{9,10},{10,... | collective-permute-start | bytes 24584 | tf_op jit(solution)/shard_map/ppermute | solution.py:338
  67.4 7.6 %collective-permute-start.21 = (f32[96,128]{1,0:T(8,128)S(1)}, f32[96,128]{1,0:T(8,128)S(1)}, u32[]{:S(2)}, u32[]{:S(2)}) collective-permute-start(f32[96,128]{1,0:T(8,128)S(1)} %get-tuple-element.131.refs_0_), channel_id=1, source_target_pairs={{4,8},{8,4},{12,16},{16,12},{20,24},{24,20},{5,9},{9,5},{13,17},{1... | collective-permute-start | bytes 147464 | tf_op jit(solution)/shard_map/ppermute | solution.py:334
  68.0 6.9 %collective-permute-start.22 = (f32[96,128]{1,0:T(8,128)S(1)}, f32[96,128]{1,0:T(8,128)S(1)}, u32[]{:S(2)}, u32[]{:S(2)}) collective-permute-start(f32[96,128]{1,0:T(8,128)S(1)} %get-tuple-element.132.refs_1_), channel_id=1, source_target_pairs={{0,4},{4,0},{8,12},{12,8},{16,20},{20,16},{24,28},{28,24},{1,5},{5... | collective-permute-start | bytes 147464 | tf_op jit(solution)/shard_map/ppermute | solution.py:329
  82.2 6.8 %collective-permute-start.26 = (f32[8,256]{1,0:T(8,128)S(1)}, f32[8,256]{1,0:T(8,128)S(1)}, u32[]{:S(2)}, u32[]{:S(2)}) collective-permute-start(f32[8,256]{1,0:T(8,128)S(1)} %get-tuple-element.140), channel_id=1, source_target_pairs={{0,8},{4,12},{8,0},{12,4},{16,24},{20,28},{24,16},{28,20},{1,9},{5... | collective-permute-start | bytes 24584 | tf_op jit(solution)/shard_map/ppermute | solution.py:329
  84.6 5.4 %collective-permute-start.27 = (f32[8,256]{1,0:T(8,128)S(1)}, f32[8,256]{1,0:T(8,128)S(1)}, u32[]{:S(2)}, u32[]{:S(2)}) collective-permute-start(f32[8,256]{1,0:T(8,128)S(1)} %get-tuple-element.141), channel_id=1, source_target_pairs={{0,3},{1,2},{2,1},{3,0},{4,7},{5,6},{6,5},{7,4},{8,11},{9,10},{10,... | collective-permute-start | bytes 24584 | tf_op jit(solution)/shard_map/ppermute | solution.py:338
  92.5 5.5 %collective-permute-start.32 = (f32[8,256]{1,0:T(8,128)S(1)}, f32[8,256]{1,0:T(8,128)S(1)}, u32[]{:S(2)}, u32[]{:S(2)}) collective-permute-start(f32[8,256]{1,0:T(8,128)S(1)} %coarse.7.refs_4_), channel_id=1, source_target_pairs={{0,3},{1,2},{2,1},{3,0},{4,7},{5,6},{6,5},{7,4},{8,11},{9,10},{10,... | collective-permute-start | bytes 24584 | tf_op jit(solution)/shard_map/ppermute | solution.py:338
  99.1 7.0 %collective-permute-start.33 = (f32[96,128]{1,0:T(8,128)S(1)}, f32[96,128]{1,0:T(8,128)S(1)}, u32[]{:S(2)}, u32[]{:S(2)}) collective-permute-start(f32[96,128]{1,0:T(8,128)S(1)} %get-tuple-element.145.refs_0_), channel_id=1, source_target_pairs={{4,8},{8,4},{12,16},{16,12},{20,24},{24,20},{5,9},{9,5},{13,17},{1... | collective-permute-start | bytes 147464 | tf_op jit(solution)/shard_map/ppermute | solution.py:334
  99.7 6.4 %collective-permute-start.34 = (f32[96,128]{1,0:T(8,128)S(1)}, f32[96,128]{1,0:T(8,128)S(1)}, u32[]{:S(2)}, u32[]{:S(2)}) collective-permute-start(f32[96,128]{1,0:T(8,128)S(1)} %get-tuple-element.146.refs_1_), channel_id=1, source_target_pairs={{0,4},{4,0},{8,12},{12,8},{16,20},{20,16},{24,28},{28,24},{1,5},{5... | collective-permute-start | bytes 147464 | tf_op jit(solution)/shard_map/ppermute | solution.py:329
  113.1 6.9 %collective-permute-start.38 = (f32[8,256]{1,0:T(8,128)S(1)}, f32[8,256]{1,0:T(8,128)S(1)}, u32[]{:S(2)}, u32[]{:S(2)}) collective-permute-start(f32[8,256]{1,0:T(8,128)S(1)} %get-tuple-element.162), channel_id=1, source_target_pairs={{0,8},{4,12},{8,0},{12,4},{16,24},{20,28},{24,16},{28,20},{1,9},{5... | collective-permute-start | bytes 24584 | tf_op jit(solution)/shard_map/ppermute | solution.py:329
  115.7 5.4 %collective-permute-start.39 = (f32[8,256]{1,0:T(8,128)S(1)}, f32[8,256]{1,0:T(8,128)S(1)}, u32[]{:S(2)}, u32[]{:S(2)}) collective-permute-start(f32[8,256]{1,0:T(8,128)S(1)} %get-tuple-element.163), channel_id=1, source_target_pairs={{0,3},{1,2},{2,1},{3,0},{4,7},{5,6},{6,5},{7,4},{8,11},{9,10},{10,... | collective-permute-start | bytes 24584 | tf_op jit(solution)/shard_map/ppermute | solution.py:338
  123.5 5.5 %collective-permute-start.44 = (f32[8,256]{1,0:T(8,128)S(1)}, f32[8,256]{1,0:T(8,128)S(1)}, u32[]{:S(2)}, u32[]{:S(2)}) collective-permute-start(f32[8,256]{1,0:T(8,128)S(1)} %coarse.8.refs_4_), channel_id=1, source_target_pairs={{0,3},{1,2},{2,1},{3,0},{4,7},{5,6},{6,5},{7,4},{8,11},{9,10},{10,... | collective-permute-start | bytes 24584 | tf_op jit(solution)/shard_map/ppermute | solution.py:338
  130.1 7.1 %collective-permute-start.45 = (f32[96,128]{1,0:T(8,128)S(1)}, f32[96,128]{1,0:T(8,128)S(1)}, u32[]{:S(2)}, u32[]{:S(2)}) collective-permute-start(f32[96,128]{1,0:T(8,128)S(1)} %get-tuple-element.167.refs_0_), channel_id=1, source_target_pairs={{4,8},{8,4},{12,16},{16,12},{20,24},{24,20},{5,9},{9,5},{13,17},{1... | collective-permute-start | bytes 147464 | tf_op jit(solution)/shard_map/ppermute | solution.py:334
  130.8 6.4 %collective-permute-start.46 = (f32[96,128]{1,0:T(8,128)S(1)}, f32[96,128]{1,0:T(8,128)S(1)}, u32[]{:S(2)}, u32[]{:S(2)}) collective-permute-start(f32[96,128]{1,0:T(8,128)S(1)} %get-tuple-element.168.refs_1_), channel_id=1, source_target_pairs={{0,4},{4,0},{8,12},{12,8},{16,20},{20,16},{24,28},{28,24},{1,5},{5... | collective-permute-start | bytes 147464 | tf_op jit(solution)/shard_map/ppermute | solution.py:329
  144.2 6.9 %collective-permute-start.50 = (f32[8,256]{1,0:T(8,128)S(1)}, f32[8,256]{1,0:T(8,128)S(1)}, u32[]{:S(2)}, u32[]{:S(2)}) collective-permute-start(f32[8,256]{1,0:T(8,128)S(1)} %get-tuple-element.184), channel_id=1, source_target_pairs={{0,8},{4,12},{8,0},{12,4},{16,24},{20,28},{24,16},{28,20},{1,9},{5... | collective-permute-start | bytes 24584 | tf_op jit(solution)/shard_map/ppermute | solution.py:329
  146.8 5.4 %collective-permute-start.51 = (f32[8,256]{1,0:T(8,128)S(1)}, f32[8,256]{1,0:T(8,128)S(1)}, u32[]{:S(2)}, u32[]{:S(2)}) collective-permute-start(f32[8,256]{1,0:T(8,128)S(1)} %get-tuple-element.185), channel_id=1, source_target_pairs={{0,3},{1,2},{2,1},{3,0},{4,7},{5,6},{6,5},{7,4},{8,11},{9,10},{10,... | collective-permute-start | bytes 24584 | tf_op jit(solution)/shard_map/ppermute | solution.py:338
  154.6 5.5 %collective-permute-start.56 = (f32[8,256]{1,0:T(8,128)S(1)}, f32[8,256]{1,0:T(8,128)S(1)}, u32[]{:S(2)}, u32[]{:S(2)}) collective-permute-start(f32[8,256]{1,0:T(8,128)S(1)} %coarse.9.refs_4_), channel_id=1, source_target_pairs={{0,3},{1,2},{2,1},{3,0},{4,7},{5,6},{6,5},{7,4},{8,11},{9,10},{10,... | collective-permute-start | bytes 24584 | tf_op jit(solution)/shard_map/ppermute | solution.py:338
  161.3 7.1 %collective-permute-start.57 = (f32[96,128]{1,0:T(8,128)S(1)}, f32[96,128]{1,0:T(8,128)S(1)}, u32[]{:S(2)}, u32[]{:S(2)}) collective-permute-start(f32[96,128]{1,0:T(8,128)S(1)} %get-tuple-element.189.refs_0_), channel_id=1, source_target_pairs={{4,8},{8,4},{12,16},{16,12},{20,24},{24,20},{5,9},{9,5},{13,17},{1... | collective-permute-start | bytes 147464 | tf_op jit(solution)/shard_map/ppermute | solution.py:334
  161.9 6.4 %collective-permute-start.58 = (f32[96,128]{1,0:T(8,128)S(1)}, f32[96,128]{1,0:T(8,128)S(1)}, u32[]{:S(2)}, u32[]{:S(2)}) collective-permute-start(f32[96,128]{1,0:T(8,128)S(1)} %get-tuple-element.190.refs_1_), channel_id=1, source_target_pairs={{0,4},{4,0},{8,12},{12,8},{16,20},{20,16},{24,28},{28,24},{1,5},{5... | collective-permute-start | bytes 147464 | tf_op jit(solution)/shard_map/ppermute | solution.py:329
  (47 other events, 221.6 us)

commit v7 on v6

--- a/solution.py
+++ b/solution.py
@@ -9,6 +9,7 @@
 CORNERS_SUB = 4
 ITERS = 5
 ROWS = 8
+STATES = 12
 NN = (((1,), (0,)), ((), ()))
 NT = (((1,), (1,)), ((), ()))
 F32 = jnp.float32
@@ -45,10 +46,9 @@
 
 
 def packed(rows):
-    totals = jnp.broadcast_to(lane_total(rows), rows.shape)
     row = lax.broadcasted_iota(jnp.int32, rows.shape, 0)
     lane = lax.broadcasted_iota(jnp.int32, rows.shape, 1)
-    return jnp.sum(jnp.where(row == lane, totals, 0.0), axis=0, keepdims=True)
+    return jnp.sum(jnp.where(row == lane, lane_total(rows), 0.0), axis=0, keepdims=True)
 
 
 def step_sizes(sums, before):
@@ -151,9 +151,9 @@
     stiffen(odd, w, w_previous, selector_ref, swap_ref, stiffness_ref, stiff_ref, near_out, far_out)
 
 
-def update(first, last, refs, m, n, n_previous, totals):
-    scalars_in, x_in, r_in, u_in, w_in, p_in, s_in, q_in, z_in = refs[:9]
-    scalars_out, x_out, r_out, u_out, w_out, p_out, s_out, q_out, z_out = refs[9:]
+def update(first, refs, m, gap, n, n_previous, totals):
+    scalars_in, x_in, r_in, u_in, w_in, p_in, s_in, q_in, z_in, gap_u_in, gap_p_in, gap_q_in = refs[:STATES]
+    scalars_out, x_out, r_out, u_out, w_out, p_out, s_out, q_out, z_out, gap_u_out, gap_p_out, gap_q_out = refs[STATES:]
     sums = lane_total(totals)
     sums = [sums[k : k + 1] for k in range(4)]
     alpha, beta, norm, curvature = step_sizes(sums, None if first else scalars_in[...])
@@ -184,37 +184,35 @@
     r_out[...] = r
     u_out[...] = u
     w_out[0] = w
-    previous = None
-    if not last:
-        z_previous = turned(n_previous, None if first else z_in.at[1])
-        previous = w_in[1] - alpha * z_previous
-        q_out[...] = q
-        z_out[0] = z
-        z_out[1] = z_previous
-        w_out[1] = previous
+    z_previous = turned(n_previous, None if first else z_in.at[1])
+    previous = w_in[1] - alpha * z_previous
+    q_out[...] = q
+    z_out[0] = z
+    z_out[1] = z_previous
+    w_out[1] = previous
+    gap_u = gap_u_in[...]
+    gap_q = turned(gap, gap_q_in)
+    gap_p_out[...] = turned(gap_u, gap_p_in)
+    gap_q_out[...] = gap_q
+    gap_u_out[...] = gap_u - alpha * gap_q
     return dot_rows(r, u, w, s, p), w, previous
 
 
-def middle_kernel(first, last, *refs):
-    (far_ref, near_ref, from_far_ref, from_near_ref, dots_ref, dots_other_ref, m_ref) = refs[:7]
-    (selector_ref, swap_ref, stiffness_ref) = refs[7:10]
-    ins = list(refs[10:19])
-    outs = list(refs[19:28])
+def middle_kernel(first, *refs):
+    (far_ref, near_ref, from_far_ref, from_near_ref, dots_ref, dots_other_ref, m_ref, gap_ref) = refs[:8]
+    (selector_ref, swap_ref, stiffness_ref) = refs[8:11]
+    states = list(refs[11 : 11 + 2 * STATES])
+    far_out, near_out, stiff_ref = refs[11 + 2 * STATES :]
     m = m_ref[...]
     iface = m.shape[0]
     odd = lax.axis_index("sub") % 2 == 1
     n, n_previous = arrived(odd, far_ref, near_ref, from_far_ref, from_near_ref, iface)
     dots, w, previous = update(
-        first, last, ins + outs, m, n, n_previous, dots_ref[...] + dots_other_ref[...]
-    )
-    if last:
-        dots_out = refs[28]
-        dots_out[...] = jnp.broadcast_to(packed(dots)[None], dots_out.shape)
-    else:
-        far_out, near_out, stiff_ref = refs[28:31]
-        near_out[iface:] = dots
-        far_out[iface:] = dots
-        stiffen(odd, w, previous, selector_ref, swap_ref, stiffness_ref, stiff_ref, near_out, far_out)
+        first, states, m, gap_ref[...], n, n_previous, dots_ref[...] + dots_other_ref[...]
+    )
+    near_out[iface:] = dots
+    far_out[iface:] = dots
+    stiffen(odd, w, previous, selector_ref, swap_ref, stiffness_ref, stiff_ref, near_out, far_out)
 
 
 def corner_kernel(
@@ -281,7 +279,7 @@
 
 
 def lift_kernel(ranks, local_ref, operators_ref, table_ref, selector_ref, *rest):
-    pieces, (far_ref, near_ref, dots_out, values_ref) = rest[:ranks], rest[ranks:]
+    pieces, (far_ref, near_ref, dots_out, lifted_ref, values_ref) = rest[:ranks], rest[ranks:]
     cells = local_ref.shape[1]
     owned = values_ref.shape[1] // ranks
     for distance in range(ranks):
@@ -308,15 +306,63 @@
         for dof in range(CORNER_DOF):
             operator = operators_ref[corner * CORNER_DOF + dof].astype(F32)
             lifted = lifted + operator * picked[dof : dof + 1, lanes]
+    lifted_ref[...] = lifted
     collect_to(lax.axis_index("sub") % 2 == 1, lifted, selector_ref[...], near_ref, far_ref)
 
 
-def final_kernel(dots_ref, scalars_ref, x_ref, r_ref, u_ref, w_ref, p_ref, s_ref, x_out, r_out):
+def gram_kernel(
+    r_ref, u_ref, w_ref, p_ref, s_ref, q_ref, z_ref, m_ref, gap_u_ref, gap_p_ref, gap_q_ref, gap_ref, lifted_ref, out_ref
+):
+    left = [u_ref[...], m_ref[...], q_ref[...], p_ref[...]]
+    gaps = [gap_u_ref[...], gap_ref[...], gap_q_ref[...], gap_p_ref[...]]
+    w, z, s = w_ref[0], z_ref[0], s_ref[...]
+    r, lifted = r_ref[...], lifted_ref[...]
+    products = []
+    for v, gap in zip(left, gaps):
+        products += [v * w, gap * lifted, v * z, v * s]
+    products += [r * v for v in left[:3]]
+    rows = [jnp.sum(product, axis=0, keepdims=True) for product in products]
+    rows.append(jnp.zeros((-len(rows) % ROWS, r.shape[1]), F32))
+    out_ref[...] = jnp.broadcast_to(packed(jnp.concatenate(rows, axis=0))[None], out_ref.shape)
+
+
+def final_kernel(
+    dots_ref, scalars_ref, x_ref, r_ref, u_ref, w_ref, p_ref, s_ref, q_ref, z_ref, m_ref,
+    far_ref, near_ref, from_far_ref, from_near_ref, x_out, r_out,
+):
     totals = jnp.sum(dots_ref[...], axis=0)
-    sums = [totals[:, k : k + 1] for k in range(4)]
-    alpha, beta, _, _ = step_sizes(sums, scalars_ref[...])
-    x_out[...] = x_ref[...] + alpha * (u_ref[...] + beta * p_ref[...])
-    r_out[...] = r_ref[...] - alpha * (w_ref[0] + beta * s_ref[...])
+    gram = [[totals[:, 4 * i + k : 4 * i + k + 1] for k in range(4)] for i in range(4)]
+    with_r = [totals[:, 16 + i : 17 + i] for i in range(3)]
+
+    def form(first, second):
+        total = None
+        for i, left in first.items():
+            row = None
+            for k, right in second.items():
+                term = gram[i][k] * right
+                row = term if row is None else row + term
+            total = left * row if total is None else total + left * row
+        return total
+
+    norm = with_r[0]
+    beta = norm / scalars_ref[0:1, 0:1]
+    one = jnp.ones_like(norm)
+    turned = {0: one, 3: beta}
+    alpha = norm / form(turned, turned)
+    stepped = {0: one, 1: -alpha, 2: -alpha * beta}
+    norm_next = with_r[0] + stepped[1] * with_r[1] + stepped[2] * with_r[2] - alpha * form(stepped, turned)
+    beta_next = norm_next / norm
+    turned_next = {0: one + beta_next, 1: stepped[1], 2: stepped[2], 3: beta_next * beta}
+    alpha_next = norm_next / form(turned_next, turned_next)
+
+    odd = lax.axis_index("sub") % 2 == 1
+    n, _ = arrived(odd, far_ref, near_ref, from_far_ref, from_near_ref, r_ref.shape[0])
+    p = u_ref[...] + beta * p_ref[...]
+    s = w_ref[0] + beta * s_ref[...]
+    u = u_ref[...] - alpha * (m_ref[...] + beta * q_ref[...])
+    w = w_ref[0] - alpha * (n + beta * z_ref[0])
+    x_out[...] = x_ref[...] + alpha * p + alpha_next * (u + beta_next * p)
+    r_out[...] = r_ref[...] - alpha * s - alpha_next * (w + beta_next * s)
 
 
 def shifted(block, distance):
@@ -398,7 +444,7 @@
     stiff_scratch = [pltpu.VMEM((iface, cells), F32)]
     stiff_cost = dict(flops=4 * iface * iface * cells, moved=4 * iface * iface * cells)
 
-    def apply_operator(near, far):
+    def apply_operator(near, far, reduce=True):
         from_far, from_near = swapped_far(far), swapped(near, 1)
         m, gap, sent, *parts, dots = call(
             lambda *refs: corner_kernel(ranks, *refs),
@@ -418,7 +464,7 @@
             moved=2 * iface * iface * cells,
             name="local",
         )(gap, inverse)
-        other = swapped(sent, 2)
+        other = swapped(sent, 2) if reduce else sent
         solved = call(
             lambda *refs: coarse_kernel(ranks, *refs),
             piece,
@@ -429,22 +475,22 @@
             name="coarse",
         )(coarse_inverse, dots, other, *arrivals)
         values = [solved] + [exchanged(solved, d) for d in range(1, ranks)]
-        far, near, dots = call(
+        far, near, dots, lifted = call(
             lambda *refs: lift_kernel(ranks, *refs),
-            (field, field, rows),
+            (field, field, rows, field),
             count=4 + ranks,
             scratch=[pltpu.VMEM((ROWS, group), F32)],
             flops=2 * 24 * iface * cells,
             moved=2 * 24 * iface * cells + group * CORNERS_SUB * cells * 2,
             name="lift",
         )(local, operators, table, selector, *values)
-        return m, near, far, dots
+        return m, gap, near, far, dots, lifted
 
     previous = shifted(right_side, 1)
     far, near = call(
         first_kernel, (message, message), count=5, scratch=stiff_scratch, name="first", **stiff_cost
     )(right_side, previous, selector, swap, stiff)
-    u, near, far, dots = apply_operator(near, far)
+    u, gap_u, near, far, _, _ = apply_operator(near, far)
     r = right_side
     from_far, from_near = swapped_far(far), swapped(near, 1)
     far, near, w = call(
@@ -456,39 +502,33 @@
         **stiff_cost,
     )(far, near, from_far, from_near, r, u, selector, swap, stiff)
 
-    scalars, x, p, s, q, z = [jnp.zeros((ROWS, cells), F32)] + [r] * 4 + [w]
-    for step in range(ITERS - 1):
-        first, last = step == 0, step == ITERS - 2
-        m, near, far, dots = apply_operator(near, far)
+    states = (jnp.zeros((ROWS, cells), F32), r, r, u, w, r, r, r, w, gap_u, r, r)
+    outs = (rows, field, field, field, pair, field, field, field, pair, field, field, field, message, message)
+    for step in range(ITERS - 2):
+        m, gap, near, far, dots, _ = apply_operator(near, far)
         from_far, from_near, other = swapped_far(far), swapped(near, 1), swapped(dots, 4)
         bit = 8
         while bit < sub_count:
             dots = dots + other
             other = swapped(dots, bit)
             bit *= 2
-        outs = (rows, field, field, field, pair, field, field, field, pair)
-        if last:
-            count = sub_count * ranks
-            outs += (shape(count, 1, cells),)
-        else:
-            outs += (message, message)
-        result = call(
-            lambda *refs, first=first, last=last: middle_kernel(first, last, *refs),
+        *states, far, near = call(
+            lambda *refs, first=step == 0: middle_kernel(first, *refs),
             outs,
-            count=19,
-            scratch=() if last else stiff_scratch,
-            name="last" if last else "middle",
-            **({} if last else stiff_cost),
-        )(
-            far, near, from_far, from_near, dots, other, m, selector, swap, stiff,
-            scalars, x, r, u, w, p, s, q, z,
-        )
-        scalars, x, r, u, w, p, s, q, z = result[:9]
-        if not last:
-            far, near = result[9:]
-    everyone = lax.all_to_all(result[9], ("sub", "grp"), 0, 0, tiled=True)
-    x, r = call(final_kernel, (field, field), count=8, name="final")(
-        everyone, scalars, x, r, u, w, p, s
+            count=11 + STATES,
+            scratch=stiff_scratch,
+            name="middle",
+            **stiff_cost,
+        )(far, near, from_far, from_near, dots, other, m, gap, selector, swap, stiff, *states)
+    scalars, x, r, u, w, p, s, q, z, gap_u, gap_p, gap_q = states
+    m, gap, near, far, _, lifted = apply_operator(near, far, reduce=False)
+    from_far, from_near = swapped_far(far), swapped(near, 1)
+    parts = call(gram_kernel, shape(sub_count * ranks, 1, cells), count=13, name="gram")(
+        r, u, w, p, s, q, z, m, gap_u, gap_p, gap_q, gap, lifted
+    )
+    everyone = lax.all_to_all(parts, ("sub", "grp"), 0, 0, tiled=True)
+    x, r = call(final_kernel, (field, field), count=15, name="final")(
+        everyone, scalars, x, r, u, w, p, s, q, z, m, far, near, from_far, from_near
     )
     return (x[:, None, :], r[:, None, :])
 

time: 182 us -> 180 us (0.989)
  starting transfers between devices: 105 us -> 102 us
    ppermute x19 -> x17, starting transfers between devices: 51.9 us -> 48.4 us  [swapped(): lax.ppermute(block, 'sub', [(i, i ^ bit) for i in range(lax.axis_size('su...]
    pallas_call x10, Pallas kernels: 10.6 us -> 12.4 us  [the longest x3 5.46 us: on_device(): call(lambda *refs, first=step == 0: middle_kernel(first, *refs), outs, co...]
    ppermute x19 -> x17, waiting for transfers between devices: 11.7 us -> 10.1 us  [swapped(): lax.ppermute(block, 'sub', [(i, i ^ bit) for i in range(lax.axis_size('su...]
  transfers between devices with their start and end apart: 60 -> 58, of which waited for: 39 -> 38; matrix products, arithmetic and copies ran while one was open for 0% -> 0% of each run, Pallas kernels for 2% -> 2%
where the time goes in v7:
time: 180 us; the launch traced here: 179 us
  starting transfers between devices  102 us (57%)
  waiting for transfers between devices  30.1 us (17%)
  Pallas kernels  25.8 us (14%)
  blocking collectives  12.1 us (7%)
  local copies, waits for them, and re-layouts  8.3 us (5%)
    ppermute x17, starting transfers between devices, swapped(): lax.ppermute(block, 'sub', [(i, i ^ bit) for i in range(lax.axis_size('su...  48.4 us
    ppermute x30, starting transfers between devices, exchanged(): lax.ppermute(block, 'grp', [(i, i ^ distance) for i in range(lax.axis_siz...  44.1 us
    ppermute x30, waiting for transfers between devices, exchanged(): lax.ppermute(block, 'grp', [(i, i ^ distance) for i in range(lax.axis_siz...  20 us
    all_to_all x1, blocking collectives, on_device(): everyone = lax.all_to_all(parts, ('sub', 'grp'), 0, 0, tiled=True)  12.1 us
    ppermute x17, waiting for transfers between devices, swapped(): lax.ppermute(block, 'sub', [(i, i ^ bit) for i in range(lax.axis_size('su...  10.1 us
    unnamed x22, local copies, waits for them, and re-layouts  8.3 us
    ppermute x10, starting transfers between devices, swapped_far(): lax.ppermute(block, 'sub', [(i, i + 1 if i % 2 else i - 1) for i in inner])  6.89 us
    pallas_call x3, Pallas kernels, on_device(): call(lambda *refs, first=step == 0: middle_kernel(first, *refs), outs, co...  5.46 us
  transfers between devices with their start and end apart: 58, of which 38 were waited for; matrix products, arithmetic and copies ran while one was open for 0% of the time, Pallas kernels for 2%

profile of v7, /device:TPU:0, one launch (start us, length us, event | category | flops | bytes accessed | tf_op | source)
XLA Modules:
  0.0 179.1 jit_solution(12780572634331254080)
XLA Ops:
  0.6 2.4 %collective-permute-start = (f32[96,128]{1,0:T(8,128)}, f32[96,128]{1,0:T(8,128)S(1)}, u32[]{:S(2)}, u32[]{:S(2)}) collective-permute-start(f32[96,128]{1,0:T(8,128)} %bitcast.33), channel_id=1, source_target_pairs={{0,4},{4,8},{8,12},{12,16},{16,20},{20,24},{24,28},{1,5},{5,9},{9,... | collective-permute-start | bytes 147464 | tf_op jit(solution)/shard_map/ppermute | solution.py:371
  3.0 2.3 %copy-done = bf16[2,96,96,1,128]{4,2,3,1,0:T(8,128)(2,1)S(1)} copy-done((bf16[2,96,96,1,128]{4,2,3,1,0:T(8,128)(2,1)S(1)}, bf16[2,96,96,1,128]{4,2,3,1,0:T(8,128)(2,1)}, u32[]{:S(2)}) %copy-start) | copy-done | bytes 4718616
  9.4 2.1 %copy-done.1 = bf16[2,96,96,1,128]{4,2,3,1,0:T(8,128)(2,1)S(1)} copy-done((bf16[2,96,96,1,128]{4,2,3,1,0:T(8,128)(2,1)S(1)}, bf16[2,96,96,1,128]{4,2,3,1,0:T(8,128)(2,1)}, u32[]{:S(2)}) %copy-start.1) | copy-done | bytes 4718616
  14.0 3.9 %collective-permute-start.2 = (f32[104,128]{1,0:T(8,128)S(1)}, f32[104,128]{1,0:T(8,128)S(1)}, u32[]{:S(2)}, u32[]{:S(2)}) collective-permute-start(f32[104,128]{1,0:T(8,128)S(1)} %get-tuple-element.111.refs_1_), channel_id=1, source_target_pairs={{0,4},{4,0},{8,12},{12,8},{16,20},{20,16},{24,28},{28,24},{1,5},{5... | collective-permute-start | bytes 159752 | tf_op jit(solution)/shard_map/ppermute | solution.py:375
  19.5 2.5 %collective-permute-start.3 = (f32[8,256]{1,0:T(8,128)S(1)}, f32[8,256]{1,0:T(8,128)S(1)}, u32[]{:S(2)}, u32[]{:S(2)}) collective-permute-start(f32[8,256]{1,0:T(8,128)S(1)} %get-tuple-element.115), channel_id=1, source_target_pairs={{0,8},{4,12},{8,0},{12,4},{16,24},{20,28},{24,16},{28,20},{1,9},{5... | collective-permute-start | bytes 24584 | tf_op jit(solution)/shard_map/ppermute | solution.py:375
  22.1 3.6 %collective-permute-start.4 = (f32[8,256]{1,0:T(8,128)S(1)}, f32[8,256]{1,0:T(8,128)S(1)}, u32[]{:S(2)}, u32[]{:S(2)}) collective-permute-start(f32[8,256]{1,0:T(8,128)S(1)} %get-tuple-element.116), channel_id=1, source_target_pairs={{0,3},{1,2},{2,1},{3,0},{4,7},{5,6},{6,5},{7,4},{8,11},{9,10},{10,... | collective-permute-start | bytes 24584 | tf_op jit(solution)/shard_map/ppermute | solution.py:384
  27.5 2.7 %collective-permute-done.5.refs_4_ = f32[8,256]{1,0:T(8,128)S(1)} collective-permute-done((f32[8,256]{1,0:T(8,128)S(1)}, f32[8,256]{1,0:T(8,128)S(1)}, u32[]{:S(2)}, u32[]{:S(2)}) %collective-permute-start.5) | collective-permute-done | bytes 8224 | tf_op jit(solution)/shard_map/ppermute | solution.py:384
  33.1 2.3 %collective-permute-start.7 = (f32[8,256]{1,0:T(8,128)S(1)}, f32[8,256]{1,0:T(8,128)S(1)}, u32[]{:S(2)}, u32[]{:S(2)}) collective-permute-start(f32[8,256]{1,0:T(8,128)S(1)} %coarse.5.refs_4_), channel_id=1, source_target_pairs={{0,1},{1,0},{2,3},{3,2},{4,5},{5,4},{6,7},{7,6},{8,9},{9,8},{10,11... | collective-permute-start | bytes 24584 | tf_op jit(solution)/shard_map/ppermute | solution.py:384
  43.5 4.3 %collective-permute-start.13 = (f32[104,128]{1,0:T(8,128)S(1)}, f32[104,128]{1,0:T(8,128)S(1)}, u32[]{:S(2)}, u32[]{:S(2)}) collective-permute-start(f32[104,128]{1,0:T(8,128)S(1)} %get-tuple-element.124.refs_1_), channel_id=1, source_target_pairs={{0,4},{4,0},{8,12},{12,8},{16,20},{20,16},{24,28},{28,24},{1,5},{5... | collective-permute-start | bytes 159752 | tf_op jit(solution)/shard_map/ppermute | solution.py:375
  49.4 3.4 %collective-permute-start.14 = (f32[8,256]{1,0:T(8,128)S(1)}, f32[8,256]{1,0:T(8,128)S(1)}, u32[]{:S(2)}, u32[]{:S(2)}) collective-permute-start(f32[8,256]{1,0:T(8,128)S(1)} %get-tuple-element.127), channel_id=1, source_target_pairs={{0,8},{4,12},{8,0},{12,4},{16,24},{20,28},{24,16},{28,20},{1,9},{5... | collective-permute-start | bytes 24584 | tf_op jit(solution)/shard_map/ppermute | solution.py:375
  52.8 2.5 %collective-permute-start.15 = (f32[8,256]{1,0:T(8,128)S(1)}, f32[8,256]{1,0:T(8,128)S(1)}, u32[]{:S(2)}, u32[]{:S(2)}) collective-permute-start(f32[8,256]{1,0:T(8,128)S(1)} %get-tuple-element.128), channel_id=1, source_target_pairs={{0,3},{1,2},{2,1},{3,0},{4,7},{5,6},{6,5},{7,4},{8,11},{9,10},{10,... | collective-permute-start | bytes 24584 | tf_op jit(solution)/shard_map/ppermute | solution.py:384
  70.1 3.7 %collective-permute-start.23 = (f32[8,128]{1,0:T(8,128)S(1)}, f32[8,128]{1,0:T(8,128)S(1)}, u32[]{:S(2)}, u32[]{:S(2)}) collective-permute-start(f32[8,128]{1,0:T(8,128)S(1)} %get-tuple-element.134.refs_4_), channel_id=1, source_target_pairs={{0,16},{4,20},{8,24},{12,28},{16,0},{20,4},{24,8},{28,12},{1,17},{... | collective-permute-start | bytes 12296 | tf_op jit(solution)/shard_map/ppermute | solution.py:375
  78.1 3.0 %collective-permute-start.25 = (f32[104,128]{1,0:T(8,128)S(1)}, f32[104,128]{1,0:T(8,128)S(1)}, u32[]{:S(2)}, u32[]{:S(2)}) collective-permute-start(f32[104,128]{1,0:T(8,128)S(1)} %get-tuple-element.138.refs_1_), channel_id=1, source_target_pairs={{0,4},{4,0},{8,12},{12,8},{16,20},{20,16},{24,28},{28,24},{1,5},{5... | collective-permute-start | bytes 159752 | tf_op jit(solution)/shard_map/ppermute | solution.py:375
  82.7 2.4 %collective-permute-start.26 = (f32[8,256]{1,0:T(8,128)S(1)}, f32[8,256]{1,0:T(8,128)S(1)}, u32[]{:S(2)}, u32[]{:S(2)}) collective-permute-start(f32[8,256]{1,0:T(8,128)S(1)} %get-tuple-element.141), channel_id=1, source_target_pairs={{0,8},{4,12},{8,0},{12,4},{16,24},{20,28},{24,16},{28,20},{1,9},{5... | collective-permute-start | bytes 24584 | tf_op jit(solution)/shard_map/ppermute | solution.py:375
  85.1 2.5 %collective-permute-start.27 = (f32[8,256]{1,0:T(8,128)S(1)}, f32[8,256]{1,0:T(8,128)S(1)}, u32[]{:S(2)}, u32[]{:S(2)}) collective-permute-start(f32[8,256]{1,0:T(8,128)S(1)} %get-tuple-element.142), channel_id=1, source_target_pairs={{0,3},{1,2},{2,1},{3,0},{4,7},{5,6},{6,5},{7,4},{8,11},{9,10},{10,... | collective-permute-start | bytes 24584 | tf_op jit(solution)/shard_map/ppermute | solution.py:384
  102.1 3.3 %collective-permute-start.35 = (f32[8,128]{1,0:T(8,128)S(1)}, f32[8,128]{1,0:T(8,128)S(1)}, u32[]{:S(2)}, u32[]{:S(2)}) collective-permute-start(f32[8,128]{1,0:T(8,128)S(1)} %get-tuple-element.148.refs_4_), channel_id=1, source_target_pairs={{0,16},{4,20},{8,24},{12,28},{16,0},{20,4},{24,8},{28,12},{1,17},{... | collective-permute-start | bytes 12296 | tf_op jit(solution)/shard_map/ppermute | solution.py:375
  109.5 3.0 %collective-permute-start.37 = (f32[104,128]{1,0:T(8,128)S(1)}, f32[104,128]{1,0:T(8,128)S(1)}, u32[]{:S(2)}, u32[]{:S(2)}) collective-permute-start(f32[104,128]{1,0:T(8,128)S(1)} %get-tuple-element.163.refs_1_), channel_id=1, source_target_pairs={{0,4},{4,0},{8,12},{12,8},{16,20},{20,16},{24,28},{28,24},{1,5},{5... | collective-permute-start | bytes 159752 | tf_op jit(solution)/shard_map/ppermute | solution.py:375
  114.0 2.5 %collective-permute-start.38 = (f32[8,256]{1,0:T(8,128)S(1)}, f32[8,256]{1,0:T(8,128)S(1)}, u32[]{:S(2)}, u32[]{:S(2)}) collective-permute-start(f32[8,256]{1,0:T(8,128)S(1)} %get-tuple-element.166), channel_id=1, source_target_pairs={{0,8},{4,12},{8,0},{12,4},{16,24},{20,28},{24,16},{28,20},{1,9},{5... | collective-permute-start | bytes 24584 | tf_op jit(solution)/shard_map/ppermute | solution.py:375
  116.6 2.5 %collective-permute-start.39 = (f32[8,256]{1,0:T(8,128)S(1)}, f32[8,256]{1,0:T(8,128)S(1)}, u32[]{:S(2)}, u32[]{:S(2)}) collective-permute-start(f32[8,256]{1,0:T(8,128)S(1)} %get-tuple-element.167), channel_id=1, source_target_pairs={{0,3},{1,2},{2,1},{3,0},{4,7},{5,6},{6,5},{7,4},{8,11},{9,10},{10,... | collective-permute-start | bytes 24584 | tf_op jit(solution)/shard_map/ppermute | solution.py:384
  133.7 3.3 %collective-permute-start.47 = (f32[8,128]{1,0:T(8,128)S(1)}, f32[8,128]{1,0:T(8,128)S(1)}, u32[]{:S(2)}, u32[]{:S(2)}) collective-permute-start(f32[8,128]{1,0:T(8,128)S(1)} %get-tuple-element.173.refs_4_), channel_id=1, source_target_pairs={{0,16},{4,20},{8,24},{12,28},{16,0},{20,4},{24,8},{28,12},{1,17},{... | collective-permute-start | bytes 12296 | tf_op jit(solution)/shard_map/ppermute | solution.py:375
  141.1 3.0 %collective-permute-start.49 = (f32[104,128]{1,0:T(8,128)S(1)}, f32[104,128]{1,0:T(8,128)S(1)}, u32[]{:S(2)}, u32[]{:S(2)}) collective-permute-start(f32[104,128]{1,0:T(8,128)S(1)} %get-tuple-element.195.refs_1_), channel_id=1, source_target_pairs={{0,4},{4,0},{8,12},{12,8},{16,20},{20,16},{24,28},{28,24},{1,5},{5... | collective-permute-start | bytes 159752 | tf_op jit(solution)/shard_map/ppermute | solution.py:375
  145.6 2.6 %collective-permute-start.50 = (f32[8,256]{1,0:T(8,128)S(1)}, f32[8,256]{1,0:T(8,128)S(1)}, u32[]{:S(2)}, u32[]{:S(2)}) collective-permute-start(f32[8,256]{1,0:T(8,128)S(1)} %get-tuple-element.203), channel_id=1, source_target_pairs={{0,3},{1,2},{2,1},{3,0},{4,7},{5,6},{6,5},{7,4},{8,11},{9,10},{10,... | collective-permute-start | bytes 24584 | tf_op jit(solution)/shard_map/ppermute | solution.py:384
  161.3 3.9 %collective-permute-start.57 = (f32[96,128]{1,0:T(8,128)S(1)}, f32[96,128]{1,0:T(8,128)S(1)}, u32[]{:S(2)}, u32[]{:S(2)}) collective-permute-start(f32[96,128]{1,0:T(8,128)S(1)} %get-tuple-element.211.near_ref), channel_id=1, source_target_pairs={{0,4},{4,0},{8,12},{12,8},{16,20},{20,16},{24,28},{28,24},{1,5},{5... | collective-permute-start | bytes 147464 | tf_op jit(solution)/shard_map/ppermute | solution.py:375
  165.4 12.1 %all_to_all.5.dots_ref = f32[32,1,128]{2,1,0:T(1,128)S(1)} all-to-all(f32[32,1,128]{2,1,0:T(1,128)S(1)} %gram.1), channel_id=1, replica_groups=mesh['sub'=8,'grp'=4] {'sub','grp'}, dimensions={0} | all-to-all | bytes 32768 | tf_op jit(solution)/shard_map/all_to_all | solution.py:529
  (144 shorter events, 98.3 us)
Async XLA Ops:
  0.6 8.8 %collective-permute-start = (f32[96,128]{1,0:T(8,128)}, f32[96,128]{1,0:T(8,128)S(1)}, u32[]{:S(2)}, u32[]{:S(2)}) collective-permute-start(f32[96,128]{1,0:T(8,128)} %bitcast.33), channel_id=1, source_target_pairs={{0,4},{4,8},{8,12},{12,16},{16,20},{20,24},{24,28},{1,5},{5,9},{9,... | collective-permute-start | bytes 147464 | tf_op jit(solution)/shard_map/ppermute | solution.py:371
  19.5 6.9 %collective-permute-start.3 = (f32[8,256]{1,0:T(8,128)S(1)}, f32[8,256]{1,0:T(8,128)S(1)}, u32[]{:S(2)}, u32[]{:S(2)}) collective-permute-start(f32[8,256]{1,0:T(8,128)S(1)} %get-tuple-element.115), channel_id=1, source_target_pairs={{0,8},{4,12},{8,0},{12,4},{16,24},{20,28},{24,16},{28,20},{1,9},{5... | collective-permute-start | bytes 24584 | tf_op jit(solution)/shard_map/ppermute | solution.py:375
  22.1 5.4 %collective-permute-start.4 = (f32[8,256]{1,0:T(8,128)S(1)}, f32[8,256]{1,0:T(8,128)S(1)}, u32[]{:S(2)}, u32[]{:S(2)}) collective-permute-start(f32[8,256]{1,0:T(8,128)S(1)} %get-tuple-element.116), channel_id=1, source_target_pairs={{0,3},{1,2},{2,1},{3,0},{4,7},{5,6},{6,5},{7,4},{8,11},{9,10},{10,... | collective-permute-start | bytes 24584 | tf_op jit(solution)/shard_map/ppermute | solution.py:384
  31.0 5.5 %collective-permute-start.9 = (f32[8,256]{1,0:T(8,128)S(1)}, f32[8,256]{1,0:T(8,128)S(1)}, u32[]{:S(2)}, u32[]{:S(2)}) collective-permute-start(f32[8,256]{1,0:T(8,128)S(1)} %coarse.5.refs_4_), channel_id=1, source_target_pairs={{0,3},{1,2},{2,1},{3,0},{4,7},{5,6},{6,5},{7,4},{8,11},{9,10},{10,... | collective-permute-start | bytes 24584 | tf_op jit(solution)/shard_map/ppermute | solution.py:384
  49.4 7.8 %collective-permute-start.14 = (f32[8,256]{1,0:T(8,128)S(1)}, f32[8,256]{1,0:T(8,128)S(1)}, u32[]{:S(2)}, u32[]{:S(2)}) collective-permute-start(f32[8,256]{1,0:T(8,128)S(1)} %get-tuple-element.127), channel_id=1, source_target_pairs={{0,8},{4,12},{8,0},{12,4},{16,24},{20,28},{24,16},{28,20},{1,9},{5... | collective-permute-start | bytes 24584 | tf_op jit(solution)/shard_map/ppermute | solution.py:375
  52.8 5.4 %collective-permute-start.15 = (f32[8,256]{1,0:T(8,128)S(1)}, f32[8,256]{1,0:T(8,128)S(1)}, u32[]{:S(2)}, u32[]{:S(2)}) collective-permute-start(f32[8,256]{1,0:T(8,128)S(1)} %get-tuple-element.128), channel_id=1, source_target_pairs={{0,3},{1,2},{2,1},{3,0},{4,7},{5,6},{6,5},{7,4},{8,11},{9,10},{10,... | collective-permute-start | bytes 24584 | tf_op jit(solution)/shard_map/ppermute | solution.py:384
  60.7 5.5 %collective-permute-start.20 = (f32[8,256]{1,0:T(8,128)S(1)}, f32[8,256]{1,0:T(8,128)S(1)}, u32[]{:S(2)}, u32[]{:S(2)}) collective-permute-start(f32[8,256]{1,0:T(8,128)S(1)} %coarse.6.refs_4_), channel_id=1, source_target_pairs={{0,3},{1,2},{2,1},{3,0},{4,7},{5,6},{6,5},{7,4},{8,11},{9,10},{10,... | collective-permute-start | bytes 24584 | tf_op jit(solution)/shard_map/ppermute | solution.py:384
  67.8 7.6 %collective-permute-start.21 = (f32[96,128]{1,0:T(8,128)S(1)}, f32[96,128]{1,0:T(8,128)S(1)}, u32[]{:S(2)}, u32[]{:S(2)}) collective-permute-start(f32[96,128]{1,0:T(8,128)S(1)} %get-tuple-element.132.refs_0_), channel_id=1, source_target_pairs={{4,8},{8,4},{12,16},{16,12},{20,24},{24,20},{5,9},{9,5},{13,17},{1... | collective-permute-start | bytes 147464 | tf_op jit(solution)/shard_map/ppermute | solution.py:380
  68.5 6.9 %collective-permute-start.22 = (f32[96,128]{1,0:T(8,128)S(1)}, f32[96,128]{1,0:T(8,128)S(1)}, u32[]{:S(2)}, u32[]{:S(2)}) collective-permute-start(f32[96,128]{1,0:T(8,128)S(1)} %get-tuple-element.133.refs_1_), channel_id=1, source_target_pairs={{0,4},{4,0},{8,12},{12,8},{16,20},{20,16},{24,28},{28,24},{1,5},{5... | collective-permute-start | bytes 147464 | tf_op jit(solution)/shard_map/ppermute | solution.py:375
  70.1 5.3 %collective-permute-start.23 = (f32[8,128]{1,0:T(8,128)S(1)}, f32[8,128]{1,0:T(8,128)S(1)}, u32[]{:S(2)}, u32[]{:S(2)}) collective-permute-start(f32[8,128]{1,0:T(8,128)S(1)} %get-tuple-element.134.refs_4_), channel_id=1, source_target_pairs={{0,16},{4,20},{8,24},{12,28},{16,0},{20,4},{24,8},{28,12},{1,17},{... | collective-permute-start | bytes 12296 | tf_op jit(solution)/shard_map/ppermute | solution.py:375
  82.7 6.8 %collective-permute-start.26 = (f32[8,256]{1,0:T(8,128)S(1)}, f32[8,256]{1,0:T(8,128)S(1)}, u32[]{:S(2)}, u32[]{:S(2)}) collective-permute-start(f32[8,256]{1,0:T(8,128)S(1)} %get-tuple-element.141), channel_id=1, source_target_pairs={{0,8},{4,12},{8,0},{12,4},{16,24},{20,28},{24,16},{28,20},{1,9},{5... | collective-permute-start | bytes 24584 | tf_op jit(solution)/shard_map/ppermute | solution.py:375
  85.1 5.4 %collective-permute-start.27 = (f32[8,256]{1,0:T(8,128)S(1)}, f32[8,256]{1,0:T(8,128)S(1)}, u32[]{:S(2)}, u32[]{:S(2)}) collective-permute-start(f32[8,256]{1,0:T(8,128)S(1)} %get-tuple-element.142), channel_id=1, source_target_pairs={{0,3},{1,2},{2,1},{3,0},{4,7},{5,6},{6,5},{7,4},{8,11},{9,10},{10,... | collective-permute-start | bytes 24584 | tf_op jit(solution)/shard_map/ppermute | solution.py:384
  92.9 5.5 %collective-permute-start.32 = (f32[8,256]{1,0:T(8,128)S(1)}, f32[8,256]{1,0:T(8,128)S(1)}, u32[]{:S(2)}, u32[]{:S(2)}) collective-permute-start(f32[8,256]{1,0:T(8,128)S(1)} %coarse.7.refs_4_), channel_id=1, source_target_pairs={{0,3},{1,2},{2,1},{3,0},{4,7},{5,6},{6,5},{7,4},{8,11},{9,10},{10,... | collective-permute-start | bytes 24584 | tf_op jit(solution)/shard_map/ppermute | solution.py:384
  100.0 7.0 %collective-permute-start.33 = (f32[96,128]{1,0:T(8,128)S(1)}, f32[96,128]{1,0:T(8,128)S(1)}, u32[]{:S(2)}, u32[]{:S(2)}) collective-permute-start(f32[96,128]{1,0:T(8,128)S(1)} %get-tuple-element.146.refs_0_), channel_id=1, source_target_pairs={{4,8},{8,4},{12,16},{16,12},{20,24},{24,20},{5,9},{9,5},{13,17},{1... | collective-permute-start | bytes 147464 | tf_op jit(solution)/shard_map/ppermute | solution.py:380
  100.6 6.4 %collective-permute-start.34 = (f32[96,128]{1,0:T(8,128)S(1)}, f32[96,128]{1,0:T(8,128)S(1)}, u32[]{:S(2)}, u32[]{:S(2)}) collective-permute-start(f32[96,128]{1,0:T(8,128)S(1)} %get-tuple-element.147.refs_1_), channel_id=1, source_target_pairs={{0,4},{4,0},{8,12},{12,8},{16,20},{20,16},{24,28},{28,24},{1,5},{5... | collective-permute-start | bytes 147464 | tf_op jit(solution)/shard_map/ppermute | solution.py:375
  114.0 6.9 %collective-permute-start.38 = (f32[8,256]{1,0:T(8,128)S(1)}, f32[8,256]{1,0:T(8,128)S(1)}, u32[]{:S(2)}, u32[]{:S(2)}) collective-permute-start(f32[8,256]{1,0:T(8,128)S(1)} %get-tuple-element.166), channel_id=1, source_target_pairs={{0,8},{4,12},{8,0},{12,4},{16,24},{20,28},{24,16},{28,20},{1,9},{5... | collective-permute-start | bytes 24584 | tf_op jit(solution)/shard_map/ppermute | solution.py:375
  116.6 5.4 %collective-permute-start.39 = (f32[8,256]{1,0:T(8,128)S(1)}, f32[8,256]{1,0:T(8,128)S(1)}, u32[]{:S(2)}, u32[]{:S(2)}) collective-permute-start(f32[8,256]{1,0:T(8,128)S(1)} %get-tuple-element.167), channel_id=1, source_target_pairs={{0,3},{1,2},{2,1},{3,0},{4,7},{5,6},{6,5},{7,4},{8,11},{9,10},{10,... | collective-permute-start | bytes 24584 | tf_op jit(solution)/shard_map/ppermute | solution.py:384
  124.4 5.5 %collective-permute-start.44 = (f32[8,256]{1,0:T(8,128)S(1)}, f32[8,256]{1,0:T(8,128)S(1)}, u32[]{:S(2)}, u32[]{:S(2)}) collective-permute-start(f32[8,256]{1,0:T(8,128)S(1)} %coarse.8.refs_4_), channel_id=1, source_target_pairs={{0,3},{1,2},{2,1},{3,0},{4,7},{5,6},{6,5},{7,4},{8,11},{9,10},{10,... | collective-permute-start | bytes 24584 | tf_op jit(solution)/shard_map/ppermute | solution.py:384
  131.5 7.1 %collective-permute-start.45 = (f32[96,128]{1,0:T(8,128)S(1)}, f32[96,128]{1,0:T(8,128)S(1)}, u32[]{:S(2)}, u32[]{:S(2)}) collective-permute-start(f32[96,128]{1,0:T(8,128)S(1)} %get-tuple-element.171.refs_0_), channel_id=1, source_target_pairs={{4,8},{8,4},{12,16},{16,12},{20,24},{24,20},{5,9},{9,5},{13,17},{1... | collective-permute-start | bytes 147464 | tf_op jit(solution)/shard_map/ppermute | solution.py:380
  132.2 6.4 %collective-permute-start.46 = (f32[96,128]{1,0:T(8,128)S(1)}, f32[96,128]{1,0:T(8,128)S(1)}, u32[]{:S(2)}, u32[]{:S(2)}) collective-permute-start(f32[96,128]{1,0:T(8,128)S(1)} %get-tuple-element.172.refs_1_), channel_id=1, source_target_pairs={{0,4},{4,0},{8,12},{12,8},{16,20},{20,16},{24,28},{28,24},{1,5},{5... | collective-permute-start | bytes 147464 | tf_op jit(solution)/shard_map/ppermute | solution.py:375
  145.6 5.5 %collective-permute-start.50 = (f32[8,256]{1,0:T(8,128)S(1)}, f32[8,256]{1,0:T(8,128)S(1)}, u32[]{:S(2)}, u32[]{:S(2)}) collective-permute-start(f32[8,256]{1,0:T(8,128)S(1)} %get-tuple-element.203), channel_id=1, source_target_pairs={{0,3},{1,2},{2,1},{3,0},{4,7},{5,6},{6,5},{7,4},{8,11},{9,10},{10,... | collective-permute-start | bytes 24584 | tf_op jit(solution)/shard_map/ppermute | solution.py:384
  153.5 5.5 %collective-permute-start.55 = (f32[8,256]{1,0:T(8,128)S(1)}, f32[8,256]{1,0:T(8,128)S(1)}, u32[]{:S(2)}, u32[]{:S(2)}) collective-permute-start(f32[8,256]{1,0:T(8,128)S(1)} %coarse.9.refs_4_), channel_id=1, source_target_pairs={{0,3},{1,2},{2,1},{3,0},{4,7},{5,6},{6,5},{7,4},{8,11},{9,10},{10,... | collective-permute-start | bytes 24584 | tf_op jit(solution)/shard_map/ppermute | solution.py:384
  160.6 16.9 %collective-permute-start.56 = (f32[96,128]{1,0:T(8,128)S(1)}, f32[96,128]{1,0:T(8,128)S(1)}, u32[]{:S(2)}, u32[]{:S(2)}) collective-permute-start(f32[96,128]{1,0:T(8,128)S(1)} %get-tuple-element.210.far_ref), channel_id=1, source_target_pairs={{4,8},{8,4},{12,16},{16,12},{20,24},{24,20},{5,9},{9,5},{13,17},{1... | collective-permute-start | bytes 147464 | tf_op jit(solution)/shard_map/ppermute | solution.py:380
  161.3 16.3 %collective-permute-start.57 = (f32[96,128]{1,0:T(8,128)S(1)}, f32[96,128]{1,0:T(8,128)S(1)}, u32[]{:S(2)}, u32[]{:S(2)}) collective-permute-start(f32[96,128]{1,0:T(8,128)S(1)} %get-tuple-element.211.near_ref), channel_id=1, source_target_pairs={{0,4},{4,0},{8,12},{12,8},{16,20},{20,16},{24,28},{28,24},{1,5},{5... | collective-permute-start | bytes 147464 | tf_op jit(solution)/shard_map/ppermute | solution.py:375
  (45 other events, 211.8 us)

commit v8 on v7

--- a/solution.py
+++ b/solution.py
@@ -10,6 +10,7 @@
 ITERS = 5
 ROWS = 8
 STATES = 12
+LOADED = 3
 NN = (((1,), (0,)), ((), ()))
 NT = (((1,), (1,)), ((), ()))
 F32 = jnp.float32
@@ -88,9 +89,14 @@
 
 
 def table_kernel(neighbour_ref, column_ref, corner_ref, *refs):
-    selector_ref, swap_ref, table_ref = refs[-3:]
+    sources, sems = refs[:LOADED], refs[-1]
+    (selector_ref, swap_ref, table_ref), targets = refs[LOADED : LOADED + 3], refs[LOADED + 3 : -1]
+    copies = [pltpu.make_async_copy(sources[k], targets[k], sems.at[k]) for k in range(LOADED)]
+    for copy in copies:
+        copy.start()
     cells = swap_ref.shape[0]
     start = lax.axis_index("sub") * cells
+
     def one_hot(row, count):
         places = lax.broadcasted_iota(jnp.int32, (count, row.shape[1]), 0)
         return jnp.where(places == row, 1.0, 0.0).astype(BF16)
@@ -107,6 +113,8 @@
         return carry
 
     lax.fori_loop(0, table_ref.shape[0] // chunk, step, 0)
+    for copy in copies:
+        copy.wait()
 
 
 def stiffen(odd, own, previous, selector_ref, swap_ref, stiffness_ref, stiff_ref, near_ref, far_ref):
@@ -278,27 +286,28 @@
     solved_ref[...] = jnp.concatenate(rows, axis=0)
 
 
-def lift_kernel(ranks, local_ref, operators_ref, table_ref, selector_ref, *rest):
-    pieces, (far_ref, near_ref, dots_out, lifted_ref, values_ref) = rest[:ranks], rest[ranks:]
+def lift_kernel(ranks, last, local_ref, operators_ref, table_ref, selector_ref, *rest):
+    pieces, (far_ref, near_ref, extra_out, values_ref) = rest[:ranks], rest[ranks:]
     cells = local_ref.shape[1]
     owned = values_ref.shape[1] // ranks
     for distance in range(ranks):
         rank = lax.axis_index("grp") ^ distance
         values_ref[:, pl.ds(pl.multiple_of(rank * owned, 128), owned)] = pieces[distance][...]
     values = values_ref[...]
-    tail = values[CORNER_DOF:, :owned]
-    for rank in range(1, ranks):
-        tail = tail + values[CORNER_DOF:, rank * owned : (rank + 1) * owned]
-    dots_out[...] = jnp.concatenate(
-        [
-            tail[0:1, :cells],
-            tail[0:1, cells : 2 * cells],
-            tail[1:2, :cells],
-            tail[1:2, cells : 2 * cells],
-            jnp.zeros((ROWS - 4, cells), F32),
-        ],
-        axis=0,
-    )
+    if not last:
+        tail = values[CORNER_DOF:, :owned]
+        for rank in range(1, ranks):
+            tail = tail + values[CORNER_DOF:, rank * owned : (rank + 1) * owned]
+        extra_out[...] = jnp.concatenate(
+            [
+                tail[0:1, :cells],
+                tail[0:1, cells : 2 * cells],
+                tail[1:2, :cells],
+                tail[1:2, cells : 2 * cells],
+                jnp.zeros((ROWS - 4, cells), F32),
+            ],
+            axis=0,
+        )
     picked = exact_dot(values, table_ref[...], NN)
     lifted = local_ref[...]
     for corner in range(CORNERS_SUB):
@@ -306,7 +315,8 @@
         for dof in range(CORNER_DOF):
             operator = operators_ref[corner * CORNER_DOF + dof].astype(F32)
             lifted = lifted + operator * picked[dof : dof + 1, lanes]
-    lifted_ref[...] = lifted
+    if last:
+        extra_out[...] = lifted
     collect_to(lax.axis_index("sub") % 2 == 1, lifted, selector_ref[...], near_ref, far_ref)
 
 
@@ -388,8 +398,8 @@
     return jax.ShapeDtypeStruct(dims, dtype)
 
 
-def call(kernel, out_shape, count=0, scratch=(), flops=0, moved=0, name=None):
-    specs = [pl.BlockSpec(memory_space=pltpu.VMEM)] * count
+def call(kernel, out_shape, count=0, kept=0, scratch=(), flops=0, moved=0, name=None):
+    specs = [pl.BlockSpec(memory_space=pltpu.VMEM)] * count + [pl.BlockSpec(memory_space=pltpu.HBM)] * kept
     out_specs = jax.tree.map(lambda _: pl.BlockSpec(memory_space=pltpu.VMEM), out_shape)
     return pl.pallas_call(
         kernel,
@@ -425,16 +435,22 @@
     group = owned * ranks
     corners = corner_index.reshape(1, CORNERS_SUB * cells)
 
-    selector, swap, table = call(
+    previous = shifted(right_side, 1)
+    large = (stiff, operators, right_side)
+    selector, swap, table, stiff, operators, right_side = call(
         table_kernel,
         (
             shape(2 * cells, cells, dtype=BF16),
             shape(cells, cells, dtype=BF16),
             shape(group, CORNERS_SUB * cells, dtype=BF16),
-        ),
-        count=6,
+        )
+        + tuple(jax.ShapeDtypeStruct(array.shape, array.dtype) for array in large),
+        count=3,
+        kept=LOADED,
+        scratch=[pltpu.SemaphoreType.DMA((LOADED,))],
+        moved=4 * iface * iface * cells,
         name="tables",
-    )(neighbour, stiff_column, corners, stiff, operators, right_side)
+    )(neighbour, stiff_column, corners, *(pltpu.with_memory_space_constraint(array, pltpu.HBM) for array in large))
 
     field = shape(iface, cells)
     pair = shape(2, iface, cells)
@@ -475,22 +491,21 @@
             name="coarse",
         )(coarse_inverse, dots, other, *arrivals)
         values = [solved] + [exchanged(solved, d) for d in range(1, ranks)]
-        far, near, dots, lifted = call(
-            lambda *refs: lift_kernel(ranks, *refs),
-            (field, field, rows, field),
+        far, near, extra = call(
+            lambda *refs: lift_kernel(ranks, not reduce, *refs),
+            (field, field, rows if reduce else field),
             count=4 + ranks,
             scratch=[pltpu.VMEM((ROWS, group), F32)],
             flops=2 * 24 * iface * cells,
             moved=2 * 24 * iface * cells + group * CORNERS_SUB * cells * 2,
             name="lift",
         )(local, operators, table, selector, *values)
-        return m, gap, near, far, dots, lifted
-
-    previous = shifted(right_side, 1)
+        return m, gap, near, far, extra
+
     far, near = call(
         first_kernel, (message, message), count=5, scratch=stiff_scratch, name="first", **stiff_cost
     )(right_side, previous, selector, swap, stiff)
-    u, gap_u, near, far, _, _ = apply_operator(near, far)
+    u, gap_u, near, far, _ = apply_operator(near, far)
     r = right_side
     from_far, from_near = swapped_far(far), swapped(near, 1)
     far, near, w = call(
@@ -505,7 +520,7 @@
     states = (jnp.zeros((ROWS, cells), F32), r, r, u, w, r, r, r, w, gap_u, r, r)
     outs = (rows, field, field, field, pair, field, field, field, pair, field, field, field, message, message)
     for step in range(ITERS - 2):
-        m, gap, near, far, dots, _ = apply_operator(near, far)
+        m, gap, near, far, dots = apply_operator(near, far)
         from_far, from_near, other = swapped_far(far), swapped(near, 1), swapped(dots, 4)
         bit = 8
         while bit < sub_count:
@@ -521,7 +536,7 @@
             **stiff_cost,
         )(far, near, from_far, from_near, dots, other, m, gap, selector, swap, stiff, *states)
     scalars, x, r, u, w, p, s, q, z, gap_u, gap_p, gap_q = states
-    m, gap, near, far, _, lifted = apply_operator(near, far, reduce=False)
+    m, gap, near, far, lifted = apply_operator(near, far, reduce=False)
     from_far, from_near = swapped_far(far), swapped(near, 1)
     parts = call(gram_kernel, shape(sub_count * ranks, 1, cells), count=13, name="gram")(
         r, u, w, p, s, q, z, m, gap_u, gap_p, gap_q, gap, lifted

time: 180 us -> 173 us (0.961)
  local copies, waits for them, and re-layouts: 8.3 us -> 2 us
    unnamed x22 -> x10, local copies, waits for them, and re-layouts: 8.3 us -> 2 us
    pallas_call x1, Pallas kernels: 0.23 us -> 2.51 us  [on_device(): call(table_kernel, (shape(2 * cells, cells, dtype=BF16), shape(cells, cel...]
    pallas_call x5, Pallas kernels: 5.19 us -> 3.29 us  [apply_operator(): call(lambda *refs: lift_kernel(ranks, not reduce, *refs), (field, field,...]
  transfers between devices with their start and end apart: 58 -> 58, of which waited for: 38 -> 38; matrix products, arithmetic and copies ran while one was open for 0% -> 0% of each run, Pallas kernels for 2% -> 3%
where the time goes in v8:
time: 173 us
  starting transfers between devices  102 us (59%)
  waiting for transfers between devices  30.1 us (17%)
  Pallas kernels  26.2 us (15%)
  blocking collectives  12.1 us (7%)
  local copies, waits for them, and re-layouts  2 us (1%)
    ppermute x17, starting transfers between devices, swapped(): lax.ppermute(block, 'sub', [(i, i ^ bit) for i in range(lax.axis_size('su...  48.4 us
    ppermute x30, starting transfers between devices, exchanged(): lax.ppermute(block, 'grp', [(i, i ^ distance) for i in range(lax.axis_siz...  44.1 us
    ppermute x30, waiting for transfers between devices, exchanged(): lax.ppermute(block, 'grp', [(i, i ^ distance) for i in range(lax.axis_siz...  20 us
    all_to_all x1, blocking collectives, on_device(): everyone = lax.all_to_all(parts, ('sub', 'grp'), 0, 0, tiled=True)  12.1 us
    ppermute x17, waiting for transfers between devices, swapped(): lax.ppermute(block, 'sub', [(i, i ^ bit) for i in range(lax.axis_size('su...  10.1 us
    ppermute x10, starting transfers between devices, swapped_far(): lax.ppermute(block, 'sub', [(i, i + 1 if i % 2 else i - 1) for i in inner])  6.81 us
    pallas_call x3, Pallas kernels, on_device(): call(lambda *refs, first=step == 0: middle_kernel(first, *refs), outs, co...  5.46 us
    pallas_call x5, Pallas kernels, apply_operator(): call(lambda *refs: coarse_kernel(ranks, *refs), piece, count=3 + ranks, s...  3.57 us
  transfers between devices with their start and end apart: 58, of which 38 were waited for; matrix products, arithmetic and copies ran while one was open for 0% of the time, Pallas kernels for 3%

profile of v8, /device:TPU:0, one launch (start us, length us, event | category | flops | bytes accessed | tf_op | source)
XLA Modules:
  0.0 173.0 jit_solution(5332271436715304214)
XLA Ops:
  0.6 2.4 %collective-permute-start = (f32[96,128]{1,0:T(8,128)}, f32[96,128]{1,0:T(8,128)S(1)}, u32[]{:S(2)}, u32[]{:S(2)}) collective-permute-start(f32[96,128]{1,0:T(8,128)} %bitcast.19), channel_id=1, source_target_pairs={{0,4},{4,8},{8,12},{12,16},{16,20},{20,24},{24,28},{1,5},{5,9},{9,... | collective-permute-start | bytes 147464 | tf_op jit(solution)/shard_map/ppermute | solution.py:381
  5.0 2.5 %tables.1 = (bf16[256,128]{1,0:T(8,128)(2,1)S(1)}, bf16[128,128]{1,0:T(8,128)(2,1)S(1)}, bf16[1024,512]{1,0:T(8,128)(2,1)S(1)}, bf16[2,96,96,128]{3,2,1,0:T(8,12...) custom-call(s32[1,128]{1,0:T(1,128)S(1)} %copy-done.3, s32[1,128]{1,0:T(1,128)S(1)} %copy-done.4, ...), custom_call_target="tpu_custom_call" | custom-call | bytes 4718592 | tf_op jit(solution)/shard_map/tables/pallas_call | solution.py:440
  9.9 3.9 %collective-permute-start.2 = (f32[104,128]{1,0:T(8,128)S(1)}, f32[104,128]{1,0:T(8,128)S(1)}, u32[]{:S(2)}, u32[]{:S(2)}) collective-permute-start(f32[104,128]{1,0:T(8,128)S(1)} %get-tuple-element.116.refs_1_), channel_id=1, source_target_pairs={{0,4},{4,0},{8,12},{12,8},{16,20},{20,16},{24,28},{28,24},{1,5},{5... | collective-permute-start | bytes 159752 | tf_op jit(solution)/shard_map/ppermute | solution.py:385
  15.4 2.5 %collective-permute-start.3 = (f32[8,256]{1,0:T(8,128)S(1)}, f32[8,256]{1,0:T(8,128)S(1)}, u32[]{:S(2)}, u32[]{:S(2)}) collective-permute-start(f32[8,256]{1,0:T(8,128)S(1)} %get-tuple-element.121), channel_id=1, source_target_pairs={{0,8},{4,12},{8,0},{12,4},{16,24},{20,28},{24,16},{28,20},{1,9},{5... | collective-permute-start | bytes 24584 | tf_op jit(solution)/shard_map/ppermute | solution.py:385
  17.9 3.6 %collective-permute-start.4 = (f32[8,256]{1,0:T(8,128)S(1)}, f32[8,256]{1,0:T(8,128)S(1)}, u32[]{:S(2)}, u32[]{:S(2)}) collective-permute-start(f32[8,256]{1,0:T(8,128)S(1)} %get-tuple-element.122), channel_id=1, source_target_pairs={{0,3},{1,2},{2,1},{3,0},{4,7},{5,6},{6,5},{7,4},{8,11},{9,10},{10,... | collective-permute-start | bytes 24584 | tf_op jit(solution)/shard_map/ppermute | solution.py:394
  23.4 2.7 %collective-permute-done.5.refs_4_ = f32[8,256]{1,0:T(8,128)S(1)} collective-permute-done((f32[8,256]{1,0:T(8,128)S(1)}, f32[8,256]{1,0:T(8,128)S(1)}, u32[]{:S(2)}, u32[]{:S(2)}) %collective-permute-start.5) | collective-permute-done | bytes 8224 | tf_op jit(solution)/shard_map/ppermute | solution.py:394
  28.9 2.3 %collective-permute-start.7 = (f32[8,256]{1,0:T(8,128)S(1)}, f32[8,256]{1,0:T(8,128)S(1)}, u32[]{:S(2)}, u32[]{:S(2)}) collective-permute-start(f32[8,256]{1,0:T(8,128)S(1)} %coarse.5.refs_4_), channel_id=1, source_target_pairs={{0,1},{1,0},{2,3},{3,2},{4,5},{5,4},{6,7},{7,6},{8,9},{9,8},{10,11... | collective-permute-start | bytes 24584 | tf_op jit(solution)/shard_map/ppermute | solution.py:394
  39.4 4.3 %collective-permute-start.13 = (f32[104,128]{1,0:T(8,128)S(1)}, f32[104,128]{1,0:T(8,128)S(1)}, u32[]{:S(2)}, u32[]{:S(2)}) collective-permute-start(f32[104,128]{1,0:T(8,128)S(1)} %get-tuple-element.130.refs_1_), channel_id=1, source_target_pairs={{0,4},{4,0},{8,12},{12,8},{16,20},{20,16},{24,28},{28,24},{1,5},{5... | collective-permute-start | bytes 159752 | tf_op jit(solution)/shard_map/ppermute | solution.py:385
  45.3 3.4 %collective-permute-start.14 = (f32[8,256]{1,0:T(8,128)S(1)}, f32[8,256]{1,0:T(8,128)S(1)}, u32[]{:S(2)}, u32[]{:S(2)}) collective-permute-start(f32[8,256]{1,0:T(8,128)S(1)} %get-tuple-element.133), channel_id=1, source_target_pairs={{0,8},{4,12},{8,0},{12,4},{16,24},{20,28},{24,16},{28,20},{1,9},{5... | collective-permute-start | bytes 24584 | tf_op jit(solution)/shard_map/ppermute | solution.py:385
  48.7 2.5 %collective-permute-start.15 = (f32[8,256]{1,0:T(8,128)S(1)}, f32[8,256]{1,0:T(8,128)S(1)}, u32[]{:S(2)}, u32[]{:S(2)}) collective-permute-start(f32[8,256]{1,0:T(8,128)S(1)} %get-tuple-element.134), channel_id=1, source_target_pairs={{0,3},{1,2},{2,1},{3,0},{4,7},{5,6},{6,5},{7,4},{8,11},{9,10},{10,... | collective-permute-start | bytes 24584 | tf_op jit(solution)/shard_map/ppermute | solution.py:394
  58.9 2.0 %collective-permute-start.18 = (f32[8,256]{1,0:T(8,128)S(1)}, f32[8,256]{1,0:T(8,128)S(1)}, u32[]{:S(2)}, u32[]{:S(2)}) collective-permute-start(f32[8,256]{1,0:T(8,128)S(1)} %coarse.6.refs_4_), channel_id=1, source_target_pairs={{0,1},{1,0},{2,3},{3,2},{4,5},{5,4},{6,7},{7,6},{8,9},{9,8},{10,11... | collective-permute-start | bytes 24584 | tf_op jit(solution)/shard_map/ppermute | solution.py:394
  65.4 3.7 %collective-permute-start.23 = (f32[8,128]{1,0:T(8,128)S(1)}, f32[8,128]{1,0:T(8,128)S(1)}, u32[]{:S(2)}, u32[]{:S(2)}) collective-permute-start(f32[8,128]{1,0:T(8,128)S(1)} %get-tuple-element.140.refs_4_), channel_id=1, source_target_pairs={{0,16},{4,20},{8,24},{12,28},{16,0},{20,4},{24,8},{28,12},{1,17},{... | collective-permute-start | bytes 12296 | tf_op jit(solution)/shard_map/ppermute | solution.py:385
  73.4 3.1 %collective-permute-start.25 = (f32[104,128]{1,0:T(8,128)S(1)}, f32[104,128]{1,0:T(8,128)S(1)}, u32[]{:S(2)}, u32[]{:S(2)}) collective-permute-start(f32[104,128]{1,0:T(8,128)S(1)} %get-tuple-element.144.refs_1_), channel_id=1, source_target_pairs={{0,4},{4,0},{8,12},{12,8},{16,20},{20,16},{24,28},{28,24},{1,5},{5... | collective-permute-start | bytes 159752 | tf_op jit(solution)/shard_map/ppermute | solution.py:385
  78.1 2.4 %collective-permute-start.26 = (f32[8,256]{1,0:T(8,128)S(1)}, f32[8,256]{1,0:T(8,128)S(1)}, u32[]{:S(2)}, u32[]{:S(2)}) collective-permute-start(f32[8,256]{1,0:T(8,128)S(1)} %get-tuple-element.147), channel_id=1, source_target_pairs={{0,8},{4,12},{8,0},{12,4},{16,24},{20,28},{24,16},{28,20},{1,9},{5... | collective-permute-start | bytes 24584 | tf_op jit(solution)/shard_map/ppermute | solution.py:385
  80.5 2.5 %collective-permute-start.27 = (f32[8,256]{1,0:T(8,128)S(1)}, f32[8,256]{1,0:T(8,128)S(1)}, u32[]{:S(2)}, u32[]{:S(2)}) collective-permute-start(f32[8,256]{1,0:T(8,128)S(1)} %get-tuple-element.148), channel_id=1, source_target_pairs={{0,3},{1,2},{2,1},{3,0},{4,7},{5,6},{6,5},{7,4},{8,11},{9,10},{10,... | collective-permute-start | bytes 24584 | tf_op jit(solution)/shard_map/ppermute | solution.py:394
  97.1 3.2 %collective-permute-start.35 = (f32[8,128]{1,0:T(8,128)S(1)}, f32[8,128]{1,0:T(8,128)S(1)}, u32[]{:S(2)}, u32[]{:S(2)}) collective-permute-start(f32[8,128]{1,0:T(8,128)S(1)} %get-tuple-element.154.refs_4_), channel_id=1, source_target_pairs={{0,16},{4,20},{8,24},{12,28},{16,0},{20,4},{24,8},{28,12},{1,17},{... | collective-permute-start | bytes 12296 | tf_op jit(solution)/shard_map/ppermute | solution.py:385
  104.4 3.0 %collective-permute-start.37 = (f32[104,128]{1,0:T(8,128)S(1)}, f32[104,128]{1,0:T(8,128)S(1)}, u32[]{:S(2)}, u32[]{:S(2)}) collective-permute-start(f32[104,128]{1,0:T(8,128)S(1)} %get-tuple-element.169.refs_1_), channel_id=1, source_target_pairs={{0,4},{4,0},{8,12},{12,8},{16,20},{20,16},{24,28},{28,24},{1,5},{5... | collective-permute-start | bytes 159752 | tf_op jit(solution)/shard_map/ppermute | solution.py:385
  108.9 2.5 %collective-permute-start.38 = (f32[8,256]{1,0:T(8,128)S(1)}, f32[8,256]{1,0:T(8,128)S(1)}, u32[]{:S(2)}, u32[]{:S(2)}) collective-permute-start(f32[8,256]{1,0:T(8,128)S(1)} %get-tuple-element.172), channel_id=1, source_target_pairs={{0,8},{4,12},{8,0},{12,4},{16,24},{20,28},{24,16},{28,20},{1,9},{5... | collective-permute-start | bytes 24584 | tf_op jit(solution)/shard_map/ppermute | solution.py:385
  111.4 2.5 %collective-permute-start.39 = (f32[8,256]{1,0:T(8,128)S(1)}, f32[8,256]{1,0:T(8,128)S(1)}, u32[]{:S(2)}, u32[]{:S(2)}) collective-permute-start(f32[8,256]{1,0:T(8,128)S(1)} %get-tuple-element.173), channel_id=1, source_target_pairs={{0,3},{1,2},{2,1},{3,0},{4,7},{5,6},{6,5},{7,4},{8,11},{9,10},{10,... | collective-permute-start | bytes 24584 | tf_op jit(solution)/shard_map/ppermute | solution.py:394
  128.1 3.3 %collective-permute-start.47 = (f32[8,128]{1,0:T(8,128)S(1)}, f32[8,128]{1,0:T(8,128)S(1)}, u32[]{:S(2)}, u32[]{:S(2)}) collective-permute-start(f32[8,128]{1,0:T(8,128)S(1)} %get-tuple-element.179.refs_4_), channel_id=1, source_target_pairs={{0,16},{4,20},{8,24},{12,28},{16,0},{20,4},{24,8},{28,12},{1,17},{... | collective-permute-start | bytes 12296 | tf_op jit(solution)/shard_map/ppermute | solution.py:385
  135.5 3.0 %collective-permute-start.49 = (f32[104,128]{1,0:T(8,128)S(1)}, f32[104,128]{1,0:T(8,128)S(1)}, u32[]{:S(2)}, u32[]{:S(2)}) collective-permute-start(f32[104,128]{1,0:T(8,128)S(1)} %get-tuple-element.201.refs_1_), channel_id=1, source_target_pairs={{0,4},{4,0},{8,12},{12,8},{16,20},{20,16},{24,28},{28,24},{1,5},{5... | collective-permute-start | bytes 159752 | tf_op jit(solution)/shard_map/ppermute | solution.py:385
  140.0 2.6 %collective-permute-start.50 = (f32[8,256]{1,0:T(8,128)S(1)}, f32[8,256]{1,0:T(8,128)S(1)}, u32[]{:S(2)}, u32[]{:S(2)}) collective-permute-start(f32[8,256]{1,0:T(8,128)S(1)} %get-tuple-element.209), channel_id=1, source_target_pairs={{0,3},{1,2},{2,1},{3,0},{4,7},{5,6},{6,5},{7,4},{8,11},{9,10},{10,... | collective-permute-start | bytes 24584 | tf_op jit(solution)/shard_map/ppermute | solution.py:394
  155.2 3.9 %collective-permute-start.57 = (f32[96,128]{1,0:T(8,128)S(1)}, f32[96,128]{1,0:T(8,128)S(1)}, u32[]{:S(2)}, u32[]{:S(2)}) collective-permute-start(f32[96,128]{1,0:T(8,128)S(1)} %get-tuple-element.217.near_ref), channel_id=1, source_target_pairs={{0,4},{4,0},{8,12},{12,8},{16,20},{20,16},{24,28},{28,24},{1,5},{5... | collective-permute-start | bytes 147464 | tf_op jit(solution)/shard_map/ppermute | solution.py:385
  159.3 12.1 %all_to_all.5.dots_ref = f32[32,1,128]{2,1,0:T(1,128)S(1)} all-to-all(f32[32,1,128]{2,1,0:T(1,128)S(1)} %gram.1), channel_id=1, replica_groups=mesh['sub'=8,'grp'=4] {'sub','grp'}, dimensions={0} | all-to-all | bytes 32768 | tf_op jit(solution)/shard_map/all_to_all | solution.py:544
  (132 shorter events, 92.0 us)
Async XLA Ops:
  0.6 6.9 %collective-permute-start = (f32[96,128]{1,0:T(8,128)}, f32[96,128]{1,0:T(8,128)S(1)}, u32[]{:S(2)}, u32[]{:S(2)}) collective-permute-start(f32[96,128]{1,0:T(8,128)} %bitcast.19), channel_id=1, source_target_pairs={{0,4},{4,8},{8,12},{12,16},{16,20},{20,24},{24,28},{1,5},{5,9},{9,... | collective-permute-start | bytes 147464 | tf_op jit(solution)/shard_map/ppermute | solution.py:381
  15.4 6.9 %collective-permute-start.3 = (f32[8,256]{1,0:T(8,128)S(1)}, f32[8,256]{1,0:T(8,128)S(1)}, u32[]{:S(2)}, u32[]{:S(2)}) collective-permute-start(f32[8,256]{1,0:T(8,128)S(1)} %get-tuple-element.121), channel_id=1, source_target_pairs={{0,8},{4,12},{8,0},{12,4},{16,24},{20,28},{24,16},{28,20},{1,9},{5... | collective-permute-start | bytes 24584 | tf_op jit(solution)/shard_map/ppermute | solution.py:385
  17.9 5.4 %collective-permute-start.4 = (f32[8,256]{1,0:T(8,128)S(1)}, f32[8,256]{1,0:T(8,128)S(1)}, u32[]{:S(2)}, u32[]{:S(2)}) collective-permute-start(f32[8,256]{1,0:T(8,128)S(1)} %get-tuple-element.122), channel_id=1, source_target_pairs={{0,3},{1,2},{2,1},{3,0},{4,7},{5,6},{6,5},{7,4},{8,11},{9,10},{10,... | collective-permute-start | bytes 24584 | tf_op jit(solution)/shard_map/ppermute | solution.py:394
  26.8 5.5 %collective-permute-start.9 = (f32[8,256]{1,0:T(8,128)S(1)}, f32[8,256]{1,0:T(8,128)S(1)}, u32[]{:S(2)}, u32[]{:S(2)}) collective-permute-start(f32[8,256]{1,0:T(8,128)S(1)} %coarse.5.refs_4_), channel_id=1, source_target_pairs={{0,3},{1,2},{2,1},{3,0},{4,7},{5,6},{6,5},{7,4},{8,11},{9,10},{10,... | collective-permute-start | bytes 24584 | tf_op jit(solution)/shard_map/ppermute | solution.py:394
  45.3 7.8 %collective-permute-start.14 = (f32[8,256]{1,0:T(8,128)S(1)}, f32[8,256]{1,0:T(8,128)S(1)}, u32[]{:S(2)}, u32[]{:S(2)}) collective-permute-start(f32[8,256]{1,0:T(8,128)S(1)} %get-tuple-element.133), channel_id=1, source_target_pairs={{0,8},{4,12},{8,0},{12,4},{16,24},{20,28},{24,16},{28,20},{1,9},{5... | collective-permute-start | bytes 24584 | tf_op jit(solution)/shard_map/ppermute | solution.py:385
  48.7 5.4 %collective-permute-start.15 = (f32[8,256]{1,0:T(8,128)S(1)}, f32[8,256]{1,0:T(8,128)S(1)}, u32[]{:S(2)}, u32[]{:S(2)}) collective-permute-start(f32[8,256]{1,0:T(8,128)S(1)} %get-tuple-element.134), channel_id=1, source_target_pairs={{0,3},{1,2},{2,1},{3,0},{4,7},{5,6},{6,5},{7,4},{8,11},{9,10},{10,... | collective-permute-start | bytes 24584 | tf_op jit(solution)/shard_map/ppermute | solution.py:394
  56.5 5.5 %collective-permute-start.20 = (f32[8,256]{1,0:T(8,128)S(1)}, f32[8,256]{1,0:T(8,128)S(1)}, u32[]{:S(2)}, u32[]{:S(2)}) collective-permute-start(f32[8,256]{1,0:T(8,128)S(1)} %coarse.6.refs_4_), channel_id=1, source_target_pairs={{0,3},{1,2},{2,1},{3,0},{4,7},{5,6},{6,5},{7,4},{8,11},{9,10},{10,... | collective-permute-start | bytes 24584 | tf_op jit(solution)/shard_map/ppermute | solution.py:394
  63.2 7.6 %collective-permute-start.21 = (f32[96,128]{1,0:T(8,128)S(1)}, f32[96,128]{1,0:T(8,128)S(1)}, u32[]{:S(2)}, u32[]{:S(2)}) collective-permute-start(f32[96,128]{1,0:T(8,128)S(1)} %get-tuple-element.138.refs_0_), channel_id=1, source_target_pairs={{4,8},{8,4},{12,16},{16,12},{20,24},{24,20},{5,9},{9,5},{13,17},{1... | collective-permute-start | bytes 147464 | tf_op jit(solution)/shard_map/ppermute | solution.py:390
  63.8 6.9 %collective-permute-start.22 = (f32[96,128]{1,0:T(8,128)S(1)}, f32[96,128]{1,0:T(8,128)S(1)}, u32[]{:S(2)}, u32[]{:S(2)}) collective-permute-start(f32[96,128]{1,0:T(8,128)S(1)} %get-tuple-element.139.refs_1_), channel_id=1, source_target_pairs={{0,4},{4,0},{8,12},{12,8},{16,20},{20,16},{24,28},{28,24},{1,5},{5... | collective-permute-start | bytes 147464 | tf_op jit(solution)/shard_map/ppermute | solution.py:385
  65.4 5.3 %collective-permute-start.23 = (f32[8,128]{1,0:T(8,128)S(1)}, f32[8,128]{1,0:T(8,128)S(1)}, u32[]{:S(2)}, u32[]{:S(2)}) collective-permute-start(f32[8,128]{1,0:T(8,128)S(1)} %get-tuple-element.140.refs_4_), channel_id=1, source_target_pairs={{0,16},{4,20},{8,24},{12,28},{16,0},{20,4},{24,8},{28,12},{1,17},{... | collective-permute-start | bytes 12296 | tf_op jit(solution)/shard_map/ppermute | solution.py:385
  78.1 6.8 %collective-permute-start.26 = (f32[8,256]{1,0:T(8,128)S(1)}, f32[8,256]{1,0:T(8,128)S(1)}, u32[]{:S(2)}, u32[]{:S(2)}) collective-permute-start(f32[8,256]{1,0:T(8,128)S(1)} %get-tuple-element.147), channel_id=1, source_target_pairs={{0,8},{4,12},{8,0},{12,4},{16,24},{20,28},{24,16},{28,20},{1,9},{5... | collective-permute-start | bytes 24584 | tf_op jit(solution)/shard_map/ppermute | solution.py:385
  80.5 5.4 %collective-permute-start.27 = (f32[8,256]{1,0:T(8,128)S(1)}, f32[8,256]{1,0:T(8,128)S(1)}, u32[]{:S(2)}, u32[]{:S(2)}) collective-permute-start(f32[8,256]{1,0:T(8,128)S(1)} %get-tuple-element.148), channel_id=1, source_target_pairs={{0,3},{1,2},{2,1},{3,0},{4,7},{5,6},{6,5},{7,4},{8,11},{9,10},{10,... | collective-permute-start | bytes 24584 | tf_op jit(solution)/shard_map/ppermute | solution.py:394
  88.3 5.5 %collective-permute-start.32 = (f32[8,256]{1,0:T(8,128)S(1)}, f32[8,256]{1,0:T(8,128)S(1)}, u32[]{:S(2)}, u32[]{:S(2)}) collective-permute-start(f32[8,256]{1,0:T(8,128)S(1)} %coarse.7.refs_4_), channel_id=1, source_target_pairs={{0,3},{1,2},{2,1},{3,0},{4,7},{5,6},{6,5},{7,4},{8,11},{9,10},{10,... | collective-permute-start | bytes 24584 | tf_op jit(solution)/shard_map/ppermute | solution.py:394
  94.9 6.9 %collective-permute-start.33 = (f32[96,128]{1,0:T(8,128)S(1)}, f32[96,128]{1,0:T(8,128)S(1)}, u32[]{:S(2)}, u32[]{:S(2)}) collective-permute-start(f32[96,128]{1,0:T(8,128)S(1)} %get-tuple-element.152.refs_0_), channel_id=1, source_target_pairs={{4,8},{8,4},{12,16},{16,12},{20,24},{24,20},{5,9},{9,5},{13,17},{1... | collective-permute-start | bytes 147464 | tf_op jit(solution)/shard_map/ppermute | solution.py:390
  95.6 6.2 %collective-permute-start.34 = (f32[96,128]{1,0:T(8,128)S(1)}, f32[96,128]{1,0:T(8,128)S(1)}, u32[]{:S(2)}, u32[]{:S(2)}) collective-permute-start(f32[96,128]{1,0:T(8,128)S(1)} %get-tuple-element.153.refs_1_), channel_id=1, source_target_pairs={{0,4},{4,0},{8,12},{12,8},{16,20},{20,16},{24,28},{28,24},{1,5},{5... | collective-permute-start | bytes 147464 | tf_op jit(solution)/shard_map/ppermute | solution.py:385
  108.9 6.9 %collective-permute-start.38 = (f32[8,256]{1,0:T(8,128)S(1)}, f32[8,256]{1,0:T(8,128)S(1)}, u32[]{:S(2)}, u32[]{:S(2)}) collective-permute-start(f32[8,256]{1,0:T(8,128)S(1)} %get-tuple-element.172), channel_id=1, source_target_pairs={{0,8},{4,12},{8,0},{12,4},{16,24},{20,28},{24,16},{28,20},{1,9},{5... | collective-permute-start | bytes 24584 | tf_op jit(solution)/shard_map/ppermute | solution.py:385
  111.4 5.4 %collective-permute-start.39 = (f32[8,256]{1,0:T(8,128)S(1)}, f32[8,256]{1,0:T(8,128)S(1)}, u32[]{:S(2)}, u32[]{:S(2)}) collective-permute-start(f32[8,256]{1,0:T(8,128)S(1)} %get-tuple-element.173), channel_id=1, source_target_pairs={{0,3},{1,2},{2,1},{3,0},{4,7},{5,6},{6,5},{7,4},{8,11},{9,10},{10,... | collective-permute-start | bytes 24584 | tf_op jit(solution)/shard_map/ppermute | solution.py:394
  119.3 5.5 %collective-permute-start.44 = (f32[8,256]{1,0:T(8,128)S(1)}, f32[8,256]{1,0:T(8,128)S(1)}, u32[]{:S(2)}, u32[]{:S(2)}) collective-permute-start(f32[8,256]{1,0:T(8,128)S(1)} %coarse.8.refs_4_), channel_id=1, source_target_pairs={{0,3},{1,2},{2,1},{3,0},{4,7},{5,6},{6,5},{7,4},{8,11},{9,10},{10,... | collective-permute-start | bytes 24584 | tf_op jit(solution)/shard_map/ppermute | solution.py:394
  125.9 7.1 %collective-permute-start.45 = (f32[96,128]{1,0:T(8,128)S(1)}, f32[96,128]{1,0:T(8,128)S(1)}, u32[]{:S(2)}, u32[]{:S(2)}) collective-permute-start(f32[96,128]{1,0:T(8,128)S(1)} %get-tuple-element.177.refs_0_), channel_id=1, source_target_pairs={{4,8},{8,4},{12,16},{16,12},{20,24},{24,20},{5,9},{9,5},{13,17},{1... | collective-permute-start | bytes 147464 | tf_op jit(solution)/shard_map/ppermute | solution.py:390
  126.6 6.4 %collective-permute-start.46 = (f32[96,128]{1,0:T(8,128)S(1)}, f32[96,128]{1,0:T(8,128)S(1)}, u32[]{:S(2)}, u32[]{:S(2)}) collective-permute-start(f32[96,128]{1,0:T(8,128)S(1)} %get-tuple-element.178.refs_1_), channel_id=1, source_target_pairs={{0,4},{4,0},{8,12},{12,8},{16,20},{20,16},{24,28},{28,24},{1,5},{5... | collective-permute-start | bytes 147464 | tf_op jit(solution)/shard_map/ppermute | solution.py:385
  140.0 5.5 %collective-permute-start.50 = (f32[8,256]{1,0:T(8,128)S(1)}, f32[8,256]{1,0:T(8,128)S(1)}, u32[]{:S(2)}, u32[]{:S(2)}) collective-permute-start(f32[8,256]{1,0:T(8,128)S(1)} %get-tuple-element.209), channel_id=1, source_target_pairs={{0,3},{1,2},{2,1},{3,0},{4,7},{5,6},{6,5},{7,4},{8,11},{9,10},{10,... | collective-permute-start | bytes 24584 | tf_op jit(solution)/shard_map/ppermute | solution.py:394
  147.9 5.5 %collective-permute-start.55 = (f32[8,256]{1,0:T(8,128)S(1)}, f32[8,256]{1,0:T(8,128)S(1)}, u32[]{:S(2)}, u32[]{:S(2)}) collective-permute-start(f32[8,256]{1,0:T(8,128)S(1)} %coarse.9.refs_4_), channel_id=1, source_target_pairs={{0,3},{1,2},{2,1},{3,0},{4,7},{5,6},{6,5},{7,4},{8,11},{9,10},{10,... | collective-permute-start | bytes 24584 | tf_op jit(solution)/shard_map/ppermute | solution.py:394
  154.5 16.9 %collective-permute-start.56 = (f32[96,128]{1,0:T(8,128)S(1)}, f32[96,128]{1,0:T(8,128)S(1)}, u32[]{:S(2)}, u32[]{:S(2)}) collective-permute-start(f32[96,128]{1,0:T(8,128)S(1)} %get-tuple-element.216.far_ref), channel_id=1, source_target_pairs={{4,8},{8,4},{12,16},{16,12},{20,24},{24,20},{5,9},{9,5},{13,17},{1... | collective-permute-start | bytes 147464 | tf_op jit(solution)/shard_map/ppermute | solution.py:390
  155.2 16.2 %collective-permute-start.57 = (f32[96,128]{1,0:T(8,128)S(1)}, f32[96,128]{1,0:T(8,128)S(1)}, u32[]{:S(2)}, u32[]{:S(2)}) collective-permute-start(f32[96,128]{1,0:T(8,128)S(1)} %get-tuple-element.217.near_ref), channel_id=1, source_target_pairs={{0,4},{4,0},{8,12},{12,8},{16,20},{20,16},{24,28},{28,24},{1,5},{5... | collective-permute-start | bytes 147464 | tf_op jit(solution)/shard_map/ppermute | solution.py:385
  (39 other events, 184.7 us)

commit v9 on v8

--- a/solution.py
+++ b/solution.py
@@ -88,12 +88,15 @@
     lax.fori_loop(0, out_ref.shape[0] // ROWS, step, 0, unroll=True)
 
 
-def table_kernel(neighbour_ref, column_ref, corner_ref, *refs):
-    sources, sems = refs[:LOADED], refs[-1]
-    (selector_ref, swap_ref, table_ref), targets = refs[LOADED : LOADED + 3], refs[LOADED + 3 : -1]
-    copies = [pltpu.make_async_copy(sources[k], targets[k], sems.at[k]) for k in range(LOADED)]
+def table_kernel(*refs):
+    sources, (selector_ref, swap_ref, table_ref), sems = refs[: LOADED + 3], refs[LOADED + 3 : LOADED + 6], refs[-1]
+    neighbour_ref, column_ref, corner_ref = refs[-4:-1]
+    targets = refs[-4:-1] + refs[LOADED + 6 : -4]
+    copies = [pltpu.make_async_copy(sources[k], targets[k], sems.at[k]) for k in range(LOADED + 3)]
     for copy in copies:
         copy.start()
+    for copy in copies[:3]:
+        copy.wait()
     cells = swap_ref.shape[0]
     start = lax.axis_index("sub") * cells
 
@@ -113,7 +116,7 @@
         return carry
 
     lax.fori_loop(0, table_ref.shape[0] // chunk, step, 0)
-    for copy in copies:
+    for copy in copies[3:]:
         copy.wait()
 
 
@@ -286,19 +289,19 @@
     solved_ref[...] = jnp.concatenate(rows, axis=0)
 
 
-def lift_kernel(ranks, last, local_ref, operators_ref, table_ref, selector_ref, *rest):
-    pieces, (far_ref, near_ref, extra_out, values_ref) = rest[:ranks], rest[ranks:]
+def lift_kernel(ranks, extra, local_ref, operators_ref, table_ref, selector_ref, *rest):
+    pieces, (far_ref, near_ref), (*extra_out, values_ref) = rest[:ranks], rest[ranks : ranks + 2], rest[ranks + 2 :]
     cells = local_ref.shape[1]
     owned = values_ref.shape[1] // ranks
     for distance in range(ranks):
         rank = lax.axis_index("grp") ^ distance
         values_ref[:, pl.ds(pl.multiple_of(rank * owned, 128), owned)] = pieces[distance][...]
     values = values_ref[...]
-    if not last:
+    if extra == "dots":
         tail = values[CORNER_DOF:, :owned]
         for rank in range(1, ranks):
             tail = tail + values[CORNER_DOF:, rank * owned : (rank + 1) * owned]
-        extra_out[...] = jnp.concatenate(
+        extra_out[0][...] = jnp.concatenate(
             [
                 tail[0:1, :cells],
                 tail[0:1, cells : 2 * cells],
@@ -315,8 +318,8 @@
         for dof in range(CORNER_DOF):
             operator = operators_ref[corner * CORNER_DOF + dof].astype(F32)
             lifted = lifted + operator * picked[dof : dof + 1, lanes]
-    if last:
-        extra_out[...] = lifted
+    if extra == "lifted":
+        extra_out[0][...] = lifted
     collect_to(lax.axis_index("sub") % 2 == 1, lifted, selector_ref[...], near_ref, far_ref)
 
 
@@ -436,6 +439,7 @@
     corners = corner_index.reshape(1, CORNERS_SUB * cells)
 
     previous = shifted(right_side, 1)
+    indices = (neighbour, stiff_column, corners)
     large = (stiff, operators, right_side)
     selector, swap, table, stiff, operators, right_side = call(
         table_kernel,
@@ -445,12 +449,11 @@
             shape(group, CORNERS_SUB * cells, dtype=BF16),
         )
         + tuple(jax.ShapeDtypeStruct(array.shape, array.dtype) for array in large),
-        count=3,
-        kept=LOADED,
-        scratch=[pltpu.SemaphoreType.DMA((LOADED,))],
+        kept=3 + LOADED,
+        scratch=[pltpu.VMEM(array.shape, jnp.int32) for array in indices] + [pltpu.SemaphoreType.DMA((3 + LOADED,))],
         moved=4 * iface * iface * cells,
         name="tables",
-    )(neighbour, stiff_column, corners, *(pltpu.with_memory_space_constraint(array, pltpu.HBM) for array in large))
+    )(*(pltpu.with_memory_space_constraint(array, pltpu.HBM) for array in indices + large))
 
     field = shape(iface, cells)
     pair = shape(2, iface, cells)
@@ -460,7 +463,7 @@
     stiff_scratch = [pltpu.VMEM((iface, cells), F32)]
     stiff_cost = dict(flops=4 * iface * iface * cells, moved=4 * iface * iface * cells)
 
-    def apply_operator(near, far, reduce=True):
+    def apply_operator(near, far, extra):
         from_far, from_near = swapped_far(far), swapped(near, 1)
         m, gap, sent, *parts, dots = call(
             lambda *refs: corner_kernel(ranks, *refs),
@@ -480,7 +483,7 @@
             moved=2 * iface * iface * cells,
             name="local",
         )(gap, inverse)
-        other = swapped(sent, 2) if reduce else sent
+        other = swapped(sent, 2) if extra == "dots" else sent
         solved = call(
             lambda *refs: coarse_kernel(ranks, *refs),
             piece,
@@ -491,21 +494,21 @@
             name="coarse",
         )(coarse_inverse, dots, other, *arrivals)
         values = [solved] + [exchanged(solved, d) for d in range(1, ranks)]
-        far, near, extra = call(
-            lambda *refs: lift_kernel(ranks, not reduce, *refs),
-            (field, field, rows if reduce else field),
+        far, near, *result = call(
+            lambda *refs: lift_kernel(ranks, extra, *refs),
+            (field, field) + {"": (), "dots": (rows,), "lifted": (field,)}[extra],
             count=4 + ranks,
             scratch=[pltpu.VMEM((ROWS, group), F32)],
             flops=2 * 24 * iface * cells,
             moved=2 * 24 * iface * cells + group * CORNERS_SUB * cells * 2,
             name="lift",
         )(local, operators, table, selector, *values)
-        return m, gap, near, far, extra
+        return m, gap, near, far, *result
 
     far, near = call(
         first_kernel, (message, message), count=5, scratch=stiff_scratch, name="first", **stiff_cost
     )(right_side, previous, selector, swap, stiff)
-    u, gap_u, near, far, _ = apply_operator(near, far)
+    u, gap_u, near, far = apply_operator(near, far, "")
     r = right_side
     from_far, from_near = swapped_far(far), swapped(near, 1)
     far, near, w = call(
@@ -520,7 +523,7 @@
     states = (jnp.zeros((ROWS, cells), F32), r, r, u, w, r, r, r, w, gap_u, r, r)
     outs = (rows, field, field, field, pair, field, field, field, pair, field, field, field, message, message)
     for step in range(ITERS - 2):
-        m, gap, near, far, dots = apply_operator(near, far)
+        m, gap, near, far, dots = apply_operator(near, far, "dots")
         from_far, from_near, other = swapped_far(far), swapped(near, 1), swapped(dots, 4)
         bit = 8
         while bit < sub_count:
@@ -536,7 +539,7 @@
             **stiff_cost,
         )(far, near, from_far, from_near, dots, other, m, gap, selector, swap, stiff, *states)
     scalars, x, r, u, w, p, s, q, z, gap_u, gap_p, gap_q = states
-    m, gap, near, far, lifted = apply_operator(near, far, reduce=False)
+    m, gap, near, far, lifted = apply_operator(near, far, "lifted")
     from_far, from_near = swapped_far(far), swapped(near, 1)
     parts = call(gram_kernel, shape(sub_count * ranks, 1, cells), count=13, name="gram")(
         r, u, w, p, s, q, z, m, gap_u, gap_p, gap_q, gap, lifted

time: 173 us -> 172 us (level)
  local copies, waits for them, and re-layouts: 2 us -> 0.01 us
    unnamed x10 -> x4, local copies, waits for them, and re-layouts: 2 us -> 0.01 us
    ppermute x17 -> x16, starting transfers between devices: 48.4 us -> 49.7 us  [swapped(): lax.ppermute(block, 'sub', [(i, i ^ bit) for i in range(lax.axis_size('su...]
    ppermute x17 -> x16, waiting for transfers between devices: 10.1 us -> 10.1 us  [swapped(): lax.ppermute(block, 'sub', [(i, i ^ bit) for i in range(lax.axis_size('su...]
  transfers between devices with their start and end apart: 58 -> 57, of which waited for: 38 -> 37; matrix products, arithmetic and copies ran while one was open for 0% -> 0% of each run, Pallas kernels for 3% -> 3%
where the time goes in v9:
time: 172 us
  starting transfers between devices  103 us (60%)
  waiting for transfers between devices  30.1 us (18%)
  Pallas kernels  25.7 us (15%)
  blocking collectives  12.1 us (7%)
    ppermute x16, starting transfers between devices, swapped(): lax.ppermute(block, 'sub', [(i, i ^ bit) for i in range(lax.axis_size('su...  49.7 us
    ppermute x30, starting transfers between devices, exchanged(): lax.ppermute(block, 'grp', [(i, i ^ distance) for i in range(lax.axis_siz...  44.1 us
    ppermute x30, waiting for transfers between devices, exchanged(): lax.ppermute(block, 'grp', [(i, i ^ distance) for i in range(lax.axis_siz...  20 us
    all_to_all x1, blocking collectives, on_device(): everyone = lax.all_to_all(parts, ('sub', 'grp'), 0, 0, tiled=True)  12.1 us
    ppermute x16, waiting for transfers between devices, swapped(): lax.ppermute(block, 'sub', [(i, i ^ bit) for i in range(lax.axis_size('su...  10.1 us
    ppermute x10, starting transfers between devices, swapped_far(): lax.ppermute(block, 'sub', [(i, i + 1 if i % 2 else i - 1) for i in inner])  6.82 us
    pallas_call x3, Pallas kernels, on_device(): call(lambda *refs, first=step == 0: middle_kernel(first, *refs), outs, co...  5.43 us
    pallas_call x5, Pallas kernels, apply_operator(): call(lambda *refs: coarse_kernel(ranks, *refs), piece, count=3 + ranks, s...  3.57 us
  transfers between devices with their start and end apart: 57, of which 37 were waited for; matrix products, arithmetic and copies ran while one was open for 0% of the time, Pallas kernels for 3%

profile of v9, /device:TPU:0, one launch (start us, length us, event | category | flops | bytes accessed | tf_op | source)
XLA Modules:
  0.0 171.9 jit_solution(13607742980604513716)
XLA Ops:
  0.6 2.4 %collective-permute-start = (f32[96,128]{1,0:T(8,128)}, f32[96,128]{1,0:T(8,128)S(1)}, u32[]{:S(2)}, u32[]{:S(2)}) collective-permute-start(f32[96,128]{1,0:T(8,128)} %bitcast.18), channel_id=1, source_target_pairs={{0,4},{4,8},{8,12},{12,16},{16,20},{20,24},{24,28},{1,5},{5,9},{9,... | collective-permute-start | bytes 147464 | tf_op jit(solution)/shard_map/ppermute | solution.py:384
  3.0 2.6 %tables.1 = (bf16[256,128]{1,0:T(8,128)(2,1)S(1)}, bf16[128,128]{1,0:T(8,128)(2,1)S(1)}, bf16[1024,512]{1,0:T(8,128)(2,1)S(1)}, bf16[2,96,96,128]{3,2,1,0:T(8,12...) custom-call(s32[1,128]{1,0:T(1,128)} %refs_0_.6, s32[1,128]{1,0:T(1,128)} %refs_1_.1, ...), custom_call_target="tpu_custom_call" | custom-call | bytes 4718592 | tf_op jit(solution)/shard_map/tables/pallas_call | solution.py:444
  8.0 5.0 %collective-permute-start.2 = (f32[104,128]{1,0:T(8,128)S(1)}, f32[104,128]{1,0:T(8,128)S(1)}, u32[]{:S(2)}, u32[]{:S(2)}) collective-permute-start(f32[104,128]{1,0:T(8,128)S(1)} %get-tuple-element.116.refs_1_), channel_id=1, source_target_pairs={{0,4},{4,0},{8,12},{12,8},{16,20},{20,16},{24,28},{28,24},{1,5},{5... | collective-permute-start | bytes 159752 | tf_op jit(solution)/shard_map/ppermute | solution.py:388
  14.5 3.7 %collective-permute-start.3 = (f32[8,256]{1,0:T(8,128)S(1)}, f32[8,256]{1,0:T(8,128)S(1)}, u32[]{:S(2)}, u32[]{:S(2)}) collective-permute-start(f32[8,256]{1,0:T(8,128)S(1)} %get-tuple-element.122), channel_id=1, source_target_pairs={{0,3},{1,2},{2,1},{3,0},{4,7},{5,6},{6,5},{7,4},{8,11},{9,10},{10,... | collective-permute-start | bytes 24584 | tf_op jit(solution)/shard_map/ppermute | solution.py:397
  20.0 2.7 %collective-permute-done.4.refs_4_ = f32[8,256]{1,0:T(8,128)S(1)} collective-permute-done((f32[8,256]{1,0:T(8,128)S(1)}, f32[8,256]{1,0:T(8,128)S(1)}, u32[]{:S(2)}, u32[]{:S(2)}) %collective-permute-start.4) | collective-permute-done | bytes 8224 | tf_op jit(solution)/shard_map/ppermute | solution.py:397
  25.7 2.2 %collective-permute-start.6 = (f32[8,256]{1,0:T(8,128)S(1)}, f32[8,256]{1,0:T(8,128)S(1)}, u32[]{:S(2)}, u32[]{:S(2)}) collective-permute-start(f32[8,256]{1,0:T(8,128)S(1)} %coarse.5.refs_4_), channel_id=1, source_target_pairs={{0,1},{1,0},{2,3},{3,2},{4,5},{5,4},{6,7},{7,6},{8,9},{9,8},{10,11... | collective-permute-start | bytes 24584 | tf_op jit(solution)/shard_map/ppermute | solution.py:397
  30.8 3.9 %collective-permute-start.10 = (f32[96,128]{1,0:T(8,128)S(1)}, f32[96,128]{1,0:T(8,128)S(1)}, u32[]{:S(2)}, u32[]{:S(2)}) collective-permute-start(f32[96,128]{1,0:T(8,128)S(1)} %get-tuple-element.127.near_ref), channel_id=1, source_target_pairs={{0,4},{4,0},{8,12},{12,8},{16,20},{20,16},{24,28},{28,24},{1,5},{5... | collective-permute-start | bytes 147464 | tf_op jit(solution)/shard_map/ppermute | solution.py:388
  38.0 4.7 %collective-permute-start.12 = (f32[104,128]{1,0:T(8,128)S(1)}, f32[104,128]{1,0:T(8,128)S(1)}, u32[]{:S(2)}, u32[]{:S(2)}) collective-permute-start(f32[104,128]{1,0:T(8,128)S(1)} %get-tuple-element.130.refs_1_), channel_id=1, source_target_pairs={{0,4},{4,0},{8,12},{12,8},{16,20},{20,16},{24,28},{28,24},{1,5},{5... | collective-permute-start | bytes 159752 | tf_op jit(solution)/shard_map/ppermute | solution.py:388
  44.2 3.4 %collective-permute-start.13 = (f32[8,256]{1,0:T(8,128)S(1)}, f32[8,256]{1,0:T(8,128)S(1)}, u32[]{:S(2)}, u32[]{:S(2)}) collective-permute-start(f32[8,256]{1,0:T(8,128)S(1)} %get-tuple-element.133), channel_id=1, source_target_pairs={{0,8},{4,12},{8,0},{12,4},{16,24},{20,28},{24,16},{28,20},{1,9},{5... | collective-permute-start | bytes 24584 | tf_op jit(solution)/shard_map/ppermute | solution.py:388
  47.6 2.5 %collective-permute-start.14 = (f32[8,256]{1,0:T(8,128)S(1)}, f32[8,256]{1,0:T(8,128)S(1)}, u32[]{:S(2)}, u32[]{:S(2)}) collective-permute-start(f32[8,256]{1,0:T(8,128)S(1)} %get-tuple-element.134), channel_id=1, source_target_pairs={{0,3},{1,2},{2,1},{3,0},{4,7},{5,6},{6,5},{7,4},{8,11},{9,10},{10,... | collective-permute-start | bytes 24584 | tf_op jit(solution)/shard_map/ppermute | solution.py:397
  64.3 3.9 %collective-permute-start.22 = (f32[8,128]{1,0:T(8,128)S(1)}, f32[8,128]{1,0:T(8,128)S(1)}, u32[]{:S(2)}, u32[]{:S(2)}) collective-permute-start(f32[8,128]{1,0:T(8,128)S(1)} %get-tuple-element.140.refs_4_), channel_id=1, source_target_pairs={{0,16},{4,20},{8,24},{12,28},{16,0},{20,4},{24,8},{28,12},{1,17},{... | collective-permute-start | bytes 12296 | tf_op jit(solution)/shard_map/ppermute | solution.py:388
  72.4 3.0 %collective-permute-start.24 = (f32[104,128]{1,0:T(8,128)S(1)}, f32[104,128]{1,0:T(8,128)S(1)}, u32[]{:S(2)}, u32[]{:S(2)}) collective-permute-start(f32[104,128]{1,0:T(8,128)S(1)} %get-tuple-element.144.refs_1_), channel_id=1, source_target_pairs={{0,4},{4,0},{8,12},{12,8},{16,20},{20,16},{24,28},{28,24},{1,5},{5... | collective-permute-start | bytes 159752 | tf_op jit(solution)/shard_map/ppermute | solution.py:388
  76.9 2.4 %collective-permute-start.25 = (f32[8,256]{1,0:T(8,128)S(1)}, f32[8,256]{1,0:T(8,128)S(1)}, u32[]{:S(2)}, u32[]{:S(2)}) collective-permute-start(f32[8,256]{1,0:T(8,128)S(1)} %get-tuple-element.147), channel_id=1, source_target_pairs={{0,8},{4,12},{8,0},{12,4},{16,24},{20,28},{24,16},{28,20},{1,9},{5... | collective-permute-start | bytes 24584 | tf_op jit(solution)/shard_map/ppermute | solution.py:388
  79.3 2.5 %collective-permute-start.26 = (f32[8,256]{1,0:T(8,128)S(1)}, f32[8,256]{1,0:T(8,128)S(1)}, u32[]{:S(2)}, u32[]{:S(2)}) collective-permute-start(f32[8,256]{1,0:T(8,128)S(1)} %get-tuple-element.148), channel_id=1, source_target_pairs={{0,3},{1,2},{2,1},{3,0},{4,7},{5,6},{6,5},{7,4},{8,11},{9,10},{10,... | collective-permute-start | bytes 24584 | tf_op jit(solution)/shard_map/ppermute | solution.py:397
  95.9 3.3 %collective-permute-start.34 = (f32[8,128]{1,0:T(8,128)S(1)}, f32[8,128]{1,0:T(8,128)S(1)}, u32[]{:S(2)}, u32[]{:S(2)}) collective-permute-start(f32[8,128]{1,0:T(8,128)S(1)} %get-tuple-element.154.refs_4_), channel_id=1, source_target_pairs={{0,16},{4,20},{8,24},{12,28},{16,0},{20,4},{24,8},{28,12},{1,17},{... | collective-permute-start | bytes 12296 | tf_op jit(solution)/shard_map/ppermute | solution.py:388
  103.3 3.0 %collective-permute-start.36 = (f32[104,128]{1,0:T(8,128)S(1)}, f32[104,128]{1,0:T(8,128)S(1)}, u32[]{:S(2)}, u32[]{:S(2)}) collective-permute-start(f32[104,128]{1,0:T(8,128)S(1)} %get-tuple-element.169.refs_1_), channel_id=1, source_target_pairs={{0,4},{4,0},{8,12},{12,8},{16,20},{20,16},{24,28},{28,24},{1,5},{5... | collective-permute-start | bytes 159752 | tf_op jit(solution)/shard_map/ppermute | solution.py:388
  107.8 2.5 %collective-permute-start.37 = (f32[8,256]{1,0:T(8,128)S(1)}, f32[8,256]{1,0:T(8,128)S(1)}, u32[]{:S(2)}, u32[]{:S(2)}) collective-permute-start(f32[8,256]{1,0:T(8,128)S(1)} %get-tuple-element.172), channel_id=1, source_target_pairs={{0,8},{4,12},{8,0},{12,4},{16,24},{20,28},{24,16},{28,20},{1,9},{5... | collective-permute-start | bytes 24584 | tf_op jit(solution)/shard_map/ppermute | solution.py:388
  110.4 2.5 %collective-permute-start.38 = (f32[8,256]{1,0:T(8,128)S(1)}, f32[8,256]{1,0:T(8,128)S(1)}, u32[]{:S(2)}, u32[]{:S(2)}) collective-permute-start(f32[8,256]{1,0:T(8,128)S(1)} %get-tuple-element.173), channel_id=1, source_target_pairs={{0,3},{1,2},{2,1},{3,0},{4,7},{5,6},{6,5},{7,4},{8,11},{9,10},{10,... | collective-permute-start | bytes 24584 | tf_op jit(solution)/shard_map/ppermute | solution.py:397
  127.0 3.3 %collective-permute-start.46 = (f32[8,128]{1,0:T(8,128)S(1)}, f32[8,128]{1,0:T(8,128)S(1)}, u32[]{:S(2)}, u32[]{:S(2)}) collective-permute-start(f32[8,128]{1,0:T(8,128)S(1)} %get-tuple-element.179.refs_4_), channel_id=1, source_target_pairs={{0,16},{4,20},{8,24},{12,28},{16,0},{20,4},{24,8},{28,12},{1,17},{... | collective-permute-start | bytes 12296 | tf_op jit(solution)/shard_map/ppermute | solution.py:388
  134.4 3.0 %collective-permute-start.48 = (f32[104,128]{1,0:T(8,128)S(1)}, f32[104,128]{1,0:T(8,128)S(1)}, u32[]{:S(2)}, u32[]{:S(2)}) collective-permute-start(f32[104,128]{1,0:T(8,128)S(1)} %get-tuple-element.201.refs_1_), channel_id=1, source_target_pairs={{0,4},{4,0},{8,12},{12,8},{16,20},{20,16},{24,28},{28,24},{1,5},{5... | collective-permute-start | bytes 159752 | tf_op jit(solution)/shard_map/ppermute | solution.py:388
  138.9 2.6 %collective-permute-start.49 = (f32[8,256]{1,0:T(8,128)S(1)}, f32[8,256]{1,0:T(8,128)S(1)}, u32[]{:S(2)}, u32[]{:S(2)}) collective-permute-start(f32[8,256]{1,0:T(8,128)S(1)} %get-tuple-element.209), channel_id=1, source_target_pairs={{0,3},{1,2},{2,1},{3,0},{4,7},{5,6},{6,5},{7,4},{8,11},{9,10},{10,... | collective-permute-start | bytes 24584 | tf_op jit(solution)/shard_map/ppermute | solution.py:397
  149.2 2.0 %collective-permute-start.52 = (f32[8,256]{1,0:T(8,128)S(1)}, f32[8,256]{1,0:T(8,128)S(1)}, u32[]{:S(2)}, u32[]{:S(2)}) collective-permute-start(f32[8,256]{1,0:T(8,128)S(1)} %coarse.9.refs_4_), channel_id=1, source_target_pairs={{0,1},{1,0},{2,3},{3,2},{4,5},{5,4},{6,7},{7,6},{8,9},{9,8},{10,11... | collective-permute-start | bytes 24584 | tf_op jit(solution)/shard_map/ppermute | solution.py:397
  154.1 3.9 %collective-permute-start.56 = (f32[96,128]{1,0:T(8,128)S(1)}, f32[96,128]{1,0:T(8,128)S(1)}, u32[]{:S(2)}, u32[]{:S(2)}) collective-permute-start(f32[96,128]{1,0:T(8,128)S(1)} %get-tuple-element.217.near_ref), channel_id=1, source_target_pairs={{0,4},{4,0},{8,12},{12,8},{16,20},{20,16},{24,28},{28,24},{1,5},{5... | collective-permute-start | bytes 147464 | tf_op jit(solution)/shard_map/ppermute | solution.py:388
  158.2 12.1 %all_to_all.5.dots_ref = f32[32,1,128]{2,1,0:T(1,128)S(1)} all-to-all(f32[32,1,128]{2,1,0:T(1,128)S(1)} %gram.1), channel_id=1, replica_groups=mesh['sub'=8,'grp'=4] {'sub','grp'}, dimensions={0} | all-to-all | bytes 32768 | tf_op jit(solution)/shard_map/all_to_all | solution.py:547
  (124 shorter events, 88.0 us)
Async XLA Ops:
  7.3 5.7 %collective-permute-start.1 = (f32[104,128]{1,0:T(8,128)S(1)}, f32[104,128]{1,0:T(8,128)S(1)}, u32[]{:S(2)}, u32[]{:S(2)}) collective-permute-start(f32[104,128]{1,0:T(8,128)S(1)} %get-tuple-element.115.refs_0_), channel_id=1, source_target_pairs={{4,8},{8,4},{12,16},{16,12},{20,24},{24,20},{5,9},{9,5},{13,17},{1... | collective-permute-start | bytes 159752 | tf_op jit(solution)/shard_map/ppermute | solution.py:393
  8.0 5.9 %collective-permute-start.2 = (f32[104,128]{1,0:T(8,128)S(1)}, f32[104,128]{1,0:T(8,128)S(1)}, u32[]{:S(2)}, u32[]{:S(2)}) collective-permute-start(f32[104,128]{1,0:T(8,128)S(1)} %get-tuple-element.116.refs_1_), channel_id=1, source_target_pairs={{0,4},{4,0},{8,12},{12,8},{16,20},{20,16},{24,28},{28,24},{1,5},{5... | collective-permute-start | bytes 159752 | tf_op jit(solution)/shard_map/ppermute | solution.py:388
  14.5 5.5 %collective-permute-start.3 = (f32[8,256]{1,0:T(8,128)S(1)}, f32[8,256]{1,0:T(8,128)S(1)}, u32[]{:S(2)}, u32[]{:S(2)}) collective-permute-start(f32[8,256]{1,0:T(8,128)S(1)} %get-tuple-element.122), channel_id=1, source_target_pairs={{0,3},{1,2},{2,1},{3,0},{4,7},{5,6},{6,5},{7,4},{8,11},{9,10},{10,... | collective-permute-start | bytes 24584 | tf_op jit(solution)/shard_map/ppermute | solution.py:397
  23.5 5.5 %collective-permute-start.8 = (f32[8,256]{1,0:T(8,128)S(1)}, f32[8,256]{1,0:T(8,128)S(1)}, u32[]{:S(2)}, u32[]{:S(2)}) collective-permute-start(f32[8,256]{1,0:T(8,128)S(1)} %coarse.5.refs_4_), channel_id=1, source_target_pairs={{0,3},{1,2},{2,1},{3,0},{4,7},{5,6},{6,5},{7,4},{8,11},{9,10},{10,... | collective-permute-start | bytes 24584 | tf_op jit(solution)/shard_map/ppermute | solution.py:397
  38.0 5.6 %collective-permute-start.12 = (f32[104,128]{1,0:T(8,128)S(1)}, f32[104,128]{1,0:T(8,128)S(1)}, u32[]{:S(2)}, u32[]{:S(2)}) collective-permute-start(f32[104,128]{1,0:T(8,128)S(1)} %get-tuple-element.130.refs_1_), channel_id=1, source_target_pairs={{0,4},{4,0},{8,12},{12,8},{16,20},{20,16},{24,28},{28,24},{1,5},{5... | collective-permute-start | bytes 159752 | tf_op jit(solution)/shard_map/ppermute | solution.py:388
  44.2 7.8 %collective-permute-start.13 = (f32[8,256]{1,0:T(8,128)S(1)}, f32[8,256]{1,0:T(8,128)S(1)}, u32[]{:S(2)}, u32[]{:S(2)}) collective-permute-start(f32[8,256]{1,0:T(8,128)S(1)} %get-tuple-element.133), channel_id=1, source_target_pairs={{0,8},{4,12},{8,0},{12,4},{16,24},{20,28},{24,16},{28,20},{1,9},{5... | collective-permute-start | bytes 24584 | tf_op jit(solution)/shard_map/ppermute | solution.py:388
  47.6 5.4 %collective-permute-start.14 = (f32[8,256]{1,0:T(8,128)S(1)}, f32[8,256]{1,0:T(8,128)S(1)}, u32[]{:S(2)}, u32[]{:S(2)}) collective-permute-start(f32[8,256]{1,0:T(8,128)S(1)} %get-tuple-element.134), channel_id=1, source_target_pairs={{0,3},{1,2},{2,1},{3,0},{4,7},{5,6},{6,5},{7,4},{8,11},{9,10},{10,... | collective-permute-start | bytes 24584 | tf_op jit(solution)/shard_map/ppermute | solution.py:397
  55.5 5.5 %collective-permute-start.19 = (f32[8,256]{1,0:T(8,128)S(1)}, f32[8,256]{1,0:T(8,128)S(1)}, u32[]{:S(2)}, u32[]{:S(2)}) collective-permute-start(f32[8,256]{1,0:T(8,128)S(1)} %coarse.6.refs_4_), channel_id=1, source_target_pairs={{0,3},{1,2},{2,1},{3,0},{4,7},{5,6},{6,5},{7,4},{8,11},{9,10},{10,... | collective-permute-start | bytes 24584 | tf_op jit(solution)/shard_map/ppermute | solution.py:397
  62.1 7.6 %collective-permute-start.20 = (f32[96,128]{1,0:T(8,128)S(1)}, f32[96,128]{1,0:T(8,128)S(1)}, u32[]{:S(2)}, u32[]{:S(2)}) collective-permute-start(f32[96,128]{1,0:T(8,128)S(1)} %get-tuple-element.138.refs_0_), channel_id=1, source_target_pairs={{4,8},{8,4},{12,16},{16,12},{20,24},{24,20},{5,9},{9,5},{13,17},{1... | collective-permute-start | bytes 147464 | tf_op jit(solution)/shard_map/ppermute | solution.py:393
  62.8 7.0 %collective-permute-start.21 = (f32[96,128]{1,0:T(8,128)S(1)}, f32[96,128]{1,0:T(8,128)S(1)}, u32[]{:S(2)}, u32[]{:S(2)}) collective-permute-start(f32[96,128]{1,0:T(8,128)S(1)} %get-tuple-element.139.refs_1_), channel_id=1, source_target_pairs={{0,4},{4,0},{8,12},{12,8},{16,20},{20,16},{24,28},{28,24},{1,5},{5... | collective-permute-start | bytes 147464 | tf_op jit(solution)/shard_map/ppermute | solution.py:388
  76.9 6.8 %collective-permute-start.25 = (f32[8,256]{1,0:T(8,128)S(1)}, f32[8,256]{1,0:T(8,128)S(1)}, u32[]{:S(2)}, u32[]{:S(2)}) collective-permute-start(f32[8,256]{1,0:T(8,128)S(1)} %get-tuple-element.147), channel_id=1, source_target_pairs={{0,8},{4,12},{8,0},{12,4},{16,24},{20,28},{24,16},{28,20},{1,9},{5... | collective-permute-start | bytes 24584 | tf_op jit(solution)/shard_map/ppermute | solution.py:388
  79.3 5.4 %collective-permute-start.26 = (f32[8,256]{1,0:T(8,128)S(1)}, f32[8,256]{1,0:T(8,128)S(1)}, u32[]{:S(2)}, u32[]{:S(2)}) collective-permute-start(f32[8,256]{1,0:T(8,128)S(1)} %get-tuple-element.148), channel_id=1, source_target_pairs={{0,3},{1,2},{2,1},{3,0},{4,7},{5,6},{6,5},{7,4},{8,11},{9,10},{10,... | collective-permute-start | bytes 24584 | tf_op jit(solution)/shard_map/ppermute | solution.py:397
  87.1 5.5 %collective-permute-start.31 = (f32[8,256]{1,0:T(8,128)S(1)}, f32[8,256]{1,0:T(8,128)S(1)}, u32[]{:S(2)}, u32[]{:S(2)}) collective-permute-start(f32[8,256]{1,0:T(8,128)S(1)} %coarse.7.refs_4_), channel_id=1, source_target_pairs={{0,3},{1,2},{2,1},{3,0},{4,7},{5,6},{6,5},{7,4},{8,11},{9,10},{10,... | collective-permute-start | bytes 24584 | tf_op jit(solution)/shard_map/ppermute | solution.py:397
  93.7 7.1 %collective-permute-start.32 = (f32[96,128]{1,0:T(8,128)S(1)}, f32[96,128]{1,0:T(8,128)S(1)}, u32[]{:S(2)}, u32[]{:S(2)}) collective-permute-start(f32[96,128]{1,0:T(8,128)S(1)} %get-tuple-element.152.refs_0_), channel_id=1, source_target_pairs={{4,8},{8,4},{12,16},{16,12},{20,24},{24,20},{5,9},{9,5},{13,17},{1... | collective-permute-start | bytes 147464 | tf_op jit(solution)/shard_map/ppermute | solution.py:393
  94.4 6.4 %collective-permute-start.33 = (f32[96,128]{1,0:T(8,128)S(1)}, f32[96,128]{1,0:T(8,128)S(1)}, u32[]{:S(2)}, u32[]{:S(2)}) collective-permute-start(f32[96,128]{1,0:T(8,128)S(1)} %get-tuple-element.153.refs_1_), channel_id=1, source_target_pairs={{0,4},{4,0},{8,12},{12,8},{16,20},{20,16},{24,28},{28,24},{1,5},{5... | collective-permute-start | bytes 147464 | tf_op jit(solution)/shard_map/ppermute | solution.py:388
  107.8 6.9 %collective-permute-start.37 = (f32[8,256]{1,0:T(8,128)S(1)}, f32[8,256]{1,0:T(8,128)S(1)}, u32[]{:S(2)}, u32[]{:S(2)}) collective-permute-start(f32[8,256]{1,0:T(8,128)S(1)} %get-tuple-element.172), channel_id=1, source_target_pairs={{0,8},{4,12},{8,0},{12,4},{16,24},{20,28},{24,16},{28,20},{1,9},{5... | collective-permute-start | bytes 24584 | tf_op jit(solution)/shard_map/ppermute | solution.py:388
  110.4 5.4 %collective-permute-start.38 = (f32[8,256]{1,0:T(8,128)S(1)}, f32[8,256]{1,0:T(8,128)S(1)}, u32[]{:S(2)}, u32[]{:S(2)}) collective-permute-start(f32[8,256]{1,0:T(8,128)S(1)} %get-tuple-element.173), channel_id=1, source_target_pairs={{0,3},{1,2},{2,1},{3,0},{4,7},{5,6},{6,5},{7,4},{8,11},{9,10},{10,... | collective-permute-start | bytes 24584 | tf_op jit(solution)/shard_map/ppermute | solution.py:397
  118.2 5.5 %collective-permute-start.43 = (f32[8,256]{1,0:T(8,128)S(1)}, f32[8,256]{1,0:T(8,128)S(1)}, u32[]{:S(2)}, u32[]{:S(2)}) collective-permute-start(f32[8,256]{1,0:T(8,128)S(1)} %coarse.8.refs_4_), channel_id=1, source_target_pairs={{0,3},{1,2},{2,1},{3,0},{4,7},{5,6},{6,5},{7,4},{8,11},{9,10},{10,... | collective-permute-start | bytes 24584 | tf_op jit(solution)/shard_map/ppermute | solution.py:397
  124.8 7.1 %collective-permute-start.44 = (f32[96,128]{1,0:T(8,128)S(1)}, f32[96,128]{1,0:T(8,128)S(1)}, u32[]{:S(2)}, u32[]{:S(2)}) collective-permute-start(f32[96,128]{1,0:T(8,128)S(1)} %get-tuple-element.177.refs_0_), channel_id=1, source_target_pairs={{4,8},{8,4},{12,16},{16,12},{20,24},{24,20},{5,9},{9,5},{13,17},{1... | collective-permute-start | bytes 147464 | tf_op jit(solution)/shard_map/ppermute | solution.py:393
  125.5 6.4 %collective-permute-start.45 = (f32[96,128]{1,0:T(8,128)S(1)}, f32[96,128]{1,0:T(8,128)S(1)}, u32[]{:S(2)}, u32[]{:S(2)}) collective-permute-start(f32[96,128]{1,0:T(8,128)S(1)} %get-tuple-element.178.refs_1_), channel_id=1, source_target_pairs={{0,4},{4,0},{8,12},{12,8},{16,20},{20,16},{24,28},{28,24},{1,5},{5... | collective-permute-start | bytes 147464 | tf_op jit(solution)/shard_map/ppermute | solution.py:388
  138.9 5.5 %collective-permute-start.49 = (f32[8,256]{1,0:T(8,128)S(1)}, f32[8,256]{1,0:T(8,128)S(1)}, u32[]{:S(2)}, u32[]{:S(2)}) collective-permute-start(f32[8,256]{1,0:T(8,128)S(1)} %get-tuple-element.209), channel_id=1, source_target_pairs={{0,3},{1,2},{2,1},{3,0},{4,7},{5,6},{6,5},{7,4},{8,11},{9,10},{10,... | collective-permute-start | bytes 24584 | tf_op jit(solution)/shard_map/ppermute | solution.py:397
  146.8 5.5 %collective-permute-start.54 = (f32[8,256]{1,0:T(8,128)S(1)}, f32[8,256]{1,0:T(8,128)S(1)}, u32[]{:S(2)}, u32[]{:S(2)}) collective-permute-start(f32[8,256]{1,0:T(8,128)S(1)} %coarse.9.refs_4_), channel_id=1, source_target_pairs={{0,3},{1,2},{2,1},{3,0},{4,7},{5,6},{6,5},{7,4},{8,11},{9,10},{10,... | collective-permute-start | bytes 24584 | tf_op jit(solution)/shard_map/ppermute | solution.py:397
  153.5 16.9 %collective-permute-start.55 = (f32[96,128]{1,0:T(8,128)S(1)}, f32[96,128]{1,0:T(8,128)S(1)}, u32[]{:S(2)}, u32[]{:S(2)}) collective-permute-start(f32[96,128]{1,0:T(8,128)S(1)} %get-tuple-element.216.far_ref), channel_id=1, source_target_pairs={{4,8},{8,4},{12,16},{16,12},{20,24},{24,20},{5,9},{9,5},{13,17},{1... | collective-permute-start | bytes 147464 | tf_op jit(solution)/shard_map/ppermute | solution.py:393
  154.1 16.3 %collective-permute-start.56 = (f32[96,128]{1,0:T(8,128)S(1)}, f32[96,128]{1,0:T(8,128)S(1)}, u32[]{:S(2)}, u32[]{:S(2)}) collective-permute-start(f32[96,128]{1,0:T(8,128)S(1)} %get-tuple-element.217.near_ref), channel_id=1, source_target_pairs={{0,4},{4,0},{8,12},{12,8},{16,20},{20,16},{24,28},{28,24},{1,5},{5... | collective-permute-start | bytes 147464 | tf_op jit(solution)/shard_map/ppermute | solution.py:388
  (35 other events, 180.4 us)

commit v10 on v9

--- a/solution.py
+++ b/solution.py
@@ -136,10 +136,9 @@
         odd, own_ref[...], previous_ref[...], selector_ref, swap_ref, stiffness_ref, stiff_ref, near_ref, far_ref
     )
     near_ref[iface:] = jnp.zeros((ROWS, cells), F32)
-    far_ref[iface:] = jnp.zeros((ROWS, cells), F32)
-
-
-def arrived(odd, far_ref, near_ref, from_far_ref, from_near_ref, iface):
+
+
+def arrived(odd, near_ref, far_ref, from_far_ref, from_near_ref, iface):
     near, far = near_ref[:iface], far_ref[:iface]
     from_near, from_far = from_near_ref[:iface], from_far_ref[:iface]
     own = jnp.where(odd, far - from_far, near - from_near)
@@ -148,17 +147,16 @@
 
 
 def second_kernel(
-    far_ref, near_ref, from_far_ref, from_near_ref, r_ref, u_ref, selector_ref, swap_ref, stiffness_ref,
+    near_ref, far_ref, from_far_ref, from_near_ref, r_ref, u_ref, selector_ref, swap_ref, stiffness_ref,
     far_out, near_out, w_out, stiff_ref,
 ):
     iface = r_ref.shape[0]
     odd = lax.axis_index("sub") % 2 == 1
-    w, w_previous = arrived(odd, far_ref, near_ref, from_far_ref, from_near_ref, iface)
+    w, w_previous = arrived(odd, near_ref, far_ref, from_far_ref, from_near_ref, iface)
     w_out[0] = w
     w_out[1] = w_previous
     dots = dot_rows(r_ref[...], u_ref[...], w)
     near_out[iface:] = dots
-    far_out[iface:] = dots
     stiffen(odd, w, w_previous, selector_ref, swap_ref, stiffness_ref, stiff_ref, near_out, far_out)
 
 
@@ -210,30 +208,29 @@
 
 
 def middle_kernel(first, *refs):
-    (far_ref, near_ref, from_far_ref, from_near_ref, dots_ref, dots_other_ref, m_ref, gap_ref) = refs[:8]
+    (near_ref, far_ref, from_far_ref, from_near_ref, dots_ref, dots_other_ref, m_ref, gap_ref) = refs[:8]
     (selector_ref, swap_ref, stiffness_ref) = refs[8:11]
     states = list(refs[11 : 11 + 2 * STATES])
     far_out, near_out, stiff_ref = refs[11 + 2 * STATES :]
     m = m_ref[...]
     iface = m.shape[0]
     odd = lax.axis_index("sub") % 2 == 1
-    n, n_previous = arrived(odd, far_ref, near_ref, from_far_ref, from_near_ref, iface)
+    n, n_previous = arrived(odd, near_ref, far_ref, from_far_ref, from_near_ref, iface)
     dots, w, previous = update(
         first, states, m, gap_ref[...], n, n_previous, dots_ref[...] + dots_other_ref[...]
     )
     near_out[iface:] = dots
-    far_out[iface:] = dots
     stiffen(odd, w, previous, selector_ref, swap_ref, stiffness_ref, stiff_ref, near_out, far_out)
 
 
 def corner_kernel(
-    ranks, far_ref, near_ref, from_far_ref, from_near_ref, selector_ref, operators_ref, table_ref,
+    ranks, near_ref, far_ref, from_far_ref, from_near_ref, selector_ref, operators_ref, table_ref,
     m_out, gap_out, *rest,
 ):
     dots_sent, outs, (dots_out, sums_ref) = rest[0], rest[1 : ranks + 1], rest[ranks + 1 :]
     iface, cells = m_out.shape
     odd = lax.axis_index("sub") % 2 == 1
-    own, previous = arrived(odd, far_ref, near_ref, from_far_ref, from_near_ref, iface)
+    own, previous = arrived(odd, near_ref, far_ref, from_far_ref, from_near_ref, iface)
     m_out[...] = own
     dots_sent[...] = jnp.zeros_like(dots_sent)
     dots = near_ref[iface:] + from_near_ref[iface:]
@@ -341,7 +338,7 @@
 
 def final_kernel(
     dots_ref, scalars_ref, x_ref, r_ref, u_ref, w_ref, p_ref, s_ref, q_ref, z_ref, m_ref,
-    far_ref, near_ref, from_far_ref, from_near_ref, x_out, r_out,
+    near_ref, far_ref, from_far_ref, from_near_ref, x_out, r_out,
 ):
     totals = jnp.sum(dots_ref[...], axis=0)
     gram = [[totals[:, 4 * i + k : 4 * i + k + 1] for k in range(4)] for i in range(4)]
@@ -369,7 +366,7 @@
     alpha_next = norm_next / form(turned_next, turned_next)
 
     odd = lax.axis_index("sub") % 2 == 1
-    n, _ = arrived(odd, far_ref, near_ref, from_far_ref, from_near_ref, r_ref.shape[0])
+    n, _ = arrived(odd, near_ref, far_ref, from_far_ref, from_near_ref, r_ref.shape[0])
     p = u_ref[...] + beta * p_ref[...]
     s = w_ref[0] + beta * s_ref[...]
     u = u_ref[...] - alpha * (m_ref[...] + beta * q_ref[...])
@@ -473,7 +470,7 @@
             flops=2 * 24 * iface * cells,
             moved=2 * 24 * iface * cells + group * CORNERS_SUB * cells * 2,
             name="corners",
-        )(far, near, from_far, from_near, selector, operators, table)
+        )(near, far, from_far, from_near, selector, operators, table)
         arrivals = [exchanged(parts[ranks - 1 - d], d) for d in range(ranks - 1, 0, -1)] + [parts[ranks - 1]]
         local = call(
             local_kernel,
@@ -506,22 +503,22 @@
         return m, gap, near, far, *result
 
     far, near = call(
-        first_kernel, (message, message), count=5, scratch=stiff_scratch, name="first", **stiff_cost
+        first_kernel, (field, message), count=5, scratch=stiff_scratch, name="first", **stiff_cost
     )(right_side, previous, selector, swap, stiff)
     u, gap_u, near, far = apply_operator(near, far, "")
     r = right_side
     from_far, from_near = swapped_far(far), swapped(near, 1)
     far, near, w = call(
         second_kernel,
-        (message, message, pair),
+        (field, message, pair),
         count=9,
         scratch=stiff_scratch,
         name="second",
         **stiff_cost,
-    )(far, near, from_far, from_near, r, u, selector, swap, stiff)
+    )(near, far, from_far, from_near, r, u, selector, swap, stiff)
 
     states = (jnp.zeros((ROWS, cells), F32), r, r, u, w, r, r, r, w, gap_u, r, r)
-    outs = (rows, field, field, field, pair, field, field, field, pair, field, field, field, message, message)
+    outs = (rows, field, field, field, pair, field, field, field, pair, field, field, field, field, message)
     for step in range(ITERS - 2):
         m, gap, near, far, dots = apply_operator(near, far, "dots")
         from_far, from_near, other = swapped_far(far), swapped(near, 1), swapped(dots, 4)
@@ -537,7 +534,7 @@
             scratch=stiff_scratch,
             name="middle",
             **stiff_cost,
-        )(far, near, from_far, from_near, dots, other, m, gap, selector, swap, stiff, *states)
+        )(near, far, from_far, from_near, dots, other, m, gap, selector, swap, stiff, *states)
     scalars, x, r, u, w, p, s, q, z, gap_u, gap_p, gap_q = states
     m, gap, near, far, lifted = apply_operator(near, far, "lifted")
     from_far, from_near = swapped_far(far), swapped(near, 1)
@@ -546,7 +543,7 @@
     )
     everyone = lax.all_to_all(parts, ("sub", "grp"), 0, 0, tiled=True)
     x, r = call(final_kernel, (field, field), count=15, name="final")(
-        everyone, scalars, x, r, u, w, p, s, q, z, m, far, near, from_far, from_near
+        everyone, scalars, x, r, u, w, p, s, q, z, m, near, far, from_far, from_near
     )
     return (x[:, None, :], r[:, None, :])
 

time: 172 us -> 170 us (0.988)
  blocking collectives: 12.1 us -> 17.9 us
  waiting for transfers between devices: 30.1 us -> 26 us
  starting transfers between devices: 103 us -> 99.1 us
    all_to_all x1, blocking collectives: 12.1 us -> 17.9 us  [on_device(): everyone = lax.all_to_all(parts, ('sub', 'grp'), 0, 0, tiled=True)]
    ppermute x16, waiting for transfers between devices: 10.1 us -> 5.9 us  [swapped(): lax.ppermute(block, 'sub', [(i, i ^ bit) for i in range(lax.axis_size('su...]
    ppermute x16, starting transfers between devices: 49.7 us -> 45.8 us  [swapped(): lax.ppermute(block, 'sub', [(i, i ^ bit) for i in range(lax.axis_size('su...]
where the time goes in v10:
time: 170 us
  starting transfers between devices  99.1 us (58%)
  waiting for transfers between devices  26 us (15%)
  Pallas kernels  25.8 us (15%)
  blocking collectives  17.9 us (11%)
    ppermute x16, starting transfers between devices, swapped(): lax.ppermute(block, 'sub', [(i, i ^ bit) for i in range(lax.axis_size('su...  45.8 us
    ppermute x30, starting transfers between devices, exchanged(): lax.ppermute(block, 'grp', [(i, i ^ distance) for i in range(lax.axis_siz...  44.1 us
    ppermute x30, waiting for transfers between devices, exchanged(): lax.ppermute(block, 'grp', [(i, i ^ distance) for i in range(lax.axis_siz...  20.1 us
    all_to_all x1, blocking collectives, on_device(): everyone = lax.all_to_all(parts, ('sub', 'grp'), 0, 0, tiled=True)  17.9 us
    ppermute x10, starting transfers between devices, swapped_far(): lax.ppermute(block, 'sub', [(i, i + 1 if i % 2 else i - 1) for i in inner])  6.73 us
    ppermute x16, waiting for transfers between devices, swapped(): lax.ppermute(block, 'sub', [(i, i ^ bit) for i in range(lax.axis_size('su...  5.9 us
    pallas_call x3, Pallas kernels, on_device(): call(lambda *refs, first=step == 0: middle_kernel(first, *refs), outs, co...  5.46 us
    pallas_call x5, Pallas kernels, apply_operator(): call(lambda *refs: coarse_kernel(ranks, *refs), piece, count=3 + ranks, s...  3.58 us
  transfers between devices with their start and end apart: 57, of which 37 were waited for; matrix products, arithmetic and copies ran while one was open for 0% of the time, Pallas kernels for 3%

profile of v10, /device:TPU:0, one launch (start us, length us, event | category | flops | bytes accessed | tf_op | source)
XLA Modules:
  0.0 169.8 jit_solution(5108290992573742136)
XLA Ops:
  0.6 2.4 %collective-permute-start = (f32[96,128]{1,0:T(8,128)}, f32[96,128]{1,0:T(8,128)S(1)}, u32[]{:S(2)}, u32[]{:S(2)}) collective-permute-start(f32[96,128]{1,0:T(8,128)} %bitcast.18), channel_id=1, source_target_pairs={{0,4},{4,8},{8,12},{12,16},{16,20},{20,24},{24,28},{1,5},{5,9},{9,... | collective-permute-start | bytes 147464 | tf_op jit(solution)/shard_map/ppermute | solution.py:381
  3.0 2.6 %tables.1 = (bf16[256,128]{1,0:T(8,128)(2,1)S(1)}, bf16[128,128]{1,0:T(8,128)(2,1)S(1)}, bf16[1024,512]{1,0:T(8,128)(2,1)S(1)}, bf16[2,96,96,128]{3,2,1,0:T(8,12...) custom-call(s32[1,128]{1,0:T(1,128)} %refs_0_.6, s32[1,128]{1,0:T(1,128)} %refs_1_.1, ...), custom_call_target="tpu_custom_call" | custom-call | bytes 4718592 | tf_op jit(solution)/shard_map/tables/pallas_call | solution.py:441
  7.3 2.7 %collective-permute-start.2 = (f32[104,128]{1,0:T(8,128)S(1)}, f32[104,128]{1,0:T(8,128)S(1)}, u32[]{:S(2)}, u32[]{:S(2)}) collective-permute-start(f32[104,128]{1,0:T(8,128)S(1)} %get-tuple-element.115.refs_0_), channel_id=1, source_target_pairs={{0,4},{4,0},{8,12},{12,8},{16,20},{20,16},{24,28},{28,24},{1,5},{5... | collective-permute-start | bytes 159752 | tf_op jit(solution)/shard_map/ppermute | solution.py:385
  11.5 3.7 %collective-permute-start.3 = (f32[8,256]{1,0:T(8,128)S(1)}, f32[8,256]{1,0:T(8,128)S(1)}, u32[]{:S(2)}, u32[]{:S(2)}) collective-permute-start(f32[8,256]{1,0:T(8,128)S(1)} %get-tuple-element.122), channel_id=1, source_target_pairs={{0,3},{1,2},{2,1},{3,0},{4,7},{5,6},{6,5},{7,4},{8,11},{9,10},{10,... | collective-permute-start | bytes 24584 | tf_op jit(solution)/shard_map/ppermute | solution.py:394
  17.1 2.7 %collective-permute-done.4.refs_4_ = f32[8,256]{1,0:T(8,128)S(1)} collective-permute-done((f32[8,256]{1,0:T(8,128)S(1)}, f32[8,256]{1,0:T(8,128)S(1)}, u32[]{:S(2)}, u32[]{:S(2)}) %collective-permute-start.4) | collective-permute-done | bytes 8224 | tf_op jit(solution)/shard_map/ppermute | solution.py:394
  22.6 2.3 %collective-permute-start.6 = (f32[8,256]{1,0:T(8,128)S(1)}, f32[8,256]{1,0:T(8,128)S(1)}, u32[]{:S(2)}, u32[]{:S(2)}) collective-permute-start(f32[8,256]{1,0:T(8,128)S(1)} %coarse.5.refs_4_), channel_id=1, source_target_pairs={{0,1},{1,0},{2,3},{3,2},{4,5},{5,4},{6,7},{7,6},{8,9},{9,8},{10,11... | collective-permute-start | bytes 24584 | tf_op jit(solution)/shard_map/ppermute | solution.py:394
  31.5 7.3 %collective-permute-start.12 = (f32[104,128]{1,0:T(8,128)S(1)}, f32[104,128]{1,0:T(8,128)S(1)}, u32[]{:S(2)}, u32[]{:S(2)}) collective-permute-start(f32[104,128]{1,0:T(8,128)S(1)} %get-tuple-element.129.refs_0_), channel_id=1, source_target_pairs={{0,4},{4,0},{8,12},{12,8},{16,20},{20,16},{24,28},{28,24},{1,5},{5... | collective-permute-start | bytes 159752 | tf_op jit(solution)/shard_map/ppermute | solution.py:385
  40.4 7.7 %collective-permute-start.13 = (f32[8,256]{1,0:T(8,128)S(1)}, f32[8,256]{1,0:T(8,128)S(1)}, u32[]{:S(2)}, u32[]{:S(2)}) collective-permute-start(f32[8,256]{1,0:T(8,128)S(1)} %get-tuple-element.133), channel_id=1, source_target_pairs={{0,8},{4,12},{8,0},{12,4},{16,24},{20,28},{24,16},{28,20},{1,9},{5... | collective-permute-start | bytes 24584 | tf_op jit(solution)/shard_map/ppermute | solution.py:385
  48.0 2.5 %collective-permute-start.14 = (f32[8,256]{1,0:T(8,128)S(1)}, f32[8,256]{1,0:T(8,128)S(1)}, u32[]{:S(2)}, u32[]{:S(2)}) collective-permute-start(f32[8,256]{1,0:T(8,128)S(1)} %get-tuple-element.134), channel_id=1, source_target_pairs={{0,3},{1,2},{2,1},{3,0},{4,7},{5,6},{6,5},{7,4},{8,11},{9,10},{10,... | collective-permute-start | bytes 24584 | tf_op jit(solution)/shard_map/ppermute | solution.py:394
  58.3 2.0 %collective-permute-start.17 = (f32[8,256]{1,0:T(8,128)S(1)}, f32[8,256]{1,0:T(8,128)S(1)}, u32[]{:S(2)}, u32[]{:S(2)}) collective-permute-start(f32[8,256]{1,0:T(8,128)S(1)} %coarse.6.refs_4_), channel_id=1, source_target_pairs={{0,1},{1,0},{2,3},{3,2},{4,5},{5,4},{6,7},{7,6},{8,9},{9,8},{10,11... | collective-permute-start | bytes 24584 | tf_op jit(solution)/shard_map/ppermute | solution.py:394
  63.3 3.0 %collective-permute-start.22 = (f32[8,128]{1,0:T(8,128)S(1)}, f32[8,128]{1,0:T(8,128)S(1)}, u32[]{:S(2)}, u32[]{:S(2)}) collective-permute-start(f32[8,128]{1,0:T(8,128)S(1)} %get-tuple-element.140.refs_4_), channel_id=1, source_target_pairs={{0,16},{4,20},{8,24},{12,28},{16,0},{20,4},{24,8},{28,12},{1,17},{... | collective-permute-start | bytes 12296 | tf_op jit(solution)/shard_map/ppermute | solution.py:385
  72.5 5.9 %collective-permute-start.25 = (f32[8,256]{1,0:T(8,128)S(1)}, f32[8,256]{1,0:T(8,128)S(1)}, u32[]{:S(2)}, u32[]{:S(2)}) collective-permute-start(f32[8,256]{1,0:T(8,128)S(1)} %get-tuple-element.147), channel_id=1, source_target_pairs={{0,8},{4,12},{8,0},{12,4},{16,24},{20,28},{24,16},{28,20},{1,9},{5... | collective-permute-start | bytes 24584 | tf_op jit(solution)/shard_map/ppermute | solution.py:385
  78.4 2.5 %collective-permute-start.26 = (f32[8,256]{1,0:T(8,128)S(1)}, f32[8,256]{1,0:T(8,128)S(1)}, u32[]{:S(2)}, u32[]{:S(2)}) collective-permute-start(f32[8,256]{1,0:T(8,128)S(1)} %get-tuple-element.148), channel_id=1, source_target_pairs={{0,3},{1,2},{2,1},{3,0},{4,7},{5,6},{6,5},{7,4},{8,11},{9,10},{10,... | collective-permute-start | bytes 24584 | tf_op jit(solution)/shard_map/ppermute | solution.py:394
  88.7 2.0 %collective-permute-start.29 = (f32[8,256]{1,0:T(8,128)S(1)}, f32[8,256]{1,0:T(8,128)S(1)}, u32[]{:S(2)}, u32[]{:S(2)}) collective-permute-start(f32[8,256]{1,0:T(8,128)S(1)} %coarse.7.refs_4_), channel_id=1, source_target_pairs={{0,1},{1,0},{2,3},{3,2},{4,5},{5,4},{6,7},{7,6},{8,9},{9,8},{10,11... | collective-permute-start | bytes 24584 | tf_op jit(solution)/shard_map/ppermute | solution.py:394
  93.7 3.1 %collective-permute-start.34 = (f32[8,128]{1,0:T(8,128)S(1)}, f32[8,128]{1,0:T(8,128)S(1)}, u32[]{:S(2)}, u32[]{:S(2)}) collective-permute-start(f32[8,128]{1,0:T(8,128)S(1)} %get-tuple-element.154.refs_4_), channel_id=1, source_target_pairs={{0,16},{4,20},{8,24},{12,28},{16,0},{20,4},{24,8},{28,12},{1,17},{... | collective-permute-start | bytes 12296 | tf_op jit(solution)/shard_map/ppermute | solution.py:385
  102.6 6.3 %collective-permute-start.37 = (f32[8,256]{1,0:T(8,128)S(1)}, f32[8,256]{1,0:T(8,128)S(1)}, u32[]{:S(2)}, u32[]{:S(2)}) collective-permute-start(f32[8,256]{1,0:T(8,128)S(1)} %get-tuple-element.172), channel_id=1, source_target_pairs={{0,8},{4,12},{8,0},{12,4},{16,24},{20,28},{24,16},{28,20},{1,9},{5... | collective-permute-start | bytes 24584 | tf_op jit(solution)/shard_map/ppermute | solution.py:385
  108.9 2.5 %collective-permute-start.38 = (f32[8,256]{1,0:T(8,128)S(1)}, f32[8,256]{1,0:T(8,128)S(1)}, u32[]{:S(2)}, u32[]{:S(2)}) collective-permute-start(f32[8,256]{1,0:T(8,128)S(1)} %get-tuple-element.173), channel_id=1, source_target_pairs={{0,3},{1,2},{2,1},{3,0},{4,7},{5,6},{6,5},{7,4},{8,11},{9,10},{10,... | collective-permute-start | bytes 24584 | tf_op jit(solution)/shard_map/ppermute | solution.py:394
  119.1 2.1 %collective-permute-start.41 = (f32[8,256]{1,0:T(8,128)S(1)}, f32[8,256]{1,0:T(8,128)S(1)}, u32[]{:S(2)}, u32[]{:S(2)}) collective-permute-start(f32[8,256]{1,0:T(8,128)S(1)} %coarse.8.refs_4_), channel_id=1, source_target_pairs={{0,1},{1,0},{2,3},{3,2},{4,5},{5,4},{6,7},{7,6},{8,9},{9,8},{10,11... | collective-permute-start | bytes 24584 | tf_op jit(solution)/shard_map/ppermute | solution.py:394
  124.2 3.2 %collective-permute-start.46 = (f32[8,128]{1,0:T(8,128)S(1)}, f32[8,128]{1,0:T(8,128)S(1)}, u32[]{:S(2)}, u32[]{:S(2)}) collective-permute-start(f32[8,128]{1,0:T(8,128)S(1)} %get-tuple-element.179.refs_4_), channel_id=1, source_target_pairs={{0,16},{4,20},{8,24},{12,28},{16,0},{20,4},{24,8},{28,12},{1,17},{... | collective-permute-start | bytes 12296 | tf_op jit(solution)/shard_map/ppermute | solution.py:385
  129.0 1.8 %middle.5 = (f32[8,128]{1,0:T(8,128)S(1)}, f32[96,128]{1,0:T(8,128)S(1)}, f32[96,128]{1,0:T(8,128)S(1)}, f32[96,128]{1,0:T(8,128)S(1)}, f32[2,96,128]{2,1,0:T(8,...) custom-call(f32[96,128]{1,0:T(8,128)S(1)} %get-tuple-element.177.ref, ...), custom_call_target="tpu_custom_call" | custom-call | flops 4718592 | bytes 4718592 | tf_op jit(solution)/shard_map/middle/pallas_call | solution.py:530
  133.0 2.6 %collective-permute-start.49 = (f32[8,256]{1,0:T(8,128)S(1)}, f32[8,256]{1,0:T(8,128)S(1)}, u32[]{:S(2)}, u32[]{:S(2)}) collective-permute-start(f32[8,256]{1,0:T(8,128)S(1)} %get-tuple-element.209), channel_id=1, source_target_pairs={{0,3},{1,2},{2,1},{3,0},{4,7},{5,6},{6,5},{7,4},{8,11},{9,10},{10,... | collective-permute-start | bytes 24584 | tf_op jit(solution)/shard_map/ppermute | solution.py:394
  143.3 2.0 %collective-permute-start.52 = (f32[8,256]{1,0:T(8,128)S(1)}, f32[8,256]{1,0:T(8,128)S(1)}, u32[]{:S(2)}, u32[]{:S(2)}) collective-permute-start(f32[8,256]{1,0:T(8,128)S(1)} %coarse.9.refs_4_), channel_id=1, source_target_pairs={{0,1},{1,0},{2,3},{3,2},{4,5},{5,4},{6,7},{7,6},{8,9},{9,8},{10,11... | collective-permute-start | bytes 24584 | tf_op jit(solution)/shard_map/ppermute | solution.py:394
  147.5 1.9 %collective-permute-start.56 = (f32[96,128]{1,0:T(8,128)S(1)}, f32[96,128]{1,0:T(8,128)S(1)}, u32[]{:S(2)}, u32[]{:S(2)}) collective-permute-start(f32[96,128]{1,0:T(8,128)S(1)} %get-tuple-element.216.near_ref), channel_id=1, source_target_pairs={{0,4},{4,0},{8,12},{12,8},{16,20},{20,16},{24,28},{28,24},{1,5},{5... | collective-permute-start | bytes 147464 | tf_op jit(solution)/shard_map/ppermute | solution.py:385
  150.3 17.9 %all_to_all.5.dots_ref = f32[32,1,128]{2,1,0:T(1,128)S(1)} all-to-all(f32[32,1,128]{2,1,0:T(1,128)S(1)} %gram.1), channel_id=1, replica_groups=mesh['sub'=8,'grp'=4] {'sub','grp'}, dimensions={0} | all-to-all | bytes 32768 | tf_op jit(solution)/shard_map/all_to_all | solution.py:544
  (124 shorter events, 76.1 us)
Async XLA Ops:
  0.6 5.0 %collective-permute-start = (f32[96,128]{1,0:T(8,128)}, f32[96,128]{1,0:T(8,128)S(1)}, u32[]{:S(2)}, u32[]{:S(2)}) collective-permute-start(f32[96,128]{1,0:T(8,128)} %bitcast.18), channel_id=1, source_target_pairs={{0,4},{4,8},{8,12},{12,16},{16,20},{20,24},{24,28},{1,5},{5,9},{9,... | collective-permute-start | bytes 147464 | tf_op jit(solution)/shard_map/ppermute | solution.py:381
  11.5 5.5 %collective-permute-start.3 = (f32[8,256]{1,0:T(8,128)S(1)}, f32[8,256]{1,0:T(8,128)S(1)}, u32[]{:S(2)}, u32[]{:S(2)}) collective-permute-start(f32[8,256]{1,0:T(8,128)S(1)} %get-tuple-element.122), channel_id=1, source_target_pairs={{0,3},{1,2},{2,1},{3,0},{4,7},{5,6},{6,5},{7,4},{8,11},{9,10},{10,... | collective-permute-start | bytes 24584 | tf_op jit(solution)/shard_map/ppermute | solution.py:394
  20.5 5.5 %collective-permute-start.8 = (f32[8,256]{1,0:T(8,128)S(1)}, f32[8,256]{1,0:T(8,128)S(1)}, u32[]{:S(2)}, u32[]{:S(2)}) collective-permute-start(f32[8,256]{1,0:T(8,128)S(1)} %coarse.5.refs_4_), channel_id=1, source_target_pairs={{0,3},{1,2},{2,1},{3,0},{4,7},{5,6},{6,5},{7,4},{8,11},{9,10},{10,... | collective-permute-start | bytes 24584 | tf_op jit(solution)/shard_map/ppermute | solution.py:394
  31.5 8.2 %collective-permute-start.12 = (f32[104,128]{1,0:T(8,128)S(1)}, f32[104,128]{1,0:T(8,128)S(1)}, u32[]{:S(2)}, u32[]{:S(2)}) collective-permute-start(f32[104,128]{1,0:T(8,128)S(1)} %get-tuple-element.129.refs_0_), channel_id=1, source_target_pairs={{0,4},{4,0},{8,12},{12,8},{16,20},{20,16},{24,28},{28,24},{1,5},{5... | collective-permute-start | bytes 159752 | tf_op jit(solution)/shard_map/ppermute | solution.py:385
  40.4 12.1 %collective-permute-start.13 = (f32[8,256]{1,0:T(8,128)S(1)}, f32[8,256]{1,0:T(8,128)S(1)}, u32[]{:S(2)}, u32[]{:S(2)}) collective-permute-start(f32[8,256]{1,0:T(8,128)S(1)} %get-tuple-element.133), channel_id=1, source_target_pairs={{0,8},{4,12},{8,0},{12,4},{16,24},{20,28},{24,16},{28,20},{1,9},{5... | collective-permute-start | bytes 24584 | tf_op jit(solution)/shard_map/ppermute | solution.py:385
  48.0 5.4 %collective-permute-start.14 = (f32[8,256]{1,0:T(8,128)S(1)}, f32[8,256]{1,0:T(8,128)S(1)}, u32[]{:S(2)}, u32[]{:S(2)}) collective-permute-start(f32[8,256]{1,0:T(8,128)S(1)} %get-tuple-element.134), channel_id=1, source_target_pairs={{0,3},{1,2},{2,1},{3,0},{4,7},{5,6},{6,5},{7,4},{8,11},{9,10},{10,... | collective-permute-start | bytes 24584 | tf_op jit(solution)/shard_map/ppermute | solution.py:394
  55.9 5.5 %collective-permute-start.19 = (f32[8,256]{1,0:T(8,128)S(1)}, f32[8,256]{1,0:T(8,128)S(1)}, u32[]{:S(2)}, u32[]{:S(2)}) collective-permute-start(f32[8,256]{1,0:T(8,128)S(1)} %coarse.6.refs_4_), channel_id=1, source_target_pairs={{0,3},{1,2},{2,1},{3,0},{4,7},{5,6},{6,5},{7,4},{8,11},{9,10},{10,... | collective-permute-start | bytes 24584 | tf_op jit(solution)/shard_map/ppermute | solution.py:394
  62.5 5.4 %collective-permute-start.21 = (f32[96,128]{1,0:T(8,128)S(1)}, f32[96,128]{1,0:T(8,128)S(1)}, u32[]{:S(2)}, u32[]{:S(2)}) collective-permute-start(f32[96,128]{1,0:T(8,128)S(1)} %get-tuple-element.138.refs_0_), channel_id=1, source_target_pairs={{0,4},{4,0},{8,12},{12,8},{16,20},{20,16},{24,28},{28,24},{1,5},{5... | collective-permute-start | bytes 147464 | tf_op jit(solution)/shard_map/ppermute | solution.py:385
  62.6 5.3 %collective-permute-start.20 = (f32[96,128]{1,0:T(8,128)S(1)}, f32[96,128]{1,0:T(8,128)S(1)}, u32[]{:S(2)}, u32[]{:S(2)}) collective-permute-start(f32[96,128]{1,0:T(8,128)S(1)} %get-tuple-element.139.refs_1_), channel_id=1, source_target_pairs={{4,8},{8,4},{12,16},{16,12},{20,24},{24,20},{5,9},{9,5},{13,17},{1... | collective-permute-start | bytes 147464 | tf_op jit(solution)/shard_map/ppermute | solution.py:390
  72.5 10.3 %collective-permute-start.25 = (f32[8,256]{1,0:T(8,128)S(1)}, f32[8,256]{1,0:T(8,128)S(1)}, u32[]{:S(2)}, u32[]{:S(2)}) collective-permute-start(f32[8,256]{1,0:T(8,128)S(1)} %get-tuple-element.147), channel_id=1, source_target_pairs={{0,8},{4,12},{8,0},{12,4},{16,24},{20,28},{24,16},{28,20},{1,9},{5... | collective-permute-start | bytes 24584 | tf_op jit(solution)/shard_map/ppermute | solution.py:385
  78.4 5.4 %collective-permute-start.26 = (f32[8,256]{1,0:T(8,128)S(1)}, f32[8,256]{1,0:T(8,128)S(1)}, u32[]{:S(2)}, u32[]{:S(2)}) collective-permute-start(f32[8,256]{1,0:T(8,128)S(1)} %get-tuple-element.148), channel_id=1, source_target_pairs={{0,3},{1,2},{2,1},{3,0},{4,7},{5,6},{6,5},{7,4},{8,11},{9,10},{10,... | collective-permute-start | bytes 24584 | tf_op jit(solution)/shard_map/ppermute | solution.py:394
  86.3 5.5 %collective-permute-start.31 = (f32[8,256]{1,0:T(8,128)S(1)}, f32[8,256]{1,0:T(8,128)S(1)}, u32[]{:S(2)}, u32[]{:S(2)}) collective-permute-start(f32[8,256]{1,0:T(8,128)S(1)} %coarse.7.refs_4_), channel_id=1, source_target_pairs={{0,3},{1,2},{2,1},{3,0},{4,7},{5,6},{6,5},{7,4},{8,11},{9,10},{10,... | collective-permute-start | bytes 24584 | tf_op jit(solution)/shard_map/ppermute | solution.py:394
  92.9 5.5 %collective-permute-start.33 = (f32[96,128]{1,0:T(8,128)S(1)}, f32[96,128]{1,0:T(8,128)S(1)}, u32[]{:S(2)}, u32[]{:S(2)}) collective-permute-start(f32[96,128]{1,0:T(8,128)S(1)} %get-tuple-element.152.refs_0_), channel_id=1, source_target_pairs={{0,4},{4,0},{8,12},{12,8},{16,20},{20,16},{24,28},{28,24},{1,5},{5... | collective-permute-start | bytes 147464 | tf_op jit(solution)/shard_map/ppermute | solution.py:385
  93.0 5.4 %collective-permute-start.32 = (f32[96,128]{1,0:T(8,128)S(1)}, f32[96,128]{1,0:T(8,128)S(1)}, u32[]{:S(2)}, u32[]{:S(2)}) collective-permute-start(f32[96,128]{1,0:T(8,128)S(1)} %get-tuple-element.153.refs_1_), channel_id=1, source_target_pairs={{4,8},{8,4},{12,16},{16,12},{20,24},{24,20},{5,9},{9,5},{13,17},{1... | collective-permute-start | bytes 147464 | tf_op jit(solution)/shard_map/ppermute | solution.py:390
  102.6 10.7 %collective-permute-start.37 = (f32[8,256]{1,0:T(8,128)S(1)}, f32[8,256]{1,0:T(8,128)S(1)}, u32[]{:S(2)}, u32[]{:S(2)}) collective-permute-start(f32[8,256]{1,0:T(8,128)S(1)} %get-tuple-element.172), channel_id=1, source_target_pairs={{0,8},{4,12},{8,0},{12,4},{16,24},{20,28},{24,16},{28,20},{1,9},{5... | collective-permute-start | bytes 24584 | tf_op jit(solution)/shard_map/ppermute | solution.py:385
  108.9 5.4 %collective-permute-start.38 = (f32[8,256]{1,0:T(8,128)S(1)}, f32[8,256]{1,0:T(8,128)S(1)}, u32[]{:S(2)}, u32[]{:S(2)}) collective-permute-start(f32[8,256]{1,0:T(8,128)S(1)} %get-tuple-element.173), channel_id=1, source_target_pairs={{0,3},{1,2},{2,1},{3,0},{4,7},{5,6},{6,5},{7,4},{8,11},{9,10},{10,... | collective-permute-start | bytes 24584 | tf_op jit(solution)/shard_map/ppermute | solution.py:394
  116.8 5.5 %collective-permute-start.43 = (f32[8,256]{1,0:T(8,128)S(1)}, f32[8,256]{1,0:T(8,128)S(1)}, u32[]{:S(2)}, u32[]{:S(2)}) collective-permute-start(f32[8,256]{1,0:T(8,128)S(1)} %coarse.8.refs_4_), channel_id=1, source_target_pairs={{0,3},{1,2},{2,1},{3,0},{4,7},{5,6},{6,5},{7,4},{8,11},{9,10},{10,... | collective-permute-start | bytes 24584 | tf_op jit(solution)/shard_map/ppermute | solution.py:394
  123.4 5.5 %collective-permute-start.45 = (f32[96,128]{1,0:T(8,128)S(1)}, f32[96,128]{1,0:T(8,128)S(1)}, u32[]{:S(2)}, u32[]{:S(2)}) collective-permute-start(f32[96,128]{1,0:T(8,128)S(1)} %get-tuple-element.177.refs_0_), channel_id=1, source_target_pairs={{0,4},{4,0},{8,12},{12,8},{16,20},{20,16},{24,28},{28,24},{1,5},{5... | collective-permute-start | bytes 147464 | tf_op jit(solution)/shard_map/ppermute | solution.py:385
  123.5 5.5 %collective-permute-start.44 = (f32[96,128]{1,0:T(8,128)S(1)}, f32[96,128]{1,0:T(8,128)S(1)}, u32[]{:S(2)}, u32[]{:S(2)}) collective-permute-start(f32[96,128]{1,0:T(8,128)S(1)} %get-tuple-element.178.refs_1_), channel_id=1, source_target_pairs={{4,8},{8,4},{12,16},{16,12},{20,24},{24,20},{5,9},{9,5},{13,17},{1... | collective-permute-start | bytes 147464 | tf_op jit(solution)/shard_map/ppermute | solution.py:390
  124.2 4.8 %collective-permute-start.46 = (f32[8,128]{1,0:T(8,128)S(1)}, f32[8,128]{1,0:T(8,128)S(1)}, u32[]{:S(2)}, u32[]{:S(2)}) collective-permute-start(f32[8,128]{1,0:T(8,128)S(1)} %get-tuple-element.179.refs_4_), channel_id=1, source_target_pairs={{0,16},{4,20},{8,24},{12,28},{16,0},{20,4},{24,8},{28,12},{1,17},{... | collective-permute-start | bytes 12296 | tf_op jit(solution)/shard_map/ppermute | solution.py:385
  133.0 5.5 %collective-permute-start.49 = (f32[8,256]{1,0:T(8,128)S(1)}, f32[8,256]{1,0:T(8,128)S(1)}, u32[]{:S(2)}, u32[]{:S(2)}) collective-permute-start(f32[8,256]{1,0:T(8,128)S(1)} %get-tuple-element.209), channel_id=1, source_target_pairs={{0,3},{1,2},{2,1},{3,0},{4,7},{5,6},{6,5},{7,4},{8,11},{9,10},{10,... | collective-permute-start | bytes 24584 | tf_op jit(solution)/shard_map/ppermute | solution.py:394
  140.9 5.5 %collective-permute-start.54 = (f32[8,256]{1,0:T(8,128)S(1)}, f32[8,256]{1,0:T(8,128)S(1)}, u32[]{:S(2)}, u32[]{:S(2)}) collective-permute-start(f32[8,256]{1,0:T(8,128)S(1)} %coarse.9.refs_4_), channel_id=1, source_target_pairs={{0,3},{1,2},{2,1},{3,0},{4,7},{5,6},{6,5},{7,4},{8,11},{9,10},{10,... | collective-permute-start | bytes 24584 | tf_op jit(solution)/shard_map/ppermute | solution.py:394
  147.5 20.7 %collective-permute-start.56 = (f32[96,128]{1,0:T(8,128)S(1)}, f32[96,128]{1,0:T(8,128)S(1)}, u32[]{:S(2)}, u32[]{:S(2)}) collective-permute-start(f32[96,128]{1,0:T(8,128)S(1)} %get-tuple-element.216.near_ref), channel_id=1, source_target_pairs={{0,4},{4,0},{8,12},{12,8},{16,20},{20,16},{24,28},{28,24},{1,5},{5... | collective-permute-start | bytes 147464 | tf_op jit(solution)/shard_map/ppermute | solution.py:385
  149.5 18.8 %collective-permute-start.55 = (f32[96,128]{1,0:T(8,128)S(1)}, f32[96,128]{1,0:T(8,128)S(1)}, u32[]{:S(2)}, u32[]{:S(2)}) collective-permute-start(f32[96,128]{1,0:T(8,128)S(1)} %get-tuple-element.217.far_ref), channel_id=1, source_target_pairs={{4,8},{8,4},{12,16},{16,12},{20,24},{24,20},{5,9},{9,5},{13,17},{1... | collective-permute-start | bytes 147464 | tf_op jit(solution)/shard_map/ppermute | solution.py:390
  (35 other events, 142.3 us)

commit v11 on v10

--- a/solution.py
+++ b/solution.py
@@ -227,7 +227,8 @@
     ranks, near_ref, far_ref, from_far_ref, from_near_ref, selector_ref, operators_ref, table_ref,
     m_out, gap_out, *rest,
 ):
-    dots_sent, outs, (dots_out, sums_ref) = rest[0], rest[1 : ranks + 1], rest[ranks + 1 :]
+    outs, (dots_out, sums_ref) = (rest[0], *rest[2 : ranks + 1]), rest[ranks + 1 :]
+    dots_sent = rest[1]
     iface, cells = m_out.shape
     odd = lax.axis_index("sub") % 2 == 1
     own, previous = arrived(odd, near_ref, far_ref, from_far_ref, from_near_ref, iface)
@@ -254,8 +255,8 @@
     apply_blocks([inverse_ref], [gap_ref[...]], local_ref)
 
 
-def coarse_kernel(ranks, coarse_ref, dots_ref, other_ref, *rest):
-    pieces, (solved_ref, sums_ref) = rest[:ranks], rest[ranks:]
+def coarse_kernel(ranks, coarse_ref, dots_ref, farthest_ref, other_ref, *rest):
+    pieces, (solved_ref, sums_ref) = (farthest_ref, *rest[: ranks - 1]), rest[ranks - 1 :]
     cells = dots_ref.shape[1]
     for distance in range(ranks):
         rank = lax.axis_index("grp") ^ distance
@@ -462,7 +463,7 @@
 
     def apply_operator(near, far, extra):
         from_far, from_near = swapped_far(far), swapped(near, 1)
-        m, gap, sent, *parts, dots = call(
+        m, gap, farthest, sent, *parts, dots = call(
             lambda *refs: corner_kernel(ranks, *refs),
             (field, field) + (piece,) * (ranks + 1) + (rows,),
             count=7,
@@ -471,6 +472,7 @@
             moved=2 * 24 * iface * cells + group * CORNERS_SUB * cells * 2,
             name="corners",
         )(near, far, from_far, from_near, selector, operators, table)
+        parts = [farthest, *parts]
         arrivals = [exchanged(parts[ranks - 1 - d], d) for d in range(ranks - 1, 0, -1)] + [parts[ranks - 1]]
         local = call(
             local_kernel,
@@ -489,7 +491,7 @@
             flops=2 * blocks_own * order * order,
             moved=2 * blocks_own * order * order,
             name="coarse",
-        )(coarse_inverse, dots, other, *arrivals)
+        )(coarse_inverse, dots, arrivals[0], other, *arrivals[1:])
         values = [solved] + [exchanged(solved, d) for d in range(1, ranks)]
         far, near, *result = call(
             lambda *refs: lift_kernel(ranks, extra, *refs),

time: 170 us -> 170 us (level)
  transfers between devices with their start and end apart: 57 -> 57, of which waited for: 37 -> 34; matrix products, arithmetic and copies ran while one was open for 0% -> 0% of each run, Pallas kernels for 3% -> 3%
where the time goes in v11:
time: 170 us
  starting transfers between devices  98.9 us (58%)
  waiting for transfers between devices  25.9 us (15%)
  Pallas kernels  25.8 us (15%)
  blocking collectives  17.8 us (10%)
    ppermute x16, starting transfers between devices, swapped(): lax.ppermute(block, 'sub', [(i, i ^ bit) for i in range(lax.axis_size('su...  45.5 us
    ppermute x30, starting transfers between devices, exchanged(): lax.ppermute(block, 'grp', [(i, i ^ distance) for i in range(lax.axis_siz...  44.4 us
    ppermute x30, waiting for transfers between devices, exchanged(): lax.ppermute(block, 'grp', [(i, i ^ distance) for i in range(lax.axis_siz...  20 us
    all_to_all x1, blocking collectives, on_device(): everyone = lax.all_to_all(parts, ('sub', 'grp'), 0, 0, tiled=True)  17.8 us
    ppermute x10, starting transfers between devices, swapped_far(): lax.ppermute(block, 'sub', [(i, i + 1 if i % 2 else i - 1) for i in inner])  6.73 us
    ppermute x16, waiting for transfers between devices, swapped(): lax.ppermute(block, 'sub', [(i, i ^ bit) for i in range(lax.axis_size('su...  5.9 us
    pallas_call x3, Pallas kernels, on_device(): call(lambda *refs, first=step == 0: middle_kernel(first, *refs), outs, co...  5.46 us
    pallas_call x5, Pallas kernels, apply_operator(): call(lambda *refs: coarse_kernel(ranks, *refs), piece, count=3 + ranks, s...  3.58 us
  transfers between devices with their start and end apart: 57, of which 34 were waited for; matrix products, arithmetic and copies ran while one was open for 0% of the time, Pallas kernels for 3%

profile of v11, /device:TPU:0, one launch (start us, length us, event | category | flops | bytes accessed | tf_op | source)
XLA Modules:
  0.0 169.5 jit_solution(3166938116013477941)
XLA Ops:
  0.6 2.4 %collective-permute-start = (f32[96,128]{1,0:T(8,128)}, f32[96,128]{1,0:T(8,128)S(1)}, u32[]{:S(2)}, u32[]{:S(2)}) collective-permute-start(f32[96,128]{1,0:T(8,128)} %bitcast.18), channel_id=1, source_target_pairs={{0,4},{4,8},{8,12},{12,16},{16,20},{20,24},{24,28},{1,5},{5,9},{9,... | collective-permute-start | bytes 147464 | tf_op jit(solution)/shard_map/ppermute | solution.py:382
  3.0 2.6 %tables.1 = (bf16[256,128]{1,0:T(8,128)(2,1)S(1)}, bf16[128,128]{1,0:T(8,128)(2,1)S(1)}, bf16[1024,512]{1,0:T(8,128)(2,1)S(1)}, bf16[2,96,96,128]{3,2,1,0:T(8,12...) custom-call(s32[1,128]{1,0:T(1,128)} %refs_0_.6, s32[1,128]{1,0:T(1,128)} %refs_1_.1, ...), custom_call_target="tpu_custom_call" | custom-call | bytes 4718592 | tf_op jit(solution)/shard_map/tables/pallas_call | solution.py:442
  7.3 2.7 %collective-permute-start.2 = (f32[104,128]{1,0:T(8,128)S(1)}, f32[104,128]{1,0:T(8,128)S(1)}, u32[]{:S(2)}, u32[]{:S(2)}) collective-permute-start(f32[104,128]{1,0:T(8,128)S(1)} %get-tuple-element.115.refs_0_), channel_id=1, source_target_pairs={{0,4},{4,0},{8,12},{12,8},{16,20},{20,16},{24,28},{28,24},{1,5},{5... | collective-permute-start | bytes 159752 | tf_op jit(solution)/shard_map/ppermute | solution.py:386
  11.5 3.7 %collective-permute-start.3 = (f32[8,256]{1,0:T(8,128)S(1)}, f32[8,256]{1,0:T(8,128)S(1)}, u32[]{:S(2)}, u32[]{:S(2)}) collective-permute-start(f32[8,256]{1,0:T(8,128)S(1)} %get-tuple-element.121), channel_id=1, source_target_pairs={{0,3},{1,2},{2,1},{3,0},{4,7},{5,6},{6,5},{7,4},{8,11},{9,10},{10,... | collective-permute-start | bytes 24584 | tf_op jit(solution)/shard_map/ppermute | solution.py:395
  17.1 2.7 %collective-permute-done.4.refs_4_ = f32[8,256]{1,0:T(8,128)S(1)} collective-permute-done((f32[8,256]{1,0:T(8,128)S(1)}, f32[8,256]{1,0:T(8,128)S(1)}, u32[]{:S(2)}, u32[]{:S(2)}) %collective-permute-start.4) | collective-permute-done | bytes 8224 | tf_op jit(solution)/shard_map/ppermute | solution.py:395
  22.6 2.3 %collective-permute-start.6 = (f32[8,256]{1,0:T(8,128)S(1)}, f32[8,256]{1,0:T(8,128)S(1)}, u32[]{:S(2)}, u32[]{:S(2)}) collective-permute-start(f32[8,256]{1,0:T(8,128)S(1)} %coarse.5.refs_4_), channel_id=1, source_target_pairs={{0,1},{1,0},{2,3},{3,2},{4,5},{5,4},{6,7},{7,6},{8,9},{9,8},{10,11... | collective-permute-start | bytes 24584 | tf_op jit(solution)/shard_map/ppermute | solution.py:395
  31.5 7.3 %collective-permute-start.12 = (f32[104,128]{1,0:T(8,128)S(1)}, f32[104,128]{1,0:T(8,128)S(1)}, u32[]{:S(2)}, u32[]{:S(2)}) collective-permute-start(f32[104,128]{1,0:T(8,128)S(1)} %get-tuple-element.129.refs_0_), channel_id=1, source_target_pairs={{0,4},{4,0},{8,12},{12,8},{16,20},{20,16},{24,28},{28,24},{1,5},{5... | collective-permute-start | bytes 159752 | tf_op jit(solution)/shard_map/ppermute | solution.py:386
  40.4 2.6 %collective-permute-start.13 = (f32[8,256]{1,0:T(8,128)S(1)}, f32[8,256]{1,0:T(8,128)S(1)}, u32[]{:S(2)}, u32[]{:S(2)}) collective-permute-start(f32[8,256]{1,0:T(8,128)S(1)} %get-tuple-element.133), channel_id=1, source_target_pairs={{0,3},{1,2},{2,1},{3,0},{4,7},{5,6},{6,5},{7,4},{8,11},{9,10},{10,... | collective-permute-start | bytes 24584 | tf_op jit(solution)/shard_map/ppermute | solution.py:395
  42.9 7.6 %collective-permute-start.14 = (f32[8,256]{1,0:T(8,128)S(1)}, f32[8,256]{1,0:T(8,128)S(1)}, u32[]{:S(2)}, u32[]{:S(2)}) collective-permute-start(f32[8,256]{1,0:T(8,128)S(1)} %get-tuple-element.134), channel_id=1, source_target_pairs={{0,8},{4,12},{8,0},{12,4},{16,24},{20,28},{24,16},{28,20},{1,9},{5... | collective-permute-start | bytes 24584 | tf_op jit(solution)/shard_map/ppermute | solution.py:386
  52.4 2.7 %collective-permute-done.15.refs_4_ = f32[8,256]{1,0:T(8,128)S(1)} collective-permute-done((f32[8,256]{1,0:T(8,128)S(1)}, f32[8,256]{1,0:T(8,128)S(1)}, u32[]{:S(2)}, u32[]{:S(2)}) %collective-permute-start.15) | collective-permute-done | bytes 8224 | tf_op jit(solution)/shard_map/ppermute | solution.py:395
  58.3 2.0 %collective-permute-start.17 = (f32[8,256]{1,0:T(8,128)S(1)}, f32[8,256]{1,0:T(8,128)S(1)}, u32[]{:S(2)}, u32[]{:S(2)}) collective-permute-start(f32[8,256]{1,0:T(8,128)S(1)} %coarse.6.refs_4_), channel_id=1, source_target_pairs={{0,1},{1,0},{2,3},{3,2},{4,5},{5,4},{6,7},{7,6},{8,9},{9,8},{10,11... | collective-permute-start | bytes 24584 | tf_op jit(solution)/shard_map/ppermute | solution.py:395
  63.3 3.0 %collective-permute-start.22 = (f32[8,128]{1,0:T(8,128)S(1)}, f32[8,128]{1,0:T(8,128)S(1)}, u32[]{:S(2)}, u32[]{:S(2)}) collective-permute-start(f32[8,128]{1,0:T(8,128)S(1)} %get-tuple-element.140.refs_4_), channel_id=1, source_target_pairs={{0,16},{4,20},{8,24},{12,28},{16,0},{20,4},{24,8},{28,12},{1,17},{... | collective-permute-start | bytes 12296 | tf_op jit(solution)/shard_map/ppermute | solution.py:386
  72.5 2.6 %collective-permute-start.25 = (f32[8,256]{1,0:T(8,128)S(1)}, f32[8,256]{1,0:T(8,128)S(1)}, u32[]{:S(2)}, u32[]{:S(2)}) collective-permute-start(f32[8,256]{1,0:T(8,128)S(1)} %get-tuple-element.147), channel_id=1, source_target_pairs={{0,3},{1,2},{2,1},{3,0},{4,7},{5,6},{6,5},{7,4},{8,11},{9,10},{10,... | collective-permute-start | bytes 24584 | tf_op jit(solution)/shard_map/ppermute | solution.py:395
  75.1 5.8 %collective-permute-start.26 = (f32[8,256]{1,0:T(8,128)S(1)}, f32[8,256]{1,0:T(8,128)S(1)}, u32[]{:S(2)}, u32[]{:S(2)}) collective-permute-start(f32[8,256]{1,0:T(8,128)S(1)} %get-tuple-element.148), channel_id=1, source_target_pairs={{0,8},{4,12},{8,0},{12,4},{16,24},{20,28},{24,16},{28,20},{1,9},{5... | collective-permute-start | bytes 24584 | tf_op jit(solution)/shard_map/ppermute | solution.py:386
  82.8 2.7 %collective-permute-done.27.refs_4_ = f32[8,256]{1,0:T(8,128)S(1)} collective-permute-done((f32[8,256]{1,0:T(8,128)S(1)}, f32[8,256]{1,0:T(8,128)S(1)}, u32[]{:S(2)}, u32[]{:S(2)}) %collective-permute-start.27) | collective-permute-done | bytes 8224 | tf_op jit(solution)/shard_map/ppermute | solution.py:395
  88.7 2.0 %collective-permute-start.29 = (f32[8,256]{1,0:T(8,128)S(1)}, f32[8,256]{1,0:T(8,128)S(1)}, u32[]{:S(2)}, u32[]{:S(2)}) collective-permute-start(f32[8,256]{1,0:T(8,128)S(1)} %coarse.7.refs_4_), channel_id=1, source_target_pairs={{0,1},{1,0},{2,3},{3,2},{4,5},{5,4},{6,7},{7,6},{8,9},{9,8},{10,11... | collective-permute-start | bytes 24584 | tf_op jit(solution)/shard_map/ppermute | solution.py:395
  93.7 3.0 %collective-permute-start.34 = (f32[8,128]{1,0:T(8,128)S(1)}, f32[8,128]{1,0:T(8,128)S(1)}, u32[]{:S(2)}, u32[]{:S(2)}) collective-permute-start(f32[8,128]{1,0:T(8,128)S(1)} %get-tuple-element.154.refs_4_), channel_id=1, source_target_pairs={{0,16},{4,20},{8,24},{12,28},{16,0},{20,4},{24,8},{28,12},{1,17},{... | collective-permute-start | bytes 12296 | tf_op jit(solution)/shard_map/ppermute | solution.py:386
  102.6 2.6 %collective-permute-start.37 = (f32[8,256]{1,0:T(8,128)S(1)}, f32[8,256]{1,0:T(8,128)S(1)}, u32[]{:S(2)}, u32[]{:S(2)}) collective-permute-start(f32[8,256]{1,0:T(8,128)S(1)} %get-tuple-element.172), channel_id=1, source_target_pairs={{0,3},{1,2},{2,1},{3,0},{4,7},{5,6},{6,5},{7,4},{8,11},{9,10},{10,... | collective-permute-start | bytes 24584 | tf_op jit(solution)/shard_map/ppermute | solution.py:395
  105.1 6.2 %collective-permute-start.38 = (f32[8,256]{1,0:T(8,128)S(1)}, f32[8,256]{1,0:T(8,128)S(1)}, u32[]{:S(2)}, u32[]{:S(2)}) collective-permute-start(f32[8,256]{1,0:T(8,128)S(1)} %get-tuple-element.173), channel_id=1, source_target_pairs={{0,8},{4,12},{8,0},{12,4},{16,24},{20,28},{24,16},{28,20},{1,9},{5... | collective-permute-start | bytes 24584 | tf_op jit(solution)/shard_map/ppermute | solution.py:386
  113.2 2.6 %collective-permute-done.39.refs_4_ = f32[8,256]{1,0:T(8,128)S(1)} collective-permute-done((f32[8,256]{1,0:T(8,128)S(1)}, f32[8,256]{1,0:T(8,128)S(1)}, u32[]{:S(2)}, u32[]{:S(2)}) %collective-permute-start.39) | collective-permute-done | bytes 8224 | tf_op jit(solution)/shard_map/ppermute | solution.py:395
  124.1 3.0 %collective-permute-start.46 = (f32[8,128]{1,0:T(8,128)S(1)}, f32[8,128]{1,0:T(8,128)S(1)}, u32[]{:S(2)}, u32[]{:S(2)}) collective-permute-start(f32[8,128]{1,0:T(8,128)S(1)} %get-tuple-element.179.refs_4_), channel_id=1, source_target_pairs={{0,16},{4,20},{8,24},{12,28},{16,0},{20,4},{24,8},{28,12},{1,17},{... | collective-permute-start | bytes 12296 | tf_op jit(solution)/shard_map/ppermute | solution.py:386
  132.9 2.6 %collective-permute-start.49 = (f32[8,256]{1,0:T(8,128)S(1)}, f32[8,256]{1,0:T(8,128)S(1)}, u32[]{:S(2)}, u32[]{:S(2)}) collective-permute-start(f32[8,256]{1,0:T(8,128)S(1)} %get-tuple-element.208), channel_id=1, source_target_pairs={{0,3},{1,2},{2,1},{3,0},{4,7},{5,6},{6,5},{7,4},{8,11},{9,10},{10,... | collective-permute-start | bytes 24584 | tf_op jit(solution)/shard_map/ppermute | solution.py:395
  143.2 2.0 %collective-permute-start.52 = (f32[8,256]{1,0:T(8,128)S(1)}, f32[8,256]{1,0:T(8,128)S(1)}, u32[]{:S(2)}, u32[]{:S(2)}) collective-permute-start(f32[8,256]{1,0:T(8,128)S(1)} %coarse.9.refs_4_), channel_id=1, source_target_pairs={{0,1},{1,0},{2,3},{3,2},{4,5},{5,4},{6,7},{7,6},{8,9},{9,8},{10,11... | collective-permute-start | bytes 24584 | tf_op jit(solution)/shard_map/ppermute | solution.py:395
  150.2 17.8 %all_to_all.5.dots_ref = f32[32,1,128]{2,1,0:T(1,128)S(1)} all-to-all(f32[32,1,128]{2,1,0:T(1,128)S(1)} %gram.1), channel_id=1, replica_groups=mesh['sub'=8,'grp'=4] {'sub','grp'}, dimensions={0} | all-to-all | bytes 32768 | tf_op jit(solution)/shard_map/all_to_all | solution.py:546
  (124 shorter events, 74.1 us)
Async XLA Ops:
  0.6 5.0 %collective-permute-start = (f32[96,128]{1,0:T(8,128)}, f32[96,128]{1,0:T(8,128)S(1)}, u32[]{:S(2)}, u32[]{:S(2)}) collective-permute-start(f32[96,128]{1,0:T(8,128)} %bitcast.18), channel_id=1, source_target_pairs={{0,4},{4,8},{8,12},{12,16},{16,20},{20,24},{24,28},{1,5},{5,9},{9,... | collective-permute-start | bytes 147464 | tf_op jit(solution)/shard_map/ppermute | solution.py:382
  11.5 5.5 %collective-permute-start.3 = (f32[8,256]{1,0:T(8,128)S(1)}, f32[8,256]{1,0:T(8,128)S(1)}, u32[]{:S(2)}, u32[]{:S(2)}) collective-permute-start(f32[8,256]{1,0:T(8,128)S(1)} %get-tuple-element.121), channel_id=1, source_target_pairs={{0,3},{1,2},{2,1},{3,0},{4,7},{5,6},{6,5},{7,4},{8,11},{9,10},{10,... | collective-permute-start | bytes 24584 | tf_op jit(solution)/shard_map/ppermute | solution.py:395
  20.5 5.5 %collective-permute-start.8 = (f32[8,256]{1,0:T(8,128)S(1)}, f32[8,256]{1,0:T(8,128)S(1)}, u32[]{:S(2)}, u32[]{:S(2)}) collective-permute-start(f32[8,256]{1,0:T(8,128)S(1)} %coarse.5.refs_4_), channel_id=1, source_target_pairs={{0,3},{1,2},{2,1},{3,0},{4,7},{5,6},{6,5},{7,4},{8,11},{9,10},{10,... | collective-permute-start | bytes 24584 | tf_op jit(solution)/shard_map/ppermute | solution.py:395
  31.5 8.2 %collective-permute-start.12 = (f32[104,128]{1,0:T(8,128)S(1)}, f32[104,128]{1,0:T(8,128)S(1)}, u32[]{:S(2)}, u32[]{:S(2)}) collective-permute-start(f32[104,128]{1,0:T(8,128)S(1)} %get-tuple-element.129.refs_0_), channel_id=1, source_target_pairs={{0,4},{4,0},{8,12},{12,8},{16,20},{20,16},{24,28},{28,24},{1,5},{5... | collective-permute-start | bytes 159752 | tf_op jit(solution)/shard_map/ppermute | solution.py:386
  40.4 12.1 %collective-permute-start.13 = (f32[8,256]{1,0:T(8,128)S(1)}, f32[8,256]{1,0:T(8,128)S(1)}, u32[]{:S(2)}, u32[]{:S(2)}) collective-permute-start(f32[8,256]{1,0:T(8,128)S(1)} %get-tuple-element.133), channel_id=1, source_target_pairs={{0,3},{1,2},{2,1},{3,0},{4,7},{5,6},{6,5},{7,4},{8,11},{9,10},{10,... | collective-permute-start | bytes 24584 | tf_op jit(solution)/shard_map/ppermute | solution.py:395
  42.9 9.5 %collective-permute-start.14 = (f32[8,256]{1,0:T(8,128)S(1)}, f32[8,256]{1,0:T(8,128)S(1)}, u32[]{:S(2)}, u32[]{:S(2)}) collective-permute-start(f32[8,256]{1,0:T(8,128)S(1)} %get-tuple-element.134), channel_id=1, source_target_pairs={{0,8},{4,12},{8,0},{12,4},{16,24},{20,28},{24,16},{28,20},{1,9},{5... | collective-permute-start | bytes 24584 | tf_op jit(solution)/shard_map/ppermute | solution.py:386
  55.9 5.5 %collective-permute-start.19 = (f32[8,256]{1,0:T(8,128)S(1)}, f32[8,256]{1,0:T(8,128)S(1)}, u32[]{:S(2)}, u32[]{:S(2)}) collective-permute-start(f32[8,256]{1,0:T(8,128)S(1)} %coarse.6.refs_4_), channel_id=1, source_target_pairs={{0,3},{1,2},{2,1},{3,0},{4,7},{5,6},{6,5},{7,4},{8,11},{9,10},{10,... | collective-permute-start | bytes 24584 | tf_op jit(solution)/shard_map/ppermute | solution.py:395
  62.5 5.3 %collective-permute-start.21 = (f32[96,128]{1,0:T(8,128)S(1)}, f32[96,128]{1,0:T(8,128)S(1)}, u32[]{:S(2)}, u32[]{:S(2)}) collective-permute-start(f32[96,128]{1,0:T(8,128)S(1)} %get-tuple-element.138.refs_0_), channel_id=1, source_target_pairs={{0,4},{4,0},{8,12},{12,8},{16,20},{20,16},{24,28},{28,24},{1,5},{5... | collective-permute-start | bytes 147464 | tf_op jit(solution)/shard_map/ppermute | solution.py:386
  62.6 5.2 %collective-permute-start.20 = (f32[96,128]{1,0:T(8,128)S(1)}, f32[96,128]{1,0:T(8,128)S(1)}, u32[]{:S(2)}, u32[]{:S(2)}) collective-permute-start(f32[96,128]{1,0:T(8,128)S(1)} %get-tuple-element.139.refs_1_), channel_id=1, source_target_pairs={{4,8},{8,4},{12,16},{16,12},{20,24},{24,20},{5,9},{9,5},{13,17},{1... | collective-permute-start | bytes 147464 | tf_op jit(solution)/shard_map/ppermute | solution.py:391
  72.5 10.3 %collective-permute-start.25 = (f32[8,256]{1,0:T(8,128)S(1)}, f32[8,256]{1,0:T(8,128)S(1)}, u32[]{:S(2)}, u32[]{:S(2)}) collective-permute-start(f32[8,256]{1,0:T(8,128)S(1)} %get-tuple-element.147), channel_id=1, source_target_pairs={{0,3},{1,2},{2,1},{3,0},{4,7},{5,6},{6,5},{7,4},{8,11},{9,10},{10,... | collective-permute-start | bytes 24584 | tf_op jit(solution)/shard_map/ppermute | solution.py:395
  75.1 7.7 %collective-permute-start.26 = (f32[8,256]{1,0:T(8,128)S(1)}, f32[8,256]{1,0:T(8,128)S(1)}, u32[]{:S(2)}, u32[]{:S(2)}) collective-permute-start(f32[8,256]{1,0:T(8,128)S(1)} %get-tuple-element.148), channel_id=1, source_target_pairs={{0,8},{4,12},{8,0},{12,4},{16,24},{20,28},{24,16},{28,20},{1,9},{5... | collective-permute-start | bytes 24584 | tf_op jit(solution)/shard_map/ppermute | solution.py:386
  86.3 5.5 %collective-permute-start.31 = (f32[8,256]{1,0:T(8,128)S(1)}, f32[8,256]{1,0:T(8,128)S(1)}, u32[]{:S(2)}, u32[]{:S(2)}) collective-permute-start(f32[8,256]{1,0:T(8,128)S(1)} %coarse.7.refs_4_), channel_id=1, source_target_pairs={{0,3},{1,2},{2,1},{3,0},{4,7},{5,6},{6,5},{7,4},{8,11},{9,10},{10,... | collective-permute-start | bytes 24584 | tf_op jit(solution)/shard_map/ppermute | solution.py:395
  92.9 5.3 %collective-permute-start.33 = (f32[96,128]{1,0:T(8,128)S(1)}, f32[96,128]{1,0:T(8,128)S(1)}, u32[]{:S(2)}, u32[]{:S(2)}) collective-permute-start(f32[96,128]{1,0:T(8,128)S(1)} %get-tuple-element.152.refs_0_), channel_id=1, source_target_pairs={{0,4},{4,0},{8,12},{12,8},{16,20},{20,16},{24,28},{28,24},{1,5},{5... | collective-permute-start | bytes 147464 | tf_op jit(solution)/shard_map/ppermute | solution.py:386
  93.0 5.3 %collective-permute-start.32 = (f32[96,128]{1,0:T(8,128)S(1)}, f32[96,128]{1,0:T(8,128)S(1)}, u32[]{:S(2)}, u32[]{:S(2)}) collective-permute-start(f32[96,128]{1,0:T(8,128)S(1)} %get-tuple-element.153.refs_1_), channel_id=1, source_target_pairs={{4,8},{8,4},{12,16},{16,12},{20,24},{24,20},{5,9},{9,5},{13,17},{1... | collective-permute-start | bytes 147464 | tf_op jit(solution)/shard_map/ppermute | solution.py:391
  102.6 10.7 %collective-permute-start.37 = (f32[8,256]{1,0:T(8,128)S(1)}, f32[8,256]{1,0:T(8,128)S(1)}, u32[]{:S(2)}, u32[]{:S(2)}) collective-permute-start(f32[8,256]{1,0:T(8,128)S(1)} %get-tuple-element.172), channel_id=1, source_target_pairs={{0,3},{1,2},{2,1},{3,0},{4,7},{5,6},{6,5},{7,4},{8,11},{9,10},{10,... | collective-permute-start | bytes 24584 | tf_op jit(solution)/shard_map/ppermute | solution.py:395
  105.1 8.1 %collective-permute-start.38 = (f32[8,256]{1,0:T(8,128)S(1)}, f32[8,256]{1,0:T(8,128)S(1)}, u32[]{:S(2)}, u32[]{:S(2)}) collective-permute-start(f32[8,256]{1,0:T(8,128)S(1)} %get-tuple-element.173), channel_id=1, source_target_pairs={{0,8},{4,12},{8,0},{12,4},{16,24},{20,28},{24,16},{28,20},{1,9},{5... | collective-permute-start | bytes 24584 | tf_op jit(solution)/shard_map/ppermute | solution.py:386
  116.7 5.5 %collective-permute-start.43 = (f32[8,256]{1,0:T(8,128)S(1)}, f32[8,256]{1,0:T(8,128)S(1)}, u32[]{:S(2)}, u32[]{:S(2)}) collective-permute-start(f32[8,256]{1,0:T(8,128)S(1)} %coarse.8.refs_4_), channel_id=1, source_target_pairs={{0,3},{1,2},{2,1},{3,0},{4,7},{5,6},{6,5},{7,4},{8,11},{9,10},{10,... | collective-permute-start | bytes 24584 | tf_op jit(solution)/shard_map/ppermute | solution.py:395
  123.3 5.4 %collective-permute-start.45 = (f32[96,128]{1,0:T(8,128)S(1)}, f32[96,128]{1,0:T(8,128)S(1)}, u32[]{:S(2)}, u32[]{:S(2)}) collective-permute-start(f32[96,128]{1,0:T(8,128)S(1)} %get-tuple-element.177.refs_0_), channel_id=1, source_target_pairs={{0,4},{4,0},{8,12},{12,8},{16,20},{20,16},{24,28},{28,24},{1,5},{5... | collective-permute-start | bytes 147464 | tf_op jit(solution)/shard_map/ppermute | solution.py:386
  123.4 5.3 %collective-permute-start.44 = (f32[96,128]{1,0:T(8,128)S(1)}, f32[96,128]{1,0:T(8,128)S(1)}, u32[]{:S(2)}, u32[]{:S(2)}) collective-permute-start(f32[96,128]{1,0:T(8,128)S(1)} %get-tuple-element.178.refs_1_), channel_id=1, source_target_pairs={{4,8},{8,4},{12,16},{16,12},{20,24},{24,20},{5,9},{9,5},{13,17},{1... | collective-permute-start | bytes 147464 | tf_op jit(solution)/shard_map/ppermute | solution.py:391
  124.1 4.6 %collective-permute-start.46 = (f32[8,128]{1,0:T(8,128)S(1)}, f32[8,128]{1,0:T(8,128)S(1)}, u32[]{:S(2)}, u32[]{:S(2)}) collective-permute-start(f32[8,128]{1,0:T(8,128)S(1)} %get-tuple-element.179.refs_4_), channel_id=1, source_target_pairs={{0,16},{4,20},{8,24},{12,28},{16,0},{20,4},{24,8},{28,12},{1,17},{... | collective-permute-start | bytes 12296 | tf_op jit(solution)/shard_map/ppermute | solution.py:386
  132.9 5.5 %collective-permute-start.49 = (f32[8,256]{1,0:T(8,128)S(1)}, f32[8,256]{1,0:T(8,128)S(1)}, u32[]{:S(2)}, u32[]{:S(2)}) collective-permute-start(f32[8,256]{1,0:T(8,128)S(1)} %get-tuple-element.208), channel_id=1, source_target_pairs={{0,3},{1,2},{2,1},{3,0},{4,7},{5,6},{6,5},{7,4},{8,11},{9,10},{10,... | collective-permute-start | bytes 24584 | tf_op jit(solution)/shard_map/ppermute | solution.py:395
  140.8 5.5 %collective-permute-start.54 = (f32[8,256]{1,0:T(8,128)S(1)}, f32[8,256]{1,0:T(8,128)S(1)}, u32[]{:S(2)}, u32[]{:S(2)}) collective-permute-start(f32[8,256]{1,0:T(8,128)S(1)} %coarse.9.refs_4_), channel_id=1, source_target_pairs={{0,3},{1,2},{2,1},{3,0},{4,7},{5,6},{6,5},{7,4},{8,11},{9,10},{10,... | collective-permute-start | bytes 24584 | tf_op jit(solution)/shard_map/ppermute | solution.py:395
  147.5 20.5 %collective-permute-start.56 = (f32[96,128]{1,0:T(8,128)S(1)}, f32[96,128]{1,0:T(8,128)S(1)}, u32[]{:S(2)}, u32[]{:S(2)}) collective-permute-start(f32[96,128]{1,0:T(8,128)S(1)} %get-tuple-element.216.near_ref), channel_id=1, source_target_pairs={{0,4},{4,0},{8,12},{12,8},{16,20},{20,16},{24,28},{28,24},{1,5},{5... | collective-permute-start | bytes 147464 | tf_op jit(solution)/shard_map/ppermute | solution.py:386
  149.3 18.7 %collective-permute-start.55 = (f32[96,128]{1,0:T(8,128)S(1)}, f32[96,128]{1,0:T(8,128)S(1)}, u32[]{:S(2)}, u32[]{:S(2)}) collective-permute-start(f32[96,128]{1,0:T(8,128)S(1)} %get-tuple-element.217.far_ref), channel_id=1, source_target_pairs={{4,8},{8,4},{12,16},{16,12},{20,24},{24,20},{5,9},{9,5},{13,17},{1... | collective-permute-start | bytes 147464 | tf_op jit(solution)/shard_map/ppermute | solution.py:391
  (35 other events, 142.4 us)
